TPU v7x, 32 devices: a whole 2x2x4 slice. The times are simulated.
32 devices in a mesh: cache: 8 (over y, x, core), batch: 4 (over z).
Axes of the slice: x: 2, y: 2, z: 4, core: 2. Of those that a mesh axis runs over, the one named last changes fastest.
Arguments:
- queries: bfloat16 [3, 4096, 768], P(None, 'batch')
- positives: int32 [3, 4096], P(None, 'batch'), may hold values from 0 to 511
- block_list: int32 [3, 32, 48], P(None, 'batch'), may hold values from 0 to 63
- block_count: int32 [3, 32], P(None, 'batch'), may hold values from 1 to 48
- refresh_owner: int32 [3], replicated, may hold values from 0 to 7, as said below
- cache: float32 [8192, 768], P('cache'), may hold values from -6 to 6
- fresh: float32 [4096, 768], P('cache')
Outputs:
- query_grad: float32 [3, 4096, 768], P(None, ('batch', 'cache'))
- cache_grad: float32 [8192, 768], P('cache')
Inputs may be any that keep to these rules, and one draw needn't show every extreme that they name: `refresh_owner`: 3 different owners; owner 0 and owner 8 - 1 are always among them.
All inputs are finite; a program needn't handle non-finite values.
Results may differ from a plain program's by a relative error of at most 0.0003.
Values sent between devices are 32-bit elements; how exact they have to be, the bound alone decides.
No kernel may reach another device: no remote copies, remote signals or barrier semaphores. Data moves between devices by JAX's collectives and lax.ppermute only.
A program may use at most 128 MiB of HBM per device.

v0:
```python
import math

import jax
import jax.numpy as jnp
from jax import lax
from jax.sharding import PartitionSpec as P

BLK = 128


def broadcast(block, axis, holder):
    block = jnp.where(lax.axis_index(axis) == holder, block, jnp.zeros_like(block))
    return lax.psum(block, axis)


def on_device(queries, positives, block_list, block_count, refresh_owner, cache, fresh):
    highest = lax.Precision.HIGHEST
    steps, group_rows, width = queries.shape
    cache_rows = cache.shape[0]
    slab_rows = fresh.shape[0]
    owners = lax.axis_size("cache")
    own_index = lax.axis_index("cache")
    share = group_rows // owners
    home_start = own_index * share
    group_blocks = block_list.shape[1]
    list_width = block_list.shape[2]
    own_blocks = cache_rows // BLK
    scale = 2.0 / math.sqrt(width)
    block_ids = own_index * own_blocks + jnp.arange(own_blocks, dtype=jnp.int32)
    current = cache
    grad_total = jnp.zeros((cache_rows, width), jnp.float32)
    results = []
    for step in range(steps):
        owner = refresh_owner[step]
        is_owner = owner == own_index
        refreshed = jnp.concatenate([fresh, current[slab_rows:]], axis=0)
        current = jnp.where(is_owner, refreshed, current)
        valid = jnp.arange(list_width, dtype=jnp.int32)[None, :] < block_count[step][:, None]
        hits = (block_list[step][:, :, None] == block_ids[None, None, :]) & valid[:, :, None]
        member = jnp.any(hits, axis=1)
        mask = jnp.broadcast_to(member[:, None, :, None], (group_blocks, BLK, own_blocks, BLK))
        mask = mask.reshape(group_rows, cache_rows)
        query_rows = queries[step].astype(jnp.float32)
        scores = scale * jnp.dot(query_rows, current.T, precision=highest)
        scores = jnp.where(mask, scores, -1e30)
        peak = jnp.max(scores, axis=1)
        slab = broadcast(fresh, "cache", owner)
        home_queries = lax.dynamic_slice_in_dim(query_rows, home_start, share, 0)
        slab_scores = scale * jnp.dot(home_queries, slab.T, precision=highest)
        filler = jnp.full((group_rows,), -1e30, jnp.float32)
        slab_peak = lax.dynamic_update_slice_in_dim(
            filler, jnp.max(slab_scores, axis=1), home_start, 0
        )
        peak = jnp.maximum(peak, slab_peak)
        top = lax.pmax(peak, "cache")
        total = jnp.sum(jnp.where(mask, jnp.exp(scores - top[:, None]), 0.0), axis=1)
        home_top = lax.dynamic_slice_in_dim(top, home_start, share, 0)
        slab_total = jnp.sum(jnp.exp(slab_scores - home_top[:, None]), axis=1)
        home_part = lax.dynamic_slice_in_dim(total, home_start, share, 0) + slab_total
        total = lax.dynamic_update_slice_in_dim(total, home_part, home_start, 0)
        total = lax.psum(total, "cache")
        lse = top + jnp.log(total)
        probs = jnp.exp(scores - lse[:, None])
        home_lse = lax.dynamic_slice_in_dim(lse, home_start, share, 0)
        slab_probs = jnp.exp(slab_scores - home_lse[:, None])
        home_pos = lax.dynamic_slice_in_dim(positives[step], home_start, share, 0)
        home_term = jnp.dot(slab_probs, slab, precision=highest) - jnp.take(slab, home_pos, axis=0)
        term = jnp.dot(probs, current, precision=highest)
        mine = lax.psum_scatter(term, "cache", scatter_dimension=0, tiled=True)
        mine = mine + home_term
        results.append(mine)
        step_grad = lax.dot_general(probs, query_rows, (((0,), (0,)), ((), ())), precision=highest)
        grad_total = grad_total + lax.psum(step_grad, "batch")
    return (jnp.stack(results, axis=0), grad_total)


def solution(mesh):
    return jax.shard_map(
        on_device,
        mesh=mesh,
        in_specs=(
            P(None, "batch", None),
            P(None, "batch"),
            P(None, "batch", None),
            P(None, "batch"),
            P(),
            P("cache", None),
            P("cache", None),
        ),
        out_specs=(P(None, ("batch", "cache"), None), P("cache", None)),
        check_vma=False,
    )
```

profile of v0, /device:TPU:0, one launch (start us, length us, event | category | flops | bytes accessed | tf_op | source)
XLA Modules:
  0.0 463.3 jit_solution(12410919920110843743)
XLA Ops:
  7.2 1.4 fusion.62
  10.5 3.8 broadcast_select_fusion.2
  16.6 1.9 copy-done.8
  18.5 0.4 fusion.6
  19.0 0.4 fusion.7
  19.4 1.1 copy-done.3
  20.7 1.6 copy-done.5
  22.4 0.6 and_reduce_fusion.2
  23.2 4.8 %fusion.60 = (bf16[1,1024,768]{2,1,0:T(8,128)(2,1)}, bf16[1,1024,768]{2,1,0:T(8,128)(2,1)}, bf16[1,1024,768]{2,1,0:T(8,128)(2,1)}) fusion(bf16[3,1024,768]{2,1,0:T(8,128)(2,1)} %param.9), kind=kLoop, calls=%fused_computation.116 | loop fusion | bytes 9437184 | tf_op jit(solution)/shard_map/slice | solution.py:43
  28.1 0.3 broadcast_in_dim.29
  28.5 9.4 %fusion.65 = (f32[1024]{0:T(1024)S(1)}, f32[1024,1024]{0,1:T(8,128)}) fusion(f32[1024,768]{1,0:T(8,128)S(1)} %copy-done.6, bf16[3,1024,768]{2,1,0:T(8,128)(2,1)} %param.9, pred[128,8,8,128]{3,2,1,0:T(8,128)(4,1)S(1)} %bitcast.113), kind=kOutput, calls=%fused_computation.121 | convolution fusion | flops 9666821120 | bytes 9965568 | tf_op jit(solution)/shard_map/dot_general | solution.py:44
  37.8 0.3 broadcast_in_dim.26
  38.2 7.3 %fusion.67 = (f32[1024]{0:T(1024)S(1)}, f32[1024,1024]{0,1:T(8,128)}) fusion(f32[1024,768]{1,0:T(8,128)S(1)} %copy-done.4, bf16[3,1024,768]{2,1,0:T(8,128)(2,1)S(1)} %bitcast.112, pred[128,8,8,128]{3,2,1,0:T(8,128)(4,1)S(1)} %bitcast.115), kind=kOutput, calls=%fused_computation.123 | convolution fusion | flops 9666821120 | bytes 9965568 | tf_op jit(solution)/shard_map/dot_general | solution.py:44
  45.5 0.3 broadcast_in_dim.30
  45.9 1.0 copy-done.17
  46.8 7.4 %fusion.63 = (f32[1024]{0:T(1024)S(1)}, f32[1024,1024]{0,1:T(8,128)}) fusion(bf16[3,1024,768]{2,1,0:T(8,128)(2,1)S(1)} %bitcast.112, f32[1024,768]{1,0:T(8,128)S(1)} %copy-done.6, f32[512,768]{1,0:T(8,128)S(1)} %copy-done, f32[512,768]{1,0:T(8,128)S(1)} %slice.79, pred[]{:T(512)S(6)} %eq.73, pred[128,8,8,128]{3,2,1,0:T(8,128)(4,1)S(1)} %bitcast.117), kind=kOutput, calls=%fused_computation.119 | convolution fusion | flops 9668393984 | bytes 13111297 | tf_op jit(solution)/shard_map/dot_general | solution.py:44
  54.3 50.2 %all-reduce.8.cloned.1.call-done = (f32[512,768]{1,0:T(8,128)}, f32[512,768]{1,0:T(8,128)}, f32[512,768]{1,0:T(8,128)}) async-done(((f32[512,768]{1,0:T(8,128)}, f32[512,768]{1,0:T(8,128)}, f32[512,768]{1,0:T(8,128)}), (f32[512,768]{1,0:T(8,128)}, f32[512,768]{1,0:T(8,128)}, f32[512,768]{1,0:T(8,128)})) %all-reduce.8.cloned.1.call-update) | async-done | bytes 4718608 | tf_op jit(solution)/shard_map/psum | solution.py:13
  104.5 3.3 fusion.64
  107.9 2.6 fusion.66
  110.5 0.2 dynamic_update_slice.20
  110.8 2.6 fusion.68
  113.4 0.6 dynamic_update_slice.18
  114.0 23.3 %all-reduce.2 = (f32[1024]{0:T(1024)S(1)}, f32[1024]{0:T(1024)S(1)}, f32[1024]{0:T(1024)S(1)}) all-reduce(f32[1024]{0:T(1024)S(1)} %max.17, f32[1024]{0:T(1024)S(1)} %max.16, f32[1024]{0:T(1024)S(1)} %max.15), channel_id=1, replica_groups=mesh['cache'=8,'batch'=4] {'cache'}, use_global_device_ids=true, to_apply=%region_22.24 | all-reduce | flops 3072 | bytes 24576 | tf_op jit(solution)/shard_map/pmax | solution.py:55
  137.3 3.7 select_reduce_fusion
  141.1 0.2 copy-done.14
  141.3 1.1 select_reduce_fusion.1
  142.5 0.8 copy-done.12
  143.3 0.3 copy-done.16
  143.6 1.1 select_reduce_fusion.2
  145.8 22.3 %all-reduce = (f32[1024]{0:T(1024)S(1)}, f32[1024]{0:T(1024)S(1)}, f32[1024]{0:T(1024)S(1)}) all-reduce(f32[1024]{0:T(1024)S(1)} %add_dynamic-update-slice_fusion, f32[1024]{0:T(1024)S(1)} %add_dynamic-update-slice_fusion.1, f32[1024]{0:T(1024)S(1)} %add_dynamic-update-slice_fusion.2), channel_id=1, replica_groups=mesh['cache'=8,'batch'=4] {'cache'}, use_global_device_ids=true, to_apply=%region_25.27 | all-reduce | flops 3072 | bytes 24576 | tf_op jit(solution)/shard_map/psum | solution.py:61
  168.1 15.0 %fusion.5 = f32[1024,768]{1,0:T(8,128)} fusion(f32[1024,1024]{0,1:T(8,128)} %get-tuple-element.40, f32[1024]{0:T(1024)S(1)} %log_add_fusion, f32[1024,768]{1,0:T(8,128)} %copy-done.5, f32[512,768]{1,0:T(8,128)S(1)} %copy-done, f32[512,768]{1,0:T(8,128)} %copy-done.9, pred[]{:T(512)S(6)} %eq.73), kind=kOutput, calls=%fused_computation.20 | convolution fusion | flops 9666297856 | bytes 13635585 | tf_op jit(solution)/shard_map/dot_general | solution.py:68
  183.1 14.5 %fusion.3 = f32[1024,768]{1,0:T(8,128)} fusion(f32[1024,768]{1,0:T(8,128)} %copy-done.5, f32[1024,1024]{0,1:T(8,128)} %get-tuple-element.44, f32[1024]{0:T(1024)S(1)} %log_add_fusion.1), kind=kOutput, calls=%fused_computation.18 | convolution fusion | flops 9664724992 | bytes 10489856 | tf_op jit(solution)/shard_map/dot_general | solution.py:68
  197.8 14.3 %fusion.1 = f32[1024,768]{1,0:T(8,128)} fusion(f32[1024,768]{1,0:T(8,128)} %copy-done.3, f32[1024,1024]{0,1:T(8,128)} %get-tuple-element.48, f32[1024]{0:T(1024)S(1)} %log_add_fusion.2), kind=kOutput, calls=%fused_computation.16 | convolution fusion | flops 9664724992 | bytes 10489856 | tf_op jit(solution)/shard_map/dot_general | solution.py:68
  212.2 8.2 %fusion = f32[1024,768]{1,0:T(8,128)S(1)} fusion(f32[1024,1024]{0,1:T(8,128)} %get-tuple-element.48, f32[1024]{0:T(1024)S(1)} %log_add_fusion.2, bf16[3,1024,768]{2,1,0:T(8,128)(2,1)} %param.9), kind=kOutput, calls=%fused_computation.15 | convolution fusion | flops 9664724992 | bytes 8916992 | tf_op jit(solution)/shard_map/dot_general | solution.py:72
  220.4 7.3 %fusion.2 = f32[1024,768]{1,0:T(8,128)S(1)} fusion(f32[1024,1024]{0,1:T(8,128)S(1)} %copy-done.11, f32[1024]{0:T(1024)S(1)} %log_add_fusion.1, bf16[3,1024,768]{2,1,0:T(8,128)(2,1)} %param.9), kind=kOutput, calls=%fused_computation.17 | convolution fusion | flops 9664724992 | bytes 8916992 | tf_op jit(solution)/shard_map/dot_general | solution.py:72
  227.7 8.8 %add_add_fusion = f32[1024,768]{1,0:T(8,128)} fusion(f32[1024,768]{1,0:T(8,128)S(1)} %fusion, f32[1024,768]{1,0:T(8,128)S(1)} %fusion.2, f32[1024,1024]{0,1:T(8,128)S(1)} %copy-done.7, f32[1024]{0:T(1024)S(1)} %log_add_fusion, bf16[3,1024,768]{2,1,0:T(8,128)(2,1)} %param.9), kind=kOutput, calls=%fused_computation.24 | convolution fusion | flops 9666297856 | bytes 15208448 | tf_op jit(solution)/shard_map/dot_general | solution.py:72
  236.6 0.7 copy-done.23
  237.6 3.2 gather_fusion.2
  240.8 1.8 gather_fusion.1
  242.6 1.6 gather_fusion
  244.2 3.6 fusion.24
  247.7 31.2 %reduce-scatter.6.cloned.1.call-done = f32[128,768]{1,0:T(8,128)} async-done(((f32[1024,768]{1,0:T(8,128)}), f32[128,768]{1,0:T(8,128)}) %reduce-scatter.6.cloned.1.call-update) | async-done | bytes 393232 | tf_op jit(solution)/shard_map/reduce_scatter | solution.py:69
  278.9 2.9 fusion.26
  281.8 47.6 %reduce-scatter.4.cloned.1.call-done = f32[128,768]{1,0:T(8,128)} async-done(((f32[1024,768]{1,0:T(8,128)}), f32[128,768]{1,0:T(8,128)}) %reduce-scatter.4.cloned.1.call-update) | async-done | bytes 393232 | tf_op jit(solution)/shard_map/reduce_scatter | solution.py:69
  329.4 2.2 fusion.28
  331.7 1.1 pad_maximum_fusion.3
  332.8 120.0 %all-reduce.6.cloned.1.call-done = f32[1024,768]{1,0:T(8,128)} async-done(((f32[1024,768]{1,0:T(8,128)}), f32[1024,768]{1,0:T(8,128)}) %all-reduce.6.cloned.1.call-update) | async-done | bytes 3145744 | tf_op jit(solution)/shard_map/psum | solution.py:73
  452.7 3.8 copy.31
  (99 shorter events, 2.9 us)
Async XLA Ops:
  7.2 97.3 %all-reduce.8.cloned.1.call-start = ((), (), s32[]{:S(2)}) async-start(), calls=%async_computation.7 | async-start | bytes 9437184 | tf_op jit(solution)/shard_map/psum | solution.py:13
  14.4 2.3 copy-start
  14.4 2.3 slice-start
  14.4 229.8 %reduce-scatter.8.cloned.1.call-start = ((), (), s32[]{:S(2)}) async-start(), calls=%async_computation.5 | async-start | bytes 3538944 | tf_op jit(solution)/shard_map/reduce_scatter | solution.py:69
  16.6 1.9 copy-start.8
  18.9 1.7 copy-start.3
  20.6 1.7 copy-start.5
  20.6 1.7 copy-start.22
  20.6 1.7 copy-start.24
  22.2 23.6 %copy-start.9 = (f32[512,768]{1,0:T(8,128)}, f32[512,768]{1,0:T(8,128)S(1)}, u32[]{:S(2)}) copy-start(f32[512,768]{1,0:T(8,128)S(1)} %slice.79) | copy-start | bytes 4718596
  23.2 5.2 %copy-start.6 = (f32[1024,768]{1,0:T(8,128)S(1)}, f32[1024,768]{1,0:T(8,128)}, u32[]{:S(2)}) copy-start(f32[1024,768]{1,0:T(8,128)} %copy-done.5) | copy-start | bytes 9437188
  28.1 10.1 %slice-start.1 = ((s8[4718592]{0:T(1024)(128)(4,1)}), s8[4194304]{0:T(1024)(128)(4,1)S(1)}, s32[]{:S(2)}) async-start(s8[4718592]{0:T(1024)(128)(4,1)} %bitcast.111), calls=%async_computation.9 | async-start | bytes 8388608
  28.4 9.4 %copy-start.13 = (pred[8,128,8,128]{1,0,3,2:T(8,128)(4,1)}, pred[8,128,8,128]{1,0,3,2:T(8,128)(4,1)S(1)}, u32[]{:S(2)}) copy-start(pred[8,128,8,128]{1,0,3,2:T(8,128)(4,1)S(1)} %broadcast_in_dim.29) | copy-start | bytes 3145732
  28.4 9.8 %copy-start.4 = (f32[1024,768]{1,0:T(8,128)S(1)}, f32[1024,768]{1,0:T(8,128)}, u32[]{:S(2)}) copy-start(f32[1024,768]{1,0:T(8,128)} %copy-done.3) | copy-start | bytes 9437188
  28.4 9.8 %slice-start.2 = ((s8[4718592]{0:T(1024)(128)(4,1)}), s8[524288]{0:T(1024)(128)(4,1)S(1)}, s32[]{:S(2)}) async-start(s8[4718592]{0:T(1024)(128)(4,1)} %bitcast.111), calls=%async_computation.10 | async-start | bytes 1048576
  38.2 7.3 %copy-start.15 = (pred[8,128,8,128]{1,0,3,2:T(8,128)(4,1)}, pred[8,128,8,128]{1,0,3,2:T(8,128)(4,1)S(1)}, u32[]{:S(2)}) copy-start(pred[8,128,8,128]{1,0,3,2:T(8,128)(4,1)S(1)} %broadcast_in_dim.26) | copy-start | bytes 3145732
  45.9 1.0 copy-start.17
  104.5 6.3 %copy-start.1 = (f32[512,768]{1,0:T(8,128)S(1)}, f32[512,768]{1,0:T(8,128)}, u32[]{:S(2)}) copy-start(f32[512,768]{1,0:T(8,128)} %get-tuple-element.11) | copy-start | bytes 4718596
  137.3 3.9 copy-start.10
  137.3 4.1 copy-start.14
  141.0 2.3 copy-start.12
  141.0 2.5 copy-start.16
  142.4 2.2 copy-start.18
  142.4 3.0 copy-start.19
  183.1 95.8 %reduce-scatter.6.cloned.1.call-start = ((), (), s32[]{:S(2)}) async-start(), calls=%async_computation.4 | async-start | bytes 3538944 | tf_op jit(solution)/shard_map/reduce_scatter | solution.py:69
  197.7 131.7 %reduce-scatter.4.cloned.1.call-start = ((), (), s32[]{:S(2)}) async-start(), calls=%async_computation.3 | async-start | bytes 3538944 | tf_op jit(solution)/shard_map/reduce_scatter | solution.py:69
  212.1 240.6 %all-reduce.6.cloned.1.call-start = ((), (), s32[]{:S(2)}) async-start(), calls=%async_computation.6 | async-start | bytes 6291456 | tf_op jit(solution)/shard_map/psum | solution.py:73
  212.2 8.2 %copy-start.11 = (f32[1024,1024]{0,1:T(8,128)S(1)}, f32[1024,1024]{0,1:T(8,128)}, u32[]{:S(2)}) copy-start(f32[1024,1024]{0,1:T(8,128)} %get-tuple-element.44) | copy-start | bytes 12582916
  220.4 7.3 %copy-start.7 = (f32[1024,1024]{0,1:T(8,128)S(1)}, f32[1024,1024]{0,1:T(8,128)}, u32[]{:S(2)}) copy-start(f32[1024,1024]{0,1:T(8,128)} %get-tuple-element.40) | copy-start | bytes 12582916
  236.5 0.7 copy-start.23
  236.5 4.2 copy-start.2
  281.8 49.8 %copy-start.20 = (f32[1,128,768]{2,1,0:T(8,128)S(1)}, f32[1,128,768]{2,1,0:T(8,128)}, u32[]{:S(2)}) copy-start(f32[1,128,768]{2,1,0:T(8,128)} %fusion.24) | copy-start | bytes 1179652
  281.8 49.8 %copy-start.21 = (f32[1,128,768]{2,1,0:T(8,128)S(1)}, f32[1,128,768]{2,1,0:T(8,128)}, u32[]{:S(2)}) copy-start(f32[1,128,768]{2,1,0:T(8,128)} %fusion.26) | copy-start | bytes 1179652
Sparse Core Ops, SparseCore 0:
  14.5 89.9 all-reduce.7
  183.2 46.0 reduce-scatter.7
  232.7 46.2 reduce-scatter.5
  283.1 46.2 reduce-scatter.3
  331.6 121.0 all-reduce.5
where the time goes:
time: 466 us; the launch traced here: 463 us
  waiting for transfers between devices  249 us (53%)
  matrix products  109 us (23%)
  blocking collectives  45.6 us (10%)
  local copies, waits for them, and re-layouts  27.1 us (6%)
  between operations  18.5 us (4%)
  other arithmetic  13.5 us (3%)
    psum x1, waiting for transfers between devices, on_device(): grad_total = grad_total + lax.psum(step_grad, 'batch')  120 us
    reduce_scatter x3, waiting for transfers between devices, on_device(): mine = lax.psum_scatter(term, 'cache', scatter_dimension=0, tiled=True)  78.8 us
    psum x1, waiting for transfers between devices, broadcast(): return lax.psum(block, axis)  50.2 us
    dot_general x3, matrix products, on_device(): term = jnp.dot(probs, current, precision=highest)  43.8 us
    dot_general x3, matrix products, on_device(): lax.dot_general(probs, query_rows, (((0,), (0,)), ((), ())), precision=hi...  24.3 us
    dot_general x3, matrix products, on_device(): scores = scale * jnp.dot(query_rows, current.T, precision=highest)  24.1 us
    pmax x1, blocking collectives, on_device(): top = lax.pmax(peak, 'cache')  23.3 us
    psum x1, blocking collectives, on_device(): total = lax.psum(total, 'cache')  22.3 us
  transfers between devices with their start and end apart: 5, of which 4 were waited for; matrix products, arithmetic and copies ran while one was open for 22% of the time, Pallas kernels for 0%

commit v1 on v0

v1 whole, which is shorter than its diff:
```python
import functools
import math

import jax
import jax.numpy as jnp
from jax import lax
from jax.experimental import pallas as pl
from jax.experimental.pallas import tpu as pltpu
from jax.sharding import PartitionSpec as P

BLK = 128
LOW = -1e30
VMEM_BYTES = 56 * 1024 * 1024


def dot(a, b, ca, cb):
    return lax.dot_general(a, b, (((ca,), (cb,)), ((), ())), preferred_element_type=jnp.float32)


def split(x):
    hi = x.astype(jnp.bfloat16)
    return hi, (x - hi.astype(jnp.float32)).astype(jnp.bfloat16)


def as_columns(row):
    return jnp.broadcast_to(row, (BLK, row.shape[1])).T


class Meta:
    def __init__(self, steps, groups, blocks, slab_blocks):
        self.steps, self.groups, self.blocks, self.slab_blocks = steps, groups, blocks, slab_blocks
        self.size = steps * groups * blocks

    def count(self, ref, s, b, j):
        return ref[(s * self.groups + b) * self.blocks + j]

    def member(self, ref, sb, j):
        return ref[self.size + sb * self.blocks + j]

    def own(self, ref, s):
        return ref[2 * self.size + s]

    def replaced(self, ref, s):
        return ref[2 * self.size + self.steps + s]

    def source(self, ref, s, j):
        return jnp.where((self.replaced(ref, s) > 0) & (j < self.slab_blocks), self.blocks + j, j)


def scores_kernel(meta, part, scale, info, q_ref, cache_ref, fresh_ref, z_ref, lse_ref, w_out, w_ref, mx, sem):
    i = pl.program_id(0)
    per = meta.groups // part
    s, first = i // per, (i % per) * part

    @pl.when(i == 0)
    def _():
        for src, at, n in ((cache_ref, 0, meta.blocks), (fresh_ref, meta.blocks, meta.slab_blocks)):
            def one(k, _, src=src, at=at):
                hi, lo = split(src[pl.ds(pl.multiple_of(k * BLK, BLK), BLK), :])
                w_ref[at + k, :BLK] = hi
                w_ref[at + k, BLK:] = lo
                return 0
            lax.fori_loop(0, n, one, 0)
        pltpu.make_async_copy(w_ref, w_out, sem).start()

    def block(j, _):
        both = dot(q_ref[0], w_ref[meta.source(info, s, j)], 1, 1)
        z = (both[:, :BLK] + both[:, BLK:]) * scale
        for b in range(part):
            zb = z[b * BLK:(b + 1) * BLK]
            z_ref[0, b, j] = zb
            zb = jnp.where(meta.count(info, s, first + b, j) > 0, zb, LOW)
            mx[b] = jnp.where(j > 0, jnp.maximum(mx[b], zb), zb)
        return 0

    lax.fori_loop(0, meta.blocks, block, 0)
    for b in range(part):
        top = jnp.max(mx[b], axis=1, keepdims=True)
        acc = jnp.zeros((BLK, BLK), jnp.float32)
        for j in range(meta.blocks):
            c = meta.count(info, s, first + b, j)
            acc += jnp.where(c > 0, jnp.exp(z_ref[0, b, j] - top), 0.0) * c.astype(jnp.float32)
        total = jnp.sum(acc, axis=1, keepdims=True)
        lse = jnp.where(total > 0, top + jnp.log(jnp.maximum(total, 1e-30)), LOW)
        lse_ref[0, b:b + 1, :] = jnp.broadcast_to(lse, (BLK, BLK)).T[:1]

    @pl.when(i == pl.num_programs(0) - 1)
    def _():
        pltpu.make_async_copy(w_ref, w_out, sem).wait()


def grad_kernel(meta, first, width, info, z_ref, q_ref, lse_ref, dep, out_ref, tok_ref, todo):
    j = first + pl.program_id(0)
    total = meta.steps * meta.groups

    def collect(sb, n):
        todo[n] = sb
        return n + meta.member(info, sb, j)

    n = lax.fori_loop(0, total, collect, 0)
    for g in range(width):
        todo[n + g] = 0
    out_ref[...] = jnp.zeros_like(out_ref)
    tok_ref[...] = jnp.zeros_like(tok_ref)

    def step(it, _):
        his, los, rows = [], [], []
        for g in range(width):
            k = it * width + g
            sb = todo[k]
            p = jnp.exp(z_ref[sb, 0].T - lse_ref[pl.ds(sb, 1), :])
            hi, lo = split(jnp.where(k < n, p, 0.0))
            his.append(hi)
            los.append(lo)
            rows.append(q_ref[sb])
        left = jnp.concatenate([jnp.concatenate(his, axis=1), jnp.concatenate(los, axis=1)], axis=0)
        acc = dot(left, jnp.concatenate(rows, axis=0), 1, 0)
        out_ref[...] += acc[:BLK] + acc[BLK:]
        return 0

    lax.fori_loop(0, (n + width - 1) // width, step, 0)


def term_kernel(meta, first, width, info, z_ref, w_ref, lse_ref, pos_ref, dep, old, out_ref, tok_ref, todo):
    b = first + pl.program_id(0)
    tok_ref[...] = jnp.zeros_like(tok_ref)
    lane = lax.broadcasted_iota(jnp.int32, (BLK, BLK), 1).astype(jnp.float32)

    def one_step(s, _):
        lse = as_columns(lse_ref[s, pl.ds(b, 1), :])
        pos = as_columns(pos_ref[s, pl.ds(b, 1), :]) - lane
        own = meta.own(info, s)

        def collect(j, n):
            todo[n] = j
            return n + (meta.count(info, s, b, j) > 0).astype(jnp.int32)

        n = lax.fori_loop(0, meta.blocks, collect, 0)
        for g in range(width):
            todo[n + g] = 0
        out_ref[0, s] = jnp.zeros(out_ref.shape[2:], jnp.float32)

        def step(it, _):
            his, los, chi, clo = [], [], [], []
            for g in range(width):
                k = it * width + g
                j = todo[k]
                p = jnp.exp(z_ref[s, 0, j] - lse) * meta.count(info, s, b, j).astype(jnp.float32)
                hot = (own > 0) & (j < meta.slab_blocks)
                p = p - jnp.where(pos == (j * BLK).astype(jnp.float32), hot.astype(jnp.float32), 0.0)
                hi, lo = split(jnp.where(k < n, p, 0.0))
                his.append(hi)
                los.append(lo)
                blk = meta.source(info, s, j)
                chi.append(w_ref[blk, :BLK])
                clo.append(w_ref[blk, BLK:])
            hi = jnp.concatenate(his, axis=1)
            acc = dot(jnp.concatenate([hi, jnp.concatenate(los, axis=1)], axis=0), jnp.concatenate(chi, axis=0), 1, 0)
            low = dot(hi, jnp.concatenate(clo, axis=0), 1, 0)
            out_ref[0, s] += acc[:BLK] + acc[BLK:] + low
            return 0

        lax.fori_loop(0, (n + width - 1) // width, step, 0)
        return 0

    lax.fori_loop(0, meta.steps, one_step, 0)


def params():
    return pltpu.CompilerParams(vmem_limit_bytes=VMEM_BYTES, dimension_semantics=("arbitrary",))


def whole(shape):
    return pl.BlockSpec(shape, lambda i, info: (0,) * len(shape))


def run_scores(meta, info, queries, cache, fresh):
    steps, rows, width = queries.shape
    part = min(4, meta.groups)
    per = meta.groups // part
    n_src = meta.blocks + meta.slab_blocks
    tok = (steps * meta.groups * meta.blocks) * BLK * BLK
    z, lse, w = pl.pallas_call(
        functools.partial(scores_kernel, meta, part, 2.0 / math.sqrt(width)),
        grid_spec=pltpu.PrefetchScalarGridSpec(
            num_scalar_prefetch=1,
            grid=(steps * per,),
            in_specs=[
                pl.BlockSpec((1, part * BLK, width), lambda i, info: (i // per, i % per, 0)),
                whole(cache.shape),
                whole(fresh.shape),
            ],
            out_specs=[
                pl.BlockSpec((1, part, meta.blocks, BLK, BLK), lambda i, info: (i // per, i % per, 0, 0, 0)),
                pl.BlockSpec((1, part, BLK), lambda i, info: (i, 0, 0)),
                pl.BlockSpec(memory_space=pl.ANY),
            ],
            scratch_shapes=[
                pltpu.VMEM((n_src, 2 * BLK, width), jnp.bfloat16),
                pltpu.VMEM((part, BLK, BLK), jnp.float32),
                pltpu.SemaphoreType.DMA,
            ],
        ),
        out_shape=[
            jax.ShapeDtypeStruct((steps, meta.groups, meta.blocks, BLK, BLK), jnp.float32),
            jax.ShapeDtypeStruct((steps * per, part, BLK), jnp.float32),
            jax.ShapeDtypeStruct((n_src, 2 * BLK, width), jnp.bfloat16),
        ],
        compiler_params=params(),
        cost_estimate=pl.CostEstimate(flops=4 * tok * width, bytes_accessed=30_000_000, transcendentals=tok),
        name="scores",
    )(info, queries, cache, fresh)
    return z, lse.reshape(steps, meta.groups, BLK), w


def run_grads(meta, info, z, queries, lse, first, count, dep):
    total = meta.steps * meta.groups
    width = queries.shape[-1]
    group = 4
    return pl.pallas_call(
        functools.partial(grad_kernel, meta, first, group),
        grid_spec=pltpu.PrefetchScalarGridSpec(
            num_scalar_prefetch=1,
            grid=(count,),
            in_specs=[
                pl.BlockSpec((total, 1, BLK, BLK), lambda i, info: (0, first + i, 0, 0)),
                whole((total, BLK, width)),
                whole((total, BLK)),
                pl.BlockSpec(memory_space=pl.ANY),
            ],
            out_specs=[pl.BlockSpec((BLK, width), lambda i, info: (i, 0)), whole((8, 128))],
            scratch_shapes=[pltpu.SMEM((total + group,), jnp.int32)],
        ),
        out_shape=[
            jax.ShapeDtypeStruct((count * BLK, width), jnp.float32),
            jax.ShapeDtypeStruct((8, 128), jnp.float32),
        ],
        compiler_params=params(),
        cost_estimate=pl.CostEstimate(
            flops=count * total * BLK * BLK * width * 2, bytes_accessed=count * 2_000_000 + 5_000_000, transcendentals=0),
        name="cache_grad",
    )(info, z.reshape(total, meta.blocks, BLK, BLK), queries.reshape(total, BLK, width), lse.reshape(total, BLK), dep)


def run_terms(meta, info, z, w, lse, pos, first, count, dep, old):
    width = w.shape[-1]
    group = 2
    shape = (meta.groups, meta.steps, BLK, width)
    aliased = old is not None
    return pl.pallas_call(
        functools.partial(term_kernel, meta, first, group),
        grid_spec=pltpu.PrefetchScalarGridSpec(
            num_scalar_prefetch=1,
            grid=(count,),
            in_specs=[
                pl.BlockSpec((meta.steps, 1, meta.blocks, BLK, BLK), lambda i, info: (0, first + i, 0, 0, 0)),
                whole(w.shape),
                whole(lse.shape),
                whole(pos.shape),
                pl.BlockSpec(memory_space=pl.ANY),
                pl.BlockSpec(memory_space=pl.ANY),
            ],
            out_specs=[
                pl.BlockSpec((1, meta.steps, BLK, width), lambda i, info: (first + i, 0, 0, 0)),
                whole((8, 128)),
            ],
            scratch_shapes=[pltpu.SMEM((meta.blocks + group,), jnp.int32)],
        ),
        out_shape=[jax.ShapeDtypeStruct(shape, jnp.float32), jax.ShapeDtypeStruct((8, 128), jnp.float32)],
        input_output_aliases={6: 0} if aliased else {},
        compiler_params=params(),
        cost_estimate=pl.CostEstimate(
            flops=count * meta.steps * meta.blocks * BLK * BLK * width * 3, bytes_accessed=count * 3_000_000 + 5_000_000,
            transcendentals=0),
        name="query_term",
    )(info, z, w, lse, pos, dep, old if aliased else dep)


def exchange_lse(lse):
    n = lax.axis_size("cache")
    bit = 1
    while bit < n:
        lse = jnp.logaddexp(lse, lax.ppermute(lse, "cache", [(i, i ^ bit) for i in range(n)]))
        bit *= 2
    return lse


def barrier(*values):
    return lax.optimization_barrier(tuple(values))


def sum_line(chunks, tok, jobs):
    if lax.axis_size("batch") != 4:
        out = [lax.psum(c, "batch") for c in chunks]
        for t in sorted(jobs):
            tok = jobs[t](tok)
        return out
    at = lax.axis_index("batch")
    end = (at == 0) | (at == 3)
    n, lag, ahead = len(chunks), 2, 3
    first, inner, second, total, third, out = {}, {}, {}, {}, {}, {}

    def send_in(k, value):
        first[k] = lax.ppermute(value, "batch", [(0, 1), (3, 2)])

    for k in range(ahead):
        send_in(k, chunks[k])
    prev = [tok]
    for t in range(n + 2 * lag):
        ops = []
        if t < n:
            ops += [chunks[t], first[t]]
        if 0 <= t - lag < n:
            ops += [inner[t - lag], second[t - lag]]
        if t >= 2 * lag:
            ops += [total[t - 2 * lag], third[t - 2 * lag]]
        if t - 1 in jobs:
            prev.append(jobs[t - 1](prev[0][:1, :1]))
        ops = list(barrier(*ops, *prev)[:len(ops)])
        new = []
        if t < n:
            new.append(ops[0] + ops[1])
            ops = ops[2:]
        if 0 <= t - lag < n:
            new.append(ops[0] + ops[1])
            ops = ops[2:]
        if t >= 2 * lag:
            new.append(jnp.where(end, ops[1], ops[0]))
        new = list(barrier(*new))
        prev = list(new)
        if t < n:
            inner[t] = new.pop(0)
            second[t] = lax.ppermute(inner[t], "batch", [(1, 2), (2, 1)])
        if 0 <= t - lag < n:
            total[t - lag] = new.pop(0)
            third[t - lag] = lax.ppermute(total[t - lag], "batch", [(1, 0), (2, 3)])
        if t >= 2 * lag:
            out[t - 2 * lag] = new.pop(0)
        if t + ahead < n:
            send_in(t + ahead, barrier(chunks[t + ahead], *prev)[0])
    return [out[k] for k in range(n)]


def on_device(queries, positives, block_list, block_count, refresh_owner, cache, fresh):
    steps, group_rows, width = queries.shape
    groups = group_rows // BLK
    blocks, slab_blocks = cache.shape[0] // BLK, fresh.shape[0] // BLK
    meta = Meta(steps, groups, blocks, slab_blocks)
    me = lax.axis_index("cache")
    block_ids = me * blocks + jnp.arange(blocks, dtype=jnp.int32)
    valid = jnp.arange(block_list.shape[2], dtype=jnp.int32)[None, None, :] < block_count[:, :, None]
    member = jnp.any((block_list[..., None] == block_ids) & valid[..., None], axis=2)
    own = refresh_owner == me
    counts = member.astype(jnp.int32) + (own[:, None, None] & (jnp.arange(blocks) < slab_blocks)).astype(jnp.int32)
    replaced = jnp.any(own[None, :] & (jnp.arange(steps)[None, :] <= jnp.arange(steps)[:, None]), axis=1)
    info = jnp.concatenate([x.astype(jnp.int32).reshape(-1) for x in (counts, member, own, replaced)])

    z, lse, w = run_scores(meta, info, queries, cache, fresh)
    lse = exchange_lse(lse)
    pos = positives.astype(jnp.float32).reshape(steps, groups, BLK)

    grad0, tok = run_grads(meta, info, z, queries, lse, 0, 1, lse)
    grad1, tok = run_grads(meta, info, z, queries, lse, 1, blocks - 1, tok)
    chunks = [grad0] + [grad1[i * BLK:(i + 1) * BLK] for i in range(blocks - 1)]
    state = {"term": None}
    pieces = 4
    size = groups // pieces

    def job(i, tok):
        state["term"], tok = run_terms(meta, info, z, w, lse, pos, i * size, size, tok, state["term"])
        return tok

    out = sum_line(chunks, tok, {i: functools.partial(job, i) for i in range(pieces)})
    mine = state["term"].reshape(groups, steps, BLK, width)
    owners = lax.axis_size("cache")
    share = group_rows // owners
    mine = jnp.swapaxes(mine, 0, 1) if share != BLK else mine
    if share == BLK:
        mine = lax.psum_scatter(mine, "cache", scatter_dimension=0, tiled=True)[0]
    else:
        mine = lax.psum_scatter(mine.reshape(steps, group_rows, width), "cache", scatter_dimension=1, tiled=True)
    return mine, jnp.concatenate(out, axis=0)


def solution(mesh):
    return jax.shard_map(
        on_device,
        mesh=mesh,
        in_specs=(
            P(None, "batch", None),
            P(None, "batch"),
            P(None, "batch", None),
            P(None, "batch"),
            P(),
            P("cache", None),
            P("cache", None),
        ),
        out_specs=(P(None, ("batch", "cache"), None), P("cache", None)),
        check_vma=False,
    )
```

time: 466 us -> 224 us (0.48)
  waiting for transfers between devices: 249 us -> 36.9 us
  matrix products: 109 us -> 0 us
  Pallas kernels: 0 us -> 94.1 us
  starting transfers between devices: 0.2 us -> 54.8 us
  blocking collectives: 45.6 us -> 0 us
  local copies, waits for them, and re-layouts: 27.1 us -> 11.8 us
    psum x2 -> x0, waiting for transfers between devices: 170 us -> none  [the longest x1 120 us: on_device(): grad_total = grad_total + lax.psum(step_grad, 'batch')]
    dot_general x15 -> x0, matrix products: 109 us -> none  [the longest x3 43.8 us: on_device(): term = jnp.dot(probs, current, precision=highest)]
    pallas_call x0 -> x7, Pallas kernels: none -> 94.1 us  [the longest x4 44.9 us: run_terms(): pl.pallas_call(functools.partial(term_kernel, meta, first, group), grid_s...]
    reduce_scatter x3 -> x1, waiting for transfers between devices: 78.8 us -> 0.01 us  [on_device(): mine = lax.psum_scatter(mine, 'cache', scatter_dimension=0, tiled=True)[0]]
    ppermute x0 -> x27, starting transfers between devices: none -> 54.7 us  [the longest x8 31.9 us: send_in(): first[k] = lax.ppermute(value, 'batch', [(0, 1), (3, 2)])]
    ppermute x0 -> x27, waiting for transfers between devices: none -> 36.9 us  [the longest x8 28.2 us: sum_line(): third[t - lag] = lax.ppermute(total[t - lag], 'batch', [(1, 0), (2, 3)])]
    pmax x1 -> x0, blocking collectives: 23.3 us -> none  [on_device(): top = lax.pmax(peak, 'cache')]
    psum x1 -> x0, blocking collectives: 22.3 us -> none  [on_device(): total = lax.psum(total, 'cache')]
  transfers between devices with their start and end apart: 5 -> 28, of which waited for: 4 -> 10; matrix products, arithmetic and copies ran while one was open for 22% -> 7% of each run, Pallas kernels for 0% -> 16%
where the time goes in v1:
time: 224 us; the launch traced here: 223 us
  Pallas kernels  94.1 us (42%)
  starting transfers between devices  54.8 us (24%)
  waiting for transfers between devices  36.9 us (16%)
  between operations  14.5 us (6%)
  local copies, waits for them, and re-layouts  11.8 us (5%)
  other arithmetic  11.1 us (5%)
    pallas_call x4, Pallas kernels, run_terms(): pl.pallas_call(functools.partial(term_kernel, meta, first, group), grid_s...  44.9 us
    ppermute x8, starting transfers between devices, send_in(): first[k] = lax.ppermute(value, 'batch', [(0, 1), (3, 2)])  31.9 us
    pallas_call x1, Pallas kernels, run_scores(): pl.pallas_call(functools.partial(scores_kernel, meta, part, 2.0 / math.sq...  29.5 us
    ppermute x8, waiting for transfers between devices, sum_line(): third[t - lag] = lax.ppermute(total[t - lag], 'batch', [(1, 0), (2, 3)])  28.2 us
    pallas_call x2, Pallas kernels, run_grads(): pl.pallas_call(functools.partial(grad_kernel, meta, first, group), grid_s...  19.7 us
    ppermute x8, starting transfers between devices, sum_line(): third[t - lag] = lax.ppermute(total[t - lag], 'batch', [(1, 0), (2, 3)])  10.3 us
    ppermute x8, starting transfers between devices, sum_line(): second[t] = lax.ppermute(inner[t], 'batch', [(1, 2), (2, 1)])  6.95 us
    unnamed x14, local copies, waits for them, and re-layouts  6.76 us
  transfers between devices with their start and end apart: 28, of which 10 were waited for; matrix products, arithmetic and copies ran while one was open for 7% of the time, Pallas kernels for 16%

profile of v1, /device:TPU:0, one launch (start us, length us, event | category | flops | bytes accessed | tf_op | source)
XLA Modules:
  0.0 223.3 jit_solution(3244903633598313269)
XLA Ops:
  8.9 1.3 and_reduce_fusion
  11.0 29.5 %scores.1 = (f32[3,8,8,128,128]{4,3,2,1,0:T(8,128)}, f32[6,4,128]{2,1,0:T(4,128)}, bf16[12,256,768]{2,1,0:T(8,128)(2,1)}) custom-call(s32[390]{0:T(512)} %pad_add_fusion.info, bf16[3,1024,768]{2,1,0:T(8,128)(2,1)} %q_ref.1, f32[1024,768]{1,0:T(8,128)} %cache_ref.1, f32[512,768]{1,0:T(8,128)} %fresh_ref.1), custom_call_target="tpu_custom_call" | custom-call | flops 9663676416 | bytes 30000000 | tf_op jit(solution)/shard_map/scores/pallas_call | solution.py:183
  41.0 1.0 collective-permute-done
  42.8 2.9 %collective-permute-start.1 = (f32[3,8,128]{2,1,0:T(8,128)S(1)}, f32[3,8,128]{2,1,0:T(8,128)S(1)}, u32[]{:S(2)}, u32[]{:S(2)}) collective-permute-start(f32[3,8,128]{2,1,0:T(8,128)S(1)} %add_select_fusion.2), channel_id=1, source_target_pairs={{0,8},{4,12},{8,0},{12,4},{16,24},{20,28},{24,16},{28,20},{1,9},{5... | collective-permute-start | bytes 36872 | tf_op jit(solution)/shard_map/ppermute | solution.py:283
  45.7 1.7 collective-permute-done.1
  47.4 2.1 collective-permute-start.2
  49.5 1.7 collective-permute-done.2
  51.8 5.6 %cache_grad.2 = (f32[128,768]{1,0:T(8,128)}, f32[8,128]{1,0:T(8,128)}) custom-call(s32[390]{0:T(512)} %pad_add_fusion.info, f32[24,8,128,128]{3,2,1,0:T(8,128)} %bitcast.12, bf16[24,128,768]{2,1,0:T(8,128)(2,1)} %bitcast.14, f32[24,128]{1,0:T(8,128)} %bitcast.16, f32[3,8,128]{2,1,0:T(8,128)} %add_select_fusion.dep.lse_ref), custom_call_target="tpu_custom_call" | custom-call | flops 603979776 | bytes 7000000 | tf_op jit(solution)/shard_map/cache_grad/pallas_call | solution.py:220
  57.4 3.5 %collective-permute-start.3 = (f32[128,768]{1,0:T(8,128)}, f32[128,768]{1,0:T(8,128)S(1)}, u32[]{:S(2)}, u32[]{:S(2)}) collective-permute-start(f32[128,768]{1,0:T(8,128)} %get-tuple-element.91), channel_id=1, source_target_pairs={{0,1},{3,2},{4,5},{7,6},{8,9},{11,10},{12,13},{15,14},{16,17},{19,... | collective-permute-start | bytes 1179656 | tf_op jit(solution)/shard_map/ppermute | solution.py:304
  61.0 14.1 %cache_grad.3 = (f32[896,768]{1,0:T(8,128)}, f32[8,128]{1,0:T(8,128)}) custom-call(s32[390]{0:T(512)} %pad_add_fusion.info, f32[24,8,128,128]{3,2,1,0:T(8,128)} %bitcast.13, bf16[24,128,768]{2,1,0:T(8,128)(2,1)} %bitcast.15, f32[24,128]{1,0:T(8,128)} %bitcast.17, f32[8,128]{1,0:T(8,128)} %get-tuple-element.88.dep), custom_call_target="tpu_custom_call" | custom-call | flops 4227858432 | bytes 19000000 | tf_op jit(solution)/shard_map/cache_grad/pallas_call | solution.py:220
  75.0 2.0 fusion.3
  77.1 1.3 collective-permute-start.5
  78.4 1.3 collective-permute-start.7
  80.5 3.1 %collective-permute-start.4 = (f32[128,768]{1,0:T(8,128)S(1)}, f32[128,768]{1,0:T(8,128)S(1)}, u32[]{:S(2)}, u32[]{:S(2)}) collective-permute-start(f32[128,768]{1,0:T(8,128)S(1)} %get-tuple-element.102), channel_id=1, source_target_pairs={{0,1},{3,2},{4,5},{7,6},{8,9},{11,10},{12,13},{15,14},{16,17},{19,... | collective-permute-start | bytes 1179656 | tf_op jit(solution)/shard_map/ppermute | solution.py:304
  83.6 4.3 %collective-permute-done.5 = f32[128,768]{1,0:T(8,128)S(1)} collective-permute-done((f32[128,768]{1,0:T(8,128)S(1)}, f32[128,768]{1,0:T(8,128)S(1)}, u32[]{:S(2)}, u32[]{:S(2)}) %collective-permute-start.5) | collective-permute-done | bytes 393248 | tf_op jit(solution)/shard_map/ppermute | solution.py:304
  90.3 11.2 %query_term.4 = (f32[8,3,128,768]{3,2,1,0:T(8,128)}, f32[8,128]{1,0:T(8,128)}) custom-call(s32[390]{0:T(512)} %pad_add_fusion.info, f32[3,8,8,128,128]{4,3,2,1,0:T(8,128)} %get-tuple-element.85.z_ref, bf16[12,256,768]{2,1,0:T(8,128)(2,1)} %get-tuple-element.86.w_ref, f32[3,8,128]{2,1,0:T(8,128)} %add_select_fusion.dep.lse_ref, f32[3,8,128]{2,1,0:T(8,128)} %bitcast.18, ...), custom_call_target="tpu_custom_call" | custom-call | flops 1811939328 | bytes 11000000 | tf_op jit(solution)/shard_map/query_term/pallas_call | solution.py:250
  101.5 10.9 %query_term.5 = (f32[8,3,128,768]{3,2,1,0:T(8,128)}, f32[8,128]{1,0:T(8,128)}) custom-call(s32[390]{0:T(512)} %pad_add_fusion.info, f32[3,8,8,128,128]{4,3,2,1,0:T(8,128)} %get-tuple-element.85.z_ref, bf16[12,256,768]{2,1,0:T(8,128)(2,1)} %get-tuple-element.86.w_ref, f32[3,8,128]{2,1,0:T(8,128)} %add_select_fusion.dep.lse_ref, ...), custom_call_target="tpu_custom_call", output_to_operand_aliasing={{0}: (6, {})} | custom-call | flops 1811939328 | bytes 11000000 | tf_op jit(solution)/shard_map/query_term/pallas_call | solution.py:250
  113.6 11.6 %query_term.6 = (f32[8,3,128,768]{3,2,1,0:T(8,128)}, f32[8,128]{1,0:T(8,128)}) custom-call(s32[390]{0:T(512)} %pad_add_fusion.info, f32[3,8,8,128,128]{4,3,2,1,0:T(8,128)} %get-tuple-element.85.z_ref, bf16[12,256,768]{2,1,0:T(8,128)(2,1)} %get-tuple-element.86.w_ref, f32[3,8,128]{2,1,0:T(8,128)} %add_select_fusion.dep.lse_ref, ...), custom_call_target="tpu_custom_call", output_to_operand_aliasing={{0}: (6, {})} | custom-call | flops 1811939328 | bytes 11000000 | tf_op jit(solution)/shard_map/query_term/pallas_call | solution.py:250
  125.3 11.3 %query_term.7 = (f32[8,3,128,768]{3,2,1,0:T(8,128)}, f32[8,128]{1,0:T(8,128)}) custom-call(s32[390]{0:T(512)} %pad_add_fusion.info, f32[3,8,8,128,128]{4,3,2,1,0:T(8,128)} %get-tuple-element.85.z_ref, bf16[12,256,768]{2,1,0:T(8,128)(2,1)} %get-tuple-element.86.w_ref, f32[3,8,128]{2,1,0:T(8,128)} %add_select_fusion.dep.lse_ref, ...), custom_call_target="tpu_custom_call", output_to_operand_aliasing={{0}: (6, {})} | custom-call | flops 1811939328 | bytes 11000000 | tf_op jit(solution)/shard_map/query_term/pallas_call | solution.py:250
  136.5 4.4 %collective-permute-start.9 = (f32[128,768]{1,0:T(8,128)S(1)}, f32[128,768]{1,0:T(8,128)S(1)}, u32[]{:S(2)}, u32[]{:S(2)}) collective-permute-start(f32[128,768]{1,0:T(8,128)S(1)} %get-tuple-element.113), channel_id=1, source_target_pairs={{0,1},{3,2},{4,5},{7,6},{8,9},{11,10},{12,13},{15,14},{16,17},{19,... | collective-permute-start | bytes 1179656 | tf_op jit(solution)/shard_map/ppermute | solution.py:304
  140.9 1.3 collective-permute-start.11
  142.2 1.4 collective-permute-start.10
  143.6 7.1 %collective-permute-start.12 = (f32[128,768]{1,0:T(8,128)S(1)}, f32[128,768]{1,0:T(8,128)}, u32[]{:S(2)}, u32[]{:S(2)}) collective-permute-start(f32[128,768]{1,0:T(8,128)S(1)} %get-tuple-element.123), channel_id=1, source_target_pairs={{0,1},{3,2},{4,5},{7,6},{8,9},{11,10},{12,13},{15,14},{16,17},{19,... | collective-permute-start | bytes 1179656 | tf_op jit(solution)/shard_map/ppermute | solution.py:304
  150.7 1.3 collective-permute-start.14
  152.8 1.4 collective-permute-start.13
  154.2 6.6 %collective-permute-start.15 = (f32[128,768]{1,0:T(8,128)S(1)}, f32[128,768]{1,0:T(8,128)S(1)}, u32[]{:S(2)}, u32[]{:S(2)}) collective-permute-start(f32[128,768]{1,0:T(8,128)S(1)} %get-tuple-element.133), channel_id=1, source_target_pairs={{0,1},{3,2},{4,5},{7,6},{8,9},{11,10},{12,13},{15,14},{16,17},{19,... | collective-permute-start | bytes 1179656 | tf_op jit(solution)/shard_map/ppermute | solution.py:304
  160.8 1.0 add.106
  161.8 1.0 add.107
  162.9 1.2 broadcast_select_fusion.7
  164.7 1.3 collective-permute-start.17
  166.0 4.6 %collective-permute-start.18 = (f32[128,768]{1,0:T(8,128)S(1)}, f32[128,768]{1,0:T(8,128)S(1)}, u32[]{:S(2)}, u32[]{:S(2)}) collective-permute-start(f32[128,768]{1,0:T(8,128)S(1)} %get-tuple-element.143), channel_id=1, source_target_pairs={{0,1},{3,2},{4,5},{7,6},{8,9},{11,10},{12,13},{15,14},{16,17},{19,... | collective-permute-start | bytes 1179656 | tf_op jit(solution)/shard_map/ppermute | solution.py:304
  170.7 1.0 add.108
  171.7 1.0 add.109
  173.5 1.3 collective-permute-start.20
  174.8 0.8 constant_dynamic-update-slice_fusion.7
  176.3 2.3 %collective-permute-done.17 = f32[128,768]{1,0:T(8,128)S(1)} collective-permute-done((f32[128,768]{1,0:T(8,128)S(1)}, f32[128,768]{1,0:T(8,128)S(1)}, u32[]{:S(2)}, u32[]{:S(2)}) %collective-permute-start.17) | collective-permute-done | bytes 393248 | tf_op jit(solution)/shard_map/ppermute | solution.py:336
  179.5 1.3 collective-permute-start.22
  180.9 6.6 %collective-permute-done.20 = f32[128,768]{1,0:T(8,128)S(1)} collective-permute-done((f32[128,768]{1,0:T(8,128)S(1)}, f32[128,768]{1,0:T(8,128)S(1)}, u32[]{:S(2)}, u32[]{:S(2)}) %collective-permute-start.20) | collective-permute-done | bytes 393248 | tf_op jit(solution)/shard_map/ppermute | solution.py:336
  188.3 1.3 collective-permute-start.24
  189.6 0.8 constant_dynamic-update-slice_fusion.5
  191.1 4.7 %collective-permute-done.22 = f32[128,768]{1,0:T(8,128)S(1)} collective-permute-done((f32[128,768]{1,0:T(8,128)S(1)}, f32[128,768]{1,0:T(8,128)S(1)}, u32[]{:S(2)}, u32[]{:S(2)}) %collective-permute-start.22) | collective-permute-done | bytes 393248 | tf_op jit(solution)/shard_map/ppermute | solution.py:336
  196.0 1.3 collective-permute-start.25
  197.3 7.0 %collective-permute-done.24 = f32[128,768]{1,0:T(8,128)S(1)} collective-permute-done((f32[128,768]{1,0:T(8,128)S(1)}, f32[128,768]{1,0:T(8,128)S(1)}, u32[]{:S(2)}, u32[]{:S(2)}) %collective-permute-start.24) | collective-permute-done | bytes 393248 | tf_op jit(solution)/shard_map/ppermute | solution.py:336
  204.4 1.3 collective-permute-start.26
  205.7 0.8 constant_dynamic-update-slice_fusion.3
  207.3 3.4 %collective-permute-done.25 = f32[128,768]{1,0:T(8,128)S(1)} collective-permute-done((f32[128,768]{1,0:T(8,128)S(1)}, f32[128,768]{1,0:T(8,128)S(1)}, u32[]{:S(2)}, u32[]{:S(2)}) %collective-permute-start.25) | collective-permute-done | bytes 393248 | tf_op jit(solution)/shard_map/ppermute | solution.py:336
  210.6 4.2 %collective-permute-done.26 = f32[128,768]{1,0:T(8,128)S(1)} collective-permute-done((f32[128,768]{1,0:T(8,128)S(1)}, f32[128,768]{1,0:T(8,128)S(1)}, u32[]{:S(2)}, u32[]{:S(2)}) %collective-permute-start.26) | collective-permute-done | bytes 393248 | tf_op jit(solution)/shard_map/ppermute | solution.py:336
  214.9 0.8 constant_dynamic-update-slice_fusion.1
  (78 shorter events, 16.0 us)
Async XLA Ops:
  7.2 209.2 %reduce-scatter.2.cloned.1.call-start = ((), (), s32[]{:S(2)}) async-start(), calls=%async_computation.1 | async-start | bytes 10616832 | tf_op jit(solution)/shard_map/reduce_scatter | solution.py:379
  40.5 1.6 collective-permute-start
  42.8 4.6 %collective-permute-start.1 = (f32[3,8,128]{2,1,0:T(8,128)S(1)}, f32[3,8,128]{2,1,0:T(8,128)S(1)}, u32[]{:S(2)}, u32[]{:S(2)}) collective-permute-start(f32[3,8,128]{2,1,0:T(8,128)S(1)} %add_select_fusion.2), channel_id=1, source_target_pairs={{0,8},{4,12},{8,0},{12,4},{16,24},{20,28},{24,16},{28,20},{1,9},{5... | collective-permute-start | bytes 36872 | tf_op jit(solution)/shard_map/ppermute | solution.py:283
  47.4 3.8 %collective-permute-start.2 = (f32[3,8,128]{2,1,0:T(8,128)S(1)}, f32[3,8,128]{2,1,0:T(8,128)S(1)}, u32[]{:S(2)}, u32[]{:S(2)}) collective-permute-start(f32[3,8,128]{2,1,0:T(8,128)S(1)} %add_select_fusion.1), channel_id=1, source_target_pairs={{0,16},{4,20},{8,24},{12,28},{16,0},{20,4},{24,8},{28,12},{1,17},{... | collective-permute-start | bytes 36872 | tf_op jit(solution)/shard_map/ppermute | solution.py:283
  57.4 22.3 %collective-permute-start.3 = (f32[128,768]{1,0:T(8,128)}, f32[128,768]{1,0:T(8,128)S(1)}, u32[]{:S(2)}, u32[]{:S(2)}) collective-permute-start(f32[128,768]{1,0:T(8,128)} %get-tuple-element.91), channel_id=1, source_target_pairs={{0,1},{3,2},{4,5},{7,6},{8,9},{11,10},{12,13},{15,14},{16,17},{19,... | collective-permute-start | bytes 1179656 | tf_op jit(solution)/shard_map/ppermute | solution.py:304
  75.0 4.7 %copy-start.1 = (f32[128,768]{1,0:T(8,128)S(1)}, f32[128,768]{1,0:T(8,128)}, u32[]{:S(2)}) copy-start(f32[128,768]{1,0:T(8,128)} %get-tuple-element.91) | copy-start | bytes 1179652
  75.0 13.6 %copy-start.2 = (s32[3,1024]{1,0:T(4,128)S(1)}, s32[3,1024]{1,0:T(4,128)}, u32[]{:S(2)}) copy-start(s32[3,1024]{1,0:T(4,128)} %param.8) | copy-start | bytes 36868
  77.1 10.9 %collective-permute-start.5 = (f32[128,768]{1,0:T(8,128)S(1)}, f32[128,768]{1,0:T(8,128)S(1)}, u32[]{:S(2)}, u32[]{:S(2)}) collective-permute-start(f32[128,768]{1,0:T(8,128)S(1)} %get-tuple-element.94), channel_id=1, source_target_pairs={{0,1},{3,2},{4,5},{7,6},{8,9},{11,10},{12,13},{15,14},{16,17},{19,... | collective-permute-start | bytes 1179656 | tf_op jit(solution)/shard_map/ppermute | solution.py:304
  78.4 34.0 %collective-permute-start.7 = (f32[128,768]{1,0:T(8,128)S(1)}, f32[128,768]{1,0:T(8,128)S(1)}, u32[]{:S(2)}, u32[]{:S(2)}) collective-permute-start(f32[128,768]{1,0:T(8,128)S(1)} %get-tuple-element.96), channel_id=1, source_target_pairs={{0,1},{3,2},{4,5},{7,6},{8,9},{11,10},{12,13},{15,14},{16,17},{19,... | collective-permute-start | bytes 1179656 | tf_op jit(solution)/shard_map/ppermute | solution.py:304
  79.8 32.6 %collective-permute-start.8 = (f32[128,768]{1,0:T(8,128)S(1)}, f32[128,768]{1,0:T(8,128)S(1)}, u32[]{:S(2)}, u32[]{:S(2)}) collective-permute-start(f32[128,768]{1,0:T(8,128)S(1)} %add.100), channel_id=1, source_target_pairs={{1,2},{2,1},{5,6},{6,5},{9,10},{10,9},{13,14},{14,13},{17,18},{18,... | collective-permute-start | bytes 1179656 | tf_op jit(solution)/shard_map/ppermute | solution.py:333
  80.5 32.6 %collective-permute-start.4 = (f32[128,768]{1,0:T(8,128)S(1)}, f32[128,768]{1,0:T(8,128)S(1)}, u32[]{:S(2)}, u32[]{:S(2)}) collective-permute-start(f32[128,768]{1,0:T(8,128)S(1)} %get-tuple-element.102), channel_id=1, source_target_pairs={{0,1},{3,2},{4,5},{7,6},{8,9},{11,10},{12,13},{15,14},{16,17},{19,... | collective-permute-start | bytes 1179656 | tf_op jit(solution)/shard_map/ppermute | solution.py:304
  88.0 25.1 %collective-permute-start.6 = (f32[128,768]{1,0:T(8,128)S(1)}, f32[128,768]{1,0:T(8,128)S(1)}, u32[]{:S(2)}, u32[]{:S(2)}) collective-permute-start(f32[128,768]{1,0:T(8,128)S(1)} %add.101), channel_id=1, source_target_pairs={{1,2},{2,1},{5,6},{6,5},{9,10},{10,9},{13,14},{14,13},{17,18},{18,... | collective-permute-start | bytes 1179656 | tf_op jit(solution)/shard_map/ppermute | solution.py:333
  136.5 15.5 %collective-permute-start.9 = (f32[128,768]{1,0:T(8,128)S(1)}, f32[128,768]{1,0:T(8,128)S(1)}, u32[]{:S(2)}, u32[]{:S(2)}) collective-permute-start(f32[128,768]{1,0:T(8,128)S(1)} %get-tuple-element.113), channel_id=1, source_target_pairs={{0,1},{3,2},{4,5},{7,6},{8,9},{11,10},{12,13},{15,14},{16,17},{19,... | collective-permute-start | bytes 1179656 | tf_op jit(solution)/shard_map/ppermute | solution.py:304
  140.9 13.3 %collective-permute-start.11 = (f32[128,768]{1,0:T(8,128)S(1)}, f32[128,768]{1,0:T(8,128)}, u32[]{:S(2)}, u32[]{:S(2)}) collective-permute-start(f32[128,768]{1,0:T(8,128)S(1)} %add.103), channel_id=1, source_target_pairs={{1,0},{2,3},{5,4},{6,7},{9,8},{10,11},{13,12},{14,15},{17,16},{18,... | collective-permute-start | bytes 1179656 | tf_op jit(solution)/shard_map/ppermute | solution.py:336
  142.2 18.6 %collective-permute-start.10 = (f32[128,768]{1,0:T(8,128)S(1)}, f32[128,768]{1,0:T(8,128)}, u32[]{:S(2)}, u32[]{:S(2)}) collective-permute-start(f32[128,768]{1,0:T(8,128)S(1)} %add.102), channel_id=1, source_target_pairs={{1,2},{2,1},{5,6},{6,5},{9,10},{10,9},{13,14},{14,13},{17,18},{18,... | collective-permute-start | bytes 1179656 | tf_op jit(solution)/shard_map/ppermute | solution.py:333
  143.6 21.1 %collective-permute-start.12 = (f32[128,768]{1,0:T(8,128)S(1)}, f32[128,768]{1,0:T(8,128)}, u32[]{:S(2)}, u32[]{:S(2)}) collective-permute-start(f32[128,768]{1,0:T(8,128)S(1)} %get-tuple-element.123), channel_id=1, source_target_pairs={{0,1},{3,2},{4,5},{7,6},{8,9},{11,10},{12,13},{15,14},{16,17},{19,... | collective-permute-start | bytes 1179656 | tf_op jit(solution)/shard_map/ppermute | solution.py:304
  150.7 15.3 %collective-permute-start.14 = (f32[128,768]{1,0:T(8,128)S(1)}, f32[128,768]{1,0:T(8,128)S(1)}, u32[]{:S(2)}, u32[]{:S(2)}) collective-permute-start(f32[128,768]{1,0:T(8,128)S(1)} %add.105), channel_id=1, source_target_pairs={{1,0},{2,3},{5,4},{6,7},{9,8},{10,11},{13,12},{14,15},{17,16},{18,... | collective-permute-start | bytes 1179656 | tf_op jit(solution)/shard_map/ppermute | solution.py:336
  152.0 0.7 copy-start
  152.8 17.9 %collective-permute-start.13 = (f32[128,768]{1,0:T(8,128)S(1)}, f32[128,768]{1,0:T(8,128)}, u32[]{:S(2)}, u32[]{:S(2)}) collective-permute-start(f32[128,768]{1,0:T(8,128)S(1)} %add.104), channel_id=1, source_target_pairs={{1,2},{2,1},{5,6},{6,5},{9,10},{10,9},{13,14},{14,13},{17,18},{18,... | collective-permute-start | bytes 1179656 | tf_op jit(solution)/shard_map/ppermute | solution.py:333
  154.2 19.3 %collective-permute-start.15 = (f32[128,768]{1,0:T(8,128)S(1)}, f32[128,768]{1,0:T(8,128)S(1)}, u32[]{:S(2)}, u32[]{:S(2)}) collective-permute-start(f32[128,768]{1,0:T(8,128)S(1)} %get-tuple-element.133), channel_id=1, source_target_pairs={{0,1},{3,2},{4,5},{7,6},{8,9},{11,10},{12,13},{15,14},{16,17},{19,... | collective-permute-start | bytes 1179656 | tf_op jit(solution)/shard_map/ppermute | solution.py:304
  164.0 12.3 %collective-permute-start.16 = (f32[128,768]{1,0:T(8,128)S(1)}, f32[128,768]{1,0:T(8,128)S(1)}, u32[]{:S(2)}, u32[]{:S(2)}) collective-permute-start(f32[128,768]{1,0:T(8,128)S(1)} %add.106), channel_id=1, source_target_pairs={{1,2},{2,1},{5,6},{6,5},{9,10},{10,9},{13,14},{14,13},{17,18},{18,... | collective-permute-start | bytes 1179656 | tf_op jit(solution)/shard_map/ppermute | solution.py:333
  164.7 13.9 %collective-permute-start.17 = (f32[128,768]{1,0:T(8,128)S(1)}, f32[128,768]{1,0:T(8,128)S(1)}, u32[]{:S(2)}, u32[]{:S(2)}) collective-permute-start(f32[128,768]{1,0:T(8,128)S(1)} %add.107), channel_id=1, source_target_pairs={{1,0},{2,3},{5,4},{6,7},{9,8},{10,11},{13,12},{14,15},{17,16},{18,... | collective-permute-start | bytes 1179656 | tf_op jit(solution)/shard_map/ppermute | solution.py:336
  166.0 14.8 %collective-permute-start.18 = (f32[128,768]{1,0:T(8,128)S(1)}, f32[128,768]{1,0:T(8,128)S(1)}, u32[]{:S(2)}, u32[]{:S(2)}) collective-permute-start(f32[128,768]{1,0:T(8,128)S(1)} %get-tuple-element.143), channel_id=1, source_target_pairs={{0,1},{3,2},{4,5},{7,6},{8,9},{11,10},{12,13},{15,14},{16,17},{19,... | collective-permute-start | bytes 1179656 | tf_op jit(solution)/shard_map/ppermute | solution.py:304
  172.8 8.1 %collective-permute-start.19 = (f32[128,768]{1,0:T(8,128)S(1)}, f32[128,768]{1,0:T(8,128)S(1)}, u32[]{:S(2)}, u32[]{:S(2)}) collective-permute-start(f32[128,768]{1,0:T(8,128)S(1)} %add.108), channel_id=1, source_target_pairs={{1,2},{2,1},{5,6},{6,5},{9,10},{10,9},{13,14},{14,13},{17,18},{18,... | collective-permute-start | bytes 1179656 | tf_op jit(solution)/shard_map/ppermute | solution.py:333
  173.5 13.9 %collective-permute-start.20 = (f32[128,768]{1,0:T(8,128)S(1)}, f32[128,768]{1,0:T(8,128)S(1)}, u32[]{:S(2)}, u32[]{:S(2)}) collective-permute-start(f32[128,768]{1,0:T(8,128)S(1)} %add.109), channel_id=1, source_target_pairs={{1,0},{2,3},{5,4},{6,7},{9,8},{10,11},{13,12},{14,15},{17,16},{18,... | collective-permute-start | bytes 1179656 | tf_op jit(solution)/shard_map/ppermute | solution.py:336
  178.8 12.3 %collective-permute-start.21 = (f32[128,768]{1,0:T(8,128)S(1)}, f32[128,768]{1,0:T(8,128)S(1)}, u32[]{:S(2)}, u32[]{:S(2)}) collective-permute-start(f32[128,768]{1,0:T(8,128)S(1)} %add.110), channel_id=1, source_target_pairs={{1,2},{2,1},{5,6},{6,5},{9,10},{10,9},{13,14},{14,13},{17,18},{18,... | collective-permute-start | bytes 1179656 | tf_op jit(solution)/shard_map/ppermute | solution.py:333
  179.5 16.3 %collective-permute-start.22 = (f32[128,768]{1,0:T(8,128)S(1)}, f32[128,768]{1,0:T(8,128)S(1)}, u32[]{:S(2)}, u32[]{:S(2)}) collective-permute-start(f32[128,768]{1,0:T(8,128)S(1)} %add.111), channel_id=1, source_target_pairs={{1,0},{2,3},{5,4},{6,7},{9,8},{10,11},{13,12},{14,15},{17,16},{18,... | collective-permute-start | bytes 1179656 | tf_op jit(solution)/shard_map/ppermute | solution.py:336
  187.6 9.7 %collective-permute-start.23 = (f32[128,768]{1,0:T(8,128)S(1)}, f32[128,768]{1,0:T(8,128)S(1)}, u32[]{:S(2)}, u32[]{:S(2)}) collective-permute-start(f32[128,768]{1,0:T(8,128)S(1)} %add.112), channel_id=1, source_target_pairs={{1,2},{2,1},{5,6},{6,5},{9,10},{10,9},{13,14},{14,13},{17,18},{18,... | collective-permute-start | bytes 1179656 | tf_op jit(solution)/shard_map/ppermute | solution.py:333
  188.3 16.0 %collective-permute-start.24 = (f32[128,768]{1,0:T(8,128)S(1)}, f32[128,768]{1,0:T(8,128)S(1)}, u32[]{:S(2)}, u32[]{:S(2)}) collective-permute-start(f32[128,768]{1,0:T(8,128)S(1)} %add.113), channel_id=1, source_target_pairs={{1,0},{2,3},{5,4},{6,7},{9,8},{10,11},{13,12},{14,15},{17,16},{18,... | collective-permute-start | bytes 1179656 | tf_op jit(solution)/shard_map/ppermute | solution.py:336
  196.0 14.6 %collective-permute-start.25 = (f32[128,768]{1,0:T(8,128)S(1)}, f32[128,768]{1,0:T(8,128)S(1)}, u32[]{:S(2)}, u32[]{:S(2)}) collective-permute-start(f32[128,768]{1,0:T(8,128)S(1)} %add.114), channel_id=1, source_target_pairs={{1,0},{2,3},{5,4},{6,7},{9,8},{10,11},{13,12},{14,15},{17,16},{18,... | collective-permute-start | bytes 1179656 | tf_op jit(solution)/shard_map/ppermute | solution.py:336
  204.4 10.4 %collective-permute-start.26 = (f32[128,768]{1,0:T(8,128)S(1)}, f32[128,768]{1,0:T(8,128)S(1)}, u32[]{:S(2)}, u32[]{:S(2)}) collective-permute-start(f32[128,768]{1,0:T(8,128)S(1)} %add.115), channel_id=1, source_target_pairs={{1,0},{2,3},{5,4},{6,7},{9,8},{10,11},{13,12},{14,15},{17,16},{18,... | collective-permute-start | bytes 1179656 | tf_op jit(solution)/shard_map/ppermute | solution.py:336
Sparse Core Ops, SparseCore 0:
  136.7 77.4 reduce-scatter.1

commit v2 on v0

v2 whole, which is shorter than its diff:
```python
import functools
import math

import jax
import jax.numpy as jnp
from jax import lax
from jax.experimental import pallas as pl
from jax.experimental.pallas import tpu as pltpu
from jax.sharding import PartitionSpec as P

BLK = 128
LOW = -1e30
LAGS = (4, 2, 2)
HOME_SLOTS = (8, 14, 18)


def dot(a, b, ca, cb):
    return lax.dot_general(a, b, (((ca,), (cb,)), ((), ())), preferred_element_type=jnp.float32)


def split(x):
    hi = x.astype(jnp.bfloat16)
    return hi, (x - hi.astype(jnp.float32)).astype(jnp.bfloat16)


def as_columns(row):
    return jnp.broadcast_to(row, (BLK, row.shape[1])).T


class Meta:
    def __init__(self, steps, groups, blocks, slab_blocks):
        self.steps, self.groups, self.blocks, self.slab_blocks = steps, groups, blocks, slab_blocks
        self.rows = steps * groups
        self.size = self.rows * blocks

    def count(self, ref, sb, j):
        return ref[sb * self.blocks + j]

    def member(self, ref, sb, j):
        return ref[self.size + sb * self.blocks + j]

    def own(self, ref, s):
        return ref[2 * self.size + s]

    def replaced(self, ref, s):
        return ref[2 * self.size + self.steps + s]

    def me(self, ref):
        return ref[2 * self.size + 2 * self.steps]

    def source(self, ref, s, j):
        return jnp.where((self.replaced(ref, s) > 0) & (j < self.slab_blocks), self.blocks + j, j)


def scores_kernel(meta, group, scale, info, q_hbm, cache_hbm, fresh_hbm, z_ref, w_ref, q_ref, lse_ref,
                  cache_ref, fresh_ref, peak, top, entries, pairs, sem):
    copies = [pltpu.make_async_copy(src, dst, sem.at[i]) for i, (src, dst) in enumerate(
        ((cache_hbm, cache_ref), (fresh_hbm, fresh_ref), (q_hbm, q_ref)))]
    for copy in copies:
        copy.start()

    def collect(sj, carry):
        n_entries, n_pairs = carry
        s, j = sj // meta.blocks, sj % meta.blocks
        m, held = 0, 0
        for b in range(meta.groups):
            sb = s * meta.groups + b
            on = (meta.count(info, sb, j) > 0).astype(jnp.int32)
            pairs[n_pairs] = sb * meta.blocks + j
            n_pairs = n_pairs + on
            held = jnp.where(m % 2 == 0, sb, held)
            entries[n_entries + m // 2] = (held * meta.rows + sb) * meta.blocks + j
            m = m + on

        @pl.when(m % 2 == 1)
        def _():
            entries[n_entries + m // 2] = (held * meta.rows + held) * meta.blocks + j

        return n_entries + (m + 1) // 2, n_pairs

    n_entries, n_pairs = lax.fori_loop(0, meta.steps * meta.blocks, collect, (0, 0))
    for g in range(group):
        entries[n_entries + g] = jnp.where(n_entries > 0, entries[0], 0)
        pairs[n_pairs + g] = 0
    peak[...] = jnp.full(peak.shape, LOW, jnp.float32)

    for copy, src, at in ((copies[0], cache_ref, 0), (copies[1], fresh_ref, meta.blocks)):
        copy.wait()

        def one(k, _, src=src, at=at):
            hi, lo = split(src[pl.ds(pl.multiple_of(k * BLK, BLK), BLK), :])
            w_ref[at + k, :BLK] = hi
            w_ref[at + k, BLK:] = lo
            return 0

        lax.fori_loop(0, src.shape[0] // BLK, one, 0)
    copies[2].wait()

    def score(it, _):
        found = []
        for g in range(group):
            e = entries[it * group + g]
            j, both = e % meta.blocks, e // meta.blocks
            sb0, sb1 = both // meta.rows, both % meta.rows
            left = jnp.concatenate([q_ref[sb0], q_ref[sb1]], axis=0)
            z = dot(left, w_ref[meta.source(info, sb0 // meta.groups, j)], 1, 1)
            found.append((sb0, sb1, j, (z[:, :BLK] + z[:, BLK:]) * scale))
        for sb0, sb1, j, z in found:
            z_ref[sb0, j] = z[:BLK]
            z_ref[sb1, j] = z[BLK:]
            peak[sb0] = jnp.maximum(peak[sb0], z[:BLK])
            peak[sb1] = jnp.maximum(peak[sb1], z[BLK:])
        return 0

    lax.fori_loop(0, (n_entries + group - 1) // group, score, 0)

    def highest(sb, _):
        top[sb] = jnp.broadcast_to(jnp.max(peak[sb], axis=1, keepdims=True), (BLK, BLK))
        peak[sb] = jnp.zeros((BLK, BLK), jnp.float32)
        return 0

    lax.fori_loop(0, meta.rows, highest, 0, unroll=4 if meta.rows % 4 == 0 else 1)

    def add(it, _):
        for g in range(group):
            k = it * group + g
            sb, j = pairs[k] // meta.blocks, pairs[k] % meta.blocks
            c = meta.count(info, sb, j).astype(jnp.float32)
            peak[sb] += jnp.where(k < n_pairs, jnp.exp(z_ref[sb, j] - top[sb]) * c, 0.0)
        return 0

    lax.fori_loop(0, (n_pairs + group - 1) // group, add, 0)

    def finish(sb, _):
        total = jnp.sum(peak[sb], axis=1, keepdims=True)
        lse = jnp.where(total > 0, top[sb][:, :1] + jnp.log(jnp.maximum(total, 1e-30)), LOW)
        lse_ref[pl.ds(sb, 1), :] = jnp.broadcast_to(lse, (BLK, BLK)).T[:1]
        return 0

    lax.fori_loop(0, meta.rows, finish, 0, unroll=4 if meta.rows % 4 == 0 else 1)


def grad_kernel(meta, first, width, info, z_ref, q_ref, lse_ref, dep, out_ref, todo):
    def block(i, _):
        j = first + i
        n = 0
        for sb in range(meta.rows):
            todo[n] = sb
            n = n + meta.member(info, sb, j)
        for g in range(width):
            todo[n + g] = 0
        at = pl.ds(pl.multiple_of(i * BLK, BLK), BLK)
        out_ref[at, :] = jnp.zeros((BLK, out_ref.shape[1]), jnp.float32)

        def step(it, _):
            his, los, rows = [], [], []
            for g in range(width):
                k = it * width + g
                sb = todo[k]
                p = jnp.exp(z_ref[sb, j].T - lse_ref[pl.ds(sb, 1), :])
                hi, lo = split(jnp.where(k < n, p, 0.0))
                his.append(hi)
                los.append(lo)
                rows.append(q_ref[sb])
            left = jnp.concatenate([jnp.concatenate(his, axis=1), jnp.concatenate(los, axis=1)], axis=0)
            acc = dot(left, jnp.concatenate(rows, axis=0), 1, 0)
            out_ref[at, :] += acc[:BLK] + acc[BLK:]
            return 0

        lax.fori_loop(0, (n + width - 1) // width, step, 0)
        return 0

    lax.fori_loop(0, out_ref.shape[0] // BLK, block, 0)


def term_kernel(meta, order, width, info, z_ref, w_ref, lse_ref, pos_ref, dep, *refs):
    outs, (todo, lcol, pcol) = refs[:-3], refs[-3:]
    lane = lax.broadcasted_iota(jnp.int32, (BLK, BLK), 1).astype(jnp.float32)

    def block(i, out_ref, first, stride):
        b = meta.me(info) ^ (first + stride * i) if order else first + stride * i
        n = 0
        for s in range(meta.steps):
            sb = s * meta.groups + b
            lcol[s] = as_columns(lse_ref[pl.ds(sb, 1), :])
            pcol[s] = as_columns(pos_ref[pl.ds(sb, 1), :]) - lane
            out_ref[i, s] = jnp.zeros((BLK, out_ref.shape[3]), jnp.float32)
            for j in range(meta.blocks):
                todo[n] = s * meta.blocks + j
                n = n + (meta.count(info, sb, j) > 0).astype(jnp.int32)
        for g in range(width):
            todo[n + g] = 0

        def step(it, _):
            found = []
            for g in range(width):
                k = it * width + g
                s, j = todo[k] // meta.blocks, todo[k] % meta.blocks
                sb = s * meta.groups + b
                p = jnp.exp(z_ref[sb, j] - lcol[s]) * meta.count(info, sb, j).astype(jnp.float32)
                hot = (meta.own(info, s) > 0) & (j < meta.slab_blocks)
                p = p - jnp.where(pcol[s] == (j * BLK).astype(jnp.float32), hot.astype(jnp.float32), 0.0)
                hi, lo = split(jnp.where(k < n, p, 0.0))
                w = w_ref[meta.source(info, s, j)]
                found.append((s, dot(jnp.concatenate([hi, hi], axis=1), w, 1, 0) + dot(lo, w[:BLK], 1, 0)))
            for s, term in found:
                out_ref[i, s] += term
            return 0

        lax.fori_loop(0, (n + width - 1) // width, step, 0)

    for o, out_ref in enumerate(outs):
        first, stride = (order[o], len(order)) if order else (0, 1)

        def one(i, _, out_ref=out_ref, first=first, stride=stride):
            block(i, out_ref, first, stride)
            return 0

        lax.fori_loop(0, out_ref.shape[0], one, 0)


def params(mib):
    return pltpu.CompilerParams(vmem_limit_bytes=mib * 1024 * 1024)


SMEM = pl.BlockSpec(memory_space=pltpu.SMEM)
VMEM = pl.BlockSpec(memory_space=pltpu.VMEM)
ANY = pl.BlockSpec(memory_space=pl.ANY)


def run_scores(meta, info, queries, cache, fresh):
    width = cache.shape[1]
    group = 4
    n_src = meta.blocks + meta.slab_blocks
    most = meta.steps * meta.blocks * ((meta.groups + 1) // 2)
    return pl.pallas_call(
        functools.partial(scores_kernel, meta, group, 2.0 / math.sqrt(width)),
        in_specs=[SMEM, ANY, ANY, ANY],
        out_specs=[VMEM] * 4,
        out_shape=[
            pltpu.VMEM((meta.rows, meta.blocks, BLK, BLK), jnp.float32),
            pltpu.VMEM((n_src, 2 * BLK, width), jnp.bfloat16),
            pltpu.VMEM((meta.rows, BLK, width), jnp.bfloat16),
            pltpu.VMEM((meta.rows, BLK), jnp.float32),
        ],
        scratch_shapes=[
            pltpu.VMEM(cache.shape, jnp.float32),
            pltpu.VMEM(fresh.shape, jnp.float32),
            pltpu.VMEM((meta.rows, BLK, BLK), jnp.float32),
            pltpu.VMEM((meta.rows, BLK, BLK), jnp.float32),
            pltpu.SMEM((most + group + 1,), jnp.int32),
            pltpu.SMEM((meta.size + group,), jnp.int32),
            pltpu.SemaphoreType.DMA((3,)),
        ],
        compiler_params=params(20),
        name="scores",
    )(info, queries.reshape(meta.rows, BLK, width), cache, fresh)


def run_grads(meta, info, z, q, lse, first, count, dep):
    group = 4
    return pl.pallas_call(
        functools.partial(grad_kernel, meta, first, group),
        in_specs=[SMEM, VMEM, VMEM, VMEM, ANY],
        out_specs=VMEM,
        out_shape=pltpu.VMEM((count * BLK, q.shape[2]), jnp.float32),
        scratch_shapes=[pltpu.SMEM((meta.rows + group,), jnp.int32)],
        compiler_params=params(10),
        name="cache_grad",
    )(info, z, q, lse, dep)


def run_terms(meta, info, z, w, lse, pos, order, dep):
    group = 4
    n_out = max(1, len(order))
    shape = (meta.groups // n_out, meta.steps, BLK, w.shape[2])
    return pl.pallas_call(
        functools.partial(term_kernel, meta, order, group),
        in_specs=[SMEM, VMEM, VMEM, VMEM, VMEM, ANY],
        out_specs=[VMEM] * n_out,
        out_shape=[pltpu.VMEM(shape, jnp.float32)] * n_out,
        scratch_shapes=[
            pltpu.SMEM((meta.steps * meta.blocks + group,), jnp.int32),
            pltpu.VMEM((meta.steps, BLK, BLK), jnp.float32),
            pltpu.VMEM((meta.steps, BLK, BLK), jnp.float32),
        ],
        compiler_params=params(10),
        name="query_term",
    )(info, z, w, lse, pos, dep)


def exchange_lse(lse):
    n = lax.axis_size("cache")
    bit = 1
    while bit < n:
        lse = jnp.logaddexp(lse, lax.ppermute(lse, "cache", [(i, i ^ bit) for i in range(n)]))
        bit *= 2
    return lse


def barrier(*values):
    return lax.optimization_barrier(tuple(values))


def token(x):
    return lax.slice(x, (0,) * x.ndim, (1,) * x.ndim).reshape(1, 1)


def sum_line(chunks, n, jobs):
    if lax.axis_size("batch") != 4:
        tok = token(chunks[0])
        for t in sorted(jobs):
            tok = jobs[t](tok)
        return [lax.psum(c, "batch") for c in chunks]
    at = lax.axis_index("batch")
    end = (at == 0) | (at == 3)
    lag_in, lag_mid, lag_out = LAGS
    late = lag_in + lag_mid
    swap, mid, inner, total, out = {}, {}, {}, {}, {}
    prev = [token(chunks[0])]
    for t in range(n + late + lag_out):
        u, k, o = t - lag_in, t - late, t - late - lag_out
        ops = []
        if 0 <= u < n:
            ops += [chunks[u], swap[u]]
        if 0 <= o < n:
            ops += [total[o], swap[o + late]]
        if 0 <= k < n:
            ops += [inner[k], mid[k]]
        if t < n:
            ops += [chunks[t]]
        ops = list(barrier(*ops, *prev)[:len(ops)])
        away = None
        if 0 <= u < n:
            inner[u] = ops.pop(0) + ops.pop(0)
        if 0 <= o < n:
            own = ops.pop(0)
            out[o] = jnp.where(end, ops.pop(0), own)
        if 0 <= k < n:
            away = total[k] = ops.pop(0) + ops.pop(0)
        if t < n:
            chunk = ops.pop(0)
            away = chunk if away is None else jnp.where(end, chunk, away)
        new = [] if away is None else [away]
        if 0 <= u < n:
            new.append(inner[u])
        if 0 <= o < n:
            new.append(out[o])
        if not new:
            continue
        new = list(barrier(*new))
        prev = [token(v) for v in new]
        if away is not None:
            swap[t] = lax.ppermute(new.pop(0), "batch", [(0, 1), (1, 0), (2, 3), (3, 2)])
        if 0 <= u < n:
            inner[u] = new.pop(0)
            mid[u] = lax.ppermute(inner[u], "batch", [(1, 2), (2, 1)])
        if 0 <= o < n:
            out[o] = new.pop(0)
        if t in jobs:
            prev.append(jobs[t](prev[0]))
    return [out[k] for k in range(n)]


class HomeSum:
    def __init__(self, odd, even):
        self.n = lax.axis_size("cache")
        self.even = even
        self.got = self.move(odd, 1)
        self.bits = [1 << i for i in range(1, self.n.bit_length() - 1)]
        self.cur = None

    def move(self, x, bit):
        return lax.ppermute(x, "cache", [(i, i ^ bit) for i in range(self.n)])

    def send(self, tok):
        orders = (self.bits, self.bits[::-1])
        if self.cur is None:
            even, got = barrier(self.even, self.got, tok)[:2]
            half = even.shape[2] // 2
            self.cur = []
            for lo in (0, half):
                both = even[:, :, lo:lo + half] + got[:, :, lo:lo + half]
                self.cur.append({2 * i: both[i] for i in range(self.n // 2)})
            self.stage = 0
        else:
            self.receive(tok)
        self.away = []
        if self.stage == len(self.bits):
            return token(self.cur[0][0])
        self.moved = []
        toks = []
        for cur, order in zip(self.cur, orders):
            bit = order[self.stage]
            far = [r for r in sorted(cur) if r & bit]
            stack = barrier(jnp.stack([cur[r] for r in far]))[0]
            toks.append(token(stack))
            self.moved.append((bit, far, self.move(stack, bit)))
        self.stage += 1
        return toks[0] + toks[1]

    def receive(self, tok):
        arrived = barrier(*[m[2] for m in self.moved], tok)
        for i, (bit, far, _) in enumerate(self.moved):
            cur = self.cur[i]
            self.cur[i] = {r ^ bit: cur[r ^ bit] + arrived[i][f] for f, r in enumerate(far)}

    def result(self):
        return jnp.concatenate([cur[0] for cur in self.cur], axis=1)


def on_device(queries, positives, block_list, block_count, refresh_owner, cache, fresh):
    steps, group_rows, width = queries.shape
    groups = group_rows // BLK
    blocks, slab_blocks = cache.shape[0] // BLK, fresh.shape[0] // BLK
    meta = Meta(steps, groups, blocks, slab_blocks)
    me = lax.axis_index("cache")
    block_ids = me * blocks + jnp.arange(blocks, dtype=jnp.int32)
    valid = jnp.arange(block_list.shape[2], dtype=jnp.int32)[None, None, :] < block_count[:, :, None]
    member = jnp.any((block_list[..., None] == block_ids) & valid[..., None], axis=2)
    own = refresh_owner == me
    counts = member.astype(jnp.int32) + (own[:, None, None] & (jnp.arange(blocks) < slab_blocks)).astype(jnp.int32)
    replaced = jnp.any(own[None, :] & (jnp.arange(steps)[None, :] <= jnp.arange(steps)[:, None]), axis=1)
    info = jnp.concatenate([x.astype(jnp.int32).reshape(-1) for x in (counts, member, own, replaced, me)])

    z, w, q, own_lse = run_scores(meta, info, queries, cache, fresh)
    lse = exchange_lse(own_lse)
    pos = positives.astype(jnp.float32).reshape(meta.rows, BLK)

    half = BLK // 2
    early = min(2, blocks)
    chunks = []

    def fill(first, count, tok):
        grad = run_grads(meta, info, z, q, lse, first, count, tok)
        chunks.extend(grad[i:i + half] for i in range(0, count * BLK, half))
        return token(grad)

    fill(0, early, lse)
    owners = lax.axis_size("cache")
    share = group_rows // owners
    jobs = {}
    state = []
    fast = share == BLK and owners == groups and owners & (owners - 1) == 0 and owners > 2

    def rest(tok):
        if early < blocks:
            tok = fill(early, blocks - early, tok)
        if fast:
            odd, even = run_terms(meta, info, z, w, lse, pos, (1, 0), tok)
            state.append(HomeSum(odd, even))
            tok = token(even)
        return tok

    jobs[min(LAGS[0], len(chunks)) - 1] = rest
    if fast:
        for t in HOME_SLOTS:
            jobs[t] = lambda tok: state[0].send(tok)
    out = sum_line(chunks, 2 * blocks, jobs)
    if fast:
        mine = state[0].result()
    else:
        term = run_terms(meta, info, z, w, lse, pos, (), lse)[0]
        term = jnp.swapaxes(term, 0, 1).reshape(steps, group_rows, width)
        mine = lax.psum_scatter(term, "cache", scatter_dimension=1, tiled=True)
    return mine, jnp.concatenate(out, axis=0)


def solution(mesh):
    return jax.shard_map(
        on_device,
        mesh=mesh,
        in_specs=(
            P(None, "batch", None),
            P(None, "batch"),
            P(None, "batch", None),
            P(None, "batch"),
            P(),
            P("cache", None),
            P("cache", None),
        ),
        out_specs=(P(None, ("batch", "cache"), None), P("cache", None)),
        check_vma=False,
    )
```

time: 466 us -> 194 us (0.42)
  waiting for transfers between devices: 249 us -> 33.3 us
  matrix products: 109 us -> 0 us
  starting transfers between devices: 0.2 us -> 85.8 us
  Pallas kernels: 0 us -> 46.2 us
  blocking collectives: 45.6 us -> 0 us
  between operations: 18.5 us -> 1.68 us
  local copies, waits for them, and re-layouts: 27.1 us -> 16.3 us
    psum x2 -> x0, waiting for transfers between devices: 170 us -> none  [the longest x1 120 us: on_device(): grad_total = grad_total + lax.psum(step_grad, 'batch')]
    dot_general x15 -> x0, matrix products: 109 us -> none  [the longest x3 43.8 us: on_device(): term = jnp.dot(probs, current, precision=highest)]
    ppermute x0 -> x46, starting transfers between devices: none -> 85.8 us  [the longest x22 68.9 us: sum_line(): lax.ppermute(new.pop(0), 'batch', [(0, 1), (1, 0), (2, 3), (3, 2)])]
    reduce_scatter x3 -> x0, waiting for transfers between devices: 78.8 us -> none  [on_device(): mine = lax.psum_scatter(term, 'cache', scatter_dimension=0, tiled=True)]
    pallas_call x0 -> x4, Pallas kernels: none -> 46.2 us  [the longest x1 17.8 us: run_terms(): pl.pallas_call(functools.partial(term_kernel, meta, order, group), in_spe...]
    ppermute x0 -> x46, waiting for transfers between devices: none -> 33.3 us  [the longest x5 19.2 us: move(): return lax.ppermute(x, 'cache', [(i, i ^ bit) for i in range(self.n)])]
    pmax x1 -> x0, blocking collectives: 23.3 us -> none  [on_device(): top = lax.pmax(peak, 'cache')]
    psum x1 -> x0, blocking collectives: 22.3 us -> none  [on_device(): total = lax.psum(total, 'cache')]
  transfers between devices with their start and end apart: 5 -> 46, of which waited for: 4 -> 13; matrix products, arithmetic and copies ran while one was open for 22% -> 4% of each run, Pallas kernels for 0% -> 9%
where the time goes in v2:
time: 194 us
  starting transfers between devices  85.8 us (44%)
  Pallas kernels  46.2 us (24%)
  waiting for transfers between devices  33.3 us (17%)
  local copies, waits for them, and re-layouts  16.3 us (8%)
  other arithmetic  10.3 us (5%)
    ppermute x22, starting transfers between devices, sum_line(): lax.ppermute(new.pop(0), 'batch', [(0, 1), (1, 0), (2, 3), (3, 2)])  68.9 us
    ppermute x5, waiting for transfers between devices, move(): return lax.ppermute(x, 'cache', [(i, i ^ bit) for i in range(self.n)])  19.2 us
    pallas_call x1, Pallas kernels, run_terms(): pl.pallas_call(functools.partial(term_kernel, meta, order, group), in_spe...  17.8 us
    pallas_call x1, Pallas kernels, run_scores(): pl.pallas_call(functools.partial(scores_kernel, meta, group, 2.0 / math.s...  17.5 us
    unnamed x51, local copies, waits for them, and re-layouts  12.8 us
    ppermute x16, starting transfers between devices, sum_line(): mid[u] = lax.ppermute(inner[u], 'batch', [(1, 2), (2, 1)])  11.3 us
    pallas_call x2, Pallas kernels, run_grads(): pl.pallas_call(functools.partial(grad_kernel, meta, first, group), in_spe...  11 us
    ppermute x22, waiting for transfers between devices, sum_line(): lax.ppermute(new.pop(0), 'batch', [(0, 1), (1, 0), (2, 3), (3, 2)])  7.94 us
  transfers between devices with their start and end apart: 46, of which 13 were waited for; matrix products, arithmetic and copies ran while one was open for 4% of the time, Pallas kernels for 9%

profile of v2, /device:TPU:0, one launch (start us, length us, event | category | flops | bytes accessed | tf_op | source)
XLA Modules:
  0.0 193.7 jit_solution(9521522854188046138)
XLA Ops:
  2.3 1.3 and_reduce_fusion
  3.8 2.3 %copy-done.2 = bf16[3,1024,768]{2,1,0:T(8,128)(2,1)S(1)} copy-done((bf16[3,1024,768]{2,1,0:T(8,128)(2,1)S(1)}, bf16[3,1024,768]{2,1,0:T(8,128)(2,1)}, u32[]{:S(2)}) %copy-start.2) | copy-done | bytes 4718616
  6.2 1.9 copy-done.5
  8.1 1.4 copy-done.6
  9.5 17.5 %scores.1 = (f32[24,8,128,128]{3,2,1,0:T(8,128)S(1)}, bf16[12,256,768]{2,1,0:T(8,128)(2,1)S(1)}, bf16[24,128,768]{2,1,0:T(8,128)(2,1)S(1)}, f32[24,128]{1,0:T(8,128)S(1)}) custom-call(s32[391]{0:T(512)S(1)} %concatenate.9.info, bf16[24,128,768]{2,1,0:T(8,128)(2,1)S(1)} %bitcast.6, f32[1024,768]{1,0:T(8,128)S(1)} %copy-done.5, f32[512,768]{1,0:T(8,128)S(1)} %copy-done.6), custom_call_target="tpu_custom_call" | custom-call | tf_op jit(solution)/shard_map/scores/pallas_call | solution.py:236
  27.0 1.3 collective-permute-start
  29.5 3.4 %collective-permute-done.1 = f32[24,128]{1,0:T(8,128)S(1)} collective-permute-done((f32[24,128]{1,0:T(8,128)S(1)}, f32[24,128]{1,0:T(8,128)S(1)}, u32[]{:S(2)}, u32[]{:S(2)}) %collective-permute-start.1) | collective-permute-done | bytes 12320 | tf_op jit(solution)/shard_map/ppermute | solution.py:296
  32.9 1.9 collective-permute-start.2
  34.8 1.9 collective-permute-done.2
  36.7 2.5 %cache_grad.2 = f32[256,768]{1,0:T(8,128)S(1)} custom-call(s32[391]{0:T(512)S(1)} %concatenate.9.info, f32[24,8,128,128]{3,2,1,0:T(8,128)S(1)} %get-tuple-element.170.z_ref, bf16[24,128,768]{2,1,0:T(8,128)(2,1)S(1)} %get-tuple-element.173.q_ref, f32[24,128]{1,0:T(8,128)S(1)} %add_select_fusion.lse_ref.dep, f32[24,128]{1,0:T(8,128)S(1)} %add_select_fusion.lse_ref.dep), custom_call_target="tpu_custom_call" | custom-call | tf_op jit(solution)/shard_map/cache_grad/pallas_call | solution.py:262
  40.7 8.5 %cache_grad.3 = f32[768,768]{1,0:T(8,128)S(1)} custom-call(s32[391]{0:T(512)S(1)} %concatenate.9.info, f32[24,8,128,128]{3,2,1,0:T(8,128)S(1)} %get-tuple-element.170.z_ref, bf16[24,128,768]{2,1,0:T(8,128)(2,1)S(1)} %get-tuple-element.173.q_ref, f32[24,128]{1,0:T(8,128)S(1)} %add_select_fusion.lse_ref.dep, f32[1,1]{1,0:T(1,128)} %slice.201.dep), custom_call_target="tpu_custom_call" | custom-call | tf_op jit(solution)/shard_map/cache_grad/pallas_call | solution.py:262
  49.2 1.2 collective-permute-start.4
  50.4 0.9 collective-permute-start.24
  51.3 1.1 fusion.7
  52.4 1.1 collective-permute-start.6
  53.5 3.6 %collective-permute-done.4 = f32[64,768]{1,0:T(8,128)S(1)} collective-permute-done((f32[64,768]{1,0:T(8,128)S(1)}, f32[64,768]{1,0:T(8,128)S(1)}, u32[]{:S(2)}, u32[]{:S(2)}) %collective-permute-start.4) | collective-permute-done | bytes 196640 | tf_op jit(solution)/shard_map/ppermute | solution.py:354
  57.8 1.3 collective-permute-start.7
  59.7 5.3 %collective-permute-start.26 = (f32[64,768]{1,0:T(8,128)}, f32[64,768]{1,0:T(8,128)S(1)}, u32[]{:S(2)}, u32[]{:S(2)}) collective-permute-start(f32[64,768]{1,0:T(8,128)} %copy-done.14), channel_id=1, source_target_pairs={{0,1},{1,0},{2,3},{3,2},{4,5},{5,4},{6,7},{7,6},{8,9},{9,8},{10,11... | collective-permute-start | bytes 589832 | tf_op jit(solution)/shard_map/ppermute | solution.py:354
  65.0 4.6 %copy-done.1 = f32[24,8,128,128]{3,2,1,0:T(8,128)S(1)} copy-done((f32[24,8,128,128]{3,2,1,0:T(8,128)S(1)}, f32[24,8,128,128]{3,2,1,0:T(8,128)}, u32[]{:S(2)}) %copy-start.1) | copy-done | bytes 12582936
  69.6 2.3 %copy-done.4 = bf16[12,256,768]{2,1,0:T(8,128)(2,1)S(1)} copy-done((bf16[12,256,768]{2,1,0:T(8,128)(2,1)S(1)}, bf16[12,256,768]{2,1,0:T(8,128)(2,1)}, u32[]{:S(2)}) %copy-start.4) | copy-done | bytes 4718616
  72.0 17.8 %query_term.1 = (f32[4,3,128,768]{3,2,1,0:T(8,128)S(1)}, f32[4,3,128,768]{3,2,1,0:T(8,128)S(1)}) custom-call(s32[391]{0:T(512)S(1)} %concatenate.9.info, f32[24,8,128,128]{3,2,1,0:T(8,128)S(1)} %copy-done.1, bf16[12,256,768]{2,1,0:T(8,128)(2,1)S(1)} %copy-done.4, f32[24,128]{1,0:T(8,128)S(1)} %add_select_fusion.lse_ref.dep, f32[24,128]{1,0:T(8,128)S(1)} %reshape.77.pos_ref, ...), custom_call_target="tpu_custom_call" | custom-call | tf_op jit(solution)/shard_map/query_term/pallas_call | solution.py:277
  89.9 1.1 add.207
  91.0 2.1 %collective-permute-start.25 = (f32[64,768]{1,0:T(8,128)S(1)}, f32[64,768]{1,0:T(8,128)S(1)}, u32[]{:S(2)}, u32[]{:S(2)}) collective-permute-start(f32[64,768]{1,0:T(8,128)S(1)} %copy-done.12), channel_id=1, source_target_pairs={{0,1},{1,0},{2,3},{3,2},{4,5},{5,4},{6,7},{7,6},{8,9},{9,8},{10,11... | collective-permute-start | bytes 589832 | tf_op jit(solution)/shard_map/ppermute | solution.py:354
  93.8 1.0 add.184
  94.8 1.1 broadcast_select_fusion.25
  95.9 1.9 collective-permute-start.8
  98.6 5.8 %collective-permute-start.28 = (f32[64,768]{1,0:T(8,128)S(1)}, f32[64,768]{1,0:T(8,128)S(1)}, u32[]{:S(2)}, u32[]{:S(2)}) collective-permute-start(f32[64,768]{1,0:T(8,128)S(1)} %get-tuple-element.256), channel_id=1, source_target_pairs={{0,1},{1,0},{2,3},{3,2},{4,5},{5,4},{6,7},{7,6},{8,9},{9,8},{10,11... | collective-permute-start | bytes 589832 | tf_op jit(solution)/shard_map/ppermute | solution.py:354
  104.4 1.7 collective-permute-done.8
  106.8 3.3 %collective-permute-start.12 = (f32[64,768]{1,0:T(8,128)S(1)}, f32[64,768]{1,0:T(8,128)S(1)}, u32[]{:S(2)}, u32[]{:S(2)}) collective-permute-start(f32[64,768]{1,0:T(8,128)S(1)} %get-tuple-element.195), channel_id=1, source_target_pairs={{0,1},{1,0},{2,3},{3,2},{4,5},{5,4},{6,7},{7,6},{8,9},{9,8},{10,11... | collective-permute-start | bytes 589832 | tf_op jit(solution)/shard_map/ppermute | solution.py:354
  111.0 4.7 %collective-permute-start.30 = (f32[64,768]{1,0:T(8,128)S(1)}, f32[64,768]{1,0:T(8,128)S(1)}, u32[]{:S(2)}, u32[]{:S(2)}) collective-permute-start(f32[64,768]{1,0:T(8,128)S(1)} %get-tuple-element.267), channel_id=1, source_target_pairs={{0,1},{1,0},{2,3},{3,2},{4,5},{5,4},{6,7},{7,6},{8,9},{9,8},{10,11... | collective-permute-start | bytes 589832 | tf_op jit(solution)/shard_map/ppermute | solution.py:354
  116.6 2.7 %collective-permute-start.14 = (f32[64,768]{1,0:T(8,128)S(1)}, f32[64,768]{1,0:T(8,128)S(1)}, u32[]{:S(2)}, u32[]{:S(2)}) collective-permute-start(f32[64,768]{1,0:T(8,128)S(1)} %get-tuple-element.206), channel_id=1, source_target_pairs={{0,1},{1,0},{2,3},{3,2},{4,5},{5,4},{6,7},{7,6},{8,9},{9,8},{10,11... | collective-permute-start | bytes 589832 | tf_op jit(solution)/shard_map/ppermute | solution.py:354
  120.4 4.3 %collective-permute-start.32 = (f32[64,768]{1,0:T(8,128)S(1)}, f32[64,768]{1,0:T(8,128)S(1)}, u32[]{:S(2)}, u32[]{:S(2)}) collective-permute-start(f32[64,768]{1,0:T(8,128)S(1)} %get-tuple-element.278), channel_id=1, source_target_pairs={{0,1},{1,0},{2,3},{3,2},{4,5},{5,4},{6,7},{7,6},{8,9},{9,8},{10,11... | collective-permute-start | bytes 589832 | tf_op jit(solution)/shard_map/ppermute | solution.py:354
  125.6 3.6 %collective-permute-start.16 = (f32[64,768]{1,0:T(8,128)S(1)}, f32[64,768]{1,0:T(8,128)S(1)}, u32[]{:S(2)}, u32[]{:S(2)}) collective-permute-start(f32[64,768]{1,0:T(8,128)S(1)} %get-tuple-element.215), channel_id=1, source_target_pairs={{0,1},{1,0},{2,3},{3,2},{4,5},{5,4},{6,7},{7,6},{8,9},{9,8},{10,11... | collective-permute-start | bytes 589832 | tf_op jit(solution)/shard_map/ppermute | solution.py:354
  130.0 4.1 %collective-permute-start.34 = (f32[64,768]{1,0:T(8,128)S(1)}, f32[64,768]{1,0:T(8,128)S(1)}, u32[]{:S(2)}, u32[]{:S(2)}) collective-permute-start(f32[64,768]{1,0:T(8,128)S(1)} %get-tuple-element.289), channel_id=1, source_target_pairs={{0,1},{1,0},{2,3},{3,2},{4,5},{5,4},{6,7},{7,6},{8,9},{9,8},{10,11... | collective-permute-start | bytes 589832 | tf_op jit(solution)/shard_map/ppermute | solution.py:354
  135.0 3.7 %collective-permute-start.20 = (f32[64,768]{1,0:T(8,128)S(1)}, f32[64,768]{1,0:T(8,128)S(1)}, u32[]{:S(2)}, u32[]{:S(2)}) collective-permute-start(f32[64,768]{1,0:T(8,128)S(1)} %get-tuple-element.224), channel_id=1, source_target_pairs={{0,1},{1,0},{2,3},{3,2},{4,5},{5,4},{6,7},{7,6},{8,9},{9,8},{10,11... | collective-permute-start | bytes 589832 | tf_op jit(solution)/shard_map/ppermute | solution.py:354
  139.9 3.9 %collective-permute-start.36 = (f32[64,768]{1,0:T(8,128)S(1)}, f32[64,768]{1,0:T(8,128)S(1)}, u32[]{:S(2)}, u32[]{:S(2)}) collective-permute-start(f32[64,768]{1,0:T(8,128)S(1)} %get-tuple-element.300), channel_id=1, source_target_pairs={{0,1},{1,0},{2,3},{3,2},{4,5},{5,4},{6,7},{7,6},{8,9},{9,8},{10,11... | collective-permute-start | bytes 589832 | tf_op jit(solution)/shard_map/ppermute | solution.py:354
  144.7 3.1 %collective-permute-start.22 = (f32[64,768]{1,0:T(8,128)S(1)}, f32[64,768]{1,0:T(8,128)S(1)}, u32[]{:S(2)}, u32[]{:S(2)}) collective-permute-start(f32[64,768]{1,0:T(8,128)S(1)} %add.198), channel_id=1, source_target_pairs={{0,1},{1,0},{2,3},{3,2},{4,5},{5,4},{6,7},{7,6},{8,9},{9,8},{10,11... | collective-permute-start | bytes 589832 | tf_op jit(solution)/shard_map/ppermute | solution.py:354
  149.1 3.7 %collective-permute-start.38 = (f32[64,768]{1,0:T(8,128)S(1)}, f32[64,768]{1,0:T(8,128)S(1)}, u32[]{:S(2)}, u32[]{:S(2)}) collective-permute-start(f32[64,768]{1,0:T(8,128)S(1)} %add.218), channel_id=1, source_target_pairs={{0,1},{1,0},{2,3},{3,2},{4,5},{5,4},{6,7},{7,6},{8,9},{9,8},{10,11... | collective-permute-start | bytes 589832 | tf_op jit(solution)/shard_map/ppermute | solution.py:354
  154.9 2.8 %collective-permute-start.40 = (f32[64,768]{1,0:T(8,128)S(1)}, f32[64,768]{1,0:T(8,128)S(1)}, u32[]{:S(2)}, u32[]{:S(2)}) collective-permute-start(f32[64,768]{1,0:T(8,128)S(1)} %add.200), channel_id=1, source_target_pairs={{0,1},{1,0},{2,3},{3,2},{4,5},{5,4},{6,7},{7,6},{8,9},{9,8},{10,11... | collective-permute-start | bytes 589832 | tf_op jit(solution)/shard_map/ppermute | solution.py:354
  158.5 3.9 %collective-permute-start.42 = (f32[64,768]{1,0:T(8,128)S(1)}, f32[64,768]{1,0:T(8,128)S(1)}, u32[]{:S(2)}, u32[]{:S(2)}) collective-permute-start(f32[64,768]{1,0:T(8,128)S(1)} %add.220), channel_id=1, source_target_pairs={{0,1},{1,0},{2,3},{3,2},{4,5},{5,4},{6,7},{7,6},{8,9},{9,8},{10,11... | collective-permute-start | bytes 589832 | tf_op jit(solution)/shard_map/ppermute | solution.py:354
  163.2 3.9 %collective-permute-start.44 = (f32[64,768]{1,0:T(8,128)S(1)}, f32[64,768]{1,0:T(8,128)S(1)}, u32[]{:S(2)}, u32[]{:S(2)}) collective-permute-start(f32[64,768]{1,0:T(8,128)S(1)} %add.222), channel_id=1, source_target_pairs={{0,1},{1,0},{2,3},{3,2},{4,5},{5,4},{6,7},{7,6},{8,9},{9,8},{10,11... | collective-permute-start | bytes 589832 | tf_op jit(solution)/shard_map/ppermute | solution.py:354
  167.1 1.1 collective-permute-done.42
  168.2 2.8 %collective-permute-start.45 = (f32[64,768]{1,0:T(8,128)S(1)}, f32[64,768]{1,0:T(8,128)S(1)}, u32[]{:S(2)}, u32[]{:S(2)}) collective-permute-start(f32[64,768]{1,0:T(8,128)S(1)} %add.223), channel_id=1, source_target_pairs={{0,1},{1,0},{2,3},{3,2},{4,5},{5,4},{6,7},{7,6},{8,9},{9,8},{10,11... | collective-permute-start | bytes 589832 | tf_op jit(solution)/shard_map/ppermute | solution.py:354
  171.0 9.5 %collective-permute-done.10 = f32[2,3,64,768]{3,2,1,0:T(8,128)S(1)} collective-permute-done((f32[2,3,64,768]{3,2,1,0:T(8,128)S(1)}, f32[2,3,64,768]{3,2,1,0:T(8,128)S(1)}, u32[]{:S(2)}, u32[]{:S(2)}) %collective-permute-start.10) | collective-permute-done | bytes 1179680 | tf_op jit(solution)/shard_map/ppermute | solution.py:374
  180.7 1.8 collective-permute-start.19
  182.7 8.0 %collective-permute-done.19 = f32[1,3,64,768]{3,2,1,0:T(8,128)S(1)} collective-permute-done((f32[1,3,64,768]{3,2,1,0:T(8,128)S(1)}, f32[1,3,64,768]{3,2,1,0:T(8,128)S(1)}, u32[]{:S(2)}, u32[]{:S(2)}) %collective-permute-start.19) | collective-permute-done | bytes 589856 | tf_op jit(solution)/shard_map/ppermute | solution.py:374
  190.6 1.7 collective-permute-done.18
  192.6 1.1 pad_maximum_fusion.1
  (178 shorter events, 20.5 us)
Async XLA Ops:
  27.0 2.2 %collective-permute-start = (f32[24,128]{1,0:T(8,128)S(1)}, f32[24,128]{1,0:T(8,128)S(1)}, u32[]{:S(2)}, u32[]{:S(2)}) collective-permute-start(f32[24,128]{1,0:T(8,128)S(1)} %get-tuple-element.172), channel_id=1, source_target_pairs={{0,4},{4,0},{8,12},{12,8},{16,20},{20,16},{24,28},{28,24},{1,5},{5... | collective-permute-start | bytes 36872 | tf_op jit(solution)/shard_map/ppermute | solution.py:296
  29.2 3.8 %collective-permute-start.1 = (f32[24,128]{1,0:T(8,128)S(1)}, f32[24,128]{1,0:T(8,128)S(1)}, u32[]{:S(2)}, u32[]{:S(2)}) collective-permute-start(f32[24,128]{1,0:T(8,128)S(1)} %add_select_fusion.2), channel_id=1, source_target_pairs={{0,8},{4,12},{8,0},{12,4},{16,24},{20,28},{24,16},{28,20},{1,9},{5... | collective-permute-start | bytes 36872 | tf_op jit(solution)/shard_map/ppermute | solution.py:296
  32.9 3.8 %collective-permute-start.2 = (f32[24,128]{1,0:T(8,128)S(1)}, f32[24,128]{1,0:T(8,128)S(1)}, u32[]{:S(2)}, u32[]{:S(2)}) collective-permute-start(f32[24,128]{1,0:T(8,128)S(1)} %add_select_fusion.1), channel_id=1, source_target_pairs={{0,16},{4,20},{8,24},{12,28},{16,0},{20,4},{24,8},{28,12},{1,17},{... | collective-permute-start | bytes 36872 | tf_op jit(solution)/shard_map/ppermute | solution.py:296
  49.2 7.9 %collective-permute-start.4 = (f32[64,768]{1,0:T(8,128)S(1)}, f32[64,768]{1,0:T(8,128)S(1)}, u32[]{:S(2)}, u32[]{:S(2)}) collective-permute-start(f32[64,768]{1,0:T(8,128)S(1)} %get-tuple-element.177), channel_id=1, source_target_pairs={{0,1},{1,0},{2,3},{3,2},{4,5},{5,4},{6,7},{7,6},{8,9},{9,8},{10,11... | collective-permute-start | bytes 589832 | tf_op jit(solution)/shard_map/ppermute | solution.py:354
  50.4 39.4 %collective-permute-start.24 = (f32[64,768]{1,0:T(8,128)}, f32[64,768]{1,0:T(8,128)}, u32[]{:S(2)}, u32[]{:S(2)}) collective-permute-start(f32[64,768]{1,0:T(8,128)} %get-tuple-element.247), channel_id=1, source_target_pairs={{0,1},{1,0},{2,3},{3,2},{4,5},{5,4},{6,7},{7,6},{8,9},{9,8},{10,11... | collective-permute-start | bytes 589832 | tf_op jit(solution)/shard_map/ppermute | solution.py:354
  52.4 38.6 %collective-permute-start.6 = (f32[64,768]{1,0:T(8,128)}, f32[64,768]{1,0:T(8,128)}, u32[]{:S(2)}, u32[]{:S(2)}) collective-permute-start(f32[64,768]{1,0:T(8,128)} %get-tuple-element.184), channel_id=1, source_target_pairs={{0,1},{1,0},{2,3},{3,2},{4,5},{5,4},{6,7},{7,6},{8,9},{9,8},{10,11... | collective-permute-start | bytes 589832 | tf_op jit(solution)/shard_map/ppermute | solution.py:354
  57.8 35.3 %collective-permute-start.7 = (f32[64,768]{1,0:T(8,128)}, f32[64,768]{1,0:T(8,128)}, u32[]{:S(2)}, u32[]{:S(2)}) collective-permute-start(f32[64,768]{1,0:T(8,128)} %add.182), channel_id=1, source_target_pairs={{1,2},{2,1},{5,6},{6,5},{9,10},{10,9},{13,14},{14,13},{17,18},{18,... | collective-permute-start | bytes 589832 | tf_op jit(solution)/shard_map/ppermute | solution.py:357
  59.7 36.2 %collective-permute-start.26 = (f32[64,768]{1,0:T(8,128)}, f32[64,768]{1,0:T(8,128)S(1)}, u32[]{:S(2)}, u32[]{:S(2)}) collective-permute-start(f32[64,768]{1,0:T(8,128)} %copy-done.14), channel_id=1, source_target_pairs={{0,1},{1,0},{2,3},{3,2},{4,5},{5,4},{6,7},{7,6},{8,9},{9,8},{10,11... | collective-permute-start | bytes 589832 | tf_op jit(solution)/shard_map/ppermute | solution.py:354
  71.9 26.6 %copy-start.15 = (f32[64,768]{1,0:T(8,128)S(1)}, f32[64,768]{1,0:T(8,128)}, u32[]{:S(2)}) copy-start(f32[64,768]{1,0:T(8,128)} %copy-done.14) | copy-start | bytes 589828
  71.9 26.6 %copy-start.10 = (f32[64,768]{1,0:T(8,128)S(1)}, f32[64,768]{1,0:T(8,128)}, u32[]{:S(2)}) copy-start(f32[64,768]{1,0:T(8,128)} %get-tuple-element.272) | copy-start | bytes 589828
  89.7 63.8 %collective-permute-start.3 = (f32[4,3,128,768]{3,2,1,0:T(8,128)S(1)}, f32[4,3,128,768]{3,2,1,0:T(8,128)S(1)}, u32[]{:S(2)}, u32[]{:S(2)}) collective-permute-start(f32[4,3,128,768]{3,2,1,0:T(8,128)S(1)} %get-tuple-element.175), channel_id=1, source_target_pairs={{0,4},{4,0},{8,12},{12,8},{16,20},{20,16},{24,28},{28,24},{1,5},{5... | collective-permute-start | bytes 14155784 | tf_op jit(solution)/shard_map/ppermute | solution.py:374
  89.8 8.8 %collective-permute-start.5 = (f32[64,768]{1,0:T(8,128)S(1)}, f32[64,768]{1,0:T(8,128)S(1)}, u32[]{:S(2)}, u32[]{:S(2)}) collective-permute-start(f32[64,768]{1,0:T(8,128)S(1)} %copy-done.13), channel_id=1, source_target_pairs={{0,1},{1,0},{2,3},{3,2},{4,5},{5,4},{6,7},{7,6},{8,9},{9,8},{10,11... | collective-permute-start | bytes 589832 | tf_op jit(solution)/shard_map/ppermute | solution.py:354
  91.0 19.1 %collective-permute-start.25 = (f32[64,768]{1,0:T(8,128)S(1)}, f32[64,768]{1,0:T(8,128)S(1)}, u32[]{:S(2)}, u32[]{:S(2)}) collective-permute-start(f32[64,768]{1,0:T(8,128)S(1)} %copy-done.12), channel_id=1, source_target_pairs={{0,1},{1,0},{2,3},{3,2},{4,5},{5,4},{6,7},{7,6},{8,9},{9,8},{10,11... | collective-permute-start | bytes 589832 | tf_op jit(solution)/shard_map/ppermute | solution.py:354
  93.1 4.7 %collective-permute-start.27 = (f32[64,768]{1,0:T(8,128)S(1)}, f32[64,768]{1,0:T(8,128)S(1)}, u32[]{:S(2)}, u32[]{:S(2)}) collective-permute-start(f32[64,768]{1,0:T(8,128)S(1)} %add.207), channel_id=1, source_target_pairs={{1,2},{2,1},{5,6},{6,5},{9,10},{10,9},{13,14},{14,13},{17,18},{18,... | collective-permute-start | bytes 589832 | tf_op jit(solution)/shard_map/ppermute | solution.py:357
  95.9 10.1 %collective-permute-start.8 = (f32[64,768]{1,0:T(8,128)S(1)}, f32[64,768]{1,0:T(8,128)S(1)}, u32[]{:S(2)}, u32[]{:S(2)}) collective-permute-start(f32[64,768]{1,0:T(8,128)S(1)} %get-tuple-element.186), channel_id=1, source_target_pairs={{0,1},{1,0},{2,3},{3,2},{4,5},{5,4},{6,7},{7,6},{8,9},{9,8},{10,11... | collective-permute-start | bytes 589832 | tf_op jit(solution)/shard_map/ppermute | solution.py:354
  97.8 8.9 %collective-permute-start.9 = (f32[64,768]{1,0:T(8,128)S(1)}, f32[64,768]{1,0:T(8,128)S(1)}, u32[]{:S(2)}, u32[]{:S(2)}) collective-permute-start(f32[64,768]{1,0:T(8,128)S(1)} %add.184), channel_id=1, source_target_pairs={{1,2},{2,1},{5,6},{6,5},{9,10},{10,9},{13,14},{14,13},{17,18},{18,... | collective-permute-start | bytes 589832 | tf_op jit(solution)/shard_map/ppermute | solution.py:357
  98.6 12.2 %collective-permute-start.28 = (f32[64,768]{1,0:T(8,128)S(1)}, f32[64,768]{1,0:T(8,128)S(1)}, u32[]{:S(2)}, u32[]{:S(2)}) collective-permute-start(f32[64,768]{1,0:T(8,128)S(1)} %get-tuple-element.256), channel_id=1, source_target_pairs={{0,1},{1,0},{2,3},{3,2},{4,5},{5,4},{6,7},{7,6},{8,9},{9,8},{10,11... | collective-permute-start | bytes 589832 | tf_op jit(solution)/shard_map/ppermute | solution.py:354
  106.1 4.8 %collective-permute-start.29 = (f32[64,768]{1,0:T(8,128)S(1)}, f32[64,768]{1,0:T(8,128)S(1)}, u32[]{:S(2)}, u32[]{:S(2)}) collective-permute-start(f32[64,768]{1,0:T(8,128)S(1)} %add.209), channel_id=1, source_target_pairs={{1,2},{2,1},{5,6},{6,5},{9,10},{10,9},{13,14},{14,13},{17,18},{18,... | collective-permute-start | bytes 589832 | tf_op jit(solution)/shard_map/ppermute | solution.py:357
  106.8 9.6 %collective-permute-start.12 = (f32[64,768]{1,0:T(8,128)S(1)}, f32[64,768]{1,0:T(8,128)S(1)}, u32[]{:S(2)}, u32[]{:S(2)}) collective-permute-start(f32[64,768]{1,0:T(8,128)S(1)} %get-tuple-element.195), channel_id=1, source_target_pairs={{0,1},{1,0},{2,3},{3,2},{4,5},{5,4},{6,7},{7,6},{8,9},{9,8},{10,11... | collective-permute-start | bytes 589832 | tf_op jit(solution)/shard_map/ppermute | solution.py:354
  110.2 6.2 %collective-permute-start.13 = (f32[64,768]{1,0:T(8,128)S(1)}, f32[64,768]{1,0:T(8,128)S(1)}, u32[]{:S(2)}, u32[]{:S(2)}) collective-permute-start(f32[64,768]{1,0:T(8,128)S(1)} %add.186), channel_id=1, source_target_pairs={{1,2},{2,1},{5,6},{6,5},{9,10},{10,9},{13,14},{14,13},{17,18},{18,... | collective-permute-start | bytes 589832 | tf_op jit(solution)/shard_map/ppermute | solution.py:357
  111.0 9.3 %collective-permute-start.30 = (f32[64,768]{1,0:T(8,128)S(1)}, f32[64,768]{1,0:T(8,128)S(1)}, u32[]{:S(2)}, u32[]{:S(2)}) collective-permute-start(f32[64,768]{1,0:T(8,128)S(1)} %get-tuple-element.267), channel_id=1, source_target_pairs={{0,1},{1,0},{2,3},{3,2},{4,5},{5,4},{6,7},{7,6},{8,9},{9,8},{10,11... | collective-permute-start | bytes 589832 | tf_op jit(solution)/shard_map/ppermute | solution.py:354
  115.7 4.6 %collective-permute-start.31 = (f32[64,768]{1,0:T(8,128)S(1)}, f32[64,768]{1,0:T(8,128)S(1)}, u32[]{:S(2)}, u32[]{:S(2)}) collective-permute-start(f32[64,768]{1,0:T(8,128)S(1)} %add.211), channel_id=1, source_target_pairs={{1,2},{2,1},{5,6},{6,5},{9,10},{10,9},{13,14},{14,13},{17,18},{18,... | collective-permute-start | bytes 589832 | tf_op jit(solution)/shard_map/ppermute | solution.py:357
  116.6 8.9 %collective-permute-start.14 = (f32[64,768]{1,0:T(8,128)S(1)}, f32[64,768]{1,0:T(8,128)S(1)}, u32[]{:S(2)}, u32[]{:S(2)}) collective-permute-start(f32[64,768]{1,0:T(8,128)S(1)} %get-tuple-element.206), channel_id=1, source_target_pairs={{0,1},{1,0},{2,3},{3,2},{4,5},{5,4},{6,7},{7,6},{8,9},{9,8},{10,11... | collective-permute-start | bytes 589832 | tf_op jit(solution)/shard_map/ppermute | solution.py:354
  119.3 6.2 %collective-permute-start.15 = (f32[64,768]{1,0:T(8,128)S(1)}, f32[64,768]{1,0:T(8,128)S(1)}, u32[]{:S(2)}, u32[]{:S(2)}) collective-permute-start(f32[64,768]{1,0:T(8,128)S(1)} %add.190), channel_id=1, source_target_pairs={{1,2},{2,1},{5,6},{6,5},{9,10},{10,9},{13,14},{14,13},{17,18},{18,... | collective-permute-start | bytes 589832 | tf_op jit(solution)/shard_map/ppermute | solution.py:357
  120.4 9.5 %collective-permute-start.32 = (f32[64,768]{1,0:T(8,128)S(1)}, f32[64,768]{1,0:T(8,128)S(1)}, u32[]{:S(2)}, u32[]{:S(2)}) collective-permute-start(f32[64,768]{1,0:T(8,128)S(1)} %get-tuple-element.278), channel_id=1, source_target_pairs={{0,1},{1,0},{2,3},{3,2},{4,5},{5,4},{6,7},{7,6},{8,9},{9,8},{10,11... | collective-permute-start | bytes 589832 | tf_op jit(solution)/shard_map/ppermute | solution.py:354
  124.7 5.2 %collective-permute-start.33 = (f32[64,768]{1,0:T(8,128)S(1)}, f32[64,768]{1,0:T(8,128)S(1)}, u32[]{:S(2)}, u32[]{:S(2)}) collective-permute-start(f32[64,768]{1,0:T(8,128)S(1)} %add.213), channel_id=1, source_target_pairs={{1,2},{2,1},{5,6},{6,5},{9,10},{10,9},{13,14},{14,13},{17,18},{18,... | collective-permute-start | bytes 589832 | tf_op jit(solution)/shard_map/ppermute | solution.py:357
  125.6 9.4 %collective-permute-start.16 = (f32[64,768]{1,0:T(8,128)S(1)}, f32[64,768]{1,0:T(8,128)S(1)}, u32[]{:S(2)}, u32[]{:S(2)}) collective-permute-start(f32[64,768]{1,0:T(8,128)S(1)} %get-tuple-element.215), channel_id=1, source_target_pairs={{0,1},{1,0},{2,3},{3,2},{4,5},{5,4},{6,7},{7,6},{8,9},{9,8},{10,11... | collective-permute-start | bytes 589832 | tf_op jit(solution)/shard_map/ppermute | solution.py:354
  129.2 5.8 %collective-permute-start.17 = (f32[64,768]{1,0:T(8,128)S(1)}, f32[64,768]{1,0:T(8,128)S(1)}, u32[]{:S(2)}, u32[]{:S(2)}) collective-permute-start(f32[64,768]{1,0:T(8,128)S(1)} %add.192), channel_id=1, source_target_pairs={{1,2},{2,1},{5,6},{6,5},{9,10},{10,9},{13,14},{14,13},{17,18},{18,... | collective-permute-start | bytes 589832 | tf_op jit(solution)/shard_map/ppermute | solution.py:357
  130.0 9.8 %collective-permute-start.34 = (f32[64,768]{1,0:T(8,128)S(1)}, f32[64,768]{1,0:T(8,128)S(1)}, u32[]{:S(2)}, u32[]{:S(2)}) collective-permute-start(f32[64,768]{1,0:T(8,128)S(1)} %get-tuple-element.289), channel_id=1, source_target_pairs={{0,1},{1,0},{2,3},{3,2},{4,5},{5,4},{6,7},{7,6},{8,9},{9,8},{10,11... | collective-permute-start | bytes 589832 | tf_op jit(solution)/shard_map/ppermute | solution.py:354
  134.1 5.8 %collective-permute-start.35 = (f32[64,768]{1,0:T(8,128)S(1)}, f32[64,768]{1,0:T(8,128)S(1)}, u32[]{:S(2)}, u32[]{:S(2)}) collective-permute-start(f32[64,768]{1,0:T(8,128)S(1)} %add.215), channel_id=1, source_target_pairs={{1,2},{2,1},{5,6},{6,5},{9,10},{10,9},{13,14},{14,13},{17,18},{18,... | collective-permute-start | bytes 589832 | tf_op jit(solution)/shard_map/ppermute | solution.py:357
  135.0 9.5 %collective-permute-start.20 = (f32[64,768]{1,0:T(8,128)S(1)}, f32[64,768]{1,0:T(8,128)S(1)}, u32[]{:S(2)}, u32[]{:S(2)}) collective-permute-start(f32[64,768]{1,0:T(8,128)S(1)} %get-tuple-element.224), channel_id=1, source_target_pairs={{0,1},{1,0},{2,3},{3,2},{4,5},{5,4},{6,7},{7,6},{8,9},{9,8},{10,11... | collective-permute-start | bytes 589832 | tf_op jit(solution)/shard_map/ppermute | solution.py:354
  138.8 5.8 %collective-permute-start.21 = (f32[64,768]{1,0:T(8,128)S(1)}, f32[64,768]{1,0:T(8,128)S(1)}, u32[]{:S(2)}, u32[]{:S(2)}) collective-permute-start(f32[64,768]{1,0:T(8,128)S(1)} %add.194), channel_id=1, source_target_pairs={{1,2},{2,1},{5,6},{6,5},{9,10},{10,9},{13,14},{14,13},{17,18},{18,... | collective-permute-start | bytes 589832 | tf_op jit(solution)/shard_map/ppermute | solution.py:357
  139.9 9.1 %collective-permute-start.36 = (f32[64,768]{1,0:T(8,128)S(1)}, f32[64,768]{1,0:T(8,128)S(1)}, u32[]{:S(2)}, u32[]{:S(2)}) collective-permute-start(f32[64,768]{1,0:T(8,128)S(1)} %get-tuple-element.300), channel_id=1, source_target_pairs={{0,1},{1,0},{2,3},{3,2},{4,5},{5,4},{6,7},{7,6},{8,9},{9,8},{10,11... | collective-permute-start | bytes 589832 | tf_op jit(solution)/shard_map/ppermute | solution.py:354
  143.8 5.2 %collective-permute-start.37 = (f32[64,768]{1,0:T(8,128)S(1)}, f32[64,768]{1,0:T(8,128)S(1)}, u32[]{:S(2)}, u32[]{:S(2)}) collective-permute-start(f32[64,768]{1,0:T(8,128)S(1)} %add.217), channel_id=1, source_target_pairs={{1,2},{2,1},{5,6},{6,5},{9,10},{10,9},{13,14},{14,13},{17,18},{18,... | collective-permute-start | bytes 589832 | tf_op jit(solution)/shard_map/ppermute | solution.py:357
  144.7 8.9 %collective-permute-start.22 = (f32[64,768]{1,0:T(8,128)S(1)}, f32[64,768]{1,0:T(8,128)S(1)}, u32[]{:S(2)}, u32[]{:S(2)}) collective-permute-start(f32[64,768]{1,0:T(8,128)S(1)} %add.198), channel_id=1, source_target_pairs={{0,1},{1,0},{2,3},{3,2},{4,5},{5,4},{6,7},{7,6},{8,9},{9,8},{10,11... | collective-permute-start | bytes 589832 | tf_op jit(solution)/shard_map/ppermute | solution.py:354
  147.8 5.8 %collective-permute-start.23 = (f32[64,768]{1,0:T(8,128)S(1)}, f32[64,768]{1,0:T(8,128)S(1)}, u32[]{:S(2)}, u32[]{:S(2)}) collective-permute-start(f32[64,768]{1,0:T(8,128)S(1)} %add.199), channel_id=1, source_target_pairs={{1,2},{2,1},{5,6},{6,5},{9,10},{10,9},{13,14},{14,13},{17,18},{18,... | collective-permute-start | bytes 589832 | tf_op jit(solution)/shard_map/ppermute | solution.py:357
  149.1 8.5 %collective-permute-start.38 = (f32[64,768]{1,0:T(8,128)S(1)}, f32[64,768]{1,0:T(8,128)S(1)}, u32[]{:S(2)}, u32[]{:S(2)}) collective-permute-start(f32[64,768]{1,0:T(8,128)S(1)} %add.218), channel_id=1, source_target_pairs={{0,1},{1,0},{2,3},{3,2},{4,5},{5,4},{6,7},{7,6},{8,9},{9,8},{10,11... | collective-permute-start | bytes 589832 | tf_op jit(solution)/shard_map/ppermute | solution.py:354
  152.8 5.5 %collective-permute-start.39 = (f32[64,768]{1,0:T(8,128)S(1)}, f32[64,768]{1,0:T(8,128)S(1)}, u32[]{:S(2)}, u32[]{:S(2)}) collective-permute-start(f32[64,768]{1,0:T(8,128)S(1)} %add.219), channel_id=1, source_target_pairs={{1,2},{2,1},{5,6},{6,5},{9,10},{10,9},{13,14},{14,13},{17,18},{18,... | collective-permute-start | bytes 589832 | tf_op jit(solution)/shard_map/ppermute | solution.py:357
  154.6 25.9 %collective-permute-start.10 = (f32[2,3,64,768]{3,2,1,0:T(8,128)S(1)}, f32[2,3,64,768]{3,2,1,0:T(8,128)S(1)}, u32[]{:S(2)}, u32[]{:S(2)}) collective-permute-start(f32[2,3,64,768]{3,2,1,0:T(8,128)S(1)} %pad_maximum_fusion), channel_id=1, source_target_pairs={{0,8},{4,12},{8,0},{12,4},{16,24},{20,28},{24,16},{28,20},{1,9},{5... | collective-permute-start | bytes 3538952 | tf_op jit(solution)/shard_map/ppermute | solution.py:374
  154.7 25.8 %collective-permute-start.11 = (f32[2,3,64,768]{3,2,1,0:T(8,128)S(1)}, f32[2,3,64,768]{3,2,1,0:T(8,128)S(1)}, u32[]{:S(2)}, u32[]{:S(2)}) collective-permute-start(f32[2,3,64,768]{3,2,1,0:T(8,128)S(1)} %stack.10), channel_id=1, source_target_pairs={{0,16},{4,20},{8,24},{12,28},{16,0},{20,4},{24,8},{28,12},{1,17},{... | collective-permute-start | bytes 3538952 | tf_op jit(solution)/shard_map/ppermute | solution.py:374
  154.9 7.6 %collective-permute-start.40 = (f32[64,768]{1,0:T(8,128)S(1)}, f32[64,768]{1,0:T(8,128)S(1)}, u32[]{:S(2)}, u32[]{:S(2)}) collective-permute-start(f32[64,768]{1,0:T(8,128)S(1)} %add.200), channel_id=1, source_target_pairs={{0,1},{1,0},{2,3},{3,2},{4,5},{5,4},{6,7},{7,6},{8,9},{9,8},{10,11... | collective-permute-start | bytes 589832 | tf_op jit(solution)/shard_map/ppermute | solution.py:354
  157.7 5.5 %collective-permute-start.41 = (f32[64,768]{1,0:T(8,128)S(1)}, f32[64,768]{1,0:T(8,128)S(1)}, u32[]{:S(2)}, u32[]{:S(2)}) collective-permute-start(f32[64,768]{1,0:T(8,128)S(1)} %add.201), channel_id=1, source_target_pairs={{1,2},{2,1},{5,6},{6,5},{9,10},{10,9},{13,14},{14,13},{17,18},{18,... | collective-permute-start | bytes 589832 | tf_op jit(solution)/shard_map/ppermute | solution.py:357
  158.5 9.7 %collective-permute-start.42 = (f32[64,768]{1,0:T(8,128)S(1)}, f32[64,768]{1,0:T(8,128)S(1)}, u32[]{:S(2)}, u32[]{:S(2)}) collective-permute-start(f32[64,768]{1,0:T(8,128)S(1)} %add.220), channel_id=1, source_target_pairs={{0,1},{1,0},{2,3},{3,2},{4,5},{5,4},{6,7},{7,6},{8,9},{9,8},{10,11... | collective-permute-start | bytes 589832 | tf_op jit(solution)/shard_map/ppermute | solution.py:354
  162.4 5.7 %collective-permute-start.43 = (f32[64,768]{1,0:T(8,128)S(1)}, f32[64,768]{1,0:T(8,128)S(1)}, u32[]{:S(2)}, u32[]{:S(2)}) collective-permute-start(f32[64,768]{1,0:T(8,128)S(1)} %add.221), channel_id=1, source_target_pairs={{1,2},{2,1},{5,6},{6,5},{9,10},{10,9},{13,14},{14,13},{17,18},{18,... | collective-permute-start | bytes 589832 | tf_op jit(solution)/shard_map/ppermute | solution.py:357
  163.2 19.3 %collective-permute-start.44 = (f32[64,768]{1,0:T(8,128)S(1)}, f32[64,768]{1,0:T(8,128)S(1)}, u32[]{:S(2)}, u32[]{:S(2)}) collective-permute-start(f32[64,768]{1,0:T(8,128)S(1)} %add.222), channel_id=1, source_target_pairs={{0,1},{1,0},{2,3},{3,2},{4,5},{5,4},{6,7},{7,6},{8,9},{9,8},{10,11... | collective-permute-start | bytes 589832 | tf_op jit(solution)/shard_map/ppermute | solution.py:354
  168.2 14.3 %collective-permute-start.45 = (f32[64,768]{1,0:T(8,128)S(1)}, f32[64,768]{1,0:T(8,128)S(1)}, u32[]{:S(2)}, u32[]{:S(2)}) collective-permute-start(f32[64,768]{1,0:T(8,128)S(1)} %add.223), channel_id=1, source_target_pairs={{0,1},{1,0},{2,3},{3,2},{4,5},{5,4},{6,7},{7,6},{8,9},{9,8},{10,11... | collective-permute-start | bytes 589832 | tf_op jit(solution)/shard_map/ppermute | solution.py:354
  180.7 9.9 %collective-permute-start.19 = (f32[1,3,64,768]{3,2,1,0:T(8,128)S(1)}, f32[1,3,64,768]{3,2,1,0:T(8,128)S(1)}, u32[]{:S(2)}, u32[]{:S(2)}) collective-permute-start(f32[1,3,64,768]{3,2,1,0:T(8,128)S(1)} %slice_add_fusion.3), channel_id=1, source_target_pairs={{0,8},{4,12},{8,0},{12,4},{16,24},{20,28},{24,16},{28,20},{1,9},{5... | collective-permute-start | bytes 1769480 | tf_op jit(solution)/shard_map/ppermute | solution.py:374
  182.5 9.9 %collective-permute-start.18 = (f32[1,3,64,768]{3,2,1,0:T(8,128)S(1)}, f32[1,3,64,768]{3,2,1,0:T(8,128)S(1)}, u32[]{:S(2)}, u32[]{:S(2)}) collective-permute-start(f32[1,3,64,768]{3,2,1,0:T(8,128)S(1)} %slice_add_fusion.4), channel_id=1, source_target_pairs={{0,16},{4,20},{8,24},{12,28},{16,0},{20,4},{24,8},{28,12},{1,17},{... | collective-permute-start | bytes 1769480 | tf_op jit(solution)/shard_map/ppermute | solution.py:374
  (16 other events, 184.5 us)

commit v3 on v2

v3 whole, which is shorter than its diff:
```python
import functools
import math

import jax
import jax.numpy as jnp
from jax import lax
from jax.experimental import pallas as pl
from jax.experimental.pallas import tpu as pltpu
from jax.sharding import PartitionSpec as P

BLK = 128
LOW = -1e30
LAGS = (4, 2, 2)
HOME_SLOTS = (8, 15, 20)
SLOT_FLOPS = 4_000_000_000


def dot(a, b, ca, cb):
    return lax.dot_general(a, b, (((ca,), (cb,)), ((), ())), preferred_element_type=jnp.float32)


def split(x):
    hi = x.astype(jnp.bfloat16)
    return hi, (x - hi.astype(jnp.float32)).astype(jnp.bfloat16)


def as_columns(row):
    return jnp.broadcast_to(row, (BLK, row.shape[1])).T


class Meta:
    def __init__(self, steps, groups, blocks, slab_blocks):
        self.steps, self.groups, self.blocks, self.slab_blocks = steps, groups, blocks, slab_blocks
        self.rows = steps * groups
        self.size = self.rows * blocks

    def flags(self, owner, out):
        me = lax.axis_index("cache")
        seen = 0
        for s in range(self.steps):
            own = (owner[s] == me).astype(jnp.int32)
            seen = jnp.maximum(seen, own)
            out[s] = own
            out[self.steps + s] = seen

    def count(self, member, flags, s, sb, j):
        return member[sb, j] + jnp.where(j < self.slab_blocks, flags[s], 0)

    def source(self, flags, s, j):
        return jnp.where((flags[self.steps + s] > 0) & (j < self.slab_blocks), self.blocks + j, j)


def scores_kernel(meta, group, scale, member, owner, q_hbm, cache_hbm, fresh_hbm, z_ref, w_ref, q_ref, lse_ref,
                  cache_ref, fresh_ref, peak, top, flags, entries, pairs, sem):
    copies = [pltpu.make_async_copy(src, dst, sem.at[i]) for i, (src, dst) in enumerate(
        ((cache_hbm, cache_ref), (fresh_hbm, fresh_ref), (q_hbm, q_ref)))]
    for copy in copies:
        copy.start()
    meta.flags(owner, flags)

    def collect(sj, carry):
        n_entries, n_pairs = carry
        s, j = sj // meta.blocks, sj % meta.blocks
        m, held = 0, 0
        for b in range(meta.groups):
            sb = s * meta.groups + b
            on = (meta.count(member, flags, s, sb, j) > 0).astype(jnp.int32)
            pairs[n_pairs] = sb * meta.blocks + j
            n_pairs = n_pairs + on
            held = jnp.where(m % 2 == 0, sb, held)
            entries[n_entries + m // 2] = (held * meta.rows + sb) * meta.blocks + j
            m = m + on

        @pl.when(m % 2 == 1)
        def _():
            entries[n_entries + m // 2] = (held * meta.rows + held) * meta.blocks + j

        return n_entries + (m + 1) // 2, n_pairs

    n_entries, n_pairs = lax.fori_loop(0, meta.steps * meta.blocks, collect, (0, 0))
    for g in range(group):
        entries[n_entries + g] = jnp.where(n_entries > 0, entries[0], 0)
        pairs[n_pairs + g] = 0
    peak[...] = jnp.full(peak.shape, LOW, jnp.float32)

    for copy, src, at in ((copies[0], cache_ref, 0), (copies[1], fresh_ref, meta.blocks)):
        copy.wait()

        def one(k, _, src=src, at=at):
            hi, lo = split(src[pl.ds(pl.multiple_of(k * BLK, BLK), BLK), :])
            w_ref[at + k, :BLK] = hi
            w_ref[at + k, BLK:] = lo
            return 0

        lax.fori_loop(0, src.shape[0] // BLK, one, 0)
    copies[2].wait()

    def score(it, _):
        found = []
        for g in range(group):
            e = entries[it * group + g]
            j, both = e % meta.blocks, e // meta.blocks
            sb0, sb1 = both // meta.rows, both % meta.rows
            left = jnp.concatenate([q_ref[sb0], q_ref[sb1]], axis=0)
            z = dot(left, w_ref[meta.source(flags, sb0 // meta.groups, j)], 1, 1)
            found.append((sb0, sb1, j, (z[:, :BLK] + z[:, BLK:]) * scale))
        for sb0, sb1, j, z in found:
            z_ref[sb0, j] = z[:BLK]
            z_ref[sb1, j] = z[BLK:]
            peak[sb0] = jnp.maximum(peak[sb0], z[:BLK])
            peak[sb1] = jnp.maximum(peak[sb1], z[BLK:])
        return 0

    lax.fori_loop(0, (n_entries + group - 1) // group, score, 0)

    def highest(sb, _):
        top[sb] = jnp.broadcast_to(jnp.max(peak[sb], axis=1, keepdims=True), (BLK, BLK))
        peak[sb] = jnp.zeros((BLK, BLK), jnp.float32)
        return 0

    lax.fori_loop(0, meta.rows, highest, 0, unroll=4 if meta.rows % 4 == 0 else 1)

    def add(it, _):
        for g in range(group):
            k = it * group + g
            sb, j = pairs[k] // meta.blocks, pairs[k] % meta.blocks
            c = meta.count(member, flags, sb // meta.groups, sb, j).astype(jnp.float32)
            peak[sb] += jnp.where(k < n_pairs, jnp.exp(z_ref[sb, j] - top[sb]) * c, 0.0)
        return 0

    lax.fori_loop(0, (n_pairs + group - 1) // group, add, 0)

    def finish(sb, _):
        total = jnp.sum(peak[sb], axis=1, keepdims=True)
        lse = jnp.where(total > 0, top[sb][:, :1] + jnp.log(jnp.maximum(total, 1e-30)), LOW)
        lse_ref[pl.ds(sb, 1), :] = jnp.broadcast_to(lse, (BLK, BLK)).T[:1]
        return 0

    lax.fori_loop(0, meta.rows, finish, 0, unroll=4 if meta.rows % 4 == 0 else 1)


def grad_kernel(meta, first, width, member, z_ref, q_ref, lse_ref, dep, out_ref, todo):
    def block(i, _):
        j = first + i
        n = 0
        for sb in range(meta.rows):
            todo[n] = sb
            n = n + member[sb, j]
        for g in range(width):
            todo[n + g] = 0
        at = pl.ds(pl.multiple_of(i * BLK, BLK), BLK)
        out_ref[at, :] = jnp.zeros((BLK, out_ref.shape[1]), jnp.float32)

        def step(it, _):
            his, los, rows = [], [], []
            for g in range(width):
                k = it * width + g
                sb = todo[k]
                p = jnp.exp(z_ref[sb, j].T - lse_ref[pl.ds(sb, 1), :])
                hi, lo = split(jnp.where(k < n, p, 0.0))
                his.append(hi)
                los.append(lo)
                rows.append(q_ref[sb])
            left = jnp.concatenate([jnp.concatenate(his, axis=1), jnp.concatenate(los, axis=1)], axis=0)
            acc = dot(left, jnp.concatenate(rows, axis=0), 1, 0)
            out_ref[at, :] += acc[:BLK] + acc[BLK:]
            return 0

        lax.fori_loop(0, (n + width - 1) // width, step, 0)
        return 0

    lax.fori_loop(0, out_ref.shape[0] // BLK, block, 0)


def term_kernel(meta, order, width, member, owner, z_ref, w_ref, lse_ref, pos_ref, dep, *refs):
    outs, (flags, todo, lcol, pcol) = refs[:-4], refs[-4:]
    meta.flags(owner, flags)
    lane = lax.broadcasted_iota(jnp.int32, (BLK, BLK), 1).astype(jnp.float32)

    def block(i, out_ref, first, stride):
        b = lax.axis_index("cache") ^ (first + stride * i) if order else first + stride * i
        n = 0
        for s in range(meta.steps):
            sb = s * meta.groups + b
            lcol[s] = as_columns(lse_ref[pl.ds(sb, 1), :])
            pcol[s] = as_columns(pos_ref[s:s + 1, pl.ds(pl.multiple_of(b * BLK, BLK), BLK)].astype(jnp.float32)) - lane
            out_ref[i, s] = jnp.zeros((BLK, out_ref.shape[3]), jnp.float32)
            for j in range(meta.blocks):
                todo[n] = s * meta.blocks + j
                n = n + (meta.count(member, flags, s, sb, j) > 0).astype(jnp.int32)
        for g in range(width):
            todo[n + g] = 0

        def step(it, _):
            found = []
            for g in range(width):
                k = it * width + g
                s, j = todo[k] // meta.blocks, todo[k] % meta.blocks
                sb = s * meta.groups + b
                p = jnp.exp(z_ref[sb, j] - lcol[s]) * meta.count(member, flags, s, sb, j).astype(jnp.float32)
                hot = (flags[s] > 0) & (j < meta.slab_blocks)
                p = p - jnp.where(pcol[s] == (j * BLK).astype(jnp.float32), hot.astype(jnp.float32), 0.0)
                hi, lo = split(jnp.where(k < n, p, 0.0))
                w = w_ref[meta.source(flags, s, j)]
                found.append((s, dot(jnp.concatenate([hi, hi], axis=1), w, 1, 0) + dot(lo, w[:BLK], 1, 0)))
            for s, term in found:
                out_ref[i, s] += term
            return 0

        lax.fori_loop(0, (n + width - 1) // width, step, 0)

    for o, out_ref in enumerate(outs):
        first, stride = (order[o], len(order)) if order else (0, 1)

        def one(i, _, out_ref=out_ref, first=first, stride=stride):
            block(i, out_ref, first, stride)
            return 0

        lax.fori_loop(0, out_ref.shape[0], one, 0)


def params(mib):
    return pltpu.CompilerParams(vmem_limit_bytes=mib * 1024 * 1024)


def free():
    return pl.CostEstimate(flops=0, bytes_accessed=0, transcendentals=0)


SMEM = pl.BlockSpec(memory_space=pltpu.SMEM)
VMEM = pl.BlockSpec(memory_space=pltpu.VMEM)
ANY = pl.BlockSpec(memory_space=pl.ANY)
HBM = pl.BlockSpec(memory_space=pltpu.HBM)


def run_scores(meta, member, owner, queries, cache, fresh):
    width = cache.shape[1]
    group = 4
    n_src = meta.blocks + meta.slab_blocks
    most = meta.steps * meta.blocks * ((meta.groups + 1) // 2)
    return pl.pallas_call(
        functools.partial(scores_kernel, meta, group, 2.0 / math.sqrt(width)),
        in_specs=[SMEM, SMEM, HBM, HBM, HBM],
        out_specs=[VMEM] * 4,
        out_shape=[
            pltpu.VMEM((meta.rows, meta.blocks, BLK, BLK), jnp.float32),
            pltpu.VMEM((n_src, 2 * BLK, width), jnp.bfloat16),
            pltpu.VMEM((meta.rows, BLK, width), jnp.bfloat16),
            pltpu.VMEM((meta.rows, BLK), jnp.float32),
        ],
        scratch_shapes=[
            pltpu.VMEM(cache.shape, jnp.float32),
            pltpu.VMEM(fresh.shape, jnp.float32),
            pltpu.VMEM((meta.rows, BLK, BLK), jnp.float32),
            pltpu.VMEM((meta.rows, BLK, BLK), jnp.float32),
            pltpu.SMEM((2 * meta.steps,), jnp.int32),
            pltpu.SMEM((most + group + 1,), jnp.int32),
            pltpu.SMEM((meta.size + group,), jnp.int32),
            pltpu.SemaphoreType.DMA((3,)),
        ],
        compiler_params=params(20),
        name="scores",
    )(member, owner, *(pltpu.with_memory_space_constraint(x, pltpu.HBM)
                       for x in (queries.reshape(meta.rows, BLK, width), cache, fresh)))


def run_grads(meta, member, z, q, lse, first, count, dep):
    group = 4
    return pl.pallas_call(
        functools.partial(grad_kernel, meta, first, group),
        in_specs=[SMEM, VMEM, VMEM, VMEM, ANY],
        out_specs=VMEM,
        out_shape=pltpu.VMEM((count * BLK, q.shape[2]), jnp.float32),
        scratch_shapes=[pltpu.SMEM((meta.rows + group,), jnp.int32)],
        compiler_params=params(10),
        cost_estimate=free(),
        name="cache_grad",
    )(member, z, q, lse, dep)


def run_terms(meta, member, owner, z, w, lse, pos, order, dep):
    group = 4
    n_out = max(1, len(order))
    shape = (meta.groups // n_out, meta.steps, BLK, w.shape[2])
    return pl.pallas_call(
        functools.partial(term_kernel, meta, order, group),
        in_specs=[SMEM, SMEM, VMEM, VMEM, VMEM, VMEM, ANY],
        out_specs=[VMEM] * n_out,
        out_shape=[pltpu.VMEM(shape, jnp.float32)] * n_out,
        scratch_shapes=[
            pltpu.SMEM((2 * meta.steps,), jnp.int32),
            pltpu.SMEM((meta.steps * meta.blocks + group,), jnp.int32),
            pltpu.VMEM((meta.steps, BLK, BLK), jnp.float32),
            pltpu.VMEM((meta.steps, BLK, BLK), jnp.float32),
        ],
        compiler_params=params(10),
        cost_estimate=free(),
        name="query_term",
    )(member, owner, z, w, lse, pos, dep)


def small(kernel, inputs, n_deps, outs, name, aliases=None, flops=0):
    n_vmem = len(inputs) - n_deps
    return pl.pallas_call(
        kernel,
        in_specs=[VMEM] * n_vmem + [ANY] * n_deps,
        out_specs=[VMEM] * len(outs),
        out_shape=[pltpu.VMEM(shape, jnp.float32) for shape in outs],
        input_output_aliases=aliases or {},
        compiler_params=params(4),
        cost_estimate=pl.CostEstimate(flops=flops, bytes_accessed=0, transcendentals=0),
        name=name,
    )(*inputs)


def merge_kernel(*refs):
    xs, out_ref = [r[...] for r in refs[:-1]], refs[-1]
    top = functools.reduce(jnp.maximum, xs)
    out_ref[...] = top + jnp.log(sum(jnp.exp(x - top) for x in xs))


def exchange_lse(lse):
    n = lax.axis_size("cache")
    bits = [1 << i for i in range(n.bit_length() - 1)]
    rounds = [bits[:1]] + [bits[i:i + 2] for i in range(1, len(bits), 2)]
    for some in rounds:
        partners = some if len(some) == 1 else [some[0], some[1], some[0] | some[1]]
        got = [lax.ppermute(lse, "cache", [(i, i ^ p) for i in range(n)]) for p in partners]
        lse = small(merge_kernel, [lse] + got, 0, [lse.shape], "merge_lse")[0]
    return lse


class Line:
    def __init__(self, n, rows, width):
        self.n, self.rows, self.width = n, rows, width
        self.lag_in, self.lag_mid, self.lag_out = LAGS
        self.late = self.lag_in + self.lag_mid
        self.slots = n + self.late + self.lag_out
        self.swap, self.mid, self.inner, self.total = {}, {}, {}, {}
        self.out = None

    def begin(self, array):
        self.swap[0] = lax.ppermute(array, "batch", [(0, 1), (1, 0), (2, 3), (3, 2)])

    def slot(self, t, chunk, deps):
        n, rows = self.n, self.rows
        u, k, o = t - self.lag_in, t - self.late, t - self.late - self.lag_out
        inputs, plan, outs = [], [], []

        def take(x):
            inputs.append(x)
            return len(inputs) - 1

        def give(shape=(rows, self.width)):
            outs.append(shape)
            return len(outs) - 1

        aliases = {}
        if 0 <= u < n:
            array, first = chunk(u)
            came, row = (self.swap[0], u * rows) if u < self.lag_in else (self.swap[u], 0)
            plan.append(("in", take(array), first, take(came), row, give()))
        if 0 <= k < n:
            plan.append(("sum", take(self.inner[k]), take(self.mid[k]), give()))
        if t < n:
            array, first = chunk(t)
            plan.append(("away", take(array), first, give()))
        if 0 <= o < n:
            args = take(self.total[o]), take(self.swap[o + self.late])
            old = None if self.out is None else take(self.out)
            new = give((n * rows, self.width))
            if old is not None:
                aliases = {old: new}
            plan.append(("out",) + args + (new,))
        n_in = len(inputs)

        def kernel(*refs):
            at = lax.axis_index("batch")
            end = (at == 0) | (at == 3)
            res = refs[n_in + len(deps):]
            total = None
            for what, *a in plan:
                if what == "in":
                    res[a[4]][...] = refs[a[0]][a[1]:a[1] + rows, :] + refs[a[2]][a[3]:a[3] + rows, :]
                elif what == "sum":
                    total = refs[a[0]][...] + refs[a[1]][...]
                    res[a[2]][...] = total
                elif what == "away":
                    value = refs[a[0]][a[1]:a[1] + rows, :]
                    res[a[2]][...] = value if total is None else jnp.where(end, value, total)
                else:
                    res[a[2]][o * rows:(o + 1) * rows, :] = jnp.where(end, refs[a[1]][...], refs[a[0]][...])

        got = small(kernel, inputs + list(deps), len(deps), outs, "line_slot", aliases, SLOT_FLOPS)
        away = None
        for what, *a in plan:
            if what == "in":
                self.inner[u] = got[a[4]]
            elif what == "sum":
                away = self.total[k] = got[a[2]]
            elif what == "away":
                away = got[a[2]]
            else:
                self.out = got[a[2]]
        if away is not None:
            self.swap[t] = lax.ppermute(away, "batch", [(0, 1), (1, 0), (2, 3), (3, 2)])
        if 0 <= u < n:
            self.mid[u] = lax.ppermute(self.inner[u], "batch", [(1, 2), (2, 1)])
        return got[0]


class HomeSum:
    def __init__(self, odd, even):
        self.n = lax.axis_size("cache")
        self.odd, self.even = odd, even
        self.steps, self.rows, self.width = even.shape[1:]
        self.bits = [1 << i for i in range(1, self.n.bit_length() - 1)]
        self.stage = 0

    def move(self, x, bit):
        return lax.ppermute(x, "cache", [(i, i ^ bit) for i in range(self.n)])

    def start(self, dep):
        def kernel(*refs):
            pass

        odd = small(kernel, [self.odd, dep], 1, [self.odd.shape], "home_start", {0: 0})[0]
        self.got = self.move(odd, 1)

    def step(self, dep):
        half = self.rows // 2
        orders = (self.bits, self.bits[::-1])
        last = self.stage == len(self.bits)
        if self.stage == 0:
            inputs = [self.even, self.got]
            sources = [({2 * i: i for i in range(self.n // 2)}, 0, 1, h * half) for h in (0, 1)]
        else:
            inputs, sources = [], []
            for (place, keep), got in zip(self.kept, self.moved):
                sources.append((place, len(inputs), len(inputs) + 1, 0))
                inputs += [keep, got]
        writes, outs, kept = [], [], []
        for h, (place, a, b, first) in enumerate(sources):
            if last:
                writes.append((h, 0, 0, h * half))
                continue
            bit = orders[h][self.stage]
            far = [r for r in sorted(place) if r & bit]
            near = [r for r in sorted(place) if not r & bit]
            for rs in (far, near):
                outs.append((len(rs), self.steps, half, self.width))
                writes += [(h, r, (len(outs) - 1, i), None) for i, r in enumerate(rs)]
            kept.append({r: i for i, r in enumerate(near)})
        if last:
            outs = [(self.steps, self.rows, self.width)]
        n_in, steps = len(inputs), self.steps

        def kernel(*refs):
            res = refs[n_in + 1:]
            for h, r, to, at in writes:
                place, a, b, first = sources[h]
                i = place[r]

                def one(s, _, a=a, b=b, i=i, first=first, to=to, at=at):
                    value = refs[a][i, s, first:first + half, :] + refs[b][i, s, first:first + half, :]
                    if at is None:
                        res[to[0]][to[1], s] = value
                    else:
                        res[0][s, at:at + half, :] = value
                    return 0

                lax.fori_loop(0, steps, one, 0)

        got = small(kernel, inputs + [dep], 1, outs, "home_sum")
        if last:
            return got[0]
        self.kept = [(kept[h], got[2 * h + 1]) for h in (0, 1)]
        self.moved = [self.move(got[2 * h], orders[h][self.stage]) for h in (0, 1)]
        self.stage += 1
        return got[1]


def on_device(queries, positives, block_list, block_count, refresh_owner, cache, fresh):
    steps, group_rows, width = queries.shape
    groups = group_rows // BLK
    blocks, slab_blocks = cache.shape[0] // BLK, fresh.shape[0] // BLK
    meta = Meta(steps, groups, blocks, slab_blocks)
    me = lax.axis_index("cache")
    block_ids = me * blocks + jnp.arange(blocks, dtype=jnp.int32)
    valid = jnp.arange(block_list.shape[2], dtype=jnp.int32)[None, None, :] < block_count[:, :, None]
    member = jnp.any((block_list[..., None] == block_ids) & valid[..., None], axis=2)
    member = member.astype(jnp.int32).reshape(meta.rows, blocks)
    owner = refresh_owner.astype(jnp.int32)

    z, w, q, own_lse = run_scores(meta, member, owner, queries, cache, fresh)
    lse = exchange_lse(own_lse)

    half = BLK // 2
    early = min(LAGS[0] * half // BLK, blocks)
    grads = [run_grads(meta, member, z, q, lse, 0, early, lse)]
    owners = lax.axis_size("cache")
    share = group_rows // owners
    fast = share == BLK and owners == groups and owners & (owners - 1) == 0 and owners > 2
    home = mine = None

    def chunk(k):
        n = early * BLK // half
        return (grads[0], k * half) if k < n else (grads[1], (k - n) * half)

    def rest(dep):
        grads.append(run_grads(meta, member, z, q, lse, early, blocks - early, dep))
        if not fast:
            return grads[1], None
        odd, even = run_terms(meta, member, owner, z, w, lse, positives, (1, 0), grads[1])
        return even, HomeSum(odd, even)

    if lax.axis_size("batch") == 4 and blocks > early:
        line = Line(2 * blocks, half, width)
        line.begin(grads[0])
        dep, home = rest(grads[0])
        deps = [dep]
        for t in range(LAGS[0], line.slots):
            deps = [line.slot(t, chunk, deps)]
            if t == LAGS[0] and fast:
                home.start(deps[0])
            if fast and t in HOME_SLOTS:
                deps.append(home.step(deps[0]))
                mine = deps[-1]
        grad = line.out
    else:
        _, home = rest(lse)
        if fast:
            home.start(lse)
        grad = lax.psum(jnp.concatenate(grads, axis=0), "batch")
    if fast:
        while home.stage < len(home.bits):
            home.step(lse)
        if mine is None or mine.ndim != 3:
            mine = home.step(lse)
    else:
        term = run_terms(meta, member, owner, z, w, lse, positives, (), lse)[0]
        term = jnp.swapaxes(term, 0, 1).reshape(steps, group_rows, width)
        mine = lax.psum_scatter(term, "cache", scatter_dimension=1, tiled=True)
    return mine, grad


def solution(mesh):
    return jax.shard_map(
        on_device,
        mesh=mesh,
        in_specs=(
            P(None, "batch", None),
            P(None, "batch"),
            P(None, "batch", None),
            P(None, "batch"),
            P(),
            P("cache", None),
            P("cache", None),
        ),
        out_specs=(P(None, ("batch", "cache"), None), P("cache", None)),
        check_vma=False,
    )
```

time: 194 us -> 158 us (0.81)
  waiting for transfers between devices: 33.3 us -> 11.2 us
  local copies, waits for them, and re-layouts: 16.3 us -> 3.54 us
  other arithmetic: 10.3 us -> 2.02 us
  starting transfers between devices: 85.8 us -> 91.6 us
    ppermute x5, waiting for transfers between devices: 19.2 us -> 0.01 us  [move(): return lax.ppermute(x, 'cache', [(i, i ^ bit) for i in range(self.n)])]
    unnamed x51 -> x7, local copies, waits for them, and re-layouts: 12.8 us -> 3.54 us
    ppermute x41 -> x39, starting transfers between devices: 83.8 us -> 88.6 us  [the longest x18 72 us: slot(): self.swap[t] = lax.ppermute(away, 'batch', [(0, 1), (1, 0), (2, 3), (3, 2)])]
    add x27 -> x0, other arithmetic: 4.41 us -> none  [the longest x16 3.19 us: sum_line(): inner[u] = ops.pop(0) + ops.pop(0)]
    slice x5 -> x0, local copies, waits for them, and re-layouts: 3.11 us -> none  [the longest x2 1.9 us: fill(): chunks.extend((grad[i:i + half] for i in range(0, count * BLK, half)))]
    ppermute x41 -> x39, waiting for transfers between devices: 14.1 us -> 11.2 us  [the longest x18 6.28 us: slot(): self.swap[t] = lax.ppermute(away, 'batch', [(0, 1), (1, 0), (2, 3), (3, 2)])]
    pallas_call x0 -> x26, Pallas kernels: none -> 2.44 us  [small(): pl.pallas_call(kernel, in_specs=[VMEM] * n_vmem + [ANY] * n_deps, out_spe...]
    pallas_call x1, Pallas kernels: 17.8 us -> 15.7 us  [run_terms(): pl.pallas_call(functools.partial(term_kernel, meta, order, group), in_spe...]
  transfers between devices with their start and end apart: 46 -> 44, of which waited for: 13 -> 8; matrix products, arithmetic and copies ran while one was open for 4% -> 1% of each run, Pallas kernels for 9% -> 16%
where the time goes in v3:
time: 158 us; the launch traced here: 156 us
  starting transfers between devices  91.6 us (58%)
  Pallas kernels  46.6 us (29%)
  waiting for transfers between devices  11.2 us (7%)
  local copies, waits for them, and re-layouts  3.54 us (2%)
  other arithmetic  2.02 us (1%)
    ppermute x18, starting transfers between devices, slot(): self.swap[t] = lax.ppermute(away, 'batch', [(0, 1), (1, 0), (2, 3), (3, 2)])  72 us
    pallas_call x1, Pallas kernels, run_scores(): pl.pallas_call(functools.partial(scores_kernel, meta, group, 2.0 / math.s...  18.1 us
    pallas_call x1, Pallas kernels, run_terms(): pl.pallas_call(functools.partial(term_kernel, meta, order, group), in_spe...  15.7 us
    ppermute x16, starting transfers between devices, slot(): self.mid[u] = lax.ppermute(self.inner[u], 'batch', [(1, 2), (2, 1)])  10.6 us
    pallas_call x2, Pallas kernels, run_grads(): pl.pallas_call(functools.partial(grad_kernel, meta, first, group), in_spe...  10.4 us
    ppermute x18, waiting for transfers between devices, slot(): self.swap[t] = lax.ppermute(away, 'batch', [(0, 1), (1, 0), (2, 3), (3, 2)])  6.28 us
    ppermute x4, starting transfers between devices, exchange_lse(): lax.ppermute(lse, 'cache', [(i, i ^ p) for i in range(n)])  4.87 us
    ppermute x4, waiting for transfers between devices, exchange_lse(): lax.ppermute(lse, 'cache', [(i, i ^ p) for i in range(n)])  4.86 us
  transfers between devices with their start and end apart: 44, of which 8 were waited for; matrix products, arithmetic and copies ran while one was open for 1% of the time, Pallas kernels for 16%

profile of v3, /device:TPU:0, one launch (start us, length us, event | category | flops | bytes accessed | tf_op | source)
XLA Modules:
  0.0 156.2 jit_solution(15433187360165374671)
XLA Ops:
  0.6 0.8 iota_compare_fusion
  1.4 1.3 and_reduce_fusion
  3.3 18.1 %scores.1 = (f32[24,8,128,128]{3,2,1,0:T(8,128)S(1)}, bf16[12,256,768]{2,1,0:T(8,128)(2,1)S(1)}, bf16[24,128,768]{2,1,0:T(8,128)(2,1)S(1)}, f32[24,128]{1,0:T(8,128)S(1)}) custom-call(s32[24,8]{1,0:T(8,128)S(1)} %convert_bitcast_fusion.member, s32[3]{0:T(128)S(1)} %copy-done.1, bf16[24,128,768]{2,1,0:T(8,128)(2,1)} %bitcast.3, f32[1024,768]{1,0:T(8,128)} %cache_hbm.1, ...), custom_call_target="tpu_custom_call" | custom-call | tf_op jit(solution)/shard_map/scores/pallas_call | solution.py:241
  21.5 1.2 collective-permute-done.refs_1_
  22.7 2.2 %collective-permute-start.3 = (f32[24,128]{1,0:T(8,128)S(1)}, f32[24,128]{1,0:T(8,128)S(1)}, u32[]{:S(2)}, u32[]{:S(2)}) collective-permute-start(f32[24,128]{1,0:T(8,128)S(1)} %merge_lse.2.refs_0_), channel_id=1, source_target_pairs={{0,24},{4,28},{8,16},{12,20},{16,8},{20,12},{24,0},{28,4},{1,25},{... | collective-permute-start | bytes 36872 | tf_op jit(solution)/shard_map/ppermute | solution.py:328
  24.9 2.6 %collective-permute-start.2 = (f32[24,128]{1,0:T(8,128)S(1)}, f32[24,128]{1,0:T(8,128)S(1)}, u32[]{:S(2)}, u32[]{:S(2)}) collective-permute-start(f32[24,128]{1,0:T(8,128)S(1)} %merge_lse.2.refs_0_), channel_id=1, source_target_pairs={{0,16},{4,20},{8,24},{12,28},{16,0},{20,4},{24,8},{28,12},{1,17},{... | collective-permute-start | bytes 36872 | tf_op jit(solution)/shard_map/ppermute | solution.py:328
  27.5 1.7 %collective-permute-done.2.refs_2_ = f32[24,128]{1,0:T(8,128)S(1)} collective-permute-done((f32[24,128]{1,0:T(8,128)S(1)}, f32[24,128]{1,0:T(8,128)S(1)}, u32[]{:S(2)}, u32[]{:S(2)}) %collective-permute-start.2) | collective-permute-done | bytes 12320 | tf_op jit(solution)/shard_map/ppermute | solution.py:328
  29.2 2.0 %collective-permute-done.1.refs_1_ = f32[24,128]{1,0:T(8,128)S(1)} collective-permute-done((f32[24,128]{1,0:T(8,128)S(1)}, f32[24,128]{1,0:T(8,128)S(1)}, u32[]{:S(2)}, u32[]{:S(2)}) %collective-permute-start.1) | collective-permute-done | bytes 12320 | tf_op jit(solution)/shard_map/ppermute | solution.py:328
  31.2 3.2 %cache_grad.2.dep.refs_0_ = f32[256,768]{1,0:T(8,128)S(1)} custom-call(s32[24,8]{1,0:T(8,128)S(1)} %convert_bitcast_fusion.member, f32[24,8,128,128]{3,2,1,0:T(8,128)S(1)} %get-tuple-element.74.z_ref, bf16[24,128,768]{2,1,0:T(8,128)(2,1)S(1)} %get-tuple-element.77.q_ref, f32[24,128]{1,0:T(8,128)S(1)} %merge_lse.3.lse_ref.dep, f32[24,128]{1,0:T(8,128)S(1)} %merge_lse.3.lse_ref.dep), custom_call_target="tpu_custom_call" | custom-call | tf_op jit(solution)/shard_map/cache_grad/pallas_call | solution.py:269
  34.4 1.1 collective-permute-start.4
  35.5 7.2 %cache_grad.3.dep.refs_2_.refs_4_.refs_0_ = f32[768,768]{1,0:T(8,128)S(1)} custom-call(s32[24,8]{1,0:T(8,128)S(1)} %convert_bitcast_fusion.member, f32[24,8,128,128]{3,2,1,0:T(8,128)S(1)} %get-tuple-element.74.z_ref, bf16[24,128,768]{2,1,0:T(8,128)(2,1)S(1)} %get-tuple-element.77.q_ref, f32[24,128]{1,0:T(8,128)S(1)} %merge_lse.3.lse_ref.dep, ...), custom_call_target="tpu_custom_call" | custom-call | tf_op jit(solution)/shard_map/cache_grad/pallas_call | solution.py:269
  42.7 15.7 %query_term.1 = (f32[4,3,128,768]{3,2,1,0:T(8,128)S(1)}, f32[4,3,128,768]{3,2,1,0:T(8,128)S(1)}) custom-call(s32[24,8]{1,0:T(8,128)S(1)} %convert_bitcast_fusion.member, s32[3]{0:T(128)S(1)} %copy-done.1, f32[24,8,128,128]{3,2,1,0:T(8,128)S(1)} %get-tuple-element.74.z_ref, bf16[12,256,768]{2,1,0:T(8,128)(2,1)S(1)} %get-tuple-element.75.w_ref, ...), custom_call_target="tpu_custom_call" | custom-call | tf_op jit(solution)/shard_map/query_term/pallas_call | solution.py:285
  58.6 0.7 collective-permute-start.7
  59.3 4.3 %collective-permute-start.6 = (f32[64,768]{1,0:T(8,128)S(1)}, f32[64,768]{1,0:T(8,128)S(1)}, u32[]{:S(2)}, u32[]{:S(2)}) collective-permute-start(f32[64,768]{1,0:T(8,128)S(1)} %get-tuple-element.81), channel_id=1, source_target_pairs={{0,1},{1,0},{2,3},{3,2},{4,5},{5,4},{6,7},{7,6},{8,9},{9,8},{10,11... | collective-permute-start | bytes 589832 | tf_op jit(solution)/shard_map/ppermute | solution.py:406
  63.7 0.7 collective-permute-start.10
  64.4 4.7 %collective-permute-start.9 = (f32[64,768]{1,0:T(8,128)S(1)}, f32[64,768]{1,0:T(8,128)S(1)}, u32[]{:S(2)}, u32[]{:S(2)}) collective-permute-start(f32[64,768]{1,0:T(8,128)S(1)} %get-tuple-element.85), channel_id=1, source_target_pairs={{0,1},{1,0},{2,3},{3,2},{4,5},{5,4},{6,7},{7,6},{8,9},{9,8},{10,11... | collective-permute-start | bytes 589832 | tf_op jit(solution)/shard_map/ppermute | solution.py:406
  69.1 0.7 collective-permute-start.8
  69.9 7.2 %collective-permute-start.13 = (f32[64,768]{1,0:T(8,128)S(1)}, f32[64,768]{1,0:T(8,128)S(1)}, u32[]{:S(2)}, u32[]{:S(2)}) collective-permute-start(f32[64,768]{1,0:T(8,128)S(1)} %get-tuple-element.92), channel_id=1, source_target_pairs={{0,1},{1,0},{2,3},{3,2},{4,5},{5,4},{6,7},{7,6},{8,9},{9,8},{10,11... | collective-permute-start | bytes 589832 | tf_op jit(solution)/shard_map/ppermute | solution.py:406
  77.4 0.7 collective-permute-start.15
  78.2 4.0 %collective-permute-start.19 = (f32[64,768]{1,0:T(8,128)S(1)}, f32[64,768]{1,0:T(8,128)S(1)}, u32[]{:S(2)}, u32[]{:S(2)}) collective-permute-start(f32[64,768]{1,0:T(8,128)S(1)} %get-tuple-element.100), channel_id=1, source_target_pairs={{0,1},{1,0},{2,3},{3,2},{4,5},{5,4},{6,7},{7,6},{8,9},{9,8},{10,11... | collective-permute-start | bytes 589832 | tf_op jit(solution)/shard_map/ppermute | solution.py:406
  82.2 0.7 collective-permute-start.18
  82.9 0.7 home_sum.3
  83.7 4.3 %collective-permute-start.17 = (f32[64,768]{1,0:T(8,128)S(1)}, f32[64,768]{1,0:T(8,128)S(1)}, u32[]{:S(2)}, u32[]{:S(2)}) collective-permute-start(f32[64,768]{1,0:T(8,128)S(1)} %get-tuple-element.98), channel_id=1, source_target_pairs={{0,1},{1,0},{2,3},{3,2},{4,5},{5,4},{6,7},{7,6},{8,9},{9,8},{10,11... | collective-permute-start | bytes 589832 | tf_op jit(solution)/shard_map/ppermute | solution.py:406
  88.8 1.6 %collective-permute-start.12 = (f32[2,3,64,768]{3,2,1,0:T(8,128)S(1)}, f32[2,3,64,768]{3,2,1,0:T(8,128)S(1)}, u32[]{:S(2)}, u32[]{:S(2)}) collective-permute-start(f32[2,3,64,768]{3,2,1,0:T(8,128)S(1)} %get-tuple-element.91), channel_id=1, source_target_pairs={{0,16},{4,20},{8,24},{12,28},{16,0},{20,4},{24,8},{28,12},{1,17},{... | collective-permute-start | bytes 3538952 | tf_op jit(solution)/shard_map/ppermute | solution.py:421
  90.5 1.8 %collective-permute-start.23 = (f32[64,768]{1,0:T(8,128)S(1)}, f32[64,768]{1,0:T(8,128)S(1)}, u32[]{:S(2)}, u32[]{:S(2)}) collective-permute-start(f32[64,768]{1,0:T(8,128)S(1)} %get-tuple-element.108), channel_id=1, source_target_pairs={{0,1},{1,0},{2,3},{3,2},{4,5},{5,4},{6,7},{7,6},{8,9},{9,8},{10,11... | collective-permute-start | bytes 589832 | tf_op jit(solution)/shard_map/ppermute | solution.py:406
  92.3 0.7 collective-permute-start.22
  93.0 6.1 %collective-permute-start.20 = (f32[64,768]{1,0:T(8,128)S(1)}, f32[64,768]{1,0:T(8,128)S(1)}, u32[]{:S(2)}, u32[]{:S(2)}) collective-permute-start(f32[64,768]{1,0:T(8,128)S(1)} %get-tuple-element.104), channel_id=1, source_target_pairs={{0,1},{1,0},{2,3},{3,2},{4,5},{5,4},{6,7},{7,6},{8,9},{9,8},{10,11... | collective-permute-start | bytes 589832 | tf_op jit(solution)/shard_map/ppermute | solution.py:406
  99.1 0.7 collective-permute-start.21
  99.9 4.5 %collective-permute-start.27 = (f32[64,768]{1,0:T(8,128)S(1)}, f32[64,768]{1,0:T(8,128)S(1)}, u32[]{:S(2)}, u32[]{:S(2)}) collective-permute-start(f32[64,768]{1,0:T(8,128)S(1)} %get-tuple-element.116), channel_id=1, source_target_pairs={{0,1},{1,0},{2,3},{3,2},{4,5},{5,4},{6,7},{7,6},{8,9},{9,8},{10,11... | collective-permute-start | bytes 589832 | tf_op jit(solution)/shard_map/ppermute | solution.py:406
  104.7 0.7 collective-permute-start.26
  105.4 3.8 %collective-permute-start.25 = (f32[64,768]{1,0:T(8,128)S(1)}, f32[64,768]{1,0:T(8,128)S(1)}, u32[]{:S(2)}, u32[]{:S(2)}) collective-permute-start(f32[64,768]{1,0:T(8,128)S(1)} %get-tuple-element.114), channel_id=1, source_target_pairs={{0,1},{1,0},{2,3},{3,2},{4,5},{5,4},{6,7},{7,6},{8,9},{9,8},{10,11... | collective-permute-start | bytes 589832 | tf_op jit(solution)/shard_map/ppermute | solution.py:406
  109.2 0.8 collective-permute-done.27.refs_6_.refs_1_
  110.8 5.4 %collective-permute-start.30 = (f32[64,768]{1,0:T(8,128)S(1)}, f32[64,768]{1,0:T(8,128)S(1)}, u32[]{:S(2)}, u32[]{:S(2)}) collective-permute-start(f32[64,768]{1,0:T(8,128)S(1)} %get-tuple-element.125), channel_id=1, source_target_pairs={{0,1},{1,0},{2,3},{3,2},{4,5},{5,4},{6,7},{7,6},{8,9},{9,8},{10,11... | collective-permute-start | bytes 589832 | tf_op jit(solution)/shard_map/ppermute | solution.py:406
  116.2 0.7 collective-permute-start.31
  117.0 4.5 %collective-permute-start.35 = (f32[64,768]{1,0:T(8,128)S(1)}, f32[64,768]{1,0:T(8,128)S(1)}, u32[]{:S(2)}, u32[]{:S(2)}) collective-permute-start(f32[64,768]{1,0:T(8,128)S(1)} %get-tuple-element.131), channel_id=1, source_target_pairs={{0,1},{1,0},{2,3},{3,2},{4,5},{5,4},{6,7},{7,6},{8,9},{9,8},{10,11... | collective-permute-start | bytes 589832 | tf_op jit(solution)/shard_map/ppermute | solution.py:406
  121.6 0.7 collective-permute-start.34
  122.6 3.8 %collective-permute-start.33 = (f32[64,768]{1,0:T(8,128)S(1)}, f32[64,768]{1,0:T(8,128)S(1)}, u32[]{:S(2)}, u32[]{:S(2)}) collective-permute-start(f32[64,768]{1,0:T(8,128)S(1)} %get-tuple-element.129.refs_4_), channel_id=1, source_target_pairs={{0,1},{1,0},{2,3},{3,2},{4,5},{5,4},{6,7},{7,6},{8,9},{9,8},{10,11... | collective-permute-start | bytes 589832 | tf_op jit(solution)/shard_map/ppermute | solution.py:406
  127.2 4.5 %collective-permute-start.39 = (f32[64,768]{1,0:T(8,128)S(1)}, f32[64,768]{1,0:T(8,128)S(1)}, u32[]{:S(2)}, u32[]{:S(2)}) collective-permute-start(f32[64,768]{1,0:T(8,128)S(1)} %get-tuple-element.137.refs_4_), channel_id=1, source_target_pairs={{0,1},{1,0},{2,3},{3,2},{4,5},{5,4},{6,7},{7,6},{8,9},{9,8},{10,11... | collective-permute-start | bytes 589832 | tf_op jit(solution)/shard_map/ppermute | solution.py:406
  132.4 1.2 collective-permute-start.29
  133.8 1.9 %collective-permute-start.37 = (f32[64,768]{1,0:T(8,128)S(1)}, f32[64,768]{1,0:T(8,128)S(1)}, u32[]{:S(2)}, u32[]{:S(2)}) collective-permute-start(f32[64,768]{1,0:T(8,128)S(1)} %get-tuple-element.136.refs_2_), channel_id=1, source_target_pairs={{0,1},{1,0},{2,3},{3,2},{4,5},{5,4},{6,7},{7,6},{8,9},{9,8},{10,11... | collective-permute-start | bytes 589832 | tf_op jit(solution)/shard_map/ppermute | solution.py:406
  135.6 1.4 collective-permute-done.39.refs_5_
  137.8 4.3 %collective-permute-start.41 = (f32[64,768]{1,0:T(8,128)S(1)}, f32[64,768]{1,0:T(8,128)S(1)}, u32[]{:S(2)}, u32[]{:S(2)}) collective-permute-start(f32[64,768]{1,0:T(8,128)S(1)} %get-tuple-element.142.refs_2_), channel_id=1, source_target_pairs={{0,1},{1,0},{2,3},{3,2},{4,5},{5,4},{6,7},{7,6},{8,9},{9,8},{10,11... | collective-permute-start | bytes 589832 | tf_op jit(solution)/shard_map/ppermute | solution.py:406
  142.1 0.7 collective-permute-start.40
  142.9 4.1 %collective-permute-start.43 = (f32[64,768]{1,0:T(8,128)S(1)}, f32[64,768]{1,0:T(8,128)S(1)}, u32[]{:S(2)}, u32[]{:S(2)}) collective-permute-start(f32[64,768]{1,0:T(8,128)S(1)} %get-tuple-element.141.refs_4_.refs_5_.refs_0_), channel_id=1, source_target_pairs={{0,1},{1,0},{2,3},{3,2},{4,5},{5,4},{6,7},{7,6},{8,9},{9,8},{10,11... | collective-permute-start | bytes 589832 | tf_op jit(solution)/shard_map/ppermute | solution.py:406
  147.1 1.0 copy.41
  148.1 2.7 %collective-permute-start.42 = (f32[64,768]{1,0:T(8,128)S(1)}, f32[64,768]{1,0:T(8,128)S(1)}, u32[]{:S(2)}, u32[]{:S(2)}) collective-permute-start(f32[64,768]{1,0:T(8,128)S(1)} %get-tuple-element.144.refs_3_.refs_0_), channel_id=1, source_target_pairs={{0,1},{1,0},{2,3},{3,2},{4,5},{5,4},{6,7},{7,6},{8,9},{9,8},{10,11... | collective-permute-start | bytes 589832 | tf_op jit(solution)/shard_map/ppermute | solution.py:406
  151.1 3.4 %collective-permute-done.42.refs_1_ = f32[64,768]{1,0:T(8,128)S(1)} collective-permute-done((f32[64,768]{1,0:T(8,128)S(1)}, f32[64,768]{1,0:T(8,128)S(1)}, u32[]{:S(2)}, u32[]{:S(2)}) %collective-permute-start.42) | collective-permute-done | bytes 196640 | tf_op jit(solution)/shard_map/ppermute | solution.py:406
  154.5 1.7 %copy.42 = f32[1024,768]{1,0:T(8,128)} copy(f32[1024,768]{1,0:T(8,128)S(1)} %line_slot.39) | data formatting | bytes 6291456
  (81 shorter events, 7.0 us)
Async XLA Ops:
  2.7 0.7 copy-start.1
  21.5 1.2 collective-permute-start
  22.7 4.8 %collective-permute-start.3 = (f32[24,128]{1,0:T(8,128)S(1)}, f32[24,128]{1,0:T(8,128)S(1)}, u32[]{:S(2)}, u32[]{:S(2)}) collective-permute-start(f32[24,128]{1,0:T(8,128)S(1)} %merge_lse.2.refs_0_), channel_id=1, source_target_pairs={{0,24},{4,28},{8,16},{12,20},{16,8},{20,12},{24,0},{28,4},{1,25},{... | collective-permute-start | bytes 36872 | tf_op jit(solution)/shard_map/ppermute | solution.py:328
  24.9 4.3 %collective-permute-start.2 = (f32[24,128]{1,0:T(8,128)S(1)}, f32[24,128]{1,0:T(8,128)S(1)}, u32[]{:S(2)}, u32[]{:S(2)}) collective-permute-start(f32[24,128]{1,0:T(8,128)S(1)} %merge_lse.2.refs_0_), channel_id=1, source_target_pairs={{0,16},{4,20},{8,24},{12,28},{16,0},{20,4},{24,8},{28,12},{1,17},{... | collective-permute-start | bytes 36872 | tf_op jit(solution)/shard_map/ppermute | solution.py:328
  27.5 3.7 %collective-permute-start.1 = (f32[24,128]{1,0:T(8,128)S(1)}, f32[24,128]{1,0:T(8,128)S(1)}, u32[]{:S(2)}, u32[]{:S(2)}) collective-permute-start(f32[24,128]{1,0:T(8,128)S(1)} %merge_lse.2.refs_0_), channel_id=1, source_target_pairs={{0,8},{4,12},{8,0},{12,4},{16,24},{20,28},{24,16},{28,20},{1,9},{5... | collective-permute-start | bytes 36872 | tf_op jit(solution)/shard_map/ppermute | solution.py:328
  34.4 8.3 %copy-start = (s32[3,1024]{1,0:T(4,128)S(1)}, s32[3,1024]{1,0:T(4,128)}, u32[]{:S(2)}) copy-start(s32[3,1024]{1,0:T(4,128)} %pos_ref.1) | copy-start | bytes 36868
  34.4 24.0 %collective-permute-start.4 = (f32[256,768]{1,0:T(8,128)S(1)}, f32[256,768]{1,0:T(8,128)S(1)}, u32[]{:S(2)}, u32[]{:S(2)}) collective-permute-start(f32[256,768]{1,0:T(8,128)S(1)} %cache_grad.2.dep.refs_0_), channel_id=1, source_target_pairs={{0,1},{1,0},{2,3},{3,2},{4,5},{5,4},{6,7},{7,6},{8,9},{9,8},{10,11... | collective-permute-start | bytes 2359304 | tf_op jit(solution)/shard_map/ppermute | solution.py:343
  58.5 23.7 %collective-permute-start.5 = (f32[4,3,128,768]{3,2,1,0:T(8,128)S(1)}, f32[4,3,128,768]{3,2,1,0:T(8,128)S(1)}, u32[]{:S(2)}, u32[]{:S(2)}) collective-permute-start(f32[4,3,128,768]{3,2,1,0:T(8,128)S(1)} %home_start.1), channel_id=1, source_target_pairs={{0,4},{4,0},{8,12},{12,8},{16,20},{20,16},{24,28},{28,24},{1,5},{5... | collective-permute-start | bytes 14155784 | tf_op jit(solution)/shard_map/ppermute | solution.py:421
  58.6 5.7 %collective-permute-start.7 = (f32[64,768]{1,0:T(8,128)S(1)}, f32[64,768]{1,0:T(8,128)S(1)}, u32[]{:S(2)}, u32[]{:S(2)}) collective-permute-start(f32[64,768]{1,0:T(8,128)S(1)} %get-tuple-element.80.refs_1_.refs_3_.refs_2_), channel_id=1, source_target_pairs={{1,2},{2,1},{5,6},{6,5},{9,10},{10,9},{13,14},{14,13},{17,18},{18,... | collective-permute-start | bytes 589832 | tf_op jit(solution)/shard_map/ppermute | solution.py:408
  59.3 10.6 %collective-permute-start.6 = (f32[64,768]{1,0:T(8,128)S(1)}, f32[64,768]{1,0:T(8,128)S(1)}, u32[]{:S(2)}, u32[]{:S(2)}) collective-permute-start(f32[64,768]{1,0:T(8,128)S(1)} %get-tuple-element.81), channel_id=1, source_target_pairs={{0,1},{1,0},{2,3},{3,2},{4,5},{5,4},{6,7},{7,6},{8,9},{9,8},{10,11... | collective-permute-start | bytes 589832 | tf_op jit(solution)/shard_map/ppermute | solution.py:406
  63.6 20.0 %collective-permute-start.14 = (f32[64,768]{1,0:T(8,128)S(1)}, f32[64,768]{1,0:T(8,128)S(1)}, u32[]{:S(2)}, u32[]{:S(2)}) collective-permute-start(f32[64,768]{1,0:T(8,128)S(1)} %get-tuple-element.93), channel_id=1, source_target_pairs={{0,1},{1,0},{2,3},{3,2},{4,5},{5,4},{6,7},{7,6},{8,9},{9,8},{10,11... | collective-permute-start | bytes 589832 | tf_op jit(solution)/shard_map/ppermute | solution.py:406
  63.7 5.5 %collective-permute-start.10 = (f32[64,768]{1,0:T(8,128)S(1)}, f32[64,768]{1,0:T(8,128)S(1)}, u32[]{:S(2)}, u32[]{:S(2)}) collective-permute-start(f32[64,768]{1,0:T(8,128)S(1)} %get-tuple-element.82.refs_5_.refs_2_), channel_id=1, source_target_pairs={{1,2},{2,1},{5,6},{6,5},{9,10},{10,9},{13,14},{14,13},{17,18},{18,... | collective-permute-start | bytes 589832 | tf_op jit(solution)/shard_map/ppermute | solution.py:408
  64.4 13.0 %collective-permute-start.9 = (f32[64,768]{1,0:T(8,128)S(1)}, f32[64,768]{1,0:T(8,128)S(1)}, u32[]{:S(2)}, u32[]{:S(2)}) collective-permute-start(f32[64,768]{1,0:T(8,128)S(1)} %get-tuple-element.85), channel_id=1, source_target_pairs={{0,1},{1,0},{2,3},{3,2},{4,5},{5,4},{6,7},{7,6},{8,9},{9,8},{10,11... | collective-permute-start | bytes 589832 | tf_op jit(solution)/shard_map/ppermute | solution.py:406
  69.1 9.0 %collective-permute-start.8 = (f32[64,768]{1,0:T(8,128)S(1)}, f32[64,768]{1,0:T(8,128)S(1)}, u32[]{:S(2)}, u32[]{:S(2)}) collective-permute-start(f32[64,768]{1,0:T(8,128)S(1)} %get-tuple-element.83.refs_5_.refs_2_), channel_id=1, source_target_pairs={{1,2},{2,1},{5,6},{6,5},{9,10},{10,9},{13,14},{14,13},{17,18},{18,... | collective-permute-start | bytes 589832 | tf_op jit(solution)/shard_map/ppermute | solution.py:408
  69.9 13.7 %collective-permute-start.13 = (f32[64,768]{1,0:T(8,128)S(1)}, f32[64,768]{1,0:T(8,128)S(1)}, u32[]{:S(2)}, u32[]{:S(2)}) collective-permute-start(f32[64,768]{1,0:T(8,128)S(1)} %get-tuple-element.92), channel_id=1, source_target_pairs={{0,1},{1,0},{2,3},{3,2},{4,5},{5,4},{6,7},{7,6},{8,9},{9,8},{10,11... | collective-permute-start | bytes 589832 | tf_op jit(solution)/shard_map/ppermute | solution.py:406
  77.4 6.2 %collective-permute-start.15 = (f32[64,768]{1,0:T(8,128)S(1)}, f32[64,768]{1,0:T(8,128)S(1)}, u32[]{:S(2)}, u32[]{:S(2)}) collective-permute-start(f32[64,768]{1,0:T(8,128)S(1)} %get-tuple-element.86.refs_7_.refs_2_), channel_id=1, source_target_pairs={{1,2},{2,1},{5,6},{6,5},{9,10},{10,9},{13,14},{14,13},{17,18},{18,... | collective-permute-start | bytes 589832 | tf_op jit(solution)/shard_map/ppermute | solution.py:408
  78.2 10.6 %collective-permute-start.19 = (f32[64,768]{1,0:T(8,128)S(1)}, f32[64,768]{1,0:T(8,128)S(1)}, u32[]{:S(2)}, u32[]{:S(2)}) collective-permute-start(f32[64,768]{1,0:T(8,128)S(1)} %get-tuple-element.100), channel_id=1, source_target_pairs={{0,1},{1,0},{2,3},{3,2},{4,5},{5,4},{6,7},{7,6},{8,9},{9,8},{10,11... | collective-permute-start | bytes 589832 | tf_op jit(solution)/shard_map/ppermute | solution.py:406
  82.2 8.1 %collective-permute-start.18 = (f32[64,768]{1,0:T(8,128)S(1)}, f32[64,768]{1,0:T(8,128)S(1)}, u32[]{:S(2)}, u32[]{:S(2)}) collective-permute-start(f32[64,768]{1,0:T(8,128)S(1)} %get-tuple-element.87.refs_2_.refs_8_), channel_id=1, source_target_pairs={{1,2},{2,1},{5,6},{6,5},{9,10},{10,9},{13,14},{14,13},{17,18},{18,... | collective-permute-start | bytes 589832 | tf_op jit(solution)/shard_map/ppermute | solution.py:408
  83.7 8.5 %collective-permute-start.17 = (f32[64,768]{1,0:T(8,128)S(1)}, f32[64,768]{1,0:T(8,128)S(1)}, u32[]{:S(2)}, u32[]{:S(2)}) collective-permute-start(f32[64,768]{1,0:T(8,128)S(1)} %get-tuple-element.98), channel_id=1, source_target_pairs={{0,1},{1,0},{2,3},{3,2},{4,5},{5,4},{6,7},{7,6},{8,9},{9,8},{10,11... | collective-permute-start | bytes 589832 | tf_op jit(solution)/shard_map/ppermute | solution.py:406
  88.0 4.9 %collective-permute-start.16 = (f32[64,768]{1,0:T(8,128)S(1)}, f32[64,768]{1,0:T(8,128)S(1)}, u32[]{:S(2)}, u32[]{:S(2)}) collective-permute-start(f32[64,768]{1,0:T(8,128)S(1)} %get-tuple-element.96.refs_8_.refs_2_), channel_id=1, source_target_pairs={{1,2},{2,1},{5,6},{6,5},{9,10},{10,9},{13,14},{14,13},{17,18},{18,... | collective-permute-start | bytes 589832 | tf_op jit(solution)/shard_map/ppermute | solution.py:408
  88.7 32.9 %collective-permute-start.11 = (f32[2,3,64,768]{3,2,1,0:T(8,128)S(1)}, f32[2,3,64,768]{3,2,1,0:T(8,128)S(1)}, u32[]{:S(2)}, u32[]{:S(2)}) collective-permute-start(f32[2,3,64,768]{3,2,1,0:T(8,128)S(1)} %get-tuple-element.89), channel_id=1, source_target_pairs={{0,8},{4,12},{8,0},{12,4},{16,24},{20,28},{24,16},{28,20},{1,9},{5... | collective-permute-start | bytes 3538952 | tf_op jit(solution)/shard_map/ppermute | solution.py:421
  88.8 33.4 %collective-permute-start.12 = (f32[2,3,64,768]{3,2,1,0:T(8,128)S(1)}, f32[2,3,64,768]{3,2,1,0:T(8,128)S(1)}, u32[]{:S(2)}, u32[]{:S(2)}) collective-permute-start(f32[2,3,64,768]{3,2,1,0:T(8,128)S(1)} %get-tuple-element.91), channel_id=1, source_target_pairs={{0,16},{4,20},{8,24},{12,28},{16,0},{20,4},{24,8},{28,12},{1,17},{... | collective-permute-start | bytes 3538952 | tf_op jit(solution)/shard_map/ppermute | solution.py:421
  90.5 8.6 %collective-permute-start.23 = (f32[64,768]{1,0:T(8,128)S(1)}, f32[64,768]{1,0:T(8,128)S(1)}, u32[]{:S(2)}, u32[]{:S(2)}) collective-permute-start(f32[64,768]{1,0:T(8,128)S(1)} %get-tuple-element.108), channel_id=1, source_target_pairs={{0,1},{1,0},{2,3},{3,2},{4,5},{5,4},{6,7},{7,6},{8,9},{9,8},{10,11... | collective-permute-start | bytes 589832 | tf_op jit(solution)/shard_map/ppermute | solution.py:406
  92.3 7.5 %collective-permute-start.22 = (f32[64,768]{1,0:T(8,128)S(1)}, f32[64,768]{1,0:T(8,128)S(1)}, u32[]{:S(2)}, u32[]{:S(2)}) collective-permute-start(f32[64,768]{1,0:T(8,128)S(1)} %get-tuple-element.103.refs_8_.refs_2_), channel_id=1, source_target_pairs={{1,2},{2,1},{5,6},{6,5},{9,10},{10,9},{13,14},{14,13},{17,18},{18,... | collective-permute-start | bytes 589832 | tf_op jit(solution)/shard_map/ppermute | solution.py:408
  93.0 11.6 %collective-permute-start.20 = (f32[64,768]{1,0:T(8,128)S(1)}, f32[64,768]{1,0:T(8,128)S(1)}, u32[]{:S(2)}, u32[]{:S(2)}) collective-permute-start(f32[64,768]{1,0:T(8,128)S(1)} %get-tuple-element.104), channel_id=1, source_target_pairs={{0,1},{1,0},{2,3},{3,2},{4,5},{5,4},{6,7},{7,6},{8,9},{9,8},{10,11... | collective-permute-start | bytes 589832 | tf_op jit(solution)/shard_map/ppermute | solution.py:406
  99.1 6.2 %collective-permute-start.21 = (f32[64,768]{1,0:T(8,128)S(1)}, f32[64,768]{1,0:T(8,128)S(1)}, u32[]{:S(2)}, u32[]{:S(2)}) collective-permute-start(f32[64,768]{1,0:T(8,128)S(1)} %get-tuple-element.105.refs_8_.refs_2_), channel_id=1, source_target_pairs={{1,2},{2,1},{5,6},{6,5},{9,10},{10,9},{13,14},{14,13},{17,18},{18,... | collective-permute-start | bytes 589832 | tf_op jit(solution)/shard_map/ppermute | solution.py:408
  99.9 10.1 %collective-permute-start.27 = (f32[64,768]{1,0:T(8,128)S(1)}, f32[64,768]{1,0:T(8,128)S(1)}, u32[]{:S(2)}, u32[]{:S(2)}) collective-permute-start(f32[64,768]{1,0:T(8,128)S(1)} %get-tuple-element.116), channel_id=1, source_target_pairs={{0,1},{1,0},{2,3},{3,2},{4,5},{5,4},{6,7},{7,6},{8,9},{9,8},{10,11... | collective-permute-start | bytes 589832 | tf_op jit(solution)/shard_map/ppermute | solution.py:406
  104.7 6.0 %collective-permute-start.26 = (f32[64,768]{1,0:T(8,128)S(1)}, f32[64,768]{1,0:T(8,128)S(1)}, u32[]{:S(2)}, u32[]{:S(2)}) collective-permute-start(f32[64,768]{1,0:T(8,128)S(1)} %get-tuple-element.111.refs_8_.refs_2_), channel_id=1, source_target_pairs={{1,2},{2,1},{5,6},{6,5},{9,10},{10,9},{13,14},{14,13},{17,18},{18,... | collective-permute-start | bytes 589832 | tf_op jit(solution)/shard_map/ppermute | solution.py:408
  105.4 10.8 %collective-permute-start.25 = (f32[64,768]{1,0:T(8,128)S(1)}, f32[64,768]{1,0:T(8,128)S(1)}, u32[]{:S(2)}, u32[]{:S(2)}) collective-permute-start(f32[64,768]{1,0:T(8,128)S(1)} %get-tuple-element.114), channel_id=1, source_target_pairs={{0,1},{1,0},{2,3},{3,2},{4,5},{5,4},{6,7},{7,6},{8,9},{9,8},{10,11... | collective-permute-start | bytes 589832 | tf_op jit(solution)/shard_map/ppermute | solution.py:406
  110.0 6.9 %collective-permute-start.24 = (f32[64,768]{1,0:T(8,128)S(1)}, f32[64,768]{1,0:T(8,128)S(1)}, u32[]{:S(2)}, u32[]{:S(2)}) collective-permute-start(f32[64,768]{1,0:T(8,128)S(1)} %get-tuple-element.112.refs_8_.refs_2_), channel_id=1, source_target_pairs={{1,2},{2,1},{5,6},{6,5},{9,10},{10,9},{13,14},{14,13},{17,18},{18,... | collective-permute-start | bytes 589832 | tf_op jit(solution)/shard_map/ppermute | solution.py:408
  110.8 11.7 %collective-permute-start.30 = (f32[64,768]{1,0:T(8,128)S(1)}, f32[64,768]{1,0:T(8,128)S(1)}, u32[]{:S(2)}, u32[]{:S(2)}) collective-permute-start(f32[64,768]{1,0:T(8,128)S(1)} %get-tuple-element.125), channel_id=1, source_target_pairs={{0,1},{1,0},{2,3},{3,2},{4,5},{5,4},{6,7},{7,6},{8,9},{9,8},{10,11... | collective-permute-start | bytes 589832 | tf_op jit(solution)/shard_map/ppermute | solution.py:406
  116.2 6.3 %collective-permute-start.31 = (f32[64,768]{1,0:T(8,128)S(1)}, f32[64,768]{1,0:T(8,128)S(1)}, u32[]{:S(2)}, u32[]{:S(2)}) collective-permute-start(f32[64,768]{1,0:T(8,128)S(1)} %get-tuple-element.119.refs_8_.refs_2_), channel_id=1, source_target_pairs={{1,2},{2,1},{5,6},{6,5},{9,10},{10,9},{13,14},{14,13},{17,18},{18,... | collective-permute-start | bytes 589832 | tf_op jit(solution)/shard_map/ppermute | solution.py:408
  117.0 10.1 %collective-permute-start.35 = (f32[64,768]{1,0:T(8,128)S(1)}, f32[64,768]{1,0:T(8,128)S(1)}, u32[]{:S(2)}, u32[]{:S(2)}) collective-permute-start(f32[64,768]{1,0:T(8,128)S(1)} %get-tuple-element.131), channel_id=1, source_target_pairs={{0,1},{1,0},{2,3},{3,2},{4,5},{5,4},{6,7},{7,6},{8,9},{9,8},{10,11... | collective-permute-start | bytes 589832 | tf_op jit(solution)/shard_map/ppermute | solution.py:406
  121.6 5.6 %collective-permute-start.34 = (f32[64,768]{1,0:T(8,128)S(1)}, f32[64,768]{1,0:T(8,128)S(1)}, u32[]{:S(2)}, u32[]{:S(2)}) collective-permute-start(f32[64,768]{1,0:T(8,128)S(1)} %get-tuple-element.120.refs_4_.refs_7_.refs_2_), channel_id=1, source_target_pairs={{1,2},{2,1},{5,6},{6,5},{9,10},{10,9},{13,14},{14,13},{17,18},{18,... | collective-permute-start | bytes 589832 | tf_op jit(solution)/shard_map/ppermute | solution.py:408
  122.6 9.8 %collective-permute-start.33 = (f32[64,768]{1,0:T(8,128)S(1)}, f32[64,768]{1,0:T(8,128)S(1)}, u32[]{:S(2)}, u32[]{:S(2)}) collective-permute-start(f32[64,768]{1,0:T(8,128)S(1)} %get-tuple-element.129.refs_4_), channel_id=1, source_target_pairs={{0,1},{1,0},{2,3},{3,2},{4,5},{5,4},{6,7},{7,6},{8,9},{9,8},{10,11... | collective-permute-start | bytes 589832 | tf_op jit(solution)/shard_map/ppermute | solution.py:406
  126.5 7.2 %collective-permute-start.32 = (f32[64,768]{1,0:T(8,128)S(1)}, f32[64,768]{1,0:T(8,128)S(1)}, u32[]{:S(2)}, u32[]{:S(2)}) collective-permute-start(f32[64,768]{1,0:T(8,128)S(1)} %get-tuple-element.128.refs_7_.refs_2_), channel_id=1, source_target_pairs={{1,2},{2,1},{5,6},{6,5},{9,10},{10,9},{13,14},{14,13},{17,18},{18,... | collective-permute-start | bytes 589832 | tf_op jit(solution)/shard_map/ppermute | solution.py:408
  127.2 9.8 %collective-permute-start.39 = (f32[64,768]{1,0:T(8,128)S(1)}, f32[64,768]{1,0:T(8,128)S(1)}, u32[]{:S(2)}, u32[]{:S(2)}) collective-permute-start(f32[64,768]{1,0:T(8,128)S(1)} %get-tuple-element.137.refs_4_), channel_id=1, source_target_pairs={{0,1},{1,0},{2,3},{3,2},{4,5},{5,4},{6,7},{7,6},{8,9},{9,8},{10,11... | collective-permute-start | bytes 589832 | tf_op jit(solution)/shard_map/ppermute | solution.py:406
  131.7 6.0 %collective-permute-start.38 = (f32[64,768]{1,0:T(8,128)S(1)}, f32[64,768]{1,0:T(8,128)S(1)}, u32[]{:S(2)}, u32[]{:S(2)}) collective-permute-start(f32[64,768]{1,0:T(8,128)S(1)} %get-tuple-element.134.refs_7_.refs_2_), channel_id=1, source_target_pairs={{1,2},{2,1},{5,6},{6,5},{9,10},{10,9},{13,14},{14,13},{17,18},{18,... | collective-permute-start | bytes 589832 | tf_op jit(solution)/shard_map/ppermute | solution.py:408
  132.3 14.6 %collective-permute-start.28 = (f32[1,3,64,768]{3,2,1,0:T(8,128)S(1)}, f32[1,3,64,768]{3,2,1,0:T(8,128)S(1)}, u32[]{:S(2)}, u32[]{:S(2)}) collective-permute-start(f32[1,3,64,768]{3,2,1,0:T(8,128)S(1)} %get-tuple-element.122), channel_id=1, source_target_pairs={{0,16},{4,20},{8,24},{12,28},{16,0},{20,4},{24,8},{28,12},{1,17},{... | collective-permute-start | bytes 1769480 | tf_op jit(solution)/shard_map/ppermute | solution.py:421
  132.4 14.5 %collective-permute-start.29 = (f32[1,3,64,768]{3,2,1,0:T(8,128)S(1)}, f32[1,3,64,768]{3,2,1,0:T(8,128)S(1)}, u32[]{:S(2)}, u32[]{:S(2)}) collective-permute-start(f32[1,3,64,768]{3,2,1,0:T(8,128)S(1)} %get-tuple-element.124), channel_id=1, source_target_pairs={{0,8},{4,12},{8,0},{12,4},{16,24},{20,28},{24,16},{28,20},{1,9},{5... | collective-permute-start | bytes 1769480 | tf_op jit(solution)/shard_map/ppermute | solution.py:421
  133.8 8.4 %collective-permute-start.37 = (f32[64,768]{1,0:T(8,128)S(1)}, f32[64,768]{1,0:T(8,128)S(1)}, u32[]{:S(2)}, u32[]{:S(2)}) collective-permute-start(f32[64,768]{1,0:T(8,128)S(1)} %get-tuple-element.136.refs_2_), channel_id=1, source_target_pairs={{0,1},{1,0},{2,3},{3,2},{4,5},{5,4},{6,7},{7,6},{8,9},{9,8},{10,11... | collective-permute-start | bytes 589832 | tf_op jit(solution)/shard_map/ppermute | solution.py:406
  137.0 5.8 %collective-permute-start.36 = (f32[64,768]{1,0:T(8,128)S(1)}, f32[64,768]{1,0:T(8,128)S(1)}, u32[]{:S(2)}, u32[]{:S(2)}) collective-permute-start(f32[64,768]{1,0:T(8,128)S(1)} %get-tuple-element.135.refs_7_.refs_0_), channel_id=1, source_target_pairs={{1,2},{2,1},{5,6},{6,5},{9,10},{10,9},{13,14},{14,13},{17,18},{18,... | collective-permute-start | bytes 589832 | tf_op jit(solution)/shard_map/ppermute | solution.py:408
  137.8 10.3 %collective-permute-start.41 = (f32[64,768]{1,0:T(8,128)S(1)}, f32[64,768]{1,0:T(8,128)S(1)}, u32[]{:S(2)}, u32[]{:S(2)}) collective-permute-start(f32[64,768]{1,0:T(8,128)S(1)} %get-tuple-element.142.refs_2_), channel_id=1, source_target_pairs={{0,1},{1,0},{2,3},{3,2},{4,5},{5,4},{6,7},{7,6},{8,9},{9,8},{10,11... | collective-permute-start | bytes 589832 | tf_op jit(solution)/shard_map/ppermute | solution.py:406
  142.1 6.0 %collective-permute-start.40 = (f32[64,768]{1,0:T(8,128)S(1)}, f32[64,768]{1,0:T(8,128)S(1)}, u32[]{:S(2)}, u32[]{:S(2)}) collective-permute-start(f32[64,768]{1,0:T(8,128)S(1)} %get-tuple-element.140.refs_5_.refs_0_), channel_id=1, source_target_pairs={{1,2},{2,1},{5,6},{6,5},{9,10},{10,9},{13,14},{14,13},{17,18},{18,... | collective-permute-start | bytes 589832 | tf_op jit(solution)/shard_map/ppermute | solution.py:408
  142.9 8.0 %collective-permute-start.43 = (f32[64,768]{1,0:T(8,128)S(1)}, f32[64,768]{1,0:T(8,128)S(1)}, u32[]{:S(2)}, u32[]{:S(2)}) collective-permute-start(f32[64,768]{1,0:T(8,128)S(1)} %get-tuple-element.141.refs_4_.refs_5_.refs_0_), channel_id=1, source_target_pairs={{0,1},{1,0},{2,3},{3,2},{4,5},{5,4},{6,7},{7,6},{8,9},{9,8},{10,11... | collective-permute-start | bytes 589832 | tf_op jit(solution)/shard_map/ppermute | solution.py:406
  148.1 6.3 %collective-permute-start.42 = (f32[64,768]{1,0:T(8,128)S(1)}, f32[64,768]{1,0:T(8,128)S(1)}, u32[]{:S(2)}, u32[]{:S(2)}) collective-permute-start(f32[64,768]{1,0:T(8,128)S(1)} %get-tuple-element.144.refs_3_.refs_0_), channel_id=1, source_target_pairs={{0,1},{1,0},{2,3},{3,2},{4,5},{5,4},{6,7},{7,6},{8,9},{9,8},{10,11... | collective-permute-start | bytes 589832 | tf_op jit(solution)/shard_map/ppermute | solution.py:406

commit v4 on v3

--- a/solution.py
+++ b/solution.py
@@ -10,8 +10,11 @@
 
 BLK = 128
 LOW = -1e30
-LAGS = (4, 2, 2)
-HOME_SLOTS = (8, 15, 20)
+LAGS = (4, 3, 2)
+HOME_SLOTS = (7, 14, 18)
+START_SLOT = 4
+TERM_SLOTS = ()
+PARTS = 1 + len(TERM_SLOTS)
 SLOT_FLOPS = 4_000_000_000
 
 
@@ -22,10 +25,6 @@
 def split(x):
     hi = x.astype(jnp.bfloat16)
     return hi, (x - hi.astype(jnp.float32)).astype(jnp.bfloat16)
-
-
-def as_columns(row):
-    return jnp.broadcast_to(row, (BLK, row.shape[1])).T
 
 
 class Meta:
@@ -50,8 +49,8 @@
         return jnp.where((flags[self.steps + s] > 0) & (j < self.slab_blocks), self.blocks + j, j)
 
 
-def scores_kernel(meta, group, scale, member, owner, q_hbm, cache_hbm, fresh_hbm, z_ref, w_ref, q_ref, lse_ref,
-                  cache_ref, fresh_ref, peak, top, flags, entries, pairs, sem):
+def scores_kernel(meta, group, scale, member, owner, q_hbm, cache_hbm, fresh_hbm, z_ref, w_ref, q_ref, lse_ref, entries,
+                  cache_ref, fresh_ref, peak, total, flags, pairs, sem):
     copies = [pltpu.make_async_copy(src, dst, sem.at[i]) for i, (src, dst) in enumerate(
         ((cache_hbm, cache_ref), (fresh_hbm, fresh_ref), (q_hbm, q_ref)))]
     for copy in copies:
@@ -81,7 +80,9 @@
     for g in range(group):
         entries[n_entries + g] = jnp.where(n_entries > 0, entries[0], 0)
         pairs[n_pairs + g] = 0
+    entries[entries.shape[0] - 1] = n_entries
     peak[...] = jnp.full(peak.shape, LOW, jnp.float32)
+    total[...] = jnp.zeros(total.shape, jnp.float32)
 
     for copy, src, at in ((copies[0], cache_ref, 0), (copies[1], fresh_ref, meta.blocks)):
         copy.wait()
@@ -101,42 +102,33 @@
             e = entries[it * group + g]
             j, both = e % meta.blocks, e // meta.blocks
             sb0, sb1 = both // meta.rows, both % meta.rows
-            left = jnp.concatenate([q_ref[sb0], q_ref[sb1]], axis=0)
-            z = dot(left, w_ref[meta.source(flags, sb0 // meta.groups, j)], 1, 1)
-            found.append((sb0, sb1, j, (z[:, :BLK] + z[:, BLK:]) * scale))
+            right = jnp.concatenate([q_ref[sb0], q_ref[sb1]], axis=0)
+            z = dot(w_ref[meta.source(flags, sb0 // meta.groups, j)], right, 1, 1)
+            found.append((sb0, sb1, j, (z[:BLK] + z[BLK:]) * scale))
         for sb0, sb1, j, z in found:
-            z_ref[sb0, j] = z[:BLK]
-            z_ref[sb1, j] = z[BLK:]
-            peak[sb0] = jnp.maximum(peak[sb0], z[:BLK])
-            peak[sb1] = jnp.maximum(peak[sb1], z[BLK:])
+            for sb, one in ((sb0, z[:, :BLK]), (sb1, z[:, BLK:])):
+                z_ref[sb, j] = one
+                row = pl.ds(sb, 1)
+                peak[row, :] = jnp.maximum(peak[row, :], jnp.max(one, axis=0, keepdims=True))
         return 0
 
     lax.fori_loop(0, (n_entries + group - 1) // group, score, 0)
 
-    def highest(sb, _):
-        top[sb] = jnp.broadcast_to(jnp.max(peak[sb], axis=1, keepdims=True), (BLK, BLK))
-        peak[sb] = jnp.zeros((BLK, BLK), jnp.float32)
-        return 0
-
-    lax.fori_loop(0, meta.rows, highest, 0, unroll=4 if meta.rows % 4 == 0 else 1)
-
     def add(it, _):
+        found = []
         for g in range(group):
             k = it * group + g
             sb, j = pairs[k] // meta.blocks, pairs[k] % meta.blocks
             c = meta.count(member, flags, sb // meta.groups, sb, j).astype(jnp.float32)
-            peak[sb] += jnp.where(k < n_pairs, jnp.exp(z_ref[sb, j] - top[sb]) * c, 0.0)
+            value = jnp.sum(jnp.exp(z_ref[sb, j] - peak[pl.ds(sb, 1), :]), axis=0, keepdims=True)
+            found.append((sb, jnp.where(k < n_pairs, value * c, 0.0)))
+        for sb, value in found:
+            total[pl.ds(sb, 1), :] += value
         return 0
 
     lax.fori_loop(0, (n_pairs + group - 1) // group, add, 0)
-
-    def finish(sb, _):
-        total = jnp.sum(peak[sb], axis=1, keepdims=True)
-        lse = jnp.where(total > 0, top[sb][:, :1] + jnp.log(jnp.maximum(total, 1e-30)), LOW)
-        lse_ref[pl.ds(sb, 1), :] = jnp.broadcast_to(lse, (BLK, BLK)).T[:1]
-        return 0
-
-    lax.fori_loop(0, meta.rows, finish, 0, unroll=4 if meta.rows % 4 == 0 else 1)
+    sums = total[...]
+    lse_ref[...] = jnp.where(sums > 0, peak[...] + jnp.log(jnp.maximum(sums, 1e-30)), LOW)
 
 
 def grad_kernel(meta, first, width, member, z_ref, q_ref, lse_ref, dep, out_ref, todo):
@@ -156,7 +148,7 @@
             for g in range(width):
                 k = it * width + g
                 sb = todo[k]
-                p = jnp.exp(z_ref[sb, j].T - lse_ref[pl.ds(sb, 1), :])
+                p = jnp.exp(z_ref[sb, j] - lse_ref[pl.ds(sb, 1), :])
                 hi, lo = split(jnp.where(k < n, p, 0.0))
                 his.append(hi)
                 los.append(lo)
@@ -172,51 +164,58 @@
     lax.fori_loop(0, out_ref.shape[0] // BLK, block, 0)
 
 
-def term_kernel(meta, order, width, member, owner, z_ref, w_ref, lse_ref, pos_ref, dep, *refs):
-    outs, (flags, todo, lcol, pcol) = refs[:-4], refs[-4:]
+def term_kernel(meta, spread, width, part, parts, member, owner, entries, z_ref, w_ref, lse_ref, pos_ref, dep, old, out_ref,
+                flags, rows_ref):
     meta.flags(owner, flags)
-    lane = lax.broadcasted_iota(jnp.int32, (BLK, BLK), 1).astype(jnp.float32)
-
-    def block(i, out_ref, first, stride):
-        b = lax.axis_index("cache") ^ (first + stride * i) if order else first + stride * i
-        n = 0
+    me = lax.axis_index("cache")
+    below = lax.broadcasted_iota(jnp.int32, (BLK, BLK), 0)
+    for s in range(meta.steps):
+        for b in range(meta.groups):
+            sb = s * meta.groups + b
+            rows_ref[sb:sb + 1, :] = pos_ref[s:s + 1, b * BLK:(b + 1) * BLK]
+
+    def clear(i, _):
         for s in range(meta.steps):
-            sb = s * meta.groups + b
-            lcol[s] = as_columns(lse_ref[pl.ds(sb, 1), :])
-            pcol[s] = as_columns(pos_ref[s:s + 1, pl.ds(pl.multiple_of(b * BLK, BLK), BLK)].astype(jnp.float32)) - lane
-            out_ref[i, s] = jnp.zeros((BLK, out_ref.shape[3]), jnp.float32)
-            for j in range(meta.blocks):
-                todo[n] = s * meta.blocks + j
-                n = n + (meta.count(member, flags, s, sb, j) > 0).astype(jnp.int32)
+            out_ref[i, s] = jnp.zeros(out_ref.shape[2:], jnp.float32)
+        return 0
+
+    if part == 0:
+        lax.fori_loop(0, meta.groups, clear, 0)
+    n = entries[entries.shape[0] - 1]
+    trips = (n + width - 1) // width
+
+    def step(it, _):
+        found = []
         for g in range(width):
-            todo[n + g] = 0
-
-        def step(it, _):
-            found = []
-            for g in range(width):
-                k = it * width + g
-                s, j = todo[k] // meta.blocks, todo[k] % meta.blocks
-                sb = s * meta.groups + b
-                p = jnp.exp(z_ref[sb, j] - lcol[s]) * meta.count(member, flags, s, sb, j).astype(jnp.float32)
-                hot = (flags[s] > 0) & (j < meta.slab_blocks)
-                p = p - jnp.where(pcol[s] == (j * BLK).astype(jnp.float32), hot.astype(jnp.float32), 0.0)
-                hi, lo = split(jnp.where(k < n, p, 0.0))
-                w = w_ref[meta.source(flags, s, j)]
-                found.append((s, dot(jnp.concatenate([hi, hi], axis=1), w, 1, 0) + dot(lo, w[:BLK], 1, 0)))
-            for s, term in found:
-                out_ref[i, s] += term
-            return 0
-
-        lax.fori_loop(0, (n + width - 1) // width, step, 0)
-
-    for o, out_ref in enumerate(outs):
-        first, stride = (order[o], len(order)) if order else (0, 1)
-
-        def one(i, _, out_ref=out_ref, first=first, stride=stride):
-            block(i, out_ref, first, stride)
-            return 0
-
-        lax.fori_loop(0, out_ref.shape[0], one, 0)
+            k = it * width + g
+            j, both = entries[k] % meta.blocks, entries[k] // meta.blocks
+            sbs = both // meta.rows, both % meta.rows
+            s = sbs[0] // meta.groups
+            hot = ((flags[s] > 0) & (j < meta.slab_blocks)).astype(jnp.float32)
+            his, los = [], []
+            for half, sb in enumerate(sbs):
+                c = meta.count(member, flags, s, sb, j).astype(jnp.float32)
+                p = jnp.exp(z_ref[sb, j] - lse_ref[pl.ds(sb, 1), :]) * c
+                row = rows_ref[pl.ds(sb, 1), :] - j * BLK
+                p = p - jnp.where(row == below, hot, 0.0)
+                live = (k < n) if half == 0 else (k < n) & (sbs[1] != sbs[0])
+                hi, lo = split(jnp.where(live, p, 0.0).T)
+                his.append(hi)
+                los.append(lo)
+            hi = jnp.concatenate(his, axis=0)
+            w = w_ref[meta.source(flags, s, j)]
+            acc = dot(jnp.concatenate([hi, hi], axis=1), w, 1, 0) + dot(jnp.concatenate(los, axis=0), w[:BLK], 1, 0)
+            found.append((s, sbs, acc))
+        for s, sbs, acc in found:
+            for half, sb in enumerate(sbs):
+                place = sb - s * meta.groups
+                if spread:
+                    r = me ^ place
+                    place = r // 2 + jnp.where(r % 2 == 1, 0, meta.groups // 2)
+                out_ref[place, s] += acc[half * BLK:(half + 1) * BLK]
+        return 0
+
+    lax.fori_loop(trips * part // parts, trips * (part + 1) // parts, step, 0)
 
 
 def params(mib):
@@ -241,20 +240,20 @@
     return pl.pallas_call(
         functools.partial(scores_kernel, meta, group, 2.0 / math.sqrt(width)),
         in_specs=[SMEM, SMEM, HBM, HBM, HBM],
-        out_specs=[VMEM] * 4,
+        out_specs=[VMEM] * 4 + [SMEM],
         out_shape=[
             pltpu.VMEM((meta.rows, meta.blocks, BLK, BLK), jnp.float32),
             pltpu.VMEM((n_src, 2 * BLK, width), jnp.bfloat16),
             pltpu.VMEM((meta.rows, BLK, width), jnp.bfloat16),
             pltpu.VMEM((meta.rows, BLK), jnp.float32),
+            jax.ShapeDtypeStruct((most + group + 2,), jnp.int32),
         ],
         scratch_shapes=[
             pltpu.VMEM(cache.shape, jnp.float32),
             pltpu.VMEM(fresh.shape, jnp.float32),
-            pltpu.VMEM((meta.rows, BLK, BLK), jnp.float32),
-            pltpu.VMEM((meta.rows, BLK, BLK), jnp.float32),
+            pltpu.VMEM((meta.rows, BLK), jnp.float32),
+            pltpu.VMEM((meta.rows, BLK), jnp.float32),
             pltpu.SMEM((2 * meta.steps,), jnp.int32),
-            pltpu.SMEM((most + group + 1,), jnp.int32),
             pltpu.SMEM((meta.size + group,), jnp.int32),
             pltpu.SemaphoreType.DMA((3,)),
         ],
@@ -278,25 +277,19 @@
     )(member, z, q, lse, dep)
 
 
-def run_terms(meta, member, owner, z, w, lse, pos, order, dep):
-    group = 4
-    n_out = max(1, len(order))
-    shape = (meta.groups // n_out, meta.steps, BLK, w.shape[2])
+def run_terms(meta, member, owner, entries, z, w, lse, pos, spread, dep, part=0, parts=1, old=None):
+    group = 3
     return pl.pallas_call(
-        functools.partial(term_kernel, meta, order, group),
-        in_specs=[SMEM, SMEM, VMEM, VMEM, VMEM, VMEM, ANY],
-        out_specs=[VMEM] * n_out,
-        out_shape=[pltpu.VMEM(shape, jnp.float32)] * n_out,
-        scratch_shapes=[
-            pltpu.SMEM((2 * meta.steps,), jnp.int32),
-            pltpu.SMEM((meta.steps * meta.blocks + group,), jnp.int32),
-            pltpu.VMEM((meta.steps, BLK, BLK), jnp.float32),
-            pltpu.VMEM((meta.steps, BLK, BLK), jnp.float32),
-        ],
+        functools.partial(term_kernel, meta, spread, group, part, parts),
+        in_specs=[SMEM, SMEM, SMEM, VMEM, VMEM, VMEM, VMEM, ANY, VMEM if part else ANY],
+        input_output_aliases={8: 0} if part else {},
+        out_specs=VMEM,
+        out_shape=pltpu.VMEM((meta.groups, meta.steps, BLK, w.shape[2]), jnp.float32),
+        scratch_shapes=[pltpu.SMEM((2 * meta.steps,), jnp.int32), pltpu.VMEM((meta.rows, BLK), jnp.int32)],
         compiler_params=params(10),
         cost_estimate=free(),
         name="query_term",
-    )(member, owner, z, w, lse, pos, dep)
+    )(member, owner, entries, z, w, lse, pos, dep, old if part else dep)
 
 
 def small(kernel, inputs, n_deps, outs, name, aliases=None, flops=0):
@@ -410,10 +403,10 @@
 
 
 class HomeSum:
-    def __init__(self, odd, even):
+    def __init__(self, terms):
         self.n = lax.axis_size("cache")
-        self.odd, self.even = odd, even
-        self.steps, self.rows, self.width = even.shape[1:]
+        self.terms = terms
+        self.steps, self.rows, self.width = terms.shape[1:]
         self.bits = [1 << i for i in range(1, self.n.bit_length() - 1)]
         self.stage = 0
 
@@ -421,10 +414,15 @@
         return lax.ppermute(x, "cache", [(i, i ^ bit) for i in range(self.n)])
 
     def start(self, dep):
-        def kernel(*refs):
-            pass
-
-        odd = small(kernel, [self.odd, dep], 1, [self.odd.shape], "home_start", {0: 0})[0]
+        def kernel(terms, dep, odd):
+            def one(i, _):
+                for s in range(odd.shape[1]):
+                    odd[i, s] = terms[i, s]
+                return 0
+
+            lax.fori_loop(0, odd.shape[0], one, 0)
+
+        odd = small(kernel, [self.terms, dep], 1, [(self.n // 2,) + self.terms.shape[1:]], "home_start")[0]
         self.got = self.move(odd, 1)
 
     def step(self, dep):
@@ -432,7 +430,7 @@
         orders = (self.bits, self.bits[::-1])
         last = self.stage == len(self.bits)
         if self.stage == 0:
-            inputs = [self.even, self.got]
+            inputs = [self.terms, self.got]
             sources = [({2 * i: i for i in range(self.n // 2)}, 0, 1, h * half) for h in (0, 1)]
         else:
             inputs, sources = [], []
@@ -454,6 +452,7 @@
         if last:
             outs = [(self.steps, self.rows, self.width)]
         n_in, steps = len(inputs), self.steps
+        skip = self.n // 2 if self.stage == 0 else 0
 
         def kernel(*refs):
             res = refs[n_in + 1:]
@@ -462,7 +461,7 @@
                 i = place[r]
 
                 def one(s, _, a=a, b=b, i=i, first=first, to=to, at=at):
-                    value = refs[a][i, s, first:first + half, :] + refs[b][i, s, first:first + half, :]
+                    value = refs[a][skip + i, s, first:first + half, :] + refs[b][i, s, first:first + half, :]
                     if at is None:
                         res[to[0]][to[1], s] = value
                     else:
@@ -492,7 +491,7 @@
     member = member.astype(jnp.int32).reshape(meta.rows, blocks)
     owner = refresh_owner.astype(jnp.int32)
 
-    z, w, q, own_lse = run_scores(meta, member, owner, queries, cache, fresh)
+    z, w, q, own_lse, entries = run_scores(meta, member, owner, queries, cache, fresh)
     lse = exchange_lse(own_lse)
 
     half = BLK // 2
@@ -511,8 +510,12 @@
         grads.append(run_grads(meta, member, z, q, lse, early, blocks - early, dep))
         if not fast:
             return grads[1], None
-        odd, even = run_terms(meta, member, owner, z, w, lse, positives, (1, 0), grads[1])
-        return even, HomeSum(odd, even)
+        terms = run_terms(meta, member, owner, entries, z, w, lse, positives, True, grads[1], 0, PARTS)
+        return terms, HomeSum(terms)
+
+    def more(part, dep):
+        home.terms = run_terms(meta, member, owner, entries, z, w, lse, positives, True, dep, part, PARTS, home.terms)
+        return home.terms
 
     if lax.axis_size("batch") == 4 and blocks > early:
         line = Line(2 * blocks, half, width)
@@ -521,7 +524,9 @@
         deps = [dep]
         for t in range(LAGS[0], line.slots):
             deps = [line.slot(t, chunk, deps)]
-            if t == LAGS[0] and fast:
+            if fast and t in TERM_SLOTS:
+                deps.append(more(1 + TERM_SLOTS.index(t), deps[0]))
+            if fast and t == START_SLOT:
                 home.start(deps[0])
             if fast and t in HOME_SLOTS:
                 deps.append(home.step(deps[0]))
@@ -530,6 +535,8 @@
     else:
         _, home = rest(lse)
         if fast:
+            for part in range(1, PARTS):
+                more(part, lse)
             home.start(lse)
         grad = lax.psum(jnp.concatenate(grads, axis=0), "batch")
     if fast:
@@ -538,7 +545,7 @@
         if mine is None or mine.ndim != 3:
             mine = home.step(lse)
     else:
-        term = run_terms(meta, member, owner, z, w, lse, positives, (), lse)[0]
+        term = run_terms(meta, member, owner, entries, z, w, lse, positives, False, lse)
         term = jnp.swapaxes(term, 0, 1).reshape(steps, group_rows, width)
         mine = lax.psum_scatter(term, "cache", scatter_dimension=1, tiled=True)
     return mine, grad

time: 158 us -> 151 us (0.956); the launches traced: 156 us -> 151 us
  waiting for transfers between devices: 11.2 us -> 23.8 us
  starting transfers between devices: 91.6 us -> 79.8 us
  Pallas kernels: 46.6 us -> 40.7 us
    ppermute x18 -> x19, starting transfers between devices: 72 us -> 52.5 us  [slot(): self.swap[t] = lax.ppermute(away, 'batch', [(0, 1), (1, 0), (2, 3), (3, 2)])]
    ppermute x18 -> x19, waiting for transfers between devices: 6.28 us -> 15.2 us  [slot(): self.swap[t] = lax.ppermute(away, 'batch', [(0, 1), (1, 0), (2, 3), (3, 2)])]
    ppermute x5, starting transfers between devices: 3.04 us -> 8.92 us  [move(): return lax.ppermute(x, 'cache', [(i, i ^ bit) for i in range(self.n)])]
    ppermute x5, waiting for transfers between devices: 0.01 us -> 5.1 us  [move(): return lax.ppermute(x, 'cache', [(i, i ^ bit) for i in range(self.n)])]
    pallas_call x1, Pallas kernels: 18.1 us -> 14.5 us  [run_scores(): pl.pallas_call(functools.partial(scores_kernel, meta, group, 2.0 / math.s...]
  transfers between devices with their start and end apart: 44 -> 45, of which waited for: 8 -> 14; matrix products, arithmetic and copies ran while one was open for 1% -> 1% of each run, Pallas kernels for 16% -> 15%
where the time goes in v4:
time: 151 us
  starting transfers between devices  79.8 us (53%)
  Pallas kernels  40.7 us (27%)
  waiting for transfers between devices  23.8 us (16%)
  local copies, waits for them, and re-layouts  3.54 us (2%)
  other arithmetic  2.02 us (1%)
    ppermute x19, starting transfers between devices, slot(): self.swap[t] = lax.ppermute(away, 'batch', [(0, 1), (1, 0), (2, 3), (3, 2)])  52.5 us
    ppermute x19, waiting for transfers between devices, slot(): self.swap[t] = lax.ppermute(away, 'batch', [(0, 1), (1, 0), (2, 3), (3, 2)])  15.2 us
    pallas_call x1, Pallas kernels, run_scores(): pl.pallas_call(functools.partial(scores_kernel, meta, group, 2.0 / math.s...  14.5 us
    pallas_call x1, Pallas kernels, run_terms(): pl.pallas_call(functools.partial(term_kernel, meta, spread, group, part,...  14.5 us
    ppermute x16, starting transfers between devices, slot(): self.mid[u] = lax.ppermute(self.inner[u], 'batch', [(1, 2), (2, 1)])  10.6 us
    pallas_call x2, Pallas kernels, run_grads(): pl.pallas_call(functools.partial(grad_kernel, meta, first, group), in_spe...  9.26 us
    ppermute x5, starting transfers between devices, move(): return lax.ppermute(x, 'cache', [(i, i ^ bit) for i in range(self.n)])  8.92 us
    ppermute x4, starting transfers between devices, exchange_lse(): lax.ppermute(lse, 'cache', [(i, i ^ p) for i in range(n)])  5.38 us
  transfers between devices with their start and end apart: 45, of which 14 were waited for; matrix products, arithmetic and copies ran while one was open for 1% of the time, Pallas kernels for 15%

profile of v4, /device:TPU:0, one launch (start us, length us, event | category | flops | bytes accessed | tf_op | source)
XLA Modules:
  0.0 151.1 jit_solution(6925763209195402267)
XLA Ops:
  0.6 0.8 iota_compare_fusion
  1.4 1.3 and_reduce_fusion
  3.3 14.5 %scores.1 = (f32[24,8,128,128]{3,2,1,0:T(8,128)S(1)}, bf16[12,256,768]{2,1,0:T(8,128)(2,1)S(1)}, bf16[24,128,768]{2,1,0:T(8,128)(2,1)S(1)}, f32[24,128]{1,0:T(8,128)S(1)}, s32[102]{0:T(128)S(1)}) custom-call(s32[24,8]{1,0:T(8,128)S(1)} %convert_bitcast_fusion.member, s32[3]{0:T(128)S(1)} %copy-done.1, bf16[24,128,768]{2,1,0:T(8,128)(2,1)} %bitcast.3, ...), custom_call_target="tpu_custom_call" | custom-call | tf_op jit(solution)/shard_map/scores/pallas_call | solution.py:240
  17.9 1.2 collective-permute-done.refs_1_
  19.1 3.5 %collective-permute-start.3 = (f32[24,128]{1,0:T(8,128)S(1)}, f32[24,128]{1,0:T(8,128)S(1)}, u32[]{:S(2)}, u32[]{:S(2)}) collective-permute-start(f32[24,128]{1,0:T(8,128)S(1)} %merge_lse.2.refs_0_), channel_id=1, source_target_pairs={{0,24},{4,28},{8,16},{12,20},{16,8},{20,12},{24,0},{28,4},{1,25},{... | collective-permute-start | bytes 36872 | tf_op jit(solution)/shard_map/ppermute | solution.py:321
  23.0 1.4 collective-permute-start.1
  24.4 1.9 %collective-permute-done.2.refs_2_ = f32[24,128]{1,0:T(8,128)S(1)} collective-permute-done((f32[24,128]{1,0:T(8,128)S(1)}, f32[24,128]{1,0:T(8,128)S(1)}, u32[]{:S(2)}, u32[]{:S(2)}) %collective-permute-start.2) | collective-permute-done | bytes 12320 | tf_op jit(solution)/shard_map/ppermute | solution.py:321
  26.7 2.5 %cache_grad.2.dep.refs_0_ = f32[256,768]{1,0:T(8,128)S(1)} custom-call(s32[24,8]{1,0:T(8,128)S(1)} %convert_bitcast_fusion.member, f32[24,8,128,128]{3,2,1,0:T(8,128)S(1)} %get-tuple-element.74.z_ref, bf16[24,128,768]{2,1,0:T(8,128)(2,1)S(1)} %get-tuple-element.77.q_ref, f32[24,128]{1,0:T(8,128)S(1)} %merge_lse.3.lse_ref.dep, f32[24,128]{1,0:T(8,128)S(1)} %merge_lse.3.lse_ref.dep), custom_call_target="tpu_custom_call" | custom-call | tf_op jit(solution)/shard_map/cache_grad/pallas_call | solution.py:268
  29.2 2.4 %collective-permute-start.4 = (f32[256,768]{1,0:T(8,128)S(1)}, f32[256,768]{1,0:T(8,128)S(1)}, u32[]{:S(2)}, u32[]{:S(2)}) collective-permute-start(f32[256,768]{1,0:T(8,128)S(1)} %cache_grad.2.dep.refs_0_), channel_id=1, source_target_pairs={{0,1},{1,0},{2,3},{3,2},{4,5},{5,4},{6,7},{7,6},{8,9},{9,8},{10,11... | collective-permute-start | bytes 2359304 | tf_op jit(solution)/shard_map/ppermute | solution.py:336
  31.6 6.8 %cache_grad.3.dep.old.refs_2_.refs_4_.refs_0_ = f32[768,768]{1,0:T(8,128)S(1)} custom-call(s32[24,8]{1,0:T(8,128)S(1)} %convert_bitcast_fusion.member, f32[24,8,128,128]{3,2,1,0:T(8,128)S(1)} %get-tuple-element.74.z_ref, bf16[24,128,768]{2,1,0:T(8,128)(2,1)S(1)} %get-tuple-element.77.q_ref, f32[24,128]{1,0:T(8,128)S(1)} %merge_lse.3.lse_ref.dep, ...), custom_call_target="tpu_custom_call" | custom-call | tf_op jit(solution)/shard_map/cache_grad/pallas_call | solution.py:268
  38.4 14.5 %query_term.1.refs_3_.terms.refs_0_ = f32[8,3,128,768]{3,2,1,0:T(8,128)S(1)} custom-call(s32[24,8]{1,0:T(8,128)S(1)} %convert_bitcast_fusion.member, s32[3]{0:T(128)S(1)} %copy-done.1, s32[102]{0:T(128)S(1)} %get-tuple-element.73.entries, f32[24,8,128,128]{3,2,1,0:T(8,128)S(1)} %get-tuple-element.74.z_ref, ...), custom_call_target="tpu_custom_call" | custom-call | tf_op jit(solution)/shard_map/query_term/pallas_call | solution.py:282
  53.3 0.7 collective-permute-start.6
  54.0 4.7 %collective-permute-start.11 = (f32[64,768]{1,0:T(8,128)S(1)}, f32[64,768]{1,0:T(8,128)S(1)}, u32[]{:S(2)}, u32[]{:S(2)}) collective-permute-start(f32[64,768]{1,0:T(8,128)S(1)} %get-tuple-element.87), channel_id=1, source_target_pairs={{0,1},{1,0},{2,3},{3,2},{4,5},{5,4},{6,7},{7,6},{8,9},{9,8},{10,11... | collective-permute-start | bytes 589832 | tf_op jit(solution)/shard_map/ppermute | solution.py:399
  58.9 0.7 collective-permute-start.12
  59.6 0.7 collective-permute-start.15
  60.4 0.9 collective-permute-done.5.refs_1_
  61.2 7.2 %collective-permute-start.9 = (f32[64,768]{1,0:T(8,128)S(1)}, f32[64,768]{1,0:T(8,128)S(1)}, u32[]{:S(2)}, u32[]{:S(2)}) collective-permute-start(f32[64,768]{1,0:T(8,128)S(1)} %get-tuple-element.86), channel_id=1, source_target_pairs={{0,1},{1,0},{2,3},{3,2},{4,5},{5,4},{6,7},{7,6},{8,9},{9,8},{10,11... | collective-permute-start | bytes 589832 | tf_op jit(solution)/shard_map/ppermute | solution.py:399
  69.0 0.7 collective-permute-start.10
  69.7 1.3 collective-permute-start.16
  71.1 0.8 collective-permute-start.13
  71.9 0.7 collective-permute-start.18
  72.6 5.5 %collective-permute-done.16.refs_6_.refs_1_ = f32[64,768]{1,0:T(8,128)S(1)} collective-permute-done((f32[64,768]{1,0:T(8,128)S(1)}, f32[64,768]{1,0:T(8,128)S(1)}, u32[]{:S(2)}, u32[]{:S(2)}) %collective-permute-start.16) | collective-permute-done | bytes 196640 | tf_op jit(solution)/shard_map/ppermute | solution.py:399
  78.1 3.1 %collective-permute-start.7 = (f32[2,3,64,768]{3,2,1,0:T(8,128)S(1)}, f32[2,3,64,768]{3,2,1,0:T(8,128)S(1)}, u32[]{:S(2)}, u32[]{:S(2)}) collective-permute-start(f32[2,3,64,768]{3,2,1,0:T(8,128)S(1)} %get-tuple-element.83), channel_id=1, source_target_pairs={{0,8},{4,12},{8,0},{12,4},{16,24},{20,28},{24,16},{28,20},{1,9},{5... | collective-permute-start | bytes 3538952 | tf_op jit(solution)/shard_map/ppermute | solution.py:414
  81.9 1.8 %collective-permute-start.19 = (f32[64,768]{1,0:T(8,128)S(1)}, f32[64,768]{1,0:T(8,128)S(1)}, u32[]{:S(2)}, u32[]{:S(2)}) collective-permute-start(f32[64,768]{1,0:T(8,128)S(1)} %get-tuple-element.98), channel_id=1, source_target_pairs={{0,1},{1,0},{2,3},{3,2},{4,5},{5,4},{6,7},{7,6},{8,9},{9,8},{10,11... | collective-permute-start | bytes 589832 | tf_op jit(solution)/shard_map/ppermute | solution.py:399
  84.5 2.3 %collective-permute-start.17 = (f32[64,768]{1,0:T(8,128)S(1)}, f32[64,768]{1,0:T(8,128)S(1)}, u32[]{:S(2)}, u32[]{:S(2)}) collective-permute-start(f32[64,768]{1,0:T(8,128)S(1)} %get-tuple-element.96), channel_id=1, source_target_pairs={{0,1},{1,0},{2,3},{3,2},{4,5},{5,4},{6,7},{7,6},{8,9},{9,8},{10,11... | collective-permute-start | bytes 589832 | tf_op jit(solution)/shard_map/ppermute | solution.py:399
  86.8 1.7 %collective-permute-done.19.refs_6_.refs_1_ = f32[64,768]{1,0:T(8,128)S(1)} collective-permute-done((f32[64,768]{1,0:T(8,128)S(1)}, f32[64,768]{1,0:T(8,128)S(1)}, u32[]{:S(2)}, u32[]{:S(2)}) %collective-permute-start.19) | collective-permute-done | bytes 196640 | tf_op jit(solution)/shard_map/ppermute | solution.py:399
  89.3 4.8 %collective-permute-start.24 = (f32[64,768]{1,0:T(8,128)S(1)}, f32[64,768]{1,0:T(8,128)S(1)}, u32[]{:S(2)}, u32[]{:S(2)}) collective-permute-start(f32[64,768]{1,0:T(8,128)S(1)} %get-tuple-element.107), channel_id=1, source_target_pairs={{0,1},{1,0},{2,3},{3,2},{4,5},{5,4},{6,7},{7,6},{8,9},{9,8},{10,11... | collective-permute-start | bytes 589832 | tf_op jit(solution)/shard_map/ppermute | solution.py:399
  94.8 3.8 %collective-permute-start.22 = (f32[64,768]{1,0:T(8,128)S(1)}, f32[64,768]{1,0:T(8,128)S(1)}, u32[]{:S(2)}, u32[]{:S(2)}) collective-permute-start(f32[64,768]{1,0:T(8,128)S(1)} %get-tuple-element.105), channel_id=1, source_target_pairs={{0,1},{1,0},{2,3},{3,2},{4,5},{5,4},{6,7},{7,6},{8,9},{9,8},{10,11... | collective-permute-start | bytes 589832 | tf_op jit(solution)/shard_map/ppermute | solution.py:399
  99.6 3.8 %collective-permute-start.29 = (f32[64,768]{1,0:T(8,128)S(1)}, f32[64,768]{1,0:T(8,128)S(1)}, u32[]{:S(2)}, u32[]{:S(2)}) collective-permute-start(f32[64,768]{1,0:T(8,128)S(1)} %get-tuple-element.119), channel_id=1, source_target_pairs={{0,1},{1,0},{2,3},{3,2},{4,5},{5,4},{6,7},{7,6},{8,9},{9,8},{10,11... | collective-permute-start | bytes 589832 | tf_op jit(solution)/shard_map/ppermute | solution.py:399
  103.4 0.7 collective-permute-start.31
  104.6 3.7 %collective-permute-start.27 = (f32[64,768]{1,0:T(8,128)S(1)}, f32[64,768]{1,0:T(8,128)S(1)}, u32[]{:S(2)}, u32[]{:S(2)}) collective-permute-start(f32[64,768]{1,0:T(8,128)S(1)} %get-tuple-element.117), channel_id=1, source_target_pairs={{0,1},{1,0},{2,3},{3,2},{4,5},{5,4},{6,7},{7,6},{8,9},{9,8},{10,11... | collective-permute-start | bytes 589832 | tf_op jit(solution)/shard_map/ppermute | solution.py:399
  109.4 2.0 %collective-permute-start.34 = (f32[64,768]{1,0:T(8,128)S(1)}, f32[64,768]{1,0:T(8,128)S(1)}, u32[]{:S(2)}, u32[]{:S(2)}) collective-permute-start(f32[64,768]{1,0:T(8,128)S(1)} %get-tuple-element.126), channel_id=1, source_target_pairs={{0,1},{1,0},{2,3},{3,2},{4,5},{5,4},{6,7},{7,6},{8,9},{9,8},{10,11... | collective-permute-start | bytes 589832 | tf_op jit(solution)/shard_map/ppermute | solution.py:399
  112.0 1.9 %collective-permute-done.27.refs_5_.refs_1_ = f32[64,768]{1,0:T(8,128)S(1)} collective-permute-done((f32[64,768]{1,0:T(8,128)S(1)}, f32[64,768]{1,0:T(8,128)S(1)}, u32[]{:S(2)}, u32[]{:S(2)}) %collective-permute-start.27) | collective-permute-done | bytes 196640 | tf_op jit(solution)/shard_map/ppermute | solution.py:399
  114.0 1.7 %collective-permute-start.32 = (f32[64,768]{1,0:T(8,128)S(1)}, f32[64,768]{1,0:T(8,128)S(1)}, u32[]{:S(2)}, u32[]{:S(2)}) collective-permute-start(f32[64,768]{1,0:T(8,128)S(1)} %get-tuple-element.124.refs_4_), channel_id=1, source_target_pairs={{0,1},{1,0},{2,3},{3,2},{4,5},{5,4},{6,7},{7,6},{8,9},{9,8},{10,11... | collective-permute-start | bytes 589832 | tf_op jit(solution)/shard_map/ppermute | solution.py:399
  116.3 3.7 %collective-permute-start.25 = (f32[1,3,64,768]{3,2,1,0:T(8,128)S(1)}, f32[1,3,64,768]{3,2,1,0:T(8,128)S(1)}, u32[]{:S(2)}, u32[]{:S(2)}) collective-permute-start(f32[1,3,64,768]{3,2,1,0:T(8,128)S(1)} %get-tuple-element.114), channel_id=1, source_target_pairs={{0,16},{4,20},{8,24},{12,28},{16,0},{20,4},{24,8},{28,12},{1,17},{... | collective-permute-start | bytes 1769480 | tf_op jit(solution)/shard_map/ppermute | solution.py:414
  120.1 1.4 collective-permute-start.26
  121.6 1.9 %collective-permute-start.36 = (f32[64,768]{1,0:T(8,128)S(1)}, f32[64,768]{1,0:T(8,128)S(1)}, u32[]{:S(2)}, u32[]{:S(2)}) collective-permute-start(f32[64,768]{1,0:T(8,128)S(1)} %get-tuple-element.132.refs_4_), channel_id=1, source_target_pairs={{0,1},{1,0},{2,3},{3,2},{4,5},{5,4},{6,7},{7,6},{8,9},{9,8},{10,11... | collective-permute-start | bytes 589832 | tf_op jit(solution)/shard_map/ppermute | solution.py:399
  124.2 3.7 %collective-permute-done.25.refs_1_ = f32[1,3,64,768]{3,2,1,0:T(8,128)S(1)} collective-permute-done((f32[1,3,64,768]{3,2,1,0:T(8,128)S(1)}, f32[1,3,64,768]{3,2,1,0:T(8,128)S(1)}, u32[]{:S(2)}, u32[]{:S(2)}) %collective-permute-start.25) | collective-permute-done | bytes 589856 | tf_op jit(solution)/shard_map/ppermute | solution.py:414
  128.0 2.3 %collective-permute-start.39 = (f32[64,768]{1,0:T(8,128)S(1)}, f32[64,768]{1,0:T(8,128)S(1)}, u32[]{:S(2)}, u32[]{:S(2)}) collective-permute-start(f32[64,768]{1,0:T(8,128)S(1)} %get-tuple-element.135.refs_2_), channel_id=1, source_target_pairs={{0,1},{1,0},{2,3},{3,2},{4,5},{5,4},{6,7},{7,6},{8,9},{9,8},{10,11... | collective-permute-start | bytes 589832 | tf_op jit(solution)/shard_map/ppermute | solution.py:399
  131.1 1.0 copy.39
  132.2 4.3 %collective-permute-start.42 = (f32[64,768]{1,0:T(8,128)S(1)}, f32[64,768]{1,0:T(8,128)S(1)}, u32[]{:S(2)}, u32[]{:S(2)}) collective-permute-start(f32[64,768]{1,0:T(8,128)S(1)} %get-tuple-element.138.refs_2_), channel_id=1, source_target_pairs={{0,1},{1,0},{2,3},{3,2},{4,5},{5,4},{6,7},{7,6},{8,9},{9,8},{10,11... | collective-permute-start | bytes 589832 | tf_op jit(solution)/shard_map/ppermute | solution.py:399
  137.2 2.3 %collective-permute-start.40 = (f32[64,768]{1,0:T(8,128)S(1)}, f32[64,768]{1,0:T(8,128)S(1)}, u32[]{:S(2)}, u32[]{:S(2)}) collective-permute-start(f32[64,768]{1,0:T(8,128)S(1)} %get-tuple-element.137.refs_5_.refs_2_), channel_id=1, source_target_pairs={{0,1},{1,0},{2,3},{3,2},{4,5},{5,4},{6,7},{7,6},{8,9},{9,8},{10,11... | collective-permute-start | bytes 589832 | tf_op jit(solution)/shard_map/ppermute | solution.py:399
  139.6 1.9 %collective-permute-done.42.refs_3_ = f32[64,768]{1,0:T(8,128)S(1)} collective-permute-done((f32[64,768]{1,0:T(8,128)S(1)}, f32[64,768]{1,0:T(8,128)S(1)}, u32[]{:S(2)}, u32[]{:S(2)}) %collective-permute-start.42) | collective-permute-done | bytes 196640 | tf_op jit(solution)/shard_map/ppermute | solution.py:399
  141.6 1.8 %collective-permute-start.44 = (f32[64,768]{1,0:T(8,128)S(1)}, f32[64,768]{1,0:T(8,128)S(1)}, u32[]{:S(2)}, u32[]{:S(2)}) collective-permute-start(f32[64,768]{1,0:T(8,128)S(1)} %get-tuple-element.141.refs_5_.refs_0_), channel_id=1, source_target_pairs={{0,1},{1,0},{2,3},{3,2},{4,5},{5,4},{6,7},{7,6},{8,9},{9,8},{10,11... | collective-permute-start | bytes 589832 | tf_op jit(solution)/shard_map/ppermute | solution.py:399
  143.7 1.8 %collective-permute-start.43 = (f32[64,768]{1,0:T(8,128)S(1)}, f32[64,768]{1,0:T(8,128)S(1)}, u32[]{:S(2)}, u32[]{:S(2)}) collective-permute-start(f32[64,768]{1,0:T(8,128)S(1)} %get-tuple-element.142.refs_3_.refs_0_), channel_id=1, source_target_pairs={{0,1},{1,0},{2,3},{3,2},{4,5},{5,4},{6,7},{7,6},{8,9},{9,8},{10,11... | collective-permute-start | bytes 589832 | tf_op jit(solution)/shard_map/ppermute | solution.py:399
  145.5 1.8 %collective-permute-done.44.refs_1_ = f32[64,768]{1,0:T(8,128)S(1)} collective-permute-done((f32[64,768]{1,0:T(8,128)S(1)}, f32[64,768]{1,0:T(8,128)S(1)}, u32[]{:S(2)}, u32[]{:S(2)}) %collective-permute-start.44) | collective-permute-done | bytes 196640 | tf_op jit(solution)/shard_map/ppermute | solution.py:399
  147.5 1.9 %collective-permute-done.43.refs_1_ = f32[64,768]{1,0:T(8,128)S(1)} collective-permute-done((f32[64,768]{1,0:T(8,128)S(1)}, f32[64,768]{1,0:T(8,128)S(1)}, u32[]{:S(2)}, u32[]{:S(2)}) %collective-permute-start.43) | collective-permute-done | bytes 196640 | tf_op jit(solution)/shard_map/ppermute | solution.py:399
  149.4 1.7 %copy.40 = f32[1024,768]{1,0:T(8,128)} copy(f32[1024,768]{1,0:T(8,128)S(1)} %line_slot.41) | data formatting | bytes 6291456
  (84 shorter events, 12.7 us)
Async XLA Ops:
  2.7 0.7 copy-start.1
  17.8 1.2 collective-permute-start
  19.1 5.3 %collective-permute-start.3 = (f32[24,128]{1,0:T(8,128)S(1)}, f32[24,128]{1,0:T(8,128)S(1)}, u32[]{:S(2)}, u32[]{:S(2)}) collective-permute-start(f32[24,128]{1,0:T(8,128)S(1)} %merge_lse.2.refs_0_), channel_id=1, source_target_pairs={{0,24},{4,28},{8,16},{12,20},{16,8},{20,12},{24,0},{28,4},{1,25},{... | collective-permute-start | bytes 36872 | tf_op jit(solution)/shard_map/ppermute | solution.py:321
  22.6 3.7 %collective-permute-start.2 = (f32[24,128]{1,0:T(8,128)S(1)}, f32[24,128]{1,0:T(8,128)S(1)}, u32[]{:S(2)}, u32[]{:S(2)}) collective-permute-start(f32[24,128]{1,0:T(8,128)S(1)} %merge_lse.2.refs_0_), channel_id=1, source_target_pairs={{0,16},{4,20},{8,24},{12,28},{16,0},{20,4},{24,8},{28,12},{1,17},{... | collective-permute-start | bytes 36872 | tf_op jit(solution)/shard_map/ppermute | solution.py:321
  23.0 3.7 %collective-permute-start.1 = (f32[24,128]{1,0:T(8,128)S(1)}, f32[24,128]{1,0:T(8,128)S(1)}, u32[]{:S(2)}, u32[]{:S(2)}) collective-permute-start(f32[24,128]{1,0:T(8,128)S(1)} %merge_lse.2.refs_0_), channel_id=1, source_target_pairs={{0,8},{4,12},{8,0},{12,4},{16,24},{20,28},{24,16},{28,20},{1,9},{5... | collective-permute-start | bytes 36872 | tf_op jit(solution)/shard_map/ppermute | solution.py:321
  29.2 9.2 %copy-start = (s32[3,1024]{1,0:T(4,128)S(1)}, s32[3,1024]{1,0:T(4,128)}, u32[]{:S(2)}) copy-start(s32[3,1024]{1,0:T(4,128)} %pos_ref.1) | copy-start | bytes 36868
  29.2 23.6 %collective-permute-start.4 = (f32[256,768]{1,0:T(8,128)S(1)}, f32[256,768]{1,0:T(8,128)S(1)}, u32[]{:S(2)}, u32[]{:S(2)}) collective-permute-start(f32[256,768]{1,0:T(8,128)S(1)} %cache_grad.2.dep.refs_0_), channel_id=1, source_target_pairs={{0,1},{1,0},{2,3},{3,2},{4,5},{5,4},{6,7},{7,6},{8,9},{9,8},{10,11... | collective-permute-start | bytes 2359304 | tf_op jit(solution)/shard_map/ppermute | solution.py:336
  53.3 8.0 %collective-permute-start.5 = (f32[4,3,128,768]{3,2,1,0:T(8,128)S(1)}, f32[4,3,128,768]{3,2,1,0:T(8,128)S(1)}, u32[]{:S(2)}, u32[]{:S(2)}) collective-permute-start(f32[4,3,128,768]{3,2,1,0:T(8,128)S(1)} %home_start.1), channel_id=1, source_target_pairs={{0,4},{4,0},{8,12},{12,8},{16,20},{20,16},{24,28},{28,24},{1,5},{5... | collective-permute-start | bytes 14155784 | tf_op jit(solution)/shard_map/ppermute | solution.py:414
  53.3 6.3 %collective-permute-start.6 = (f32[64,768]{1,0:T(8,128)S(1)}, f32[64,768]{1,0:T(8,128)S(1)}, u32[]{:S(2)}, u32[]{:S(2)}) collective-permute-start(f32[64,768]{1,0:T(8,128)S(1)} %get-tuple-element.78.dep.refs_3_.refs_2_), channel_id=1, source_target_pairs={{1,2},{2,1},{5,6},{6,5},{9,10},{10,9},{13,14},{14,13},{17,18},{18,... | collective-permute-start | bytes 589832 | tf_op jit(solution)/shard_map/ppermute | solution.py:401
  54.0 15.0 %collective-permute-start.11 = (f32[64,768]{1,0:T(8,128)S(1)}, f32[64,768]{1,0:T(8,128)S(1)}, u32[]{:S(2)}, u32[]{:S(2)}) collective-permute-start(f32[64,768]{1,0:T(8,128)S(1)} %get-tuple-element.87), channel_id=1, source_target_pairs={{0,1},{1,0},{2,3},{3,2},{4,5},{5,4},{6,7},{7,6},{8,9},{9,8},{10,11... | collective-permute-start | bytes 589832 | tf_op jit(solution)/shard_map/ppermute | solution.py:399
  58.8 12.3 %collective-permute-start.14 = (f32[64,768]{1,0:T(8,128)S(1)}, f32[64,768]{1,0:T(8,128)S(1)}, u32[]{:S(2)}, u32[]{:S(2)}) collective-permute-start(f32[64,768]{1,0:T(8,128)S(1)} %get-tuple-element.90), channel_id=1, source_target_pairs={{0,1},{1,0},{2,3},{3,2},{4,5},{5,4},{6,7},{7,6},{8,9},{9,8},{10,11... | collective-permute-start | bytes 589832 | tf_op jit(solution)/shard_map/ppermute | solution.py:399
  58.9 10.8 %collective-permute-start.12 = (f32[64,768]{1,0:T(8,128)S(1)}, f32[64,768]{1,0:T(8,128)S(1)}, u32[]{:S(2)}, u32[]{:S(2)}) collective-permute-start(f32[64,768]{1,0:T(8,128)S(1)} %get-tuple-element.79.refs_3_.refs_2_), channel_id=1, source_target_pairs={{1,2},{2,1},{5,6},{6,5},{9,10},{10,9},{13,14},{14,13},{17,18},{18,... | collective-permute-start | bytes 589832 | tf_op jit(solution)/shard_map/ppermute | solution.py:401
  59.6 12.3 %collective-permute-start.15 = (f32[64,768]{1,0:T(8,128)S(1)}, f32[64,768]{1,0:T(8,128)S(1)}, u32[]{:S(2)}, u32[]{:S(2)}) collective-permute-start(f32[64,768]{1,0:T(8,128)S(1)} %get-tuple-element.80.refs_5_.refs_2_), channel_id=1, source_target_pairs={{1,2},{2,1},{5,6},{6,5},{9,10},{10,9},{13,14},{14,13},{17,18},{18,... | collective-permute-start | bytes 589832 | tf_op jit(solution)/shard_map/ppermute | solution.py:401
  61.2 20.0 %collective-permute-start.9 = (f32[64,768]{1,0:T(8,128)S(1)}, f32[64,768]{1,0:T(8,128)S(1)}, u32[]{:S(2)}, u32[]{:S(2)}) collective-permute-start(f32[64,768]{1,0:T(8,128)S(1)} %get-tuple-element.86), channel_id=1, source_target_pairs={{0,1},{1,0},{2,3},{3,2},{4,5},{5,4},{6,7},{7,6},{8,9},{9,8},{10,11... | collective-permute-start | bytes 589832 | tf_op jit(solution)/shard_map/ppermute | solution.py:399
  69.0 12.9 %collective-permute-start.10 = (f32[64,768]{1,0:T(8,128)S(1)}, f32[64,768]{1,0:T(8,128)S(1)}, u32[]{:S(2)}, u32[]{:S(2)}) collective-permute-start(f32[64,768]{1,0:T(8,128)S(1)} %get-tuple-element.81.refs_2_.refs_5_), channel_id=1, source_target_pairs={{1,2},{2,1},{5,6},{6,5},{9,10},{10,9},{13,14},{14,13},{17,18},{18,... | collective-permute-start | bytes 589832 | tf_op jit(solution)/shard_map/ppermute | solution.py:401
  69.7 8.4 %collective-permute-start.16 = (f32[64,768]{1,0:T(8,128)S(1)}, f32[64,768]{1,0:T(8,128)S(1)}, u32[]{:S(2)}, u32[]{:S(2)}) collective-permute-start(f32[64,768]{1,0:T(8,128)S(1)} %get-tuple-element.92), channel_id=1, source_target_pairs={{0,1},{1,0},{2,3},{3,2},{4,5},{5,4},{6,7},{7,6},{8,9},{9,8},{10,11... | collective-permute-start | bytes 589832 | tf_op jit(solution)/shard_map/ppermute | solution.py:399
  71.1 12.6 %collective-permute-start.13 = (f32[64,768]{1,0:T(8,128)S(1)}, f32[64,768]{1,0:T(8,128)S(1)}, u32[]{:S(2)}, u32[]{:S(2)}) collective-permute-start(f32[64,768]{1,0:T(8,128)S(1)} %get-tuple-element.89), channel_id=1, source_target_pairs={{0,1},{1,0},{2,3},{3,2},{4,5},{5,4},{6,7},{7,6},{8,9},{9,8},{10,11... | collective-permute-start | bytes 589832 | tf_op jit(solution)/shard_map/ppermute | solution.py:399
  71.9 12.6 %collective-permute-start.18 = (f32[64,768]{1,0:T(8,128)S(1)}, f32[64,768]{1,0:T(8,128)S(1)}, u32[]{:S(2)}, u32[]{:S(2)}) collective-permute-start(f32[64,768]{1,0:T(8,128)S(1)} %get-tuple-element.93.refs_7_.refs_2_), channel_id=1, source_target_pairs={{1,2},{2,1},{5,6},{6,5},{9,10},{10,9},{13,14},{14,13},{17,18},{18,... | collective-permute-start | bytes 589832 | tf_op jit(solution)/shard_map/ppermute | solution.py:401
  78.1 26.5 %collective-permute-start.7 = (f32[2,3,64,768]{3,2,1,0:T(8,128)S(1)}, f32[2,3,64,768]{3,2,1,0:T(8,128)S(1)}, u32[]{:S(2)}, u32[]{:S(2)}) collective-permute-start(f32[2,3,64,768]{3,2,1,0:T(8,128)S(1)} %get-tuple-element.83), channel_id=1, source_target_pairs={{0,8},{4,12},{8,0},{12,4},{16,24},{20,28},{24,16},{28,20},{1,9},{5... | collective-permute-start | bytes 3538952 | tf_op jit(solution)/shard_map/ppermute | solution.py:414
  81.3 27.0 %collective-permute-start.8 = (f32[2,3,64,768]{3,2,1,0:T(8,128)S(1)}, f32[2,3,64,768]{3,2,1,0:T(8,128)S(1)}, u32[]{:S(2)}, u32[]{:S(2)}) collective-permute-start(f32[2,3,64,768]{3,2,1,0:T(8,128)S(1)} %get-tuple-element.85), channel_id=1, source_target_pairs={{0,16},{4,20},{8,24},{12,28},{16,0},{20,4},{24,8},{28,12},{1,17},{... | collective-permute-start | bytes 3538952 | tf_op jit(solution)/shard_map/ppermute | solution.py:414
  81.9 6.6 %collective-permute-start.19 = (f32[64,768]{1,0:T(8,128)S(1)}, f32[64,768]{1,0:T(8,128)S(1)}, u32[]{:S(2)}, u32[]{:S(2)}) collective-permute-start(f32[64,768]{1,0:T(8,128)S(1)} %get-tuple-element.98), channel_id=1, source_target_pairs={{0,1},{1,0},{2,3},{3,2},{4,5},{5,4},{6,7},{7,6},{8,9},{9,8},{10,11... | collective-permute-start | bytes 589832 | tf_op jit(solution)/shard_map/ppermute | solution.py:399
  83.7 5.5 %collective-permute-start.21 = (f32[64,768]{1,0:T(8,128)S(1)}, f32[64,768]{1,0:T(8,128)S(1)}, u32[]{:S(2)}, u32[]{:S(2)}) collective-permute-start(f32[64,768]{1,0:T(8,128)S(1)} %get-tuple-element.95.refs_8_.refs_2_), channel_id=1, source_target_pairs={{1,2},{2,1},{5,6},{6,5},{9,10},{10,9},{13,14},{14,13},{17,18},{18,... | collective-permute-start | bytes 589832 | tf_op jit(solution)/shard_map/ppermute | solution.py:401
  84.5 9.6 %collective-permute-start.17 = (f32[64,768]{1,0:T(8,128)S(1)}, f32[64,768]{1,0:T(8,128)S(1)}, u32[]{:S(2)}, u32[]{:S(2)}) collective-permute-start(f32[64,768]{1,0:T(8,128)S(1)} %get-tuple-element.96), channel_id=1, source_target_pairs={{0,1},{1,0},{2,3},{3,2},{4,5},{5,4},{6,7},{7,6},{8,9},{9,8},{10,11... | collective-permute-start | bytes 589832 | tf_op jit(solution)/shard_map/ppermute | solution.py:399
  88.5 6.3 %collective-permute-start.23 = (f32[64,768]{1,0:T(8,128)S(1)}, f32[64,768]{1,0:T(8,128)S(1)}, u32[]{:S(2)}, u32[]{:S(2)}) collective-permute-start(f32[64,768]{1,0:T(8,128)S(1)} %get-tuple-element.100.refs_8_.refs_2_), channel_id=1, source_target_pairs={{1,2},{2,1},{5,6},{6,5},{9,10},{10,9},{13,14},{14,13},{17,18},{18,... | collective-permute-start | bytes 589832 | tf_op jit(solution)/shard_map/ppermute | solution.py:401
  89.3 9.5 %collective-permute-start.24 = (f32[64,768]{1,0:T(8,128)S(1)}, f32[64,768]{1,0:T(8,128)S(1)}, u32[]{:S(2)}, u32[]{:S(2)}) collective-permute-start(f32[64,768]{1,0:T(8,128)S(1)} %get-tuple-element.107), channel_id=1, source_target_pairs={{0,1},{1,0},{2,3},{3,2},{4,5},{5,4},{6,7},{7,6},{8,9},{9,8},{10,11... | collective-permute-start | bytes 589832 | tf_op jit(solution)/shard_map/ppermute | solution.py:399
  94.1 5.5 %collective-permute-start.20 = (f32[64,768]{1,0:T(8,128)S(1)}, f32[64,768]{1,0:T(8,128)S(1)}, u32[]{:S(2)}, u32[]{:S(2)}) collective-permute-start(f32[64,768]{1,0:T(8,128)S(1)} %get-tuple-element.101.refs_8_.refs_2_), channel_id=1, source_target_pairs={{1,2},{2,1},{5,6},{6,5},{9,10},{10,9},{13,14},{14,13},{17,18},{18,... | collective-permute-start | bytes 589832 | tf_op jit(solution)/shard_map/ppermute | solution.py:401
  94.8 8.5 %collective-permute-start.22 = (f32[64,768]{1,0:T(8,128)S(1)}, f32[64,768]{1,0:T(8,128)S(1)}, u32[]{:S(2)}, u32[]{:S(2)}) collective-permute-start(f32[64,768]{1,0:T(8,128)S(1)} %get-tuple-element.105), channel_id=1, source_target_pairs={{0,1},{1,0},{2,3},{3,2},{4,5},{5,4},{6,7},{7,6},{8,9},{9,8},{10,11... | collective-permute-start | bytes 589832 | tf_op jit(solution)/shard_map/ppermute | solution.py:399
  98.8 10.5 %collective-permute-start.28 = (f32[64,768]{1,0:T(8,128)S(1)}, f32[64,768]{1,0:T(8,128)S(1)}, u32[]{:S(2)}, u32[]{:S(2)}) collective-permute-start(f32[64,768]{1,0:T(8,128)S(1)} %get-tuple-element.109.refs_8_.refs_2_), channel_id=1, source_target_pairs={{1,2},{2,1},{5,6},{6,5},{9,10},{10,9},{13,14},{14,13},{17,18},{18,... | collective-permute-start | bytes 589832 | tf_op jit(solution)/shard_map/ppermute | solution.py:401
  99.6 9.7 %collective-permute-start.29 = (f32[64,768]{1,0:T(8,128)S(1)}, f32[64,768]{1,0:T(8,128)S(1)}, u32[]{:S(2)}, u32[]{:S(2)}) collective-permute-start(f32[64,768]{1,0:T(8,128)S(1)} %get-tuple-element.119), channel_id=1, source_target_pairs={{0,1},{1,0},{2,3},{3,2},{4,5},{5,4},{6,7},{7,6},{8,9},{9,8},{10,11... | collective-permute-start | bytes 589832 | tf_op jit(solution)/shard_map/ppermute | solution.py:399
  103.4 8.7 %collective-permute-start.31 = (f32[64,768]{1,0:T(8,128)S(1)}, f32[64,768]{1,0:T(8,128)S(1)}, u32[]{:S(2)}, u32[]{:S(2)}) collective-permute-start(f32[64,768]{1,0:T(8,128)S(1)} %get-tuple-element.111.refs_8_.refs_2_), channel_id=1, source_target_pairs={{1,2},{2,1},{5,6},{6,5},{9,10},{10,9},{13,14},{14,13},{17,18},{18,... | collective-permute-start | bytes 589832 | tf_op jit(solution)/shard_map/ppermute | solution.py:401
  104.6 9.3 %collective-permute-start.27 = (f32[64,768]{1,0:T(8,128)S(1)}, f32[64,768]{1,0:T(8,128)S(1)}, u32[]{:S(2)}, u32[]{:S(2)}) collective-permute-start(f32[64,768]{1,0:T(8,128)S(1)} %get-tuple-element.117), channel_id=1, source_target_pairs={{0,1},{1,0},{2,3},{3,2},{4,5},{5,4},{6,7},{7,6},{8,9},{9,8},{10,11... | collective-permute-start | bytes 589832 | tf_op jit(solution)/shard_map/ppermute | solution.py:399
  108.3 8.0 %collective-permute-start.33 = (f32[64,768]{1,0:T(8,128)S(1)}, f32[64,768]{1,0:T(8,128)S(1)}, u32[]{:S(2)}, u32[]{:S(2)}) collective-permute-start(f32[64,768]{1,0:T(8,128)S(1)} %get-tuple-element.112.refs_4_.refs_8_.refs_2_), channel_id=1, source_target_pairs={{1,2},{2,1},{5,6},{6,5},{9,10},{10,9},{13,14},{14,13},{17,18},{18,... | collective-permute-start | bytes 589832 | tf_op jit(solution)/shard_map/ppermute | solution.py:401
  109.4 10.7 %collective-permute-start.34 = (f32[64,768]{1,0:T(8,128)S(1)}, f32[64,768]{1,0:T(8,128)S(1)}, u32[]{:S(2)}, u32[]{:S(2)}) collective-permute-start(f32[64,768]{1,0:T(8,128)S(1)} %get-tuple-element.126), channel_id=1, source_target_pairs={{0,1},{1,0},{2,3},{3,2},{4,5},{5,4},{6,7},{7,6},{8,9},{9,8},{10,11... | collective-permute-start | bytes 589832 | tf_op jit(solution)/shard_map/ppermute | solution.py:399
  111.4 10.2 %collective-permute-start.30 = (f32[64,768]{1,0:T(8,128)S(1)}, f32[64,768]{1,0:T(8,128)S(1)}, u32[]{:S(2)}, u32[]{:S(2)}) collective-permute-start(f32[64,768]{1,0:T(8,128)S(1)} %get-tuple-element.121.refs_7_.refs_2_), channel_id=1, source_target_pairs={{1,2},{2,1},{5,6},{6,5},{9,10},{10,9},{13,14},{14,13},{17,18},{18,... | collective-permute-start | bytes 589832 | tf_op jit(solution)/shard_map/ppermute | solution.py:401
  114.0 9.5 %collective-permute-start.32 = (f32[64,768]{1,0:T(8,128)S(1)}, f32[64,768]{1,0:T(8,128)S(1)}, u32[]{:S(2)}, u32[]{:S(2)}) collective-permute-start(f32[64,768]{1,0:T(8,128)S(1)} %get-tuple-element.124.refs_4_), channel_id=1, source_target_pairs={{0,1},{1,0},{2,3},{3,2},{4,5},{5,4},{6,7},{7,6},{8,9},{9,8},{10,11... | collective-permute-start | bytes 589832 | tf_op jit(solution)/shard_map/ppermute | solution.py:399
  115.7 16.4 %collective-permute-start.35 = (f32[64,768]{1,0:T(8,128)S(1)}, f32[64,768]{1,0:T(8,128)S(1)}, u32[]{:S(2)}, u32[]{:S(2)}) collective-permute-start(f32[64,768]{1,0:T(8,128)S(1)} %get-tuple-element.128.refs_7_.refs_2_), channel_id=1, source_target_pairs={{1,2},{2,1},{5,6},{6,5},{9,10},{10,9},{13,14},{14,13},{17,18},{18,... | collective-permute-start | bytes 589832 | tf_op jit(solution)/shard_map/ppermute | solution.py:401
  116.3 11.6 %collective-permute-start.25 = (f32[1,3,64,768]{3,2,1,0:T(8,128)S(1)}, f32[1,3,64,768]{3,2,1,0:T(8,128)S(1)}, u32[]{:S(2)}, u32[]{:S(2)}) collective-permute-start(f32[1,3,64,768]{3,2,1,0:T(8,128)S(1)} %get-tuple-element.114), channel_id=1, source_target_pairs={{0,16},{4,20},{8,24},{12,28},{16,0},{20,4},{24,8},{28,12},{1,17},{... | collective-permute-start | bytes 1769480 | tf_op jit(solution)/shard_map/ppermute | solution.py:414
  120.1 10.1 %collective-permute-start.26 = (f32[1,3,64,768]{3,2,1,0:T(8,128)S(1)}, f32[1,3,64,768]{3,2,1,0:T(8,128)S(1)}, u32[]{:S(2)}, u32[]{:S(2)}) collective-permute-start(f32[1,3,64,768]{3,2,1,0:T(8,128)S(1)} %get-tuple-element.116), channel_id=1, source_target_pairs={{0,8},{4,12},{8,0},{12,4},{16,24},{20,28},{24,16},{28,20},{1,9},{5... | collective-permute-start | bytes 1769480 | tf_op jit(solution)/shard_map/ppermute | solution.py:414
  121.6 10.5 %collective-permute-start.36 = (f32[64,768]{1,0:T(8,128)S(1)}, f32[64,768]{1,0:T(8,128)S(1)}, u32[]{:S(2)}, u32[]{:S(2)}) collective-permute-start(f32[64,768]{1,0:T(8,128)S(1)} %get-tuple-element.132.refs_4_), channel_id=1, source_target_pairs={{0,1},{1,0},{2,3},{3,2},{4,5},{5,4},{6,7},{7,6},{8,9},{9,8},{10,11... | collective-permute-start | bytes 589832 | tf_op jit(solution)/shard_map/ppermute | solution.py:399
  123.5 13.7 %collective-permute-start.38 = (f32[64,768]{1,0:T(8,128)S(1)}, f32[64,768]{1,0:T(8,128)S(1)}, u32[]{:S(2)}, u32[]{:S(2)}) collective-permute-start(f32[64,768]{1,0:T(8,128)S(1)} %get-tuple-element.130.refs_7_.refs_0_), channel_id=1, source_target_pairs={{1,2},{2,1},{5,6},{6,5},{9,10},{10,9},{13,14},{14,13},{17,18},{18,... | collective-permute-start | bytes 589832 | tf_op jit(solution)/shard_map/ppermute | solution.py:401
  128.0 9.2 %collective-permute-start.39 = (f32[64,768]{1,0:T(8,128)S(1)}, f32[64,768]{1,0:T(8,128)S(1)}, u32[]{:S(2)}, u32[]{:S(2)}) collective-permute-start(f32[64,768]{1,0:T(8,128)S(1)} %get-tuple-element.135.refs_2_), channel_id=1, source_target_pairs={{0,1},{1,0},{2,3},{3,2},{4,5},{5,4},{6,7},{7,6},{8,9},{9,8},{10,11... | collective-permute-start | bytes 589832 | tf_op jit(solution)/shard_map/ppermute | solution.py:399
  130.2 9.3 %collective-permute-start.41 = (f32[64,768]{1,0:T(8,128)S(1)}, f32[64,768]{1,0:T(8,128)S(1)}, u32[]{:S(2)}, u32[]{:S(2)}) collective-permute-start(f32[64,768]{1,0:T(8,128)S(1)} %get-tuple-element.131.refs_4_.refs_7_.refs_0_), channel_id=1, source_target_pairs={{1,2},{2,1},{5,6},{6,5},{9,10},{10,9},{13,14},{14,13},{17,18},{18,... | collective-permute-start | bytes 589832 | tf_op jit(solution)/shard_map/ppermute | solution.py:401
  132.2 9.3 %collective-permute-start.42 = (f32[64,768]{1,0:T(8,128)S(1)}, f32[64,768]{1,0:T(8,128)S(1)}, u32[]{:S(2)}, u32[]{:S(2)}) collective-permute-start(f32[64,768]{1,0:T(8,128)S(1)} %get-tuple-element.138.refs_2_), channel_id=1, source_target_pairs={{0,1},{1,0},{2,3},{3,2},{4,5},{5,4},{6,7},{7,6},{8,9},{9,8},{10,11... | collective-permute-start | bytes 589832 | tf_op jit(solution)/shard_map/ppermute | solution.py:399
  136.5 7.1 %collective-permute-start.37 = (f32[64,768]{1,0:T(8,128)S(1)}, f32[64,768]{1,0:T(8,128)S(1)}, u32[]{:S(2)}, u32[]{:S(2)}) collective-permute-start(f32[64,768]{1,0:T(8,128)S(1)} %get-tuple-element.134.refs_5_.refs_0_), channel_id=1, source_target_pairs={{1,2},{2,1},{5,6},{6,5},{9,10},{10,9},{13,14},{14,13},{17,18},{18,... | collective-permute-start | bytes 589832 | tf_op jit(solution)/shard_map/ppermute | solution.py:401
  137.2 6.4 %collective-permute-start.40 = (f32[64,768]{1,0:T(8,128)S(1)}, f32[64,768]{1,0:T(8,128)S(1)}, u32[]{:S(2)}, u32[]{:S(2)}) collective-permute-start(f32[64,768]{1,0:T(8,128)S(1)} %get-tuple-element.137.refs_5_.refs_2_), channel_id=1, source_target_pairs={{0,1},{1,0},{2,3},{3,2},{4,5},{5,4},{6,7},{7,6},{8,9},{9,8},{10,11... | collective-permute-start | bytes 589832 | tf_op jit(solution)/shard_map/ppermute | solution.py:399
  141.6 5.7 %collective-permute-start.44 = (f32[64,768]{1,0:T(8,128)S(1)}, f32[64,768]{1,0:T(8,128)S(1)}, u32[]{:S(2)}, u32[]{:S(2)}) collective-permute-start(f32[64,768]{1,0:T(8,128)S(1)} %get-tuple-element.141.refs_5_.refs_0_), channel_id=1, source_target_pairs={{0,1},{1,0},{2,3},{3,2},{4,5},{5,4},{6,7},{7,6},{8,9},{9,8},{10,11... | collective-permute-start | bytes 589832 | tf_op jit(solution)/shard_map/ppermute | solution.py:399
  143.7 5.7 %collective-permute-start.43 = (f32[64,768]{1,0:T(8,128)S(1)}, f32[64,768]{1,0:T(8,128)S(1)}, u32[]{:S(2)}, u32[]{:S(2)}) collective-permute-start(f32[64,768]{1,0:T(8,128)S(1)} %get-tuple-element.142.refs_3_.refs_0_), channel_id=1, source_target_pairs={{0,1},{1,0},{2,3},{3,2},{4,5},{5,4},{6,7},{7,6},{8,9},{9,8},{10,11... | collective-permute-start | bytes 589832 | tf_op jit(solution)/shard_map/ppermute | solution.py:399

commit v5 on v4

--- a/solution.py
+++ b/solution.py
@@ -10,11 +10,9 @@
 
 BLK = 128
 LOW = -1e30
-LAGS = (4, 3, 2)
-HOME_SLOTS = (7, 14, 18)
-START_SLOT = 4
-TERM_SLOTS = ()
-PARTS = 1 + len(TERM_SLOTS)
+LAGS = (4, 2, 2)
+HOME_SLOTS = (9, 17, 21)
+START_SLOT = 6
 SLOT_FLOPS = 4_000_000_000
 
 
@@ -164,8 +162,7 @@
     lax.fori_loop(0, out_ref.shape[0] // BLK, block, 0)
 
 
-def term_kernel(meta, spread, width, part, parts, member, owner, entries, z_ref, w_ref, lse_ref, pos_ref, dep, old, out_ref,
-                flags, rows_ref):
+def term_kernel(meta, spread, width, member, owner, entries, z_ref, w_ref, lse_ref, pos_ref, dep, out_ref, flags, rows_ref):
     meta.flags(owner, flags)
     me = lax.axis_index("cache")
     below = lax.broadcasted_iota(jnp.int32, (BLK, BLK), 0)
@@ -179,10 +176,8 @@
             out_ref[i, s] = jnp.zeros(out_ref.shape[2:], jnp.float32)
         return 0
 
-    if part == 0:
-        lax.fori_loop(0, meta.groups, clear, 0)
+    lax.fori_loop(0, meta.groups, clear, 0)
     n = entries[entries.shape[0] - 1]
-    trips = (n + width - 1) // width
 
     def step(it, _):
         found = []
@@ -215,7 +210,7 @@
                 out_ref[place, s] += acc[half * BLK:(half + 1) * BLK]
         return 0
 
-    lax.fori_loop(trips * part // parts, trips * (part + 1) // parts, step, 0)
+    lax.fori_loop(0, (n + width - 1) // width, step, 0)
 
 
 def params(mib):
@@ -277,19 +272,18 @@
     )(member, z, q, lse, dep)
 
 
-def run_terms(meta, member, owner, entries, z, w, lse, pos, spread, dep, part=0, parts=1, old=None):
+def run_terms(meta, member, owner, entries, z, w, lse, pos, spread, dep):
     group = 3
     return pl.pallas_call(
-        functools.partial(term_kernel, meta, spread, group, part, parts),
-        in_specs=[SMEM, SMEM, SMEM, VMEM, VMEM, VMEM, VMEM, ANY, VMEM if part else ANY],
-        input_output_aliases={8: 0} if part else {},
+        functools.partial(term_kernel, meta, spread, group),
+        in_specs=[SMEM, SMEM, SMEM, VMEM, VMEM, VMEM, VMEM, ANY],
         out_specs=VMEM,
         out_shape=pltpu.VMEM((meta.groups, meta.steps, BLK, w.shape[2]), jnp.float32),
         scratch_shapes=[pltpu.SMEM((2 * meta.steps,), jnp.int32), pltpu.VMEM((meta.rows, BLK), jnp.int32)],
         compiler_params=params(10),
         cost_estimate=free(),
         name="query_term",
-    )(member, owner, entries, z, w, lse, pos, dep, old if part else dep)
+    )(member, owner, entries, z, w, lse, pos, dep)
 
 
 def small(kernel, inputs, n_deps, outs, name, aliases=None, flops=0):
@@ -332,8 +326,22 @@
         self.swap, self.mid, self.inner, self.total = {}, {}, {}, {}
         self.out = None
 
-    def begin(self, array):
-        self.swap[0] = lax.ppermute(array, "batch", [(0, 1), (1, 0), (2, 3), (3, 2)])
+    def swapped(self, array):
+        return lax.ppermute(array, "batch", [(0, 1), (1, 0), (2, 3), (3, 2)])
+
+    def swapped_mid(self, array):
+        return lax.ppermute(array, "batch", [(1, 2), (2, 1)])
+
+    def begin(self, array, more):
+        self.swap_a, self.swap_b = self.swapped(array), self.swapped(more)
+
+    def early(self, array, dep):
+        def kernel(own, came, dep, out):
+            out[...] = own[...] + came[...]
+
+        self.inner_a = small(kernel, [array, self.swap_a, dep], 1, [array.shape], "line_early")[0]
+        self.mid_a = self.swapped_mid(self.inner_a)
+        return self.inner_a
 
     def slot(self, t, chunk, deps):
         n, rows = self.n, self.rows
@@ -351,10 +359,11 @@
         aliases = {}
         if 0 <= u < n:
             array, first = chunk(u)
-            came, row = (self.swap[0], u * rows) if u < self.lag_in else (self.swap[u], 0)
+            came, row = (self.swap_b, (u - self.lag_mid) * rows) if u < self.late else (self.swap[u], 0)
             plan.append(("in", take(array), first, take(came), row, give()))
         if 0 <= k < n:
-            plan.append(("sum", take(self.inner[k]), take(self.mid[k]), give()))
+            pair, row = ((self.inner_a, self.mid_a), k * rows) if k < self.lag_mid else ((self.inner[k], self.mid[k]), 0)
+            plan.append(("sum", take(pair[0]), take(pair[1]), row, give()))
         if t < n:
             array, first = chunk(t)
             plan.append(("away", take(array), first, give()))
@@ -376,8 +385,8 @@
                 if what == "in":
                     res[a[4]][...] = refs[a[0]][a[1]:a[1] + rows, :] + refs[a[2]][a[3]:a[3] + rows, :]
                 elif what == "sum":
-                    total = refs[a[0]][...] + refs[a[1]][...]
-                    res[a[2]][...] = total
+                    total = refs[a[0]][a[2]:a[2] + rows, :] + refs[a[1]][a[2]:a[2] + rows, :]
+                    res[a[3]][...] = total
                 elif what == "away":
                     value = refs[a[0]][a[1]:a[1] + rows, :]
                     res[a[2]][...] = value if total is None else jnp.where(end, value, total)
@@ -390,15 +399,15 @@
             if what == "in":
                 self.inner[u] = got[a[4]]
             elif what == "sum":
-                away = self.total[k] = got[a[2]]
+                away = self.total[k] = got[a[3]]
             elif what == "away":
                 away = got[a[2]]
             else:
                 self.out = got[a[2]]
         if away is not None:
-            self.swap[t] = lax.ppermute(away, "batch", [(0, 1), (1, 0), (2, 3), (3, 2)])
+            self.swap[t] = self.swapped(away)
         if 0 <= u < n:
-            self.mid[u] = lax.ppermute(self.inner[u], "batch", [(1, 2), (2, 1)])
+            self.mid[u] = self.swapped_mid(self.inner[u])
         return got[0]
 
 
@@ -495,37 +504,38 @@
     lse = exchange_lse(own_lse)
 
     half = BLK // 2
-    early = min(LAGS[0] * half // BLK, blocks)
-    grads = [run_grads(meta, member, z, q, lse, 0, early, lse)]
+    line = Line(2 * blocks, half, width)
+    parts = [line.lag_mid * half // BLK, line.lag_in * half // BLK]
+    parts.append(max(blocks - sum(parts), 0))
+    in_line = lax.axis_size("batch") == 4 and parts[2] > 0
+    if not in_line:
+        parts = [blocks]
+    grads, dep = [], lse
+    for i, part in enumerate(parts):
+        grads.append(run_grads(meta, member, z, q, lse, sum(parts[:i]), part, dep))
+        dep = grads[-1]
     owners = lax.axis_size("cache")
     share = group_rows // owners
     fast = share == BLK and owners == groups and owners & (owners - 1) == 0 and owners > 2
     home = mine = None
 
     def chunk(k):
-        n = early * BLK // half
-        return (grads[0], k * half) if k < n else (grads[1], (k - n) * half)
-
-    def rest(dep):
-        grads.append(run_grads(meta, member, z, q, lse, early, blocks - early, dep))
-        if not fast:
-            return grads[1], None
-        terms = run_terms(meta, member, owner, entries, z, w, lse, positives, True, grads[1], 0, PARTS)
-        return terms, HomeSum(terms)
-
-    def more(part, dep):
-        home.terms = run_terms(meta, member, owner, entries, z, w, lse, positives, True, dep, part, PARTS, home.terms)
-        return home.terms
-
-    if lax.axis_size("batch") == 4 and blocks > early:
-        line = Line(2 * blocks, half, width)
-        line.begin(grads[0])
-        dep, home = rest(grads[0])
+        row = k * half
+        for part, grad in zip(parts, grads):
+            if row < part * BLK:
+                return grad, row
+            row -= part * BLK
+
+    if in_line:
+        line.begin(grads[0], grads[1])
+        dep = line.early(grads[0], grads[2])
+    if fast:
+        dep = run_terms(meta, member, owner, entries, z, w, lse, positives, True, dep)
+        home = HomeSum(dep)
+    if in_line:
         deps = [dep]
-        for t in range(LAGS[0], line.slots):
+        for t in range(line.late, line.slots):
             deps = [line.slot(t, chunk, deps)]
-            if fast and t in TERM_SLOTS:
-                deps.append(more(1 + TERM_SLOTS.index(t), deps[0]))
             if fast and t == START_SLOT:
                 home.start(deps[0])
             if fast and t in HOME_SLOTS:
@@ -533,12 +543,9 @@
                 mine = deps[-1]
         grad = line.out
     else:
-        _, home = rest(lse)
+        grad = lax.psum(grads[0], "batch")
         if fast:
-            for part in range(1, PARTS):
-                more(part, lse)
             home.start(lse)
-        grad = lax.psum(jnp.concatenate(grads, axis=0), "batch")
     if fast:
         while home.stage < len(home.bits):
             home.step(lse)

time: 151 us -> 142 us (0.940)
  starting transfers between devices: 79.8 us -> 71.6 us
  waiting for transfers between devices: 23.8 us -> 20.2 us
  Pallas kernels: 40.7 us -> 42.3 us
    ppermute x5, starting transfers between devices: 8.92 us -> 2.88 us  [move(): return lax.ppermute(x, 'cache', [(i, i ^ bit) for i in range(self.n)])]
    ppermute x36 -> x33, waiting for transfers between devices: 15.3 us -> 12.5 us  [the longest x18 12.5 us: swapped(): return lax.ppermute(array, 'batch', [(0, 1), (1, 0), (2, 3), (3, 2)])]
    ppermute x36 -> x33, starting transfers between devices: 65.5 us -> 63.6 us  [the longest x18 53.7 us: swapped(): return lax.ppermute(array, 'batch', [(0, 1), (1, 0), (2, 3), (3, 2)])]
    ppermute x5, waiting for transfers between devices: 5.1 us -> 3.47 us  [move(): return lax.ppermute(x, 'cache', [(i, i ^ bit) for i in range(self.n)])]
    pallas_call x2 -> x3, Pallas kernels: 9.26 us -> 10 us  [run_grads(): pl.pallas_call(functools.partial(grad_kernel, meta, first, group), in_spe...]
  transfers between devices with their start and end apart: 45 -> 42, of which waited for: 14 -> 13; matrix products, arithmetic and copies ran while one was open for 1% -> 1% of each run, Pallas kernels for 15% -> 18%
where the time goes in v5:
time: 142 us; the launch traced here: 141 us
  starting transfers between devices  71.6 us (50%)
  Pallas kernels  42.3 us (30%)
  waiting for transfers between devices  20.2 us (14%)
  local copies, waits for them, and re-layouts  3.54 us (2%)
  other arithmetic  2.02 us (1%)
    ppermute x18, starting transfers between devices, swapped(): return lax.ppermute(array, 'batch', [(0, 1), (1, 0), (2, 3), (3, 2)])  53.7 us
    pallas_call x1, Pallas kernels, run_terms(): pl.pallas_call(functools.partial(term_kernel, meta, spread, group), in_sp...  15.3 us
    pallas_call x1, Pallas kernels, run_scores(): pl.pallas_call(functools.partial(scores_kernel, meta, group, 2.0 / math.s...  14.5 us
    ppermute x18, waiting for transfers between devices, swapped(): return lax.ppermute(array, 'batch', [(0, 1), (1, 0), (2, 3), (3, 2)])  12.5 us
    pallas_call x3, Pallas kernels, run_grads(): pl.pallas_call(functools.partial(grad_kernel, meta, first, group), in_spe...  10 us
    ppermute x15, starting transfers between devices, swapped_mid(): return lax.ppermute(array, 'batch', [(1, 2), (2, 1)])  9.96 us
    ppermute x4, starting transfers between devices, exchange_lse(): lax.ppermute(lse, 'cache', [(i, i ^ p) for i in range(n)])  5.04 us
    ppermute x4, waiting for transfers between devices, exchange_lse(): lax.ppermute(lse, 'cache', [(i, i ^ p) for i in range(n)])  4.22 us
  transfers between devices with their start and end apart: 42, of which 13 were waited for; matrix products, arithmetic and copies ran while one was open for 1% of the time, Pallas kernels for 18%

profile of v5, /device:TPU:0, one launch (start us, length us, event | category | flops | bytes accessed | tf_op | source)
XLA Modules:
  0.0 140.8 jit_solution(18156488775691624897)
XLA Ops:
  0.6 0.8 iota_compare_fusion
  1.4 1.3 and_reduce_fusion
  3.3 14.5 %scores.1 = (f32[24,8,128,128]{3,2,1,0:T(8,128)S(1)}, bf16[12,256,768]{2,1,0:T(8,128)(2,1)S(1)}, bf16[24,128,768]{2,1,0:T(8,128)(2,1)S(1)}, f32[24,128]{1,0:T(8,128)S(1)}, s32[102]{0:T(128)S(1)}) custom-call(s32[24,8]{1,0:T(8,128)S(1)} %convert_bitcast_fusion.member, s32[3]{0:T(128)S(1)} %copy-done.1, bf16[24,128,768]{2,1,0:T(8,128)(2,1)} %bitcast.3, ...), custom_call_target="tpu_custom_call" | custom-call | tf_op jit(solution)/shard_map/scores/pallas_call | solution.py:235
  17.9 1.2 collective-permute-done.refs_1_
  19.1 4.3 %collective-permute-start.3 = (f32[24,128]{1,0:T(8,128)S(1)}, f32[24,128]{1,0:T(8,128)S(1)}, u32[]{:S(2)}, u32[]{:S(2)}) collective-permute-start(f32[24,128]{1,0:T(8,128)S(1)} %merge_lse.2.refs_0_), channel_id=1, source_target_pairs={{0,24},{4,28},{8,16},{12,20},{16,8},{20,12},{24,0},{28,4},{1,25},{... | collective-permute-start | bytes 36872 | tf_op jit(solution)/shard_map/ppermute | solution.py:315
  24.1 1.0 collective-permute-done.3.refs_3_
  25.1 2.0 %collective-permute-done.2.refs_2_ = f32[24,128]{1,0:T(8,128)S(1)} collective-permute-done((f32[24,128]{1,0:T(8,128)S(1)}, f32[24,128]{1,0:T(8,128)S(1)}, u32[]{:S(2)}, u32[]{:S(2)}) %collective-permute-start.2) | collective-permute-done | bytes 12320 | tf_op jit(solution)/shard_map/ppermute | solution.py:315
  27.2 1.5 %cache_grad.3.dep.own = f32[128,768]{1,0:T(8,128)S(1)} custom-call(s32[24,8]{1,0:T(8,128)S(1)} %convert_bitcast_fusion.member, f32[24,8,128,128]{3,2,1,0:T(8,128)S(1)} %get-tuple-element.70.z_ref, bf16[24,128,768]{2,1,0:T(8,128)(2,1)S(1)} %get-tuple-element.73.q_ref, f32[24,128]{1,0:T(8,128)S(1)} %merge_lse.3.lse_ref.dep, f32[24,128]{1,0:T(8,128)S(1)} %merge_lse.3.lse_ref.dep), custom_call_target="tpu_custom_call" | custom-call | tf_op jit(solution)/shard_map/cache_grad/pallas_call | solution.py:263
  28.7 1.7 %collective-permute-start.4 = (f32[128,768]{1,0:T(8,128)S(1)}, f32[128,768]{1,0:T(8,128)S(1)}, u32[]{:S(2)}, u32[]{:S(2)}) collective-permute-start(f32[128,768]{1,0:T(8,128)S(1)} %cache_grad.3.dep.own), channel_id=1, source_target_pairs={{0,1},{1,0},{2,3},{3,2},{4,5},{5,4},{6,7},{7,6},{8,9},{9,8},{10,11... | collective-permute-start | bytes 1179656 | tf_op jit(solution)/shard_map/ppermute | solution.py:330
  30.3 2.8 %cache_grad.4.dep.refs_0_ = f32[256,768]{1,0:T(8,128)S(1)} custom-call(s32[24,8]{1,0:T(8,128)S(1)} %convert_bitcast_fusion.member, f32[24,8,128,128]{3,2,1,0:T(8,128)S(1)} %get-tuple-element.70.z_ref, bf16[24,128,768]{2,1,0:T(8,128)(2,1)S(1)} %get-tuple-element.73.q_ref, f32[24,128]{1,0:T(8,128)S(1)} %merge_lse.3.lse_ref.dep, f32[128,768]{1,0:T(8,128)S(1)} %cache_grad.3.dep.own), custom_call_target="tpu_custom_call" | custom-call | tf_op jit(solution)/shard_map/cache_grad/pallas_call | solution.py:263
  33.7 5.7 %cache_grad.5.dep.refs_4_.refs_0_ = f32[640,768]{1,0:T(8,128)S(1)} custom-call(s32[24,8]{1,0:T(8,128)S(1)} %convert_bitcast_fusion.member, f32[24,8,128,128]{3,2,1,0:T(8,128)S(1)} %get-tuple-element.70.z_ref, bf16[24,128,768]{2,1,0:T(8,128)(2,1)S(1)} %get-tuple-element.73.q_ref, f32[24,128]{1,0:T(8,128)S(1)} %merge_lse.3.lse_ref.dep, ...), custom_call_target="tpu_custom_call" | custom-call | tf_op jit(solution)/shard_map/cache_grad/pallas_call | solution.py:263
  39.4 1.4 %collective-permute-done.4.came = f32[128,768]{1,0:T(8,128)S(1)} collective-permute-done((f32[128,768]{1,0:T(8,128)S(1)}, f32[128,768]{1,0:T(8,128)S(1)}, u32[]{:S(2)}, u32[]{:S(2)}) %collective-permute-start.4) | collective-permute-done | bytes 393248 | tf_op jit(solution)/shard_map/ppermute | solution.py:330
  40.9 0.7 collective-permute-start.6
  41.6 15.3 %query_term.1.refs_5_.terms.refs_0_ = f32[8,3,128,768]{3,2,1,0:T(8,128)S(1)} custom-call(s32[24,8]{1,0:T(8,128)S(1)} %convert_bitcast_fusion.member, s32[3]{0:T(128)S(1)} %copy-done.1, s32[102]{0:T(128)S(1)} %get-tuple-element.69.entries, f32[24,8,128,128]{3,2,1,0:T(8,128)S(1)} %get-tuple-element.70.z_ref, ...), custom_call_target="tpu_custom_call" | custom-call | tf_op jit(solution)/shard_map/query_term/pallas_call | solution.py:277
  57.4 0.7 collective-permute-start.10
  58.1 5.0 %collective-permute-start.11 = (f32[64,768]{1,0:T(8,128)S(1)}, f32[64,768]{1,0:T(8,128)S(1)}, u32[]{:S(2)}, u32[]{:S(2)}) collective-permute-start(f32[64,768]{1,0:T(8,128)S(1)} %get-tuple-element.79), channel_id=1, source_target_pairs={{0,1},{1,0},{2,3},{3,2},{4,5},{5,4},{6,7},{7,6},{8,9},{9,8},{10,11... | collective-permute-start | bytes 589832 | tf_op jit(solution)/shard_map/ppermute | solution.py:330
  63.2 0.7 collective-permute-start.8
  63.9 4.9 %collective-permute-done.11.refs_6_.refs_1_ = f32[64,768]{1,0:T(8,128)S(1)} collective-permute-done((f32[64,768]{1,0:T(8,128)S(1)}, f32[64,768]{1,0:T(8,128)S(1)}, u32[]{:S(2)}, u32[]{:S(2)}) %collective-permute-start.11) | collective-permute-done | bytes 196640 | tf_op jit(solution)/shard_map/ppermute | solution.py:330
  68.9 2.0 %collective-permute-start.17 = (f32[64,768]{1,0:T(8,128)S(1)}, f32[64,768]{1,0:T(8,128)S(1)}, u32[]{:S(2)}, u32[]{:S(2)}) collective-permute-start(f32[64,768]{1,0:T(8,128)S(1)} %get-tuple-element.90), channel_id=1, source_target_pairs={{0,1},{1,0},{2,3},{3,2},{4,5},{5,4},{6,7},{7,6},{8,9},{9,8},{10,11... | collective-permute-start | bytes 589832 | tf_op jit(solution)/shard_map/ppermute | solution.py:330
  70.9 0.7 collective-permute-start.16
  71.6 1.5 %collective-permute-done.9.refs_6_.refs_1_ = f32[64,768]{1,0:T(8,128)S(1)} collective-permute-done((f32[64,768]{1,0:T(8,128)S(1)}, f32[64,768]{1,0:T(8,128)S(1)}, u32[]{:S(2)}, u32[]{:S(2)}) %collective-permute-start.9) | collective-permute-done | bytes 196640 | tf_op jit(solution)/shard_map/ppermute | solution.py:330
  73.1 2.0 %collective-permute-start.14 = (f32[64,768]{1,0:T(8,128)S(1)}, f32[64,768]{1,0:T(8,128)S(1)}, u32[]{:S(2)}, u32[]{:S(2)}) collective-permute-start(f32[64,768]{1,0:T(8,128)S(1)} %get-tuple-element.87), channel_id=1, source_target_pairs={{0,1},{1,0},{2,3},{3,2},{4,5},{5,4},{6,7},{7,6},{8,9},{9,8},{10,11... | collective-permute-start | bytes 589832 | tf_op jit(solution)/shard_map/ppermute | solution.py:330
  76.3 0.9 collective-permute-done.17.refs_6_.refs_1_
  77.3 2.5 %collective-permute-start.21 = (f32[64,768]{1,0:T(8,128)S(1)}, f32[64,768]{1,0:T(8,128)S(1)}, u32[]{:S(2)}, u32[]{:S(2)}) collective-permute-start(f32[64,768]{1,0:T(8,128)S(1)} %get-tuple-element.98), channel_id=1, source_target_pairs={{0,1},{1,0},{2,3},{3,2},{4,5},{5,4},{6,7},{7,6},{8,9},{9,8},{10,11... | collective-permute-start | bytes 589832 | tf_op jit(solution)/shard_map/ppermute | solution.py:330
  80.5 0.9 collective-permute-done.14.refs_6_.refs_1_
  81.5 2.0 %collective-permute-start.19 = (f32[64,768]{1,0:T(8,128)S(1)}, f32[64,768]{1,0:T(8,128)S(1)}, u32[]{:S(2)}, u32[]{:S(2)}) collective-permute-start(f32[64,768]{1,0:T(8,128)S(1)} %get-tuple-element.96), channel_id=1, source_target_pairs={{0,1},{1,0},{2,3},{3,2},{4,5},{5,4},{6,7},{7,6},{8,9},{9,8},{10,11... | collective-permute-start | bytes 589832 | tf_op jit(solution)/shard_map/ppermute | solution.py:330
  84.3 1.4 collective-permute-done.21.refs_6_.refs_1_
  86.4 3.4 %collective-permute-start.25 = (f32[64,768]{1,0:T(8,128)S(1)}, f32[64,768]{1,0:T(8,128)S(1)}, u32[]{:S(2)}, u32[]{:S(2)}) collective-permute-start(f32[64,768]{1,0:T(8,128)S(1)} %get-tuple-element.106), channel_id=1, source_target_pairs={{0,1},{1,0},{2,3},{3,2},{4,5},{5,4},{6,7},{7,6},{8,9},{9,8},{10,11... | collective-permute-start | bytes 589832 | tf_op jit(solution)/shard_map/ppermute | solution.py:330
  89.9 0.7 collective-permute-start.24
  90.6 5.3 %collective-permute-start.22 = (f32[64,768]{1,0:T(8,128)S(1)}, f32[64,768]{1,0:T(8,128)S(1)}, u32[]{:S(2)}, u32[]{:S(2)}) collective-permute-start(f32[64,768]{1,0:T(8,128)S(1)} %get-tuple-element.102), channel_id=1, source_target_pairs={{0,1},{1,0},{2,3},{3,2},{4,5},{5,4},{6,7},{7,6},{8,9},{9,8},{10,11... | collective-permute-start | bytes 589832 | tf_op jit(solution)/shard_map/ppermute | solution.py:330
  95.9 0.7 collective-permute-start.23
  96.7 3.3 %collective-permute-start.29 = (f32[64,768]{1,0:T(8,128)S(1)}, f32[64,768]{1,0:T(8,128)S(1)}, u32[]{:S(2)}, u32[]{:S(2)}) collective-permute-start(f32[64,768]{1,0:T(8,128)S(1)} %get-tuple-element.114), channel_id=1, source_target_pairs={{0,1},{1,0},{2,3},{3,2},{4,5},{5,4},{6,7},{7,6},{8,9},{9,8},{10,11... | collective-permute-start | bytes 589832 | tf_op jit(solution)/shard_map/ppermute | solution.py:330
  100.0 0.7 collective-permute-start.28
  100.8 3.9 %collective-permute-start.27 = (f32[64,768]{1,0:T(8,128)S(1)}, f32[64,768]{1,0:T(8,128)S(1)}, u32[]{:S(2)}, u32[]{:S(2)}) collective-permute-start(f32[64,768]{1,0:T(8,128)S(1)} %get-tuple-element.112), channel_id=1, source_target_pairs={{0,1},{1,0},{2,3},{3,2},{4,5},{5,4},{6,7},{7,6},{8,9},{9,8},{10,11... | collective-permute-start | bytes 589832 | tf_op jit(solution)/shard_map/ppermute | solution.py:330
  104.7 0.7 collective-permute-start.26
  105.5 5.5 %collective-permute-start.35 = (f32[64,768]{1,0:T(8,128)S(1)}, f32[64,768]{1,0:T(8,128)S(1)}, u32[]{:S(2)}, u32[]{:S(2)}) collective-permute-start(f32[64,768]{1,0:T(8,128)S(1)} %get-tuple-element.124.refs_4_), channel_id=1, source_target_pairs={{0,1},{1,0},{2,3},{3,2},{4,5},{5,4},{6,7},{7,6},{8,9},{9,8},{10,11... | collective-permute-start | bytes 589832 | tf_op jit(solution)/shard_map/ppermute | solution.py:330
  111.0 0.7 collective-permute-start.34
  111.7 5.3 %collective-permute-start.33 = (f32[64,768]{1,0:T(8,128)S(1)}, f32[64,768]{1,0:T(8,128)S(1)}, u32[]{:S(2)}, u32[]{:S(2)}) collective-permute-start(f32[64,768]{1,0:T(8,128)S(1)} %get-tuple-element.123.refs_4_), channel_id=1, source_target_pairs={{0,1},{1,0},{2,3},{3,2},{4,5},{5,4},{6,7},{7,6},{8,9},{9,8},{10,11... | collective-permute-start | bytes 589832 | tf_op jit(solution)/shard_map/ppermute | solution.py:330
  117.0 0.7 collective-permute-start.32
  118.1 2.7 %collective-permute-start.39 = (f32[64,768]{1,0:T(8,128)S(1)}, f32[64,768]{1,0:T(8,128)S(1)}, u32[]{:S(2)}, u32[]{:S(2)}) collective-permute-start(f32[64,768]{1,0:T(8,128)S(1)} %get-tuple-element.130.refs_2_), channel_id=1, source_target_pairs={{0,1},{1,0},{2,3},{3,2},{4,5},{5,4},{6,7},{7,6},{8,9},{9,8},{10,11... | collective-permute-start | bytes 589832 | tf_op jit(solution)/shard_map/ppermute | solution.py:330
  121.4 1.4 collective-permute-done.33.refs_5_
  122.9 3.7 %collective-permute-start.37 = (f32[64,768]{1,0:T(8,128)S(1)}, f32[64,768]{1,0:T(8,128)S(1)}, u32[]{:S(2)}, u32[]{:S(2)}) collective-permute-start(f32[64,768]{1,0:T(8,128)S(1)} %get-tuple-element.129.refs_2_), channel_id=1, source_target_pairs={{0,1},{1,0},{2,3},{3,2},{4,5},{5,4},{6,7},{7,6},{8,9},{9,8},{10,11... | collective-permute-start | bytes 589832 | tf_op jit(solution)/shard_map/ppermute | solution.py:330
  127.9 1.5 %collective-permute-start.31 = (f32[1,3,64,768]{3,2,1,0:T(8,128)S(1)}, f32[1,3,64,768]{3,2,1,0:T(8,128)S(1)}, u32[]{:S(2)}, u32[]{:S(2)}) collective-permute-start(f32[1,3,64,768]{3,2,1,0:T(8,128)S(1)} %get-tuple-element.122), channel_id=1, source_target_pairs={{0,8},{4,12},{8,0},{12,4},{16,24},{20,28},{24,16},{28,20},{1,9},{5... | collective-permute-start | bytes 1769480 | tf_op jit(solution)/shard_map/ppermute | solution.py:423
  129.4 2.1 %collective-permute-start.41 = (f32[64,768]{1,0:T(8,128)S(1)}, f32[64,768]{1,0:T(8,128)S(1)}, u32[]{:S(2)}, u32[]{:S(2)}) collective-permute-start(f32[64,768]{1,0:T(8,128)S(1)} %get-tuple-element.133.refs_5_.refs_0_), channel_id=1, source_target_pairs={{0,1},{1,0},{2,3},{3,2},{4,5},{5,4},{6,7},{7,6},{8,9},{9,8},{10,11... | collective-permute-start | bytes 589832 | tf_op jit(solution)/shard_map/ppermute | solution.py:330
  131.5 2.8 %collective-permute-start.40 = (f32[64,768]{1,0:T(8,128)S(1)}, f32[64,768]{1,0:T(8,128)S(1)}, u32[]{:S(2)}, u32[]{:S(2)}) collective-permute-start(f32[64,768]{1,0:T(8,128)S(1)} %get-tuple-element.134.refs_4_.refs_3_.refs_0_), channel_id=1, source_target_pairs={{0,1},{1,0},{2,3},{3,2},{4,5},{5,4},{6,7},{7,6},{8,9},{9,8},{10,11... | collective-permute-start | bytes 589832 | tf_op jit(solution)/shard_map/ppermute | solution.py:330
  134.3 2.9 %collective-permute-done.30.refs_1_ = f32[1,3,64,768]{3,2,1,0:T(8,128)S(1)} collective-permute-done((f32[1,3,64,768]{3,2,1,0:T(8,128)S(1)}, f32[1,3,64,768]{3,2,1,0:T(8,128)S(1)}, u32[]{:S(2)}, u32[]{:S(2)}) %collective-permute-start.30) | collective-permute-done | bytes 589856 | tf_op jit(solution)/shard_map/ppermute | solution.py:423
  137.9 1.0 copy.39
  139.2 1.7 %copy.40 = f32[1024,768]{1,0:T(8,128)} copy(f32[1024,768]{1,0:T(8,128)S(1)} %line_slot.35) | data formatting | bytes 6291456
  (77 shorter events, 10.1 us)
Async XLA Ops:
  2.7 0.7 copy-start.1
  17.8 1.2 collective-permute-start
  19.1 6.0 %collective-permute-start.3 = (f32[24,128]{1,0:T(8,128)S(1)}, f32[24,128]{1,0:T(8,128)S(1)}, u32[]{:S(2)}, u32[]{:S(2)}) collective-permute-start(f32[24,128]{1,0:T(8,128)S(1)} %merge_lse.2.refs_0_), channel_id=1, source_target_pairs={{0,24},{4,28},{8,16},{12,20},{16,8},{20,12},{24,0},{28,4},{1,25},{... | collective-permute-start | bytes 36872 | tf_op jit(solution)/shard_map/ppermute | solution.py:315
  23.4 3.7 %collective-permute-start.2 = (f32[24,128]{1,0:T(8,128)S(1)}, f32[24,128]{1,0:T(8,128)S(1)}, u32[]{:S(2)}, u32[]{:S(2)}) collective-permute-start(f32[24,128]{1,0:T(8,128)S(1)} %merge_lse.2.refs_0_), channel_id=1, source_target_pairs={{0,16},{4,20},{8,24},{12,28},{16,0},{20,4},{24,8},{28,12},{1,17},{... | collective-permute-start | bytes 36872 | tf_op jit(solution)/shard_map/ppermute | solution.py:315
  23.4 3.7 %collective-permute-start.1 = (f32[24,128]{1,0:T(8,128)S(1)}, f32[24,128]{1,0:T(8,128)S(1)}, u32[]{:S(2)}, u32[]{:S(2)}) collective-permute-start(f32[24,128]{1,0:T(8,128)S(1)} %merge_lse.2.refs_0_), channel_id=1, source_target_pairs={{0,8},{4,12},{8,0},{12,4},{16,24},{20,28},{24,16},{28,20},{1,9},{5... | collective-permute-start | bytes 36872 | tf_op jit(solution)/shard_map/ppermute | solution.py:315
  28.7 12.1 %collective-permute-start.4 = (f32[128,768]{1,0:T(8,128)S(1)}, f32[128,768]{1,0:T(8,128)S(1)}, u32[]{:S(2)}, u32[]{:S(2)}) collective-permute-start(f32[128,768]{1,0:T(8,128)S(1)} %cache_grad.3.dep.own), channel_id=1, source_target_pairs={{0,1},{1,0},{2,3},{3,2},{4,5},{5,4},{6,7},{7,6},{8,9},{9,8},{10,11... | collective-permute-start | bytes 1179656 | tf_op jit(solution)/shard_map/ppermute | solution.py:330
  33.2 23.8 %collective-permute-start.5 = (f32[256,768]{1,0:T(8,128)S(1)}, f32[256,768]{1,0:T(8,128)S(1)}, u32[]{:S(2)}, u32[]{:S(2)}) collective-permute-start(f32[256,768]{1,0:T(8,128)S(1)} %cache_grad.4.dep.refs_0_), channel_id=1, source_target_pairs={{0,1},{1,0},{2,3},{3,2},{4,5},{5,4},{6,7},{7,6},{8,9},{9,8},{10,11... | collective-permute-start | bytes 2359304 | tf_op jit(solution)/shard_map/ppermute | solution.py:330
  39.4 2.2 %copy-start = (s32[3,1024]{1,0:T(4,128)S(1)}, s32[3,1024]{1,0:T(4,128)}, u32[]{:S(2)}) copy-start(s32[3,1024]{1,0:T(4,128)} %pos_ref.1) | copy-start | bytes 36868
  40.9 16.0 %collective-permute-start.6 = (f32[128,768]{1,0:T(8,128)S(1)}, f32[128,768]{1,0:T(8,128)S(1)}, u32[]{:S(2)}, u32[]{:S(2)}) collective-permute-start(f32[128,768]{1,0:T(8,128)S(1)} %line_early.1.dep.refs_2_), channel_id=1, source_target_pairs={{1,2},{2,1},{5,6},{6,5},{9,10},{10,9},{13,14},{14,13},{17,18},{18,... | collective-permute-start | bytes 1179656 | tf_op jit(solution)/shard_map/ppermute | solution.py:333
  57.3 18.4 %collective-permute-start.7 = (f32[4,3,128,768]{3,2,1,0:T(8,128)S(1)}, f32[4,3,128,768]{3,2,1,0:T(8,128)S(1)}, u32[]{:S(2)}, u32[]{:S(2)}) collective-permute-start(f32[4,3,128,768]{3,2,1,0:T(8,128)S(1)} %home_start.1), channel_id=1, source_target_pairs={{0,4},{4,0},{8,12},{12,8},{16,20},{20,16},{24,28},{28,24},{1,5},{5... | collective-permute-start | bytes 14155784 | tf_op jit(solution)/shard_map/ppermute | solution.py:423
  57.4 11.4 %collective-permute-start.10 = (f32[64,768]{1,0:T(8,128)S(1)}, f32[64,768]{1,0:T(8,128)S(1)}, u32[]{:S(2)}, u32[]{:S(2)}) collective-permute-start(f32[64,768]{1,0:T(8,128)S(1)} %get-tuple-element.74.dep.refs_5_.refs_2_), channel_id=1, source_target_pairs={{1,2},{2,1},{5,6},{6,5},{9,10},{10,9},{13,14},{14,13},{17,18},{18,... | collective-permute-start | bytes 589832 | tf_op jit(solution)/shard_map/ppermute | solution.py:333
  58.1 10.7 %collective-permute-start.11 = (f32[64,768]{1,0:T(8,128)S(1)}, f32[64,768]{1,0:T(8,128)S(1)}, u32[]{:S(2)}, u32[]{:S(2)}) collective-permute-start(f32[64,768]{1,0:T(8,128)S(1)} %get-tuple-element.79), channel_id=1, source_target_pairs={{0,1},{1,0},{2,3},{3,2},{4,5},{5,4},{6,7},{7,6},{8,9},{9,8},{10,11... | collective-permute-start | bytes 589832 | tf_op jit(solution)/shard_map/ppermute | solution.py:330
  63.1 9.9 %collective-permute-start.9 = (f32[64,768]{1,0:T(8,128)S(1)}, f32[64,768]{1,0:T(8,128)S(1)}, u32[]{:S(2)}, u32[]{:S(2)}) collective-permute-start(f32[64,768]{1,0:T(8,128)S(1)} %get-tuple-element.77), channel_id=1, source_target_pairs={{0,1},{1,0},{2,3},{3,2},{4,5},{5,4},{6,7},{7,6},{8,9},{9,8},{10,11... | collective-permute-start | bytes 589832 | tf_op jit(solution)/shard_map/ppermute | solution.py:330
  63.2 9.8 %collective-permute-start.8 = (f32[64,768]{1,0:T(8,128)S(1)}, f32[64,768]{1,0:T(8,128)S(1)}, u32[]{:S(2)}, u32[]{:S(2)}) collective-permute-start(f32[64,768]{1,0:T(8,128)S(1)} %get-tuple-element.75.refs_7_.refs_2_), channel_id=1, source_target_pairs={{1,2},{2,1},{5,6},{6,5},{9,10},{10,9},{13,14},{14,13},{17,18},{18,... | collective-permute-start | bytes 589832 | tf_op jit(solution)/shard_map/ppermute | solution.py:333
  68.9 8.3 %collective-permute-start.17 = (f32[64,768]{1,0:T(8,128)S(1)}, f32[64,768]{1,0:T(8,128)S(1)}, u32[]{:S(2)}, u32[]{:S(2)}) collective-permute-start(f32[64,768]{1,0:T(8,128)S(1)} %get-tuple-element.90), channel_id=1, source_target_pairs={{0,1},{1,0},{2,3},{3,2},{4,5},{5,4},{6,7},{7,6},{8,9},{9,8},{10,11... | collective-permute-start | bytes 589832 | tf_op jit(solution)/shard_map/ppermute | solution.py:330
  70.9 6.3 %collective-permute-start.16 = (f32[64,768]{1,0:T(8,128)S(1)}, f32[64,768]{1,0:T(8,128)S(1)}, u32[]{:S(2)}, u32[]{:S(2)}) collective-permute-start(f32[64,768]{1,0:T(8,128)S(1)} %get-tuple-element.81.refs_8_.refs_2_), channel_id=1, source_target_pairs={{1,2},{2,1},{5,6},{6,5},{9,10},{10,9},{13,14},{14,13},{17,18},{18,... | collective-permute-start | bytes 589832 | tf_op jit(solution)/shard_map/ppermute | solution.py:333
  73.1 8.3 %collective-permute-start.14 = (f32[64,768]{1,0:T(8,128)S(1)}, f32[64,768]{1,0:T(8,128)S(1)}, u32[]{:S(2)}, u32[]{:S(2)}) collective-permute-start(f32[64,768]{1,0:T(8,128)S(1)} %get-tuple-element.87), channel_id=1, source_target_pairs={{0,1},{1,0},{2,3},{3,2},{4,5},{5,4},{6,7},{7,6},{8,9},{9,8},{10,11... | collective-permute-start | bytes 589832 | tf_op jit(solution)/shard_map/ppermute | solution.py:330
  75.1 6.3 %collective-permute-start.15 = (f32[64,768]{1,0:T(8,128)S(1)}, f32[64,768]{1,0:T(8,128)S(1)}, u32[]{:S(2)}, u32[]{:S(2)}) collective-permute-start(f32[64,768]{1,0:T(8,128)S(1)} %get-tuple-element.82.refs_2_.refs_8_), channel_id=1, source_target_pairs={{1,2},{2,1},{5,6},{6,5},{9,10},{10,9},{13,14},{14,13},{17,18},{18,... | collective-permute-start | bytes 589832 | tf_op jit(solution)/shard_map/ppermute | solution.py:333
  77.3 8.3 %collective-permute-start.21 = (f32[64,768]{1,0:T(8,128)S(1)}, f32[64,768]{1,0:T(8,128)S(1)}, u32[]{:S(2)}, u32[]{:S(2)}) collective-permute-start(f32[64,768]{1,0:T(8,128)S(1)} %get-tuple-element.98), channel_id=1, source_target_pairs={{0,1},{1,0},{2,3},{3,2},{4,5},{5,4},{6,7},{7,6},{8,9},{9,8},{10,11... | collective-permute-start | bytes 589832 | tf_op jit(solution)/shard_map/ppermute | solution.py:330
  79.8 6.5 %collective-permute-start.20 = (f32[64,768]{1,0:T(8,128)S(1)}, f32[64,768]{1,0:T(8,128)S(1)}, u32[]{:S(2)}, u32[]{:S(2)}) collective-permute-start(f32[64,768]{1,0:T(8,128)S(1)} %get-tuple-element.93.refs_8_.refs_2_), channel_id=1, source_target_pairs={{1,2},{2,1},{5,6},{6,5},{9,10},{10,9},{13,14},{14,13},{17,18},{18,... | collective-permute-start | bytes 589832 | tf_op jit(solution)/shard_map/ppermute | solution.py:333
  81.5 8.3 %collective-permute-start.19 = (f32[64,768]{1,0:T(8,128)S(1)}, f32[64,768]{1,0:T(8,128)S(1)}, u32[]{:S(2)}, u32[]{:S(2)}) collective-permute-start(f32[64,768]{1,0:T(8,128)S(1)} %get-tuple-element.96), channel_id=1, source_target_pairs={{0,1},{1,0},{2,3},{3,2},{4,5},{5,4},{6,7},{7,6},{8,9},{9,8},{10,11... | collective-permute-start | bytes 589832 | tf_op jit(solution)/shard_map/ppermute | solution.py:330
  83.5 7.0 %collective-permute-start.18 = (f32[64,768]{1,0:T(8,128)S(1)}, f32[64,768]{1,0:T(8,128)S(1)}, u32[]{:S(2)}, u32[]{:S(2)}) collective-permute-start(f32[64,768]{1,0:T(8,128)S(1)} %get-tuple-element.94.refs_8_.refs_2_), channel_id=1, source_target_pairs={{1,2},{2,1},{5,6},{6,5},{9,10},{10,9},{13,14},{14,13},{17,18},{18,... | collective-permute-start | bytes 589832 | tf_op jit(solution)/shard_map/ppermute | solution.py:333
  84.2 32.9 %collective-permute-start.12 = (f32[2,3,64,768]{3,2,1,0:T(8,128)S(1)}, f32[2,3,64,768]{3,2,1,0:T(8,128)S(1)}, u32[]{:S(2)}, u32[]{:S(2)}) collective-permute-start(f32[2,3,64,768]{3,2,1,0:T(8,128)S(1)} %get-tuple-element.84), channel_id=1, source_target_pairs={{0,8},{4,12},{8,0},{12,4},{16,24},{20,28},{24,16},{28,20},{1,9},{5... | collective-permute-start | bytes 3538952 | tf_op jit(solution)/shard_map/ppermute | solution.py:423
  85.6 32.1 %collective-permute-start.13 = (f32[2,3,64,768]{3,2,1,0:T(8,128)S(1)}, f32[2,3,64,768]{3,2,1,0:T(8,128)S(1)}, u32[]{:S(2)}, u32[]{:S(2)}) collective-permute-start(f32[2,3,64,768]{3,2,1,0:T(8,128)S(1)} %get-tuple-element.86), channel_id=1, source_target_pairs={{0,16},{4,20},{8,24},{12,28},{16,0},{20,4},{24,8},{28,12},{1,17},{... | collective-permute-start | bytes 3538952 | tf_op jit(solution)/shard_map/ppermute | solution.py:423
  86.4 9.6 %collective-permute-start.25 = (f32[64,768]{1,0:T(8,128)S(1)}, f32[64,768]{1,0:T(8,128)S(1)}, u32[]{:S(2)}, u32[]{:S(2)}) collective-permute-start(f32[64,768]{1,0:T(8,128)S(1)} %get-tuple-element.106), channel_id=1, source_target_pairs={{0,1},{1,0},{2,3},{3,2},{4,5},{5,4},{6,7},{7,6},{8,9},{9,8},{10,11... | collective-permute-start | bytes 589832 | tf_op jit(solution)/shard_map/ppermute | solution.py:330
  89.9 6.7 %collective-permute-start.24 = (f32[64,768]{1,0:T(8,128)S(1)}, f32[64,768]{1,0:T(8,128)S(1)}, u32[]{:S(2)}, u32[]{:S(2)}) collective-permute-start(f32[64,768]{1,0:T(8,128)S(1)} %get-tuple-element.101.refs_8_.refs_2_), channel_id=1, source_target_pairs={{1,2},{2,1},{5,6},{6,5},{9,10},{10,9},{13,14},{14,13},{17,18},{18,... | collective-permute-start | bytes 589832 | tf_op jit(solution)/shard_map/ppermute | solution.py:333
  90.6 9.4 %collective-permute-start.22 = (f32[64,768]{1,0:T(8,128)S(1)}, f32[64,768]{1,0:T(8,128)S(1)}, u32[]{:S(2)}, u32[]{:S(2)}) collective-permute-start(f32[64,768]{1,0:T(8,128)S(1)} %get-tuple-element.102), channel_id=1, source_target_pairs={{0,1},{1,0},{2,3},{3,2},{4,5},{5,4},{6,7},{7,6},{8,9},{9,8},{10,11... | collective-permute-start | bytes 589832 | tf_op jit(solution)/shard_map/ppermute | solution.py:330
  95.9 4.8 %collective-permute-start.23 = (f32[64,768]{1,0:T(8,128)S(1)}, f32[64,768]{1,0:T(8,128)S(1)}, u32[]{:S(2)}, u32[]{:S(2)}) collective-permute-start(f32[64,768]{1,0:T(8,128)S(1)} %get-tuple-element.103.refs_8_.refs_2_), channel_id=1, source_target_pairs={{1,2},{2,1},{5,6},{6,5},{9,10},{10,9},{13,14},{14,13},{17,18},{18,... | collective-permute-start | bytes 589832 | tf_op jit(solution)/shard_map/ppermute | solution.py:333
  96.7 8.0 %collective-permute-start.29 = (f32[64,768]{1,0:T(8,128)S(1)}, f32[64,768]{1,0:T(8,128)S(1)}, u32[]{:S(2)}, u32[]{:S(2)}) collective-permute-start(f32[64,768]{1,0:T(8,128)S(1)} %get-tuple-element.114), channel_id=1, source_target_pairs={{0,1},{1,0},{2,3},{3,2},{4,5},{5,4},{6,7},{7,6},{8,9},{9,8},{10,11... | collective-permute-start | bytes 589832 | tf_op jit(solution)/shard_map/ppermute | solution.py:330
  100.0 5.4 %collective-permute-start.28 = (f32[64,768]{1,0:T(8,128)S(1)}, f32[64,768]{1,0:T(8,128)S(1)}, u32[]{:S(2)}, u32[]{:S(2)}) collective-permute-start(f32[64,768]{1,0:T(8,128)S(1)} %get-tuple-element.109.refs_8_.refs_2_), channel_id=1, source_target_pairs={{1,2},{2,1},{5,6},{6,5},{9,10},{10,9},{13,14},{14,13},{17,18},{18,... | collective-permute-start | bytes 589832 | tf_op jit(solution)/shard_map/ppermute | solution.py:333
  100.8 10.2 %collective-permute-start.27 = (f32[64,768]{1,0:T(8,128)S(1)}, f32[64,768]{1,0:T(8,128)S(1)}, u32[]{:S(2)}, u32[]{:S(2)}) collective-permute-start(f32[64,768]{1,0:T(8,128)S(1)} %get-tuple-element.112), channel_id=1, source_target_pairs={{0,1},{1,0},{2,3},{3,2},{4,5},{5,4},{6,7},{7,6},{8,9},{9,8},{10,11... | collective-permute-start | bytes 589832 | tf_op jit(solution)/shard_map/ppermute | solution.py:330
  104.7 6.9 %collective-permute-start.26 = (f32[64,768]{1,0:T(8,128)S(1)}, f32[64,768]{1,0:T(8,128)S(1)}, u32[]{:S(2)}, u32[]{:S(2)}) collective-permute-start(f32[64,768]{1,0:T(8,128)S(1)} %get-tuple-element.110.refs_7_.refs_2_), channel_id=1, source_target_pairs={{1,2},{2,1},{5,6},{6,5},{9,10},{10,9},{13,14},{14,13},{17,18},{18,... | collective-permute-start | bytes 589832 | tf_op jit(solution)/shard_map/ppermute | solution.py:333
  105.5 12.5 %collective-permute-start.35 = (f32[64,768]{1,0:T(8,128)S(1)}, f32[64,768]{1,0:T(8,128)S(1)}, u32[]{:S(2)}, u32[]{:S(2)}) collective-permute-start(f32[64,768]{1,0:T(8,128)S(1)} %get-tuple-element.124.refs_4_), channel_id=1, source_target_pairs={{0,1},{1,0},{2,3},{3,2},{4,5},{5,4},{6,7},{7,6},{8,9},{9,8},{10,11... | collective-permute-start | bytes 589832 | tf_op jit(solution)/shard_map/ppermute | solution.py:330
  111.0 7.1 %collective-permute-start.34 = (f32[64,768]{1,0:T(8,128)S(1)}, f32[64,768]{1,0:T(8,128)S(1)}, u32[]{:S(2)}, u32[]{:S(2)}) collective-permute-start(f32[64,768]{1,0:T(8,128)S(1)} %get-tuple-element.117.refs_7_.refs_2_), channel_id=1, source_target_pairs={{1,2},{2,1},{5,6},{6,5},{9,10},{10,9},{13,14},{14,13},{17,18},{18,... | collective-permute-start | bytes 589832 | tf_op jit(solution)/shard_map/ppermute | solution.py:333
  111.7 11.1 %collective-permute-start.33 = (f32[64,768]{1,0:T(8,128)S(1)}, f32[64,768]{1,0:T(8,128)S(1)}, u32[]{:S(2)}, u32[]{:S(2)}) collective-permute-start(f32[64,768]{1,0:T(8,128)S(1)} %get-tuple-element.123.refs_4_), channel_id=1, source_target_pairs={{0,1},{1,0},{2,3},{3,2},{4,5},{5,4},{6,7},{7,6},{8,9},{9,8},{10,11... | collective-permute-start | bytes 589832 | tf_op jit(solution)/shard_map/ppermute | solution.py:330
  117.0 5.8 %collective-permute-start.32 = (f32[64,768]{1,0:T(8,128)S(1)}, f32[64,768]{1,0:T(8,128)S(1)}, u32[]{:S(2)}, u32[]{:S(2)}) collective-permute-start(f32[64,768]{1,0:T(8,128)S(1)} %get-tuple-element.118.refs_4_.refs_7_.refs_2_), channel_id=1, source_target_pairs={{1,2},{2,1},{5,6},{6,5},{9,10},{10,9},{13,14},{14,13},{17,18},{18,... | collective-permute-start | bytes 589832 | tf_op jit(solution)/shard_map/ppermute | solution.py:333
  118.1 9.7 %collective-permute-start.39 = (f32[64,768]{1,0:T(8,128)S(1)}, f32[64,768]{1,0:T(8,128)S(1)}, u32[]{:S(2)}, u32[]{:S(2)}) collective-permute-start(f32[64,768]{1,0:T(8,128)S(1)} %get-tuple-element.130.refs_2_), channel_id=1, source_target_pairs={{0,1},{1,0},{2,3},{3,2},{4,5},{5,4},{6,7},{7,6},{8,9},{9,8},{10,11... | collective-permute-start | bytes 589832 | tf_op jit(solution)/shard_map/ppermute | solution.py:330
  120.8 8.6 %collective-permute-start.38 = (f32[64,768]{1,0:T(8,128)S(1)}, f32[64,768]{1,0:T(8,128)S(1)}, u32[]{:S(2)}, u32[]{:S(2)}) collective-permute-start(f32[64,768]{1,0:T(8,128)S(1)} %get-tuple-element.127.refs_7_.refs_0_), channel_id=1, source_target_pairs={{1,2},{2,1},{5,6},{6,5},{9,10},{10,9},{13,14},{14,13},{17,18},{18,... | collective-permute-start | bytes 589832 | tf_op jit(solution)/shard_map/ppermute | solution.py:333
  122.9 8.6 %collective-permute-start.37 = (f32[64,768]{1,0:T(8,128)S(1)}, f32[64,768]{1,0:T(8,128)S(1)}, u32[]{:S(2)}, u32[]{:S(2)}) collective-permute-start(f32[64,768]{1,0:T(8,128)S(1)} %get-tuple-element.129.refs_2_), channel_id=1, source_target_pairs={{0,1},{1,0},{2,3},{3,2},{4,5},{5,4},{6,7},{7,6},{8,9},{9,8},{10,11... | collective-permute-start | bytes 589832 | tf_op jit(solution)/shard_map/ppermute | solution.py:330
  126.6 4.9 %collective-permute-start.36 = (f32[64,768]{1,0:T(8,128)S(1)}, f32[64,768]{1,0:T(8,128)S(1)}, u32[]{:S(2)}, u32[]{:S(2)}) collective-permute-start(f32[64,768]{1,0:T(8,128)S(1)} %get-tuple-element.128.refs_5_.refs_0_), channel_id=1, source_target_pairs={{1,2},{2,1},{5,6},{6,5},{9,10},{10,9},{13,14},{14,13},{17,18},{18,... | collective-permute-start | bytes 589832 | tf_op jit(solution)/shard_map/ppermute | solution.py:333
  127.3 9.9 %collective-permute-start.30 = (f32[1,3,64,768]{3,2,1,0:T(8,128)S(1)}, f32[1,3,64,768]{3,2,1,0:T(8,128)S(1)}, u32[]{:S(2)}, u32[]{:S(2)}) collective-permute-start(f32[1,3,64,768]{3,2,1,0:T(8,128)S(1)} %get-tuple-element.120), channel_id=1, source_target_pairs={{0,16},{4,20},{8,24},{12,28},{16,0},{20,4},{24,8},{28,12},{1,17},{... | collective-permute-start | bytes 1769480 | tf_op jit(solution)/shard_map/ppermute | solution.py:423
  127.9 9.9 %collective-permute-start.31 = (f32[1,3,64,768]{3,2,1,0:T(8,128)S(1)}, f32[1,3,64,768]{3,2,1,0:T(8,128)S(1)}, u32[]{:S(2)}, u32[]{:S(2)}) collective-permute-start(f32[1,3,64,768]{3,2,1,0:T(8,128)S(1)} %get-tuple-element.122), channel_id=1, source_target_pairs={{0,8},{4,12},{8,0},{12,4},{16,24},{20,28},{24,16},{28,20},{1,9},{5... | collective-permute-start | bytes 1769480 | tf_op jit(solution)/shard_map/ppermute | solution.py:423
  129.4 9.5 %collective-permute-start.41 = (f32[64,768]{1,0:T(8,128)S(1)}, f32[64,768]{1,0:T(8,128)S(1)}, u32[]{:S(2)}, u32[]{:S(2)}) collective-permute-start(f32[64,768]{1,0:T(8,128)S(1)} %get-tuple-element.133.refs_5_.refs_0_), channel_id=1, source_target_pairs={{0,1},{1,0},{2,3},{3,2},{4,5},{5,4},{6,7},{7,6},{8,9},{9,8},{10,11... | collective-permute-start | bytes 589832 | tf_op jit(solution)/shard_map/ppermute | solution.py:330
  131.5 7.6 %collective-permute-start.40 = (f32[64,768]{1,0:T(8,128)S(1)}, f32[64,768]{1,0:T(8,128)S(1)}, u32[]{:S(2)}, u32[]{:S(2)}) collective-permute-start(f32[64,768]{1,0:T(8,128)S(1)} %get-tuple-element.134.refs_4_.refs_3_.refs_0_), channel_id=1, source_target_pairs={{0,1},{1,0},{2,3},{3,2},{4,5},{5,4},{6,7},{7,6},{8,9},{9,8},{10,11... | collective-permute-start | bytes 589832 | tf_op jit(solution)/shard_map/ppermute | solution.py:330

commit v6 on v5

--- a/solution.py
+++ b/solution.py
@@ -11,9 +11,9 @@
 BLK = 128
 LOW = -1e30
 LAGS = (4, 2, 2)
-HOME_SLOTS = (9, 17, 21)
-START_SLOT = 6
-SLOT_FLOPS = 4_000_000_000
+HOME_SLOTS = (11, 17, 21)
+START_SLOT = 8
+SLOT_FLOPS = 3_000_000_000
 
 
 def dot(a, b, ca, cb):
@@ -162,7 +162,8 @@
     lax.fori_loop(0, out_ref.shape[0] // BLK, block, 0)
 
 
-def term_kernel(meta, spread, width, member, owner, entries, z_ref, w_ref, lse_ref, pos_ref, dep, out_ref, flags, rows_ref):
+def term_kernel(meta, spread, width, part, parts, member, owner, entries, z_ref, w_ref, lse_ref, pos_ref, dep, *refs):
+    out_ref, flags, rows_ref = refs[-3:]
     meta.flags(owner, flags)
     me = lax.axis_index("cache")
     below = lax.broadcasted_iota(jnp.int32, (BLK, BLK), 0)
@@ -176,8 +177,10 @@
             out_ref[i, s] = jnp.zeros(out_ref.shape[2:], jnp.float32)
         return 0
 
-    lax.fori_loop(0, meta.groups, clear, 0)
+    if part == 0:
+        lax.fori_loop(0, meta.groups, clear, 0)
     n = entries[entries.shape[0] - 1]
+    trips = (n + width - 1) // width
 
     def step(it, _):
         found = []
@@ -210,7 +213,7 @@
                 out_ref[place, s] += acc[half * BLK:(half + 1) * BLK]
         return 0
 
-    lax.fori_loop(0, (n + width - 1) // width, step, 0)
+    lax.fori_loop(trips * part // parts, trips * (part + 1) // parts, step, 0)
 
 
 def params(mib):
@@ -272,18 +275,19 @@
     )(member, z, q, lse, dep)
 
 
-def run_terms(meta, member, owner, entries, z, w, lse, pos, spread, dep):
+def run_terms(meta, member, owner, entries, z, w, lse, pos, spread, dep, part=0, parts=1, old=None):
     group = 3
     return pl.pallas_call(
-        functools.partial(term_kernel, meta, spread, group),
-        in_specs=[SMEM, SMEM, SMEM, VMEM, VMEM, VMEM, VMEM, ANY],
+        functools.partial(term_kernel, meta, spread, group, part, parts),
+        in_specs=[SMEM, SMEM, SMEM, VMEM, VMEM, VMEM, VMEM, ANY] + [VMEM] * (part > 0),
+        input_output_aliases={8: 0} if part else {},
         out_specs=VMEM,
         out_shape=pltpu.VMEM((meta.groups, meta.steps, BLK, w.shape[2]), jnp.float32),
         scratch_shapes=[pltpu.SMEM((2 * meta.steps,), jnp.int32), pltpu.VMEM((meta.rows, BLK), jnp.int32)],
         compiler_params=params(10),
         cost_estimate=free(),
         name="query_term",
-    )(member, owner, entries, z, w, lse, pos, dep)
+    )(member, owner, entries, z, w, lse, pos, dep, *([old] if part else []))
 
 
 def small(kernel, inputs, n_deps, outs, name, aliases=None, flops=0):
@@ -332,16 +336,29 @@
     def swapped_mid(self, array):
         return lax.ppermute(array, "batch", [(1, 2), (2, 1)])
 
-    def begin(self, array, more):
-        self.swap_a, self.swap_b = self.swapped(array), self.swapped(more)
-
-    def early(self, array, dep):
+    def begin(self, a, b, c):
+        self.came = [self.swapped(x) for x in (a, b, c)]
+
+    def early(self, a, dep):
         def kernel(own, came, dep, out):
             out[...] = own[...] + came[...]
 
-        self.inner_a = small(kernel, [array, self.swap_a, dep], 1, [array.shape], "line_early")[0]
+        self.inner_a = small(kernel, [a, self.came[0], dep], 1, [a.shape], "line_early")[0]
         self.mid_a = self.swapped_mid(self.inner_a)
         return self.inner_a
+
+    def early_more(self, b, rest, dep):
+        def kernel(inner, mid, own, came, more, dep, total, away, inner_b):
+            at = lax.axis_index("batch")
+            total[...] = inner[...] + mid[...]
+            away[...] = jnp.where((at == 0) | (at == 3), more[:inner.shape[0], :], total[...])
+            inner_b[...] = own[...] + came[...]
+
+        inputs = [self.inner_a, self.mid_a, b, self.came[1], rest, dep]
+        self.total_a, away, self.inner_b = small(kernel, inputs, 1, [b.shape] * 3, "line_early_more")
+        self.came.append(self.swapped(away))
+        self.mid_b = self.swapped_mid(self.inner_b)
+        return self.inner_b
 
     def slot(self, t, chunk, deps):
         n, rows = self.n, self.rows
@@ -359,22 +376,24 @@
         aliases = {}
         if 0 <= u < n:
             array, first = chunk(u)
-            came, row = (self.swap_b, (u - self.lag_mid) * rows) if u < self.late else (self.swap[u], 0)
+            came, row = (self.came[u // 2], u % 2 * rows) if u < 8 else (self.swap[u], 0)
             plan.append(("in", take(array), first, take(came), row, give()))
         if 0 <= k < n:
-            pair, row = ((self.inner_a, self.mid_a), k * rows) if k < self.lag_mid else ((self.inner[k], self.mid[k]), 0)
+            pair, row = ((self.inner_b, self.mid_b), k % 2 * rows) if k < 4 else ((self.inner[k], self.mid[k]), 0)
             plan.append(("sum", take(pair[0]), take(pair[1]), row, give()))
         if t < n:
             array, first = chunk(t)
             plan.append(("away", take(array), first, give()))
         if 0 <= o < n:
-            args = take(self.total[o]), take(self.swap[o + self.late])
+            pair, row = ((self.total_a, self.came[3]), o * rows) if o < 2 else ((self.total[o], self.swap[o + self.late]), 0)
+            args = take(pair[0]), take(pair[1])
             old = None if self.out is None else take(self.out)
             new = give((n * rows, self.width))
             if old is not None:
                 aliases = {old: new}
             plan.append(("out",) + args + (new,))
         n_in = len(inputs)
+        row_out = row if 0 <= o < 2 else 0
 
         def kernel(*refs):
             at = lax.axis_index("batch")
@@ -391,7 +410,8 @@
                     value = refs[a[0]][a[1]:a[1] + rows, :]
                     res[a[2]][...] = value if total is None else jnp.where(end, value, total)
                 else:
-                    res[a[2]][o * rows:(o + 1) * rows, :] = jnp.where(end, refs[a[1]][...], refs[a[0]][...])
+                    here = slice(row_out, row_out + rows)
+                    res[a[2]][o * rows:(o + 1) * rows, :] = jnp.where(end, refs[a[1]][here, :], refs[a[0]][here, :])
 
         got = small(kernel, inputs + list(deps), len(deps), outs, "line_slot", aliases, SLOT_FLOPS)
         away = None
@@ -495,8 +515,9 @@
     meta = Meta(steps, groups, blocks, slab_blocks)
     me = lax.axis_index("cache")
     block_ids = me * blocks + jnp.arange(blocks, dtype=jnp.int32)
-    valid = jnp.arange(block_list.shape[2], dtype=jnp.int32)[None, None, :] < block_count[:, :, None]
-    member = jnp.any((block_list[..., None] == block_ids) & valid[..., None], axis=2)
+    used = jnp.arange(block_list.shape[2], dtype=jnp.int32)[None, None, :] < block_count[:, :, None]
+    ids = jnp.where(used, block_list, -1)
+    member = jnp.any(ids[..., None] == block_ids, axis=2)
     member = member.astype(jnp.int32).reshape(meta.rows, blocks)
     owner = refresh_owner.astype(jnp.int32)
 
@@ -505,11 +526,8 @@
 
     half = BLK // 2
     line = Line(2 * blocks, half, width)
-    parts = [line.lag_mid * half // BLK, line.lag_in * half // BLK]
-    parts.append(max(blocks - sum(parts), 0))
-    in_line = lax.axis_size("batch") == 4 and parts[2] > 0
-    if not in_line:
-        parts = [blocks]
+    in_line = lax.axis_size("batch") == 4 and blocks > 4
+    parts = [1, 1, 1, blocks - 3] if in_line else [blocks]
     grads, dep = [], lse
     for i, part in enumerate(parts):
         grads.append(run_grads(meta, member, z, q, lse, sum(parts[:i]), part, dep))
@@ -527,14 +545,18 @@
             row -= part * BLK
 
     if in_line:
-        line.begin(grads[0], grads[1])
-        dep = line.early(grads[0], grads[2])
+        line.begin(*grads[:3])
+        dep = line.early(grads[0], grads[3])
     if fast:
-        dep = run_terms(meta, member, owner, entries, z, w, lse, positives, True, dep)
+        terms = dep = run_terms(meta, member, owner, entries, z, w, lse, positives, True, dep, 0, 2)
+    if in_line:
+        dep = line.early_more(grads[1], grads[3], dep)
+    if fast:
+        dep = run_terms(meta, member, owner, entries, z, w, lse, positives, True, dep, 1, 2, terms)
         home = HomeSum(dep)
     if in_line:
         deps = [dep]
-        for t in range(line.late, line.slots):
+        for t in range(8, line.slots):
             deps = [line.slot(t, chunk, deps)]
             if fast and t == START_SLOT:
                 home.start(deps[0])

time: 142 us -> 139 us (0.979); the launches traced: 141 us -> 139 us
  starting transfers between devices: 71.6 us -> 68.6 us
  Pallas kernels: 42.3 us -> 44.4 us
    ppermute x5, waiting for transfers between devices: 3.47 us -> 1.24 us  [move(): return lax.ppermute(x, 'cache', [(i, i ^ bit) for i in range(self.n)])]
    ppermute x18, waiting for transfers between devices: 12.5 us -> 14.6 us  [swapped(): return lax.ppermute(array, 'batch', [(0, 1), (1, 0), (2, 3), (3, 2)])]
    pallas_call x1 -> x2, Pallas kernels: 15.3 us -> 16.6 us  [run_terms(): pl.pallas_call(functools.partial(term_kernel, meta, spread, group, part,...]
    pallas_call x3 -> x4, Pallas kernels: 10 us -> 10.7 us  [run_grads(): pl.pallas_call(functools.partial(grad_kernel, meta, first, group), in_spe...]
    ppermute x15 -> x14, starting transfers between devices: 9.96 us -> 9.44 us  [swapped_mid(): return lax.ppermute(array, 'batch', [(1, 2), (2, 1)])]
    unnamed x7 -> x9, local copies, waits for them, and re-layouts: 3.54 us -> 3.55 us
  transfers between devices with their start and end apart: 42 -> 41, of which waited for: 13 -> 12; matrix products, arithmetic and copies ran while one was open for 1% -> 1% of each run, Pallas kernels for 18% -> 20%
where the time goes in v6:
time: 139 us
  starting transfers between devices  68.6 us (49%)
  Pallas kernels  44.4 us (32%)
  waiting for transfers between devices  20.5 us (15%)
  local copies, waits for them, and re-layouts  3.55 us (3%)
    ppermute x18, starting transfers between devices, swapped(): return lax.ppermute(array, 'batch', [(0, 1), (1, 0), (2, 3), (3, 2)])  53 us
    pallas_call x2, Pallas kernels, run_terms(): pl.pallas_call(functools.partial(term_kernel, meta, spread, group, part,...  16.6 us
    ppermute x18, waiting for transfers between devices, swapped(): return lax.ppermute(array, 'batch', [(0, 1), (1, 0), (2, 3), (3, 2)])  14.6 us
    pallas_call x1, Pallas kernels, run_scores(): pl.pallas_call(functools.partial(scores_kernel, meta, group, 2.0 / math.s...  14.6 us
    pallas_call x4, Pallas kernels, run_grads(): pl.pallas_call(functools.partial(grad_kernel, meta, first, group), in_spe...  10.7 us
    ppermute x14, starting transfers between devices, swapped_mid(): return lax.ppermute(array, 'batch', [(1, 2), (2, 1)])  9.44 us
    ppermute x4, waiting for transfers between devices, exchange_lse(): lax.ppermute(lse, 'cache', [(i, i ^ p) for i in range(n)])  4.54 us
    ppermute x4, starting transfers between devices, exchange_lse(): lax.ppermute(lse, 'cache', [(i, i ^ p) for i in range(n)])  4.4 us
  transfers between devices with their start and end apart: 41, of which 12 were waited for; matrix products, arithmetic and copies ran while one was open for 1% of the time, Pallas kernels for 20%

profile of v6, /device:TPU:0, one launch (start us, length us, event | category | flops | bytes accessed | tf_op | source)
XLA Modules:
  0.0 139.4 jit_solution(2288371899419178536)
XLA Ops:
  0.6 0.8 fusion
  2.7 14.6 %scores.1 = (f32[24,8,128,128]{3,2,1,0:T(8,128)S(1)}, bf16[12,256,768]{2,1,0:T(8,128)(2,1)S(1)}, bf16[24,128,768]{2,1,0:T(8,128)(2,1)S(1)}, f32[24,128]{1,0:T(8,128)S(1)}, s32[102]{0:T(128)S(1)}) custom-call(s32[24,8]{1,0:T(8,128)S(1)} %convert_bitcast_fusion.member, s32[3]{0:T(128)S(1)} %copy-done.1, bf16[24,128,768]{2,1,0:T(8,128)(2,1)} %bitcast.3, ...), custom_call_target="tpu_custom_call" | custom-call | tf_op jit(solution)/shard_map/scores/pallas_call | solution.py:238
  17.3 1.2 collective-permute-done.refs_1_
  18.6 3.0 %collective-permute-start.2 = (f32[24,128]{1,0:T(8,128)S(1)}, f32[24,128]{1,0:T(8,128)S(1)}, u32[]{:S(2)}, u32[]{:S(2)}) collective-permute-start(f32[24,128]{1,0:T(8,128)S(1)} %merge_lse.2.refs_0_), channel_id=1, source_target_pairs={{0,16},{4,20},{8,24},{12,28},{16,0},{20,4},{24,8},{28,12},{1,17},{... | collective-permute-start | bytes 36872 | tf_op jit(solution)/shard_map/ppermute | solution.py:319
  21.6 1.2 collective-permute-start.3
  23.3 2.9 %collective-permute-done.3.refs_3_ = f32[24,128]{1,0:T(8,128)S(1)} collective-permute-done((f32[24,128]{1,0:T(8,128)S(1)}, f32[24,128]{1,0:T(8,128)S(1)}, u32[]{:S(2)}, u32[]{:S(2)}) %collective-permute-start.3) | collective-permute-done | bytes 12320 | tf_op jit(solution)/shard_map/ppermute | solution.py:319
  26.2 1.5 %cache_grad.4.dep.own = f32[128,768]{1,0:T(8,128)S(1)} custom-call(s32[24,8]{1,0:T(8,128)S(1)} %convert_bitcast_fusion.member, f32[24,8,128,128]{3,2,1,0:T(8,128)S(1)} %get-tuple-element.67.z_ref, bf16[24,128,768]{2,1,0:T(8,128)(2,1)S(1)} %get-tuple-element.70.q_ref, f32[24,128]{1,0:T(8,128)S(1)} %merge_lse.3.lse_ref.dep, f32[24,128]{1,0:T(8,128)S(1)} %merge_lse.3.lse_ref.dep), custom_call_target="tpu_custom_call" | custom-call | tf_op jit(solution)/shard_map/cache_grad/pallas_call | solution.py:266
  27.8 1.8 %collective-permute-start.4 = (f32[128,768]{1,0:T(8,128)S(1)}, f32[128,768]{1,0:T(8,128)S(1)}, u32[]{:S(2)}, u32[]{:S(2)}) collective-permute-start(f32[128,768]{1,0:T(8,128)S(1)} %cache_grad.4.dep.own), channel_id=1, source_target_pairs={{0,1},{1,0},{2,3},{3,2},{4,5},{5,4},{6,7},{7,6},{8,9},{9,8},{10,11... | collective-permute-start | bytes 1179656 | tf_op jit(solution)/shard_map/ppermute | solution.py:334
  29.6 1.9 %cache_grad.5.dep.own = f32[128,768]{1,0:T(8,128)S(1)} custom-call(s32[24,8]{1,0:T(8,128)S(1)} %convert_bitcast_fusion.member, f32[24,8,128,128]{3,2,1,0:T(8,128)S(1)} %get-tuple-element.67.z_ref, bf16[24,128,768]{2,1,0:T(8,128)(2,1)S(1)} %get-tuple-element.70.q_ref, f32[24,128]{1,0:T(8,128)S(1)} %merge_lse.3.lse_ref.dep, f32[128,768]{1,0:T(8,128)S(1)} %cache_grad.4.dep.own), custom_call_target="tpu_custom_call" | custom-call | tf_op jit(solution)/shard_map/cache_grad/pallas_call | solution.py:266
  31.5 1.5 %cache_grad.6.dep.refs_0_ = f32[128,768]{1,0:T(8,128)S(1)} custom-call(s32[24,8]{1,0:T(8,128)S(1)} %convert_bitcast_fusion.member, f32[24,8,128,128]{3,2,1,0:T(8,128)S(1)} %get-tuple-element.67.z_ref, bf16[24,128,768]{2,1,0:T(8,128)(2,1)S(1)} %get-tuple-element.70.q_ref, f32[24,128]{1,0:T(8,128)S(1)} %merge_lse.3.lse_ref.dep, f32[128,768]{1,0:T(8,128)S(1)} %cache_grad.5.dep.own), custom_call_target="tpu_custom_call" | custom-call | tf_op jit(solution)/shard_map/cache_grad/pallas_call | solution.py:266
  33.1 5.7 %cache_grad.7.dep.more.refs_4_.refs_0_ = f32[640,768]{1,0:T(8,128)S(1)} custom-call(s32[24,8]{1,0:T(8,128)S(1)} %convert_bitcast_fusion.member, f32[24,8,128,128]{3,2,1,0:T(8,128)S(1)} %get-tuple-element.67.z_ref, bf16[24,128,768]{2,1,0:T(8,128)(2,1)S(1)} %get-tuple-element.70.q_ref, f32[24,128]{1,0:T(8,128)S(1)} %merge_lse.3.lse_ref.dep, ...), custom_call_target="tpu_custom_call" | custom-call | tf_op jit(solution)/shard_map/cache_grad/pallas_call | solution.py:266
  38.8 1.0 collective-permute-done.4.came
  39.9 0.7 collective-permute-start.5
  40.6 5.2 %collective-permute-start.7 = (f32[128,768]{1,0:T(8,128)S(1)}, f32[128,768]{1,0:T(8,128)S(1)}, u32[]{:S(2)}, u32[]{:S(2)}) collective-permute-start(f32[128,768]{1,0:T(8,128)S(1)} %cache_grad.6.dep.refs_0_), channel_id=1, source_target_pairs={{0,1},{1,0},{2,3},{3,2},{4,5},{5,4},{6,7},{7,6},{8,9},{9,8},{10,11... | collective-permute-start | bytes 1179656 | tf_op jit(solution)/shard_map/ppermute | solution.py:334
  45.9 8.6 %query_term.2.dep.refs_0_ = f32[8,3,128,768]{3,2,1,0:T(8,128)S(1)} custom-call(s32[24,8]{1,0:T(8,128)S(1)} %convert_bitcast_fusion.member, s32[3]{0:T(128)S(1)} %copy-done.2, s32[102]{0:T(128)S(1)} %get-tuple-element.66.entries, f32[24,8,128,128]{3,2,1,0:T(8,128)S(1)} %get-tuple-element.67.z_ref, bf16[12,256,768]{2,1,0:T(8,128)(2,1)S(1)} %get-tuple-element.68.w_ref, ...), custom_call_target="tpu_custom_call" | custom-call | tf_op jit(solution)/shard_map/query_term/pallas_call | solution.py:280
  54.7 0.7 collective-permute-start.8
  55.3 1.2 collective-permute-start.9
  56.5 8.0 %query_term.3.refs_7_.terms.refs_0_ = f32[8,3,128,768]{3,2,1,0:T(8,128)S(1)} custom-call(s32[24,8]{1,0:T(8,128)S(1)} %convert_bitcast_fusion.member, s32[3]{0:T(128)S(1)} %copy-done.2, s32[102]{0:T(128)S(1)} %get-tuple-element.66.entries, f32[24,8,128,128]{3,2,1,0:T(8,128)S(1)} %get-tuple-element.67.z_ref, ...), custom_call_target="tpu_custom_call", output_to_operand_aliasing={{}: (8, {})} | custom-call | tf_op jit(solution)/shard_map/query_term/pallas_call | solution.py:280
  65.1 0.7 collective-permute-start.13
  65.8 4.5 %collective-permute-start.14 = (f32[64,768]{1,0:T(8,128)S(1)}, f32[64,768]{1,0:T(8,128)S(1)}, u32[]{:S(2)}, u32[]{:S(2)}) collective-permute-start(f32[64,768]{1,0:T(8,128)S(1)} %get-tuple-element.80), channel_id=1, source_target_pairs={{0,1},{1,0},{2,3},{3,2},{4,5},{5,4},{6,7},{7,6},{8,9},{9,8},{10,11... | collective-permute-start | bytes 589832 | tf_op jit(solution)/shard_map/ppermute | solution.py:334
  70.3 0.7 collective-permute-start.11
  71.0 1.8 %collective-permute-start.12 = (f32[64,768]{1,0:T(8,128)S(1)}, f32[64,768]{1,0:T(8,128)S(1)}, u32[]{:S(2)}, u32[]{:S(2)}) collective-permute-start(f32[64,768]{1,0:T(8,128)S(1)} %get-tuple-element.78), channel_id=1, source_target_pairs={{0,1},{1,0},{2,3},{3,2},{4,5},{5,4},{6,7},{7,6},{8,9},{9,8},{10,11... | collective-permute-start | bytes 589832 | tf_op jit(solution)/shard_map/ppermute | solution.py:334
  72.8 3.1 %collective-permute-done.14.refs_6_.refs_1_ = f32[64,768]{1,0:T(8,128)S(1)} collective-permute-done((f32[64,768]{1,0:T(8,128)S(1)}, f32[64,768]{1,0:T(8,128)S(1)}, u32[]{:S(2)}, u32[]{:S(2)}) %collective-permute-start.14) | collective-permute-done | bytes 196640 | tf_op jit(solution)/shard_map/ppermute | solution.py:334
  76.0 0.7 collective-permute-start.19
  76.7 3.4 %collective-permute-start.20 = (f32[64,768]{1,0:T(8,128)S(1)}, f32[64,768]{1,0:T(8,128)S(1)}, u32[]{:S(2)}, u32[]{:S(2)}) collective-permute-start(f32[64,768]{1,0:T(8,128)S(1)} %get-tuple-element.92), channel_id=1, source_target_pairs={{0,1},{1,0},{2,3},{3,2},{4,5},{5,4},{6,7},{7,6},{8,9},{9,8},{10,11... | collective-permute-start | bytes 589832 | tf_op jit(solution)/shard_map/ppermute | solution.py:334
  80.1 0.7 collective-permute-start.17
  80.8 3.3 %collective-permute-start.18 = (f32[64,768]{1,0:T(8,128)S(1)}, f32[64,768]{1,0:T(8,128)S(1)}, u32[]{:S(2)}, u32[]{:S(2)}) collective-permute-start(f32[64,768]{1,0:T(8,128)S(1)} %get-tuple-element.90), channel_id=1, source_target_pairs={{0,1},{1,0},{2,3},{3,2},{4,5},{5,4},{6,7},{7,6},{8,9},{9,8},{10,11... | collective-permute-start | bytes 589832 | tf_op jit(solution)/shard_map/ppermute | solution.py:334
  85.5 4.7 %collective-permute-start.24 = (f32[64,768]{1,0:T(8,128)S(1)}, f32[64,768]{1,0:T(8,128)S(1)}, u32[]{:S(2)}, u32[]{:S(2)}) collective-permute-start(f32[64,768]{1,0:T(8,128)S(1)} %get-tuple-element.100), channel_id=1, source_target_pairs={{0,1},{1,0},{2,3},{3,2},{4,5},{5,4},{6,7},{7,6},{8,9},{9,8},{10,11... | collective-permute-start | bytes 589832 | tf_op jit(solution)/shard_map/ppermute | solution.py:334
  92.3 2.4 %collective-permute-done.24.refs_6_.refs_1_ = f32[64,768]{1,0:T(8,128)S(1)} collective-permute-done((f32[64,768]{1,0:T(8,128)S(1)}, f32[64,768]{1,0:T(8,128)S(1)}, u32[]{:S(2)}, u32[]{:S(2)}) %collective-permute-start.24) | collective-permute-done | bytes 196640 | tf_op jit(solution)/shard_map/ppermute | solution.py:334
  95.4 1.5 %collective-permute-done.21.refs_6_.refs_1_ = f32[64,768]{1,0:T(8,128)S(1)} collective-permute-done((f32[64,768]{1,0:T(8,128)S(1)}, f32[64,768]{1,0:T(8,128)S(1)}, u32[]{:S(2)}, u32[]{:S(2)}) %collective-permute-start.21) | collective-permute-done | bytes 196640 | tf_op jit(solution)/shard_map/ppermute | solution.py:334
  96.9 3.3 %collective-permute-start.28 = (f32[64,768]{1,0:T(8,128)S(1)}, f32[64,768]{1,0:T(8,128)S(1)}, u32[]{:S(2)}, u32[]{:S(2)}) collective-permute-start(f32[64,768]{1,0:T(8,128)S(1)} %get-tuple-element.108), channel_id=1, source_target_pairs={{0,1},{1,0},{2,3},{3,2},{4,5},{5,4},{6,7},{7,6},{8,9},{9,8},{10,11... | collective-permute-start | bytes 589832 | tf_op jit(solution)/shard_map/ppermute | solution.py:334
  100.9 6.6 %collective-permute-start.26 = (f32[64,768]{1,0:T(8,128)S(1)}, f32[64,768]{1,0:T(8,128)S(1)}, u32[]{:S(2)}, u32[]{:S(2)}) collective-permute-start(f32[64,768]{1,0:T(8,128)S(1)} %get-tuple-element.106), channel_id=1, source_target_pairs={{0,1},{1,0},{2,3},{3,2},{4,5},{5,4},{6,7},{7,6},{8,9},{9,8},{10,11... | collective-permute-start | bytes 589832 | tf_op jit(solution)/shard_map/ppermute | solution.py:334
  107.6 0.7 collective-permute-start.33
  108.3 3.4 %collective-permute-start.34 = (f32[64,768]{1,0:T(8,128)S(1)}, f32[64,768]{1,0:T(8,128)S(1)}, u32[]{:S(2)}, u32[]{:S(2)}) collective-permute-start(f32[64,768]{1,0:T(8,128)S(1)} %get-tuple-element.118.refs_4_), channel_id=1, source_target_pairs={{0,1},{1,0},{2,3},{3,2},{4,5},{5,4},{6,7},{7,6},{8,9},{9,8},{10,11... | collective-permute-start | bytes 589832 | tf_op jit(solution)/shard_map/ppermute | solution.py:334
  111.7 1.0 collective-permute-done.26.refs_5_.refs_1_
  112.7 0.7 collective-permute-start.31
  113.4 1.2 collective-permute-done.15.refs_1_
  114.6 2.7 %collective-permute-start.32 = (f32[64,768]{1,0:T(8,128)S(1)}, f32[64,768]{1,0:T(8,128)S(1)}, u32[]{:S(2)}, u32[]{:S(2)}) collective-permute-start(f32[64,768]{1,0:T(8,128)S(1)} %get-tuple-element.117.refs_4_), channel_id=1, source_target_pairs={{0,1},{1,0},{2,3},{3,2},{4,5},{5,4},{6,7},{7,6},{8,9},{9,8},{10,11... | collective-permute-start | bytes 589832 | tf_op jit(solution)/shard_map/ppermute | solution.py:334
  117.7 0.7 collective-permute-start.37
  118.4 2.9 %collective-permute-start.38 = (f32[64,768]{1,0:T(8,128)S(1)}, f32[64,768]{1,0:T(8,128)S(1)}, u32[]{:S(2)}, u32[]{:S(2)}) collective-permute-start(f32[64,768]{1,0:T(8,128)S(1)} %get-tuple-element.124.refs_2_), channel_id=1, source_target_pairs={{0,1},{1,0},{2,3},{3,2},{4,5},{5,4},{6,7},{7,6},{8,9},{9,8},{10,11... | collective-permute-start | bytes 589832 | tf_op jit(solution)/shard_map/ppermute | solution.py:334
  122.3 0.7 collective-permute-start.35
  122.9 3.7 %collective-permute-start.36 = (f32[64,768]{1,0:T(8,128)S(1)}, f32[64,768]{1,0:T(8,128)S(1)}, u32[]{:S(2)}, u32[]{:S(2)}) collective-permute-start(f32[64,768]{1,0:T(8,128)S(1)} %get-tuple-element.123.refs_2_), channel_id=1, source_target_pairs={{0,1},{1,0},{2,3},{3,2},{4,5},{5,4},{6,7},{7,6},{8,9},{9,8},{10,11... | collective-permute-start | bytes 589832 | tf_op jit(solution)/shard_map/ppermute | solution.py:334
  127.2 2.1 %collective-permute-start.40 = (f32[64,768]{1,0:T(8,128)S(1)}, f32[64,768]{1,0:T(8,128)S(1)}, u32[]{:S(2)}, u32[]{:S(2)}) collective-permute-start(f32[64,768]{1,0:T(8,128)S(1)} %get-tuple-element.127.refs_5_.refs_0_), channel_id=1, source_target_pairs={{0,1},{1,0},{2,3},{3,2},{4,5},{5,4},{6,7},{7,6},{8,9},{9,8},{10,11... | collective-permute-start | bytes 589832 | tf_op jit(solution)/shard_map/ppermute | solution.py:334
  129.3 2.6 %collective-permute-done.36.refs_3_ = f32[64,768]{1,0:T(8,128)S(1)} collective-permute-done((f32[64,768]{1,0:T(8,128)S(1)}, f32[64,768]{1,0:T(8,128)S(1)}, u32[]{:S(2)}, u32[]{:S(2)}) %collective-permute-start.36) | collective-permute-done | bytes 196640 | tf_op jit(solution)/shard_map/ppermute | solution.py:334
  132.0 1.8 %collective-permute-start.39 = (f32[64,768]{1,0:T(8,128)S(1)}, f32[64,768]{1,0:T(8,128)S(1)}, u32[]{:S(2)}, u32[]{:S(2)}) collective-permute-start(f32[64,768]{1,0:T(8,128)S(1)} %get-tuple-element.128.refs_4_.refs_3_.refs_0_), channel_id=1, source_target_pairs={{0,1},{1,0},{2,3},{3,2},{4,5},{5,4},{6,7},{7,6},{8,9},{9,8},{10,11... | collective-permute-start | bytes 589832 | tf_op jit(solution)/shard_map/ppermute | solution.py:334
  133.9 1.0 copy.41
  135.2 2.5 %collective-permute-done.39.refs_1_ = f32[64,768]{1,0:T(8,128)S(1)} collective-permute-done((f32[64,768]{1,0:T(8,128)S(1)}, f32[64,768]{1,0:T(8,128)S(1)}, u32[]{:S(2)}, u32[]{:S(2)}) %collective-permute-start.39) | collective-permute-done | bytes 196640 | tf_op jit(solution)/shard_map/ppermute | solution.py:334
  137.7 1.7 %copy.42 = f32[1024,768]{1,0:T(8,128)} copy(f32[1024,768]{1,0:T(8,128)S(1)} %line_slot.31) | data formatting | bytes 6291456
  (78 shorter events, 10.0 us)
Async XLA Ops:
  2.0 0.7 copy-start.1
  17.2 1.2 collective-permute-start
  18.5 4.3 %collective-permute-start.1 = (f32[24,128]{1,0:T(8,128)S(1)}, f32[24,128]{1,0:T(8,128)S(1)}, u32[]{:S(2)}, u32[]{:S(2)}) collective-permute-start(f32[24,128]{1,0:T(8,128)S(1)} %merge_lse.2.refs_0_), channel_id=1, source_target_pairs={{0,8},{4,12},{8,0},{12,4},{16,24},{20,28},{24,16},{28,20},{1,9},{5... | collective-permute-start | bytes 36872 | tf_op jit(solution)/shard_map/ppermute | solution.py:319
  18.6 4.7 %collective-permute-start.2 = (f32[24,128]{1,0:T(8,128)S(1)}, f32[24,128]{1,0:T(8,128)S(1)}, u32[]{:S(2)}, u32[]{:S(2)}) collective-permute-start(f32[24,128]{1,0:T(8,128)S(1)} %merge_lse.2.refs_0_), channel_id=1, source_target_pairs={{0,16},{4,20},{8,24},{12,28},{16,0},{20,4},{24,8},{28,12},{1,17},{... | collective-permute-start | bytes 36872 | tf_op jit(solution)/shard_map/ppermute | solution.py:319
  21.6 4.6 %collective-permute-start.3 = (f32[24,128]{1,0:T(8,128)S(1)}, f32[24,128]{1,0:T(8,128)S(1)}, u32[]{:S(2)}, u32[]{:S(2)}) collective-permute-start(f32[24,128]{1,0:T(8,128)S(1)} %merge_lse.2.refs_0_), channel_id=1, source_target_pairs={{0,24},{4,28},{8,16},{12,20},{16,8},{20,12},{24,0},{28,4},{1,25},{... | collective-permute-start | bytes 36872 | tf_op jit(solution)/shard_map/ppermute | solution.py:319
  27.8 12.1 %collective-permute-start.4 = (f32[128,768]{1,0:T(8,128)S(1)}, f32[128,768]{1,0:T(8,128)S(1)}, u32[]{:S(2)}, u32[]{:S(2)}) collective-permute-start(f32[128,768]{1,0:T(8,128)S(1)} %cache_grad.4.dep.own), channel_id=1, source_target_pairs={{0,1},{1,0},{2,3},{3,2},{4,5},{5,4},{6,7},{7,6},{8,9},{9,8},{10,11... | collective-permute-start | bytes 1179656 | tf_op jit(solution)/shard_map/ppermute | solution.py:334
  33.0 21.5 %collective-permute-start.6 = (f32[128,768]{1,0:T(8,128)S(1)}, f32[128,768]{1,0:T(8,128)S(1)}, u32[]{:S(2)}, u32[]{:S(2)}) collective-permute-start(f32[128,768]{1,0:T(8,128)S(1)} %cache_grad.5.dep.own), channel_id=1, source_target_pairs={{0,1},{1,0},{2,3},{3,2},{4,5},{5,4},{6,7},{7,6},{8,9},{9,8},{10,11... | collective-permute-start | bytes 1179656 | tf_op jit(solution)/shard_map/ppermute | solution.py:334
  38.8 7.0 %copy-start = (s32[3,1024]{1,0:T(4,128)S(1)}, s32[3,1024]{1,0:T(4,128)}, u32[]{:S(2)}) copy-start(s32[3,1024]{1,0:T(4,128)} %pos_ref.3) | copy-start | bytes 36868
  38.8 7.0 %copy-start.2 = (s32[3]{0:T(128)S(1)}, s32[3]{0:T(128)}, u32[]{:S(2)}) copy-start(s32[3]{0:T(128)} %owner.5) | copy-start | bytes 40
  39.9 14.6 %collective-permute-start.5 = (f32[128,768]{1,0:T(8,128)S(1)}, f32[128,768]{1,0:T(8,128)S(1)}, u32[]{:S(2)}, u32[]{:S(2)}) collective-permute-start(f32[128,768]{1,0:T(8,128)S(1)} %line_early.1.dep.inner), channel_id=1, source_target_pairs={{1,2},{2,1},{5,6},{6,5},{9,10},{10,9},{13,14},{14,13},{17,18},{18,... | collective-permute-start | bytes 1179656 | tf_op jit(solution)/shard_map/ppermute | solution.py:337
  40.6 24.0 %collective-permute-start.7 = (f32[128,768]{1,0:T(8,128)S(1)}, f32[128,768]{1,0:T(8,128)S(1)}, u32[]{:S(2)}, u32[]{:S(2)}) collective-permute-start(f32[128,768]{1,0:T(8,128)S(1)} %cache_grad.6.dep.refs_0_), channel_id=1, source_target_pairs={{0,1},{1,0},{2,3},{3,2},{4,5},{5,4},{6,7},{7,6},{8,9},{9,8},{10,11... | collective-permute-start | bytes 1179656 | tf_op jit(solution)/shard_map/ppermute | solution.py:334
  54.7 9.9 %collective-permute-start.8 = (f32[128,768]{1,0:T(8,128)S(1)}, f32[128,768]{1,0:T(8,128)S(1)}, u32[]{:S(2)}, u32[]{:S(2)}) collective-permute-start(f32[128,768]{1,0:T(8,128)S(1)} %get-tuple-element.71.dep.refs_2_), channel_id=1, source_target_pairs={{1,2},{2,1},{5,6},{6,5},{9,10},{10,9},{13,14},{14,13},{17,18},{18,... | collective-permute-start | bytes 1179656 | tf_op jit(solution)/shard_map/ppermute | solution.py:337
  55.3 9.3 %collective-permute-start.9 = (f32[128,768]{1,0:T(8,128)S(1)}, f32[128,768]{1,0:T(8,128)S(1)}, u32[]{:S(2)}, u32[]{:S(2)}) collective-permute-start(f32[128,768]{1,0:T(8,128)S(1)} %get-tuple-element.73), channel_id=1, source_target_pairs={{0,1},{1,0},{2,3},{3,2},{4,5},{5,4},{6,7},{7,6},{8,9},{9,8},{10,11... | collective-permute-start | bytes 1179656 | tf_op jit(solution)/shard_map/ppermute | solution.py:334
  65.0 19.2 %collective-permute-start.10 = (f32[4,3,128,768]{3,2,1,0:T(8,128)S(1)}, f32[4,3,128,768]{3,2,1,0:T(8,128)S(1)}, u32[]{:S(2)}, u32[]{:S(2)}) collective-permute-start(f32[4,3,128,768]{3,2,1,0:T(8,128)S(1)} %home_start.1), channel_id=1, source_target_pairs={{0,4},{4,0},{8,12},{12,8},{16,20},{20,16},{24,28},{28,24},{1,5},{5... | collective-permute-start | bytes 14155784 | tf_op jit(solution)/shard_map/ppermute | solution.py:443
  65.1 7.7 %collective-permute-start.13 = (f32[64,768]{1,0:T(8,128)S(1)}, f32[64,768]{1,0:T(8,128)S(1)}, u32[]{:S(2)}, u32[]{:S(2)}) collective-permute-start(f32[64,768]{1,0:T(8,128)S(1)} %get-tuple-element.74.dep.refs_8_.refs_2_), channel_id=1, source_target_pairs={{1,2},{2,1},{5,6},{6,5},{9,10},{10,9},{13,14},{14,13},{17,18},{18,... | collective-permute-start | bytes 589832 | tf_op jit(solution)/shard_map/ppermute | solution.py:337
  65.8 10.1 %collective-permute-start.14 = (f32[64,768]{1,0:T(8,128)S(1)}, f32[64,768]{1,0:T(8,128)S(1)}, u32[]{:S(2)}, u32[]{:S(2)}) collective-permute-start(f32[64,768]{1,0:T(8,128)S(1)} %get-tuple-element.80), channel_id=1, source_target_pairs={{0,1},{1,0},{2,3},{3,2},{4,5},{5,4},{6,7},{7,6},{8,9},{9,8},{10,11... | collective-permute-start | bytes 589832 | tf_op jit(solution)/shard_map/ppermute | solution.py:334
  70.3 9.7 %collective-permute-start.11 = (f32[64,768]{1,0:T(8,128)S(1)}, f32[64,768]{1,0:T(8,128)S(1)}, u32[]{:S(2)}, u32[]{:S(2)}) collective-permute-start(f32[64,768]{1,0:T(8,128)S(1)} %get-tuple-element.76.refs_8_.refs_2_), channel_id=1, source_target_pairs={{1,2},{2,1},{5,6},{6,5},{9,10},{10,9},{13,14},{14,13},{17,18},{18,... | collective-permute-start | bytes 589832 | tf_op jit(solution)/shard_map/ppermute | solution.py:337
  71.0 9.1 %collective-permute-start.12 = (f32[64,768]{1,0:T(8,128)S(1)}, f32[64,768]{1,0:T(8,128)S(1)}, u32[]{:S(2)}, u32[]{:S(2)}) collective-permute-start(f32[64,768]{1,0:T(8,128)S(1)} %get-tuple-element.78), channel_id=1, source_target_pairs={{0,1},{1,0},{2,3},{3,2},{4,5},{5,4},{6,7},{7,6},{8,9},{9,8},{10,11... | collective-permute-start | bytes 589832 | tf_op jit(solution)/shard_map/ppermute | solution.py:334
  76.0 8.7 %collective-permute-start.19 = (f32[64,768]{1,0:T(8,128)S(1)}, f32[64,768]{1,0:T(8,128)S(1)}, u32[]{:S(2)}, u32[]{:S(2)}) collective-permute-start(f32[64,768]{1,0:T(8,128)S(1)} %get-tuple-element.83.refs_8_.refs_2_), channel_id=1, source_target_pairs={{1,2},{2,1},{5,6},{6,5},{9,10},{10,9},{13,14},{14,13},{17,18},{18,... | collective-permute-start | bytes 589832 | tf_op jit(solution)/shard_map/ppermute | solution.py:337
  76.7 8.1 %collective-permute-start.20 = (f32[64,768]{1,0:T(8,128)S(1)}, f32[64,768]{1,0:T(8,128)S(1)}, u32[]{:S(2)}, u32[]{:S(2)}) collective-permute-start(f32[64,768]{1,0:T(8,128)S(1)} %get-tuple-element.92), channel_id=1, source_target_pairs={{0,1},{1,0},{2,3},{3,2},{4,5},{5,4},{6,7},{7,6},{8,9},{9,8},{10,11... | collective-permute-start | bytes 589832 | tf_op jit(solution)/shard_map/ppermute | solution.py:334
  80.1 10.5 %collective-permute-start.17 = (f32[64,768]{1,0:T(8,128)S(1)}, f32[64,768]{1,0:T(8,128)S(1)}, u32[]{:S(2)}, u32[]{:S(2)}) collective-permute-start(f32[64,768]{1,0:T(8,128)S(1)} %get-tuple-element.84.refs_2_.refs_8_), channel_id=1, source_target_pairs={{1,2},{2,1},{5,6},{6,5},{9,10},{10,9},{13,14},{14,13},{17,18},{18,... | collective-permute-start | bytes 589832 | tf_op jit(solution)/shard_map/ppermute | solution.py:337
  80.8 10.3 %collective-permute-start.18 = (f32[64,768]{1,0:T(8,128)S(1)}, f32[64,768]{1,0:T(8,128)S(1)}, u32[]{:S(2)}, u32[]{:S(2)}) collective-permute-start(f32[64,768]{1,0:T(8,128)S(1)} %get-tuple-element.90), channel_id=1, source_target_pairs={{0,1},{1,0},{2,3},{3,2},{4,5},{5,4},{6,7},{7,6},{8,9},{9,8},{10,11... | collective-permute-start | bytes 589832 | tf_op jit(solution)/shard_map/ppermute | solution.py:334
  84.8 6.8 %collective-permute-start.23 = (f32[64,768]{1,0:T(8,128)S(1)}, f32[64,768]{1,0:T(8,128)S(1)}, u32[]{:S(2)}, u32[]{:S(2)}) collective-permute-start(f32[64,768]{1,0:T(8,128)S(1)} %get-tuple-element.95.refs_8_.refs_2_), channel_id=1, source_target_pairs={{1,2},{2,1},{5,6},{6,5},{9,10},{10,9},{13,14},{14,13},{17,18},{18,... | collective-permute-start | bytes 589832 | tf_op jit(solution)/shard_map/ppermute | solution.py:337
  85.5 9.1 %collective-permute-start.24 = (f32[64,768]{1,0:T(8,128)S(1)}, f32[64,768]{1,0:T(8,128)S(1)}, u32[]{:S(2)}, u32[]{:S(2)}) collective-permute-start(f32[64,768]{1,0:T(8,128)S(1)} %get-tuple-element.100), channel_id=1, source_target_pairs={{0,1},{1,0},{2,3},{3,2},{4,5},{5,4},{6,7},{7,6},{8,9},{9,8},{10,11... | collective-permute-start | bytes 589832 | tf_op jit(solution)/shard_map/ppermute | solution.py:334
  90.2 24.4 %collective-permute-start.15 = (f32[2,3,64,768]{3,2,1,0:T(8,128)S(1)}, f32[2,3,64,768]{3,2,1,0:T(8,128)S(1)}, u32[]{:S(2)}, u32[]{:S(2)}) collective-permute-start(f32[2,3,64,768]{3,2,1,0:T(8,128)S(1)} %get-tuple-element.86), channel_id=1, source_target_pairs={{0,8},{4,12},{8,0},{12,4},{16,24},{20,28},{24,16},{28,20},{1,9},{5... | collective-permute-start | bytes 3538952 | tf_op jit(solution)/shard_map/ppermute | solution.py:443
  90.6 26.8 %collective-permute-start.16 = (f32[2,3,64,768]{3,2,1,0:T(8,128)S(1)}, f32[2,3,64,768]{3,2,1,0:T(8,128)S(1)}, u32[]{:S(2)}, u32[]{:S(2)}) collective-permute-start(f32[2,3,64,768]{3,2,1,0:T(8,128)S(1)} %get-tuple-element.88), channel_id=1, source_target_pairs={{0,16},{4,20},{8,24},{12,28},{16,0},{20,4},{24,8},{28,12},{1,17},{... | collective-permute-start | bytes 3538952 | tf_op jit(solution)/shard_map/ppermute | solution.py:443
  91.2 5.7 %collective-permute-start.21 = (f32[64,768]{1,0:T(8,128)S(1)}, f32[64,768]{1,0:T(8,128)S(1)}, u32[]{:S(2)}, u32[]{:S(2)}) collective-permute-start(f32[64,768]{1,0:T(8,128)S(1)} %get-tuple-element.96), channel_id=1, source_target_pairs={{0,1},{1,0},{2,3},{3,2},{4,5},{5,4},{6,7},{7,6},{8,9},{9,8},{10,11... | collective-permute-start | bytes 589832 | tf_op jit(solution)/shard_map/ppermute | solution.py:334
  91.6 8.6 %collective-permute-start.22 = (f32[64,768]{1,0:T(8,128)S(1)}, f32[64,768]{1,0:T(8,128)S(1)}, u32[]{:S(2)}, u32[]{:S(2)}) collective-permute-start(f32[64,768]{1,0:T(8,128)S(1)} %get-tuple-element.97.refs_8_.refs_2_), channel_id=1, source_target_pairs={{1,2},{2,1},{5,6},{6,5},{9,10},{10,9},{13,14},{14,13},{17,18},{18,... | collective-permute-start | bytes 589832 | tf_op jit(solution)/shard_map/ppermute | solution.py:337
  94.7 6.2 %collective-permute-start.27 = (f32[64,768]{1,0:T(8,128)S(1)}, f32[64,768]{1,0:T(8,128)S(1)}, u32[]{:S(2)}, u32[]{:S(2)}) collective-permute-start(f32[64,768]{1,0:T(8,128)S(1)} %get-tuple-element.103.refs_8_.refs_2_), channel_id=1, source_target_pairs={{1,2},{2,1},{5,6},{6,5},{9,10},{10,9},{13,14},{14,13},{17,18},{18,... | collective-permute-start | bytes 589832 | tf_op jit(solution)/shard_map/ppermute | solution.py:337
  96.9 10.6 %collective-permute-start.28 = (f32[64,768]{1,0:T(8,128)S(1)}, f32[64,768]{1,0:T(8,128)S(1)}, u32[]{:S(2)}, u32[]{:S(2)}) collective-permute-start(f32[64,768]{1,0:T(8,128)S(1)} %get-tuple-element.108), channel_id=1, source_target_pairs={{0,1},{1,0},{2,3},{3,2},{4,5},{5,4},{6,7},{7,6},{8,9},{9,8},{10,11... | collective-permute-start | bytes 589832 | tf_op jit(solution)/shard_map/ppermute | solution.py:334
  100.2 8.0 %collective-permute-start.25 = (f32[64,768]{1,0:T(8,128)S(1)}, f32[64,768]{1,0:T(8,128)S(1)}, u32[]{:S(2)}, u32[]{:S(2)}) collective-permute-start(f32[64,768]{1,0:T(8,128)S(1)} %get-tuple-element.104.refs_7_.refs_2_), channel_id=1, source_target_pairs={{1,2},{2,1},{5,6},{6,5},{9,10},{10,9},{13,14},{14,13},{17,18},{18,... | collective-permute-start | bytes 589832 | tf_op jit(solution)/shard_map/ppermute | solution.py:337
  100.9 11.7 %collective-permute-start.26 = (f32[64,768]{1,0:T(8,128)S(1)}, f32[64,768]{1,0:T(8,128)S(1)}, u32[]{:S(2)}, u32[]{:S(2)}) collective-permute-start(f32[64,768]{1,0:T(8,128)S(1)} %get-tuple-element.106), channel_id=1, source_target_pairs={{0,1},{1,0},{2,3},{3,2},{4,5},{5,4},{6,7},{7,6},{8,9},{9,8},{10,11... | collective-permute-start | bytes 589832 | tf_op jit(solution)/shard_map/ppermute | solution.py:334
  107.6 10.1 %collective-permute-start.33 = (f32[64,768]{1,0:T(8,128)S(1)}, f32[64,768]{1,0:T(8,128)S(1)}, u32[]{:S(2)}, u32[]{:S(2)}) collective-permute-start(f32[64,768]{1,0:T(8,128)S(1)} %get-tuple-element.111.refs_7_.refs_2_), channel_id=1, source_target_pairs={{1,2},{2,1},{5,6},{6,5},{9,10},{10,9},{13,14},{14,13},{17,18},{18,... | collective-permute-start | bytes 589832 | tf_op jit(solution)/shard_map/ppermute | solution.py:337
  108.3 9.4 %collective-permute-start.34 = (f32[64,768]{1,0:T(8,128)S(1)}, f32[64,768]{1,0:T(8,128)S(1)}, u32[]{:S(2)}, u32[]{:S(2)}) collective-permute-start(f32[64,768]{1,0:T(8,128)S(1)} %get-tuple-element.118.refs_4_), channel_id=1, source_target_pairs={{0,1},{1,0},{2,3},{3,2},{4,5},{5,4},{6,7},{7,6},{8,9},{9,8},{10,11... | collective-permute-start | bytes 589832 | tf_op jit(solution)/shard_map/ppermute | solution.py:334
  112.7 8.9 %collective-permute-start.31 = (f32[64,768]{1,0:T(8,128)S(1)}, f32[64,768]{1,0:T(8,128)S(1)}, u32[]{:S(2)}, u32[]{:S(2)}) collective-permute-start(f32[64,768]{1,0:T(8,128)S(1)} %get-tuple-element.112.refs_4_.refs_7_.refs_2_), channel_id=1, source_target_pairs={{1,2},{2,1},{5,6},{6,5},{9,10},{10,9},{13,14},{14,13},{17,18},{18,... | collective-permute-start | bytes 589832 | tf_op jit(solution)/shard_map/ppermute | solution.py:337
  114.6 7.5 %collective-permute-start.32 = (f32[64,768]{1,0:T(8,128)S(1)}, f32[64,768]{1,0:T(8,128)S(1)}, u32[]{:S(2)}, u32[]{:S(2)}) collective-permute-start(f32[64,768]{1,0:T(8,128)S(1)} %get-tuple-element.117.refs_4_), channel_id=1, source_target_pairs={{0,1},{1,0},{2,3},{3,2},{4,5},{5,4},{6,7},{7,6},{8,9},{9,8},{10,11... | collective-permute-start | bytes 589832 | tf_op jit(solution)/shard_map/ppermute | solution.py:334
  117.7 5.2 %collective-permute-start.37 = (f32[64,768]{1,0:T(8,128)S(1)}, f32[64,768]{1,0:T(8,128)S(1)}, u32[]{:S(2)}, u32[]{:S(2)}) collective-permute-start(f32[64,768]{1,0:T(8,128)S(1)} %get-tuple-element.121.refs_7_.refs_0_), channel_id=1, source_target_pairs={{1,2},{2,1},{5,6},{6,5},{9,10},{10,9},{13,14},{14,13},{17,18},{18,... | collective-permute-start | bytes 589832 | tf_op jit(solution)/shard_map/ppermute | solution.py:337
  118.4 8.7 %collective-permute-start.38 = (f32[64,768]{1,0:T(8,128)S(1)}, f32[64,768]{1,0:T(8,128)S(1)}, u32[]{:S(2)}, u32[]{:S(2)}) collective-permute-start(f32[64,768]{1,0:T(8,128)S(1)} %get-tuple-element.124.refs_2_), channel_id=1, source_target_pairs={{0,1},{1,0},{2,3},{3,2},{4,5},{5,4},{6,7},{7,6},{8,9},{9,8},{10,11... | collective-permute-start | bytes 589832 | tf_op jit(solution)/shard_map/ppermute | solution.py:334
  121.3 12.4 %collective-permute-start.29 = (f32[1,3,64,768]{3,2,1,0:T(8,128)S(1)}, f32[1,3,64,768]{3,2,1,0:T(8,128)S(1)}, u32[]{:S(2)}, u32[]{:S(2)}) collective-permute-start(f32[1,3,64,768]{3,2,1,0:T(8,128)S(1)} %get-tuple-element.114), channel_id=1, source_target_pairs={{0,16},{4,20},{8,24},{12,28},{16,0},{20,4},{24,8},{28,12},{1,17},{... | collective-permute-start | bytes 1769480 | tf_op jit(solution)/shard_map/ppermute | solution.py:443
  121.6 12.1 %collective-permute-start.30 = (f32[1,3,64,768]{3,2,1,0:T(8,128)S(1)}, f32[1,3,64,768]{3,2,1,0:T(8,128)S(1)}, u32[]{:S(2)}, u32[]{:S(2)}) collective-permute-start(f32[1,3,64,768]{3,2,1,0:T(8,128)S(1)} %get-tuple-element.116), channel_id=1, source_target_pairs={{0,8},{4,12},{8,0},{12,4},{16,24},{20,28},{24,16},{28,20},{1,9},{5... | collective-permute-start | bytes 1769480 | tf_op jit(solution)/shard_map/ppermute | solution.py:443
  122.3 7.0 %collective-permute-start.35 = (f32[64,768]{1,0:T(8,128)S(1)}, f32[64,768]{1,0:T(8,128)S(1)}, u32[]{:S(2)}, u32[]{:S(2)}) collective-permute-start(f32[64,768]{1,0:T(8,128)S(1)} %get-tuple-element.122.refs_5_.refs_0_), channel_id=1, source_target_pairs={{1,2},{2,1},{5,6},{6,5},{9,10},{10,9},{13,14},{14,13},{17,18},{18,... | collective-permute-start | bytes 589832 | tf_op jit(solution)/shard_map/ppermute | solution.py:337
  122.9 9.0 %collective-permute-start.36 = (f32[64,768]{1,0:T(8,128)S(1)}, f32[64,768]{1,0:T(8,128)S(1)}, u32[]{:S(2)}, u32[]{:S(2)}) collective-permute-start(f32[64,768]{1,0:T(8,128)S(1)} %get-tuple-element.123.refs_2_), channel_id=1, source_target_pairs={{0,1},{1,0},{2,3},{3,2},{4,5},{5,4},{6,7},{7,6},{8,9},{9,8},{10,11... | collective-permute-start | bytes 589832 | tf_op jit(solution)/shard_map/ppermute | solution.py:334
  127.2 7.7 %collective-permute-start.40 = (f32[64,768]{1,0:T(8,128)S(1)}, f32[64,768]{1,0:T(8,128)S(1)}, u32[]{:S(2)}, u32[]{:S(2)}) collective-permute-start(f32[64,768]{1,0:T(8,128)S(1)} %get-tuple-element.127.refs_5_.refs_0_), channel_id=1, source_target_pairs={{0,1},{1,0},{2,3},{3,2},{4,5},{5,4},{6,7},{7,6},{8,9},{9,8},{10,11... | collective-permute-start | bytes 589832 | tf_op jit(solution)/shard_map/ppermute | solution.py:334
  132.0 5.7 %collective-permute-start.39 = (f32[64,768]{1,0:T(8,128)S(1)}, f32[64,768]{1,0:T(8,128)S(1)}, u32[]{:S(2)}, u32[]{:S(2)}) collective-permute-start(f32[64,768]{1,0:T(8,128)S(1)} %get-tuple-element.128.refs_4_.refs_3_.refs_0_), channel_id=1, source_target_pairs={{0,1},{1,0},{2,3},{3,2},{4,5},{5,4},{6,7},{7,6},{8,9},{9,8},{10,11... | collective-permute-start | bytes 589832 | tf_op jit(solution)/shard_map/ppermute | solution.py:334

commit v7 on v6

--- a/solution.py
+++ b/solution.py
@@ -232,7 +232,7 @@
 
 def run_scores(meta, member, owner, queries, cache, fresh):
     width = cache.shape[1]
-    group = 4
+    group = 6
     n_src = meta.blocks + meta.slab_blocks
     most = meta.steps * meta.blocks * ((meta.groups + 1) // 2)
     return pl.pallas_call(

time: 139 us -> 139 us (level)
  Pallas kernels: 44.4 us -> 41.7 us
  starting transfers between devices: 68.6 us -> 70.6 us
  transfers between devices with their start and end apart: 41 -> 41, of which waited for: 12 -> 12; matrix products, arithmetic and copies ran while one was open for 1% -> 1% of each run, Pallas kernels for 20% -> 19%
where the time goes in v7:
time: 139 us; the launch traced here: 138 us
  starting transfers between devices  70.6 us (51%)
  Pallas kernels  41.7 us (30%)
  waiting for transfers between devices  20 us (14%)
  local copies, waits for them, and re-layouts  3.55 us (3%)
    ppermute x18, starting transfers between devices, swapped(): return lax.ppermute(array, 'batch', [(0, 1), (1, 0), (2, 3), (3, 2)])  53.8 us
    pallas_call x2, Pallas kernels, run_terms(): pl.pallas_call(functools.partial(term_kernel, meta, spread, group, part,...  15.8 us
    pallas_call x1, Pallas kernels, run_scores(): pl.pallas_call(functools.partial(scores_kernel, meta, group, 2.0 / math.s...  13.5 us
    ppermute x18, waiting for transfers between devices, swapped(): return lax.ppermute(array, 'batch', [(0, 1), (1, 0), (2, 3), (3, 2)])  13.4 us
    pallas_call x4, Pallas kernels, run_grads(): pl.pallas_call(functools.partial(grad_kernel, meta, first, group), in_spe...  9.92 us
    ppermute x14, starting transfers between devices, swapped_mid(): return lax.ppermute(array, 'batch', [(1, 2), (2, 1)])  9.44 us
    ppermute x4, starting transfers between devices, exchange_lse(): lax.ppermute(lse, 'cache', [(i, i ^ p) for i in range(n)])  5.52 us
    ppermute x4, waiting for transfers between devices, exchange_lse(): lax.ppermute(lse, 'cache', [(i, i ^ p) for i in range(n)])  5.42 us
  transfers between devices with their start and end apart: 41, of which 12 were waited for; matrix products, arithmetic and copies ran while one was open for 1% of the time, Pallas kernels for 19%

profile of v7, /device:TPU:0, one launch (start us, length us, event | category | flops | bytes accessed | tf_op | source)
XLA Modules:
  0.0 138.3 jit_solution(11810115691864403246)
XLA Ops:
  0.6 0.8 fusion
  2.7 13.5 %scores.1 = (f32[24,8,128,128]{3,2,1,0:T(8,128)S(1)}, bf16[12,256,768]{2,1,0:T(8,128)(2,1)S(1)}, bf16[24,128,768]{2,1,0:T(8,128)(2,1)S(1)}, f32[24,128]{1,0:T(8,128)S(1)}, s32[104]{0:T(128)S(1)}) custom-call(s32[24,8]{1,0:T(8,128)S(1)} %convert_bitcast_fusion.member, s32[3]{0:T(128)S(1)} %copy-done.1, bf16[24,128,768]{2,1,0:T(8,128)(2,1)} %bitcast.3, ...), custom_call_target="tpu_custom_call" | custom-call | tf_op jit(solution)/shard_map/scores/pallas_call | solution.py:238
  16.7 0.8 collective-permute-done.refs_1_
  17.5 0.8 collective-permute-start.1
  18.3 4.3 %collective-permute-start.2 = (f32[24,128]{1,0:T(8,128)S(1)}, f32[24,128]{1,0:T(8,128)S(1)}, u32[]{:S(2)}, u32[]{:S(2)}) collective-permute-start(f32[24,128]{1,0:T(8,128)S(1)} %merge_lse.2.refs_0_), channel_id=1, source_target_pairs={{0,16},{4,20},{8,24},{12,28},{16,0},{20,4},{24,8},{28,12},{1,17},{... | collective-permute-start | bytes 36872 | tf_op jit(solution)/shard_map/ppermute | solution.py:319
  22.6 1.7 %collective-permute-done.2.refs_2_ = f32[24,128]{1,0:T(8,128)S(1)} collective-permute-done((f32[24,128]{1,0:T(8,128)S(1)}, f32[24,128]{1,0:T(8,128)S(1)}, u32[]{:S(2)}, u32[]{:S(2)}) %collective-permute-start.2) | collective-permute-done | bytes 12320 | tf_op jit(solution)/shard_map/ppermute | solution.py:319
  24.2 2.9 %collective-permute-done.3.refs_3_ = f32[24,128]{1,0:T(8,128)S(1)} collective-permute-done((f32[24,128]{1,0:T(8,128)S(1)}, f32[24,128]{1,0:T(8,128)S(1)}, u32[]{:S(2)}, u32[]{:S(2)}) %collective-permute-start.3) | collective-permute-done | bytes 12320 | tf_op jit(solution)/shard_map/ppermute | solution.py:319
  27.2 1.5 %cache_grad.4.dep.own = f32[128,768]{1,0:T(8,128)S(1)} custom-call(s32[24,8]{1,0:T(8,128)S(1)} %convert_bitcast_fusion.member, f32[24,8,128,128]{3,2,1,0:T(8,128)S(1)} %get-tuple-element.67.z_ref, bf16[24,128,768]{2,1,0:T(8,128)(2,1)S(1)} %get-tuple-element.70.q_ref, f32[24,128]{1,0:T(8,128)S(1)} %merge_lse.3.lse_ref.dep, f32[24,128]{1,0:T(8,128)S(1)} %merge_lse.3.lse_ref.dep), custom_call_target="tpu_custom_call" | custom-call | tf_op jit(solution)/shard_map/cache_grad/pallas_call | solution.py:266
  28.7 2.1 %collective-permute-start.4 = (f32[128,768]{1,0:T(8,128)S(1)}, f32[128,768]{1,0:T(8,128)S(1)}, u32[]{:S(2)}, u32[]{:S(2)}) collective-permute-start(f32[128,768]{1,0:T(8,128)S(1)} %cache_grad.4.dep.own), channel_id=1, source_target_pairs={{0,1},{1,0},{2,3},{3,2},{4,5},{5,4},{6,7},{7,6},{8,9},{9,8},{10,11... | collective-permute-start | bytes 1179656 | tf_op jit(solution)/shard_map/ppermute | solution.py:334
  30.8 1.5 %cache_grad.5.dep.own = f32[128,768]{1,0:T(8,128)S(1)} custom-call(s32[24,8]{1,0:T(8,128)S(1)} %convert_bitcast_fusion.member, f32[24,8,128,128]{3,2,1,0:T(8,128)S(1)} %get-tuple-element.67.z_ref, bf16[24,128,768]{2,1,0:T(8,128)(2,1)S(1)} %get-tuple-element.70.q_ref, f32[24,128]{1,0:T(8,128)S(1)} %merge_lse.3.lse_ref.dep, f32[128,768]{1,0:T(8,128)S(1)} %cache_grad.4.dep.own), custom_call_target="tpu_custom_call" | custom-call | tf_op jit(solution)/shard_map/cache_grad/pallas_call | solution.py:266
  32.4 1.5 %cache_grad.6.dep.refs_0_ = f32[128,768]{1,0:T(8,128)S(1)} custom-call(s32[24,8]{1,0:T(8,128)S(1)} %convert_bitcast_fusion.member, f32[24,8,128,128]{3,2,1,0:T(8,128)S(1)} %get-tuple-element.67.z_ref, bf16[24,128,768]{2,1,0:T(8,128)(2,1)S(1)} %get-tuple-element.70.q_ref, f32[24,128]{1,0:T(8,128)S(1)} %merge_lse.3.lse_ref.dep, f32[128,768]{1,0:T(8,128)S(1)} %cache_grad.5.dep.own), custom_call_target="tpu_custom_call" | custom-call | tf_op jit(solution)/shard_map/cache_grad/pallas_call | solution.py:266
  34.0 5.3 %cache_grad.7.dep.more.refs_4_.refs_0_ = f32[640,768]{1,0:T(8,128)S(1)} custom-call(s32[24,8]{1,0:T(8,128)S(1)} %convert_bitcast_fusion.member, f32[24,8,128,128]{3,2,1,0:T(8,128)S(1)} %get-tuple-element.67.z_ref, bf16[24,128,768]{2,1,0:T(8,128)(2,1)S(1)} %get-tuple-element.70.q_ref, f32[24,128]{1,0:T(8,128)S(1)} %merge_lse.3.lse_ref.dep, ...), custom_call_target="tpu_custom_call" | custom-call | tf_op jit(solution)/shard_map/cache_grad/pallas_call | solution.py:266
  39.4 1.5 %collective-permute-done.4.came = f32[128,768]{1,0:T(8,128)S(1)} collective-permute-done((f32[128,768]{1,0:T(8,128)S(1)}, f32[128,768]{1,0:T(8,128)S(1)}, u32[]{:S(2)}, u32[]{:S(2)}) %collective-permute-start.4) | collective-permute-done | bytes 393248 | tf_op jit(solution)/shard_map/ppermute | solution.py:334
  40.9 0.7 collective-permute-start.5
  41.6 3.5 %collective-permute-start.7 = (f32[128,768]{1,0:T(8,128)S(1)}, f32[128,768]{1,0:T(8,128)S(1)}, u32[]{:S(2)}, u32[]{:S(2)}) collective-permute-start(f32[128,768]{1,0:T(8,128)S(1)} %cache_grad.6.dep.refs_0_), channel_id=1, source_target_pairs={{0,1},{1,0},{2,3},{3,2},{4,5},{5,4},{6,7},{7,6},{8,9},{9,8},{10,11... | collective-permute-start | bytes 1179656 | tf_op jit(solution)/shard_map/ppermute | solution.py:334
  45.1 7.7 %query_term.2.dep.refs_0_ = f32[8,3,128,768]{3,2,1,0:T(8,128)S(1)} custom-call(s32[24,8]{1,0:T(8,128)S(1)} %convert_bitcast_fusion.member, s32[3]{0:T(128)S(1)} %copy-done.2, s32[104]{0:T(128)S(1)} %get-tuple-element.66.entries, f32[24,8,128,128]{3,2,1,0:T(8,128)S(1)} %get-tuple-element.67.z_ref, bf16[12,256,768]{2,1,0:T(8,128)(2,1)S(1)} %get-tuple-element.68.w_ref, ...), custom_call_target="tpu_custom_call" | custom-call | tf_op jit(solution)/shard_map/query_term/pallas_call | solution.py:280
  53.1 0.7 collective-permute-start.8
  53.7 4.0 %collective-permute-start.9 = (f32[128,768]{1,0:T(8,128)S(1)}, f32[128,768]{1,0:T(8,128)S(1)}, u32[]{:S(2)}, u32[]{:S(2)}) collective-permute-start(f32[128,768]{1,0:T(8,128)S(1)} %get-tuple-element.73), channel_id=1, source_target_pairs={{0,1},{1,0},{2,3},{3,2},{4,5},{5,4},{6,7},{7,6},{8,9},{9,8},{10,11... | collective-permute-start | bytes 1179656 | tf_op jit(solution)/shard_map/ppermute | solution.py:334
  57.7 8.0 %query_term.3.refs_7_.terms.refs_0_ = f32[8,3,128,768]{3,2,1,0:T(8,128)S(1)} custom-call(s32[24,8]{1,0:T(8,128)S(1)} %convert_bitcast_fusion.member, s32[3]{0:T(128)S(1)} %copy-done.2, s32[104]{0:T(128)S(1)} %get-tuple-element.66.entries, f32[24,8,128,128]{3,2,1,0:T(8,128)S(1)} %get-tuple-element.67.z_ref, ...), custom_call_target="tpu_custom_call", output_to_operand_aliasing={{}: (8, {})} | custom-call | tf_op jit(solution)/shard_map/query_term/pallas_call | solution.py:280
  66.3 0.7 collective-permute-start.13
  66.9 2.1 %collective-permute-start.14 = (f32[64,768]{1,0:T(8,128)S(1)}, f32[64,768]{1,0:T(8,128)S(1)}, u32[]{:S(2)}, u32[]{:S(2)}) collective-permute-start(f32[64,768]{1,0:T(8,128)S(1)} %get-tuple-element.80), channel_id=1, source_target_pairs={{0,1},{1,0},{2,3},{3,2},{4,5},{5,4},{6,7},{7,6},{8,9},{9,8},{10,11... | collective-permute-start | bytes 589832 | tf_op jit(solution)/shard_map/ppermute | solution.py:334
  69.1 0.7 collective-permute-start.11
  69.8 2.6 %collective-permute-start.12 = (f32[64,768]{1,0:T(8,128)S(1)}, f32[64,768]{1,0:T(8,128)S(1)}, u32[]{:S(2)}, u32[]{:S(2)}) collective-permute-start(f32[64,768]{1,0:T(8,128)S(1)} %get-tuple-element.78), channel_id=1, source_target_pairs={{0,1},{1,0},{2,3},{3,2},{4,5},{5,4},{6,7},{7,6},{8,9},{9,8},{10,11... | collective-permute-start | bytes 589832 | tf_op jit(solution)/shard_map/ppermute | solution.py:334
  72.4 2.3 %collective-permute-done.14.refs_6_.refs_1_ = f32[64,768]{1,0:T(8,128)S(1)} collective-permute-done((f32[64,768]{1,0:T(8,128)S(1)}, f32[64,768]{1,0:T(8,128)S(1)}, u32[]{:S(2)}, u32[]{:S(2)}) %collective-permute-start.14) | collective-permute-done | bytes 196640 | tf_op jit(solution)/shard_map/ppermute | solution.py:334
  74.8 0.7 collective-permute-start.19
  75.5 4.6 %collective-permute-start.20 = (f32[64,768]{1,0:T(8,128)S(1)}, f32[64,768]{1,0:T(8,128)S(1)}, u32[]{:S(2)}, u32[]{:S(2)}) collective-permute-start(f32[64,768]{1,0:T(8,128)S(1)} %get-tuple-element.92), channel_id=1, source_target_pairs={{0,1},{1,0},{2,3},{3,2},{4,5},{5,4},{6,7},{7,6},{8,9},{9,8},{10,11... | collective-permute-start | bytes 589832 | tf_op jit(solution)/shard_map/ppermute | solution.py:334
  80.2 0.7 collective-permute-start.17
  80.9 2.7 %collective-permute-start.18 = (f32[64,768]{1,0:T(8,128)S(1)}, f32[64,768]{1,0:T(8,128)S(1)}, u32[]{:S(2)}, u32[]{:S(2)}) collective-permute-start(f32[64,768]{1,0:T(8,128)S(1)} %get-tuple-element.90), channel_id=1, source_target_pairs={{0,1},{1,0},{2,3},{3,2},{4,5},{5,4},{6,7},{7,6},{8,9},{9,8},{10,11... | collective-permute-start | bytes 589832 | tf_op jit(solution)/shard_map/ppermute | solution.py:334
  84.9 4.1 %collective-permute-start.24 = (f32[64,768]{1,0:T(8,128)S(1)}, f32[64,768]{1,0:T(8,128)S(1)}, u32[]{:S(2)}, u32[]{:S(2)}) collective-permute-start(f32[64,768]{1,0:T(8,128)S(1)} %get-tuple-element.100), channel_id=1, source_target_pairs={{0,1},{1,0},{2,3},{3,2},{4,5},{5,4},{6,7},{7,6},{8,9},{9,8},{10,11... | collective-permute-start | bytes 589832 | tf_op jit(solution)/shard_map/ppermute | solution.py:334
  89.0 1.1 collective-permute-start.16
  90.2 1.4 collective-permute-start.21
  92.3 2.1 %collective-permute-done.24.refs_6_.refs_1_ = f32[64,768]{1,0:T(8,128)S(1)} collective-permute-done((f32[64,768]{1,0:T(8,128)S(1)}, f32[64,768]{1,0:T(8,128)S(1)}, u32[]{:S(2)}, u32[]{:S(2)}) %collective-permute-start.24) | collective-permute-done | bytes 196640 | tf_op jit(solution)/shard_map/ppermute | solution.py:334
  95.1 1.3 collective-permute-done.21.refs_6_.refs_1_
  96.4 3.5 %collective-permute-start.28 = (f32[64,768]{1,0:T(8,128)S(1)}, f32[64,768]{1,0:T(8,128)S(1)}, u32[]{:S(2)}, u32[]{:S(2)}) collective-permute-start(f32[64,768]{1,0:T(8,128)S(1)} %get-tuple-element.108), channel_id=1, source_target_pairs={{0,1},{1,0},{2,3},{3,2},{4,5},{5,4},{6,7},{7,6},{8,9},{9,8},{10,11... | collective-permute-start | bytes 589832 | tf_op jit(solution)/shard_map/ppermute | solution.py:334
  100.7 5.9 %collective-permute-start.26 = (f32[64,768]{1,0:T(8,128)S(1)}, f32[64,768]{1,0:T(8,128)S(1)}, u32[]{:S(2)}, u32[]{:S(2)}) collective-permute-start(f32[64,768]{1,0:T(8,128)S(1)} %get-tuple-element.106), channel_id=1, source_target_pairs={{0,1},{1,0},{2,3},{3,2},{4,5},{5,4},{6,7},{7,6},{8,9},{9,8},{10,11... | collective-permute-start | bytes 589832 | tf_op jit(solution)/shard_map/ppermute | solution.py:334
  107.3 3.4 %collective-permute-start.34 = (f32[64,768]{1,0:T(8,128)S(1)}, f32[64,768]{1,0:T(8,128)S(1)}, u32[]{:S(2)}, u32[]{:S(2)}) collective-permute-start(f32[64,768]{1,0:T(8,128)S(1)} %get-tuple-element.118.refs_4_), channel_id=1, source_target_pairs={{0,1},{1,0},{2,3},{3,2},{4,5},{5,4},{6,7},{7,6},{8,9},{9,8},{10,11... | collective-permute-start | bytes 589832 | tf_op jit(solution)/shard_map/ppermute | solution.py:334
  110.7 0.9 collective-permute-done.26.refs_5_.refs_1_
  112.3 1.1 collective-permute-done.15.refs_1_
  113.4 3.0 %collective-permute-start.32 = (f32[64,768]{1,0:T(8,128)S(1)}, f32[64,768]{1,0:T(8,128)S(1)}, u32[]{:S(2)}, u32[]{:S(2)}) collective-permute-start(f32[64,768]{1,0:T(8,128)S(1)} %get-tuple-element.117.refs_4_), channel_id=1, source_target_pairs={{0,1},{1,0},{2,3},{3,2},{4,5},{5,4},{6,7},{7,6},{8,9},{9,8},{10,11... | collective-permute-start | bytes 589832 | tf_op jit(solution)/shard_map/ppermute | solution.py:334
  117.5 3.1 %collective-permute-start.38 = (f32[64,768]{1,0:T(8,128)S(1)}, f32[64,768]{1,0:T(8,128)S(1)}, u32[]{:S(2)}, u32[]{:S(2)}) collective-permute-start(f32[64,768]{1,0:T(8,128)S(1)} %get-tuple-element.124.refs_2_), channel_id=1, source_target_pairs={{0,1},{1,0},{2,3},{3,2},{4,5},{5,4},{6,7},{7,6},{8,9},{9,8},{10,11... | collective-permute-start | bytes 589832 | tf_op jit(solution)/shard_map/ppermute | solution.py:334
  120.6 0.7 collective-permute-start.30
  122.1 3.8 %collective-permute-start.36 = (f32[64,768]{1,0:T(8,128)S(1)}, f32[64,768]{1,0:T(8,128)S(1)}, u32[]{:S(2)}, u32[]{:S(2)}) collective-permute-start(f32[64,768]{1,0:T(8,128)S(1)} %get-tuple-element.123.refs_2_), channel_id=1, source_target_pairs={{0,1},{1,0},{2,3},{3,2},{4,5},{5,4},{6,7},{7,6},{8,9},{9,8},{10,11... | collective-permute-start | bytes 589832 | tf_op jit(solution)/shard_map/ppermute | solution.py:334
  126.4 2.1 %collective-permute-start.40 = (f32[64,768]{1,0:T(8,128)S(1)}, f32[64,768]{1,0:T(8,128)S(1)}, u32[]{:S(2)}, u32[]{:S(2)}) collective-permute-start(f32[64,768]{1,0:T(8,128)S(1)} %get-tuple-element.127.refs_5_.refs_0_), channel_id=1, source_target_pairs={{0,1},{1,0},{2,3},{3,2},{4,5},{5,4},{6,7},{7,6},{8,9},{9,8},{10,11... | collective-permute-start | bytes 589832 | tf_op jit(solution)/shard_map/ppermute | solution.py:334
  128.5 2.3 %collective-permute-done.36.refs_3_ = f32[64,768]{1,0:T(8,128)S(1)} collective-permute-done((f32[64,768]{1,0:T(8,128)S(1)}, f32[64,768]{1,0:T(8,128)S(1)}, u32[]{:S(2)}, u32[]{:S(2)}) %collective-permute-start.36) | collective-permute-done | bytes 196640 | tf_op jit(solution)/shard_map/ppermute | solution.py:334
  130.9 1.9 %collective-permute-start.39 = (f32[64,768]{1,0:T(8,128)S(1)}, f32[64,768]{1,0:T(8,128)S(1)}, u32[]{:S(2)}, u32[]{:S(2)}) collective-permute-start(f32[64,768]{1,0:T(8,128)S(1)} %get-tuple-element.128.refs_4_.refs_3_.refs_0_), channel_id=1, source_target_pairs={{0,1},{1,0},{2,3},{3,2},{4,5},{5,4},{6,7},{7,6},{8,9},{9,8},{10,11... | collective-permute-start | bytes 589832 | tf_op jit(solution)/shard_map/ppermute | solution.py:334
  132.9 1.0 copy.41
  134.2 2.4 %collective-permute-done.39.refs_1_ = f32[64,768]{1,0:T(8,128)S(1)} collective-permute-done((f32[64,768]{1,0:T(8,128)S(1)}, f32[64,768]{1,0:T(8,128)S(1)}, u32[]{:S(2)}, u32[]{:S(2)}) %collective-permute-start.39) | collective-permute-done | bytes 196640 | tf_op jit(solution)/shard_map/ppermute | solution.py:334
  136.6 1.7 %copy.42 = f32[1024,768]{1,0:T(8,128)} copy(f32[1024,768]{1,0:T(8,128)S(1)} %line_slot.31) | data formatting | bytes 6291456
  (78 shorter events, 10.6 us)
Async XLA Ops:
  2.0 0.7 copy-start.1
  16.2 1.3 collective-permute-start
  17.5 5.0 %collective-permute-start.1 = (f32[24,128]{1,0:T(8,128)S(1)}, f32[24,128]{1,0:T(8,128)S(1)}, u32[]{:S(2)}, u32[]{:S(2)}) collective-permute-start(f32[24,128]{1,0:T(8,128)S(1)} %merge_lse.2.refs_0_), channel_id=1, source_target_pairs={{0,8},{4,12},{8,0},{12,4},{16,24},{20,28},{24,16},{28,20},{1,9},{5... | collective-permute-start | bytes 36872 | tf_op jit(solution)/shard_map/ppermute | solution.py:319
  18.3 5.9 %collective-permute-start.2 = (f32[24,128]{1,0:T(8,128)S(1)}, f32[24,128]{1,0:T(8,128)S(1)}, u32[]{:S(2)}, u32[]{:S(2)}) collective-permute-start(f32[24,128]{1,0:T(8,128)S(1)} %merge_lse.2.refs_0_), channel_id=1, source_target_pairs={{0,16},{4,20},{8,24},{12,28},{16,0},{20,4},{24,8},{28,12},{1,17},{... | collective-permute-start | bytes 36872 | tf_op jit(solution)/shard_map/ppermute | solution.py:319
  22.6 4.6 %collective-permute-start.3 = (f32[24,128]{1,0:T(8,128)S(1)}, f32[24,128]{1,0:T(8,128)S(1)}, u32[]{:S(2)}, u32[]{:S(2)}) collective-permute-start(f32[24,128]{1,0:T(8,128)S(1)} %merge_lse.2.refs_0_), channel_id=1, source_target_pairs={{0,24},{4,28},{8,16},{12,20},{16,8},{20,12},{24,0},{28,4},{1,25},{... | collective-permute-start | bytes 36872 | tf_op jit(solution)/shard_map/ppermute | solution.py:319
  28.7 12.2 %collective-permute-start.4 = (f32[128,768]{1,0:T(8,128)S(1)}, f32[128,768]{1,0:T(8,128)S(1)}, u32[]{:S(2)}, u32[]{:S(2)}) collective-permute-start(f32[128,768]{1,0:T(8,128)S(1)} %cache_grad.4.dep.own), channel_id=1, source_target_pairs={{0,1},{1,0},{2,3},{3,2},{4,5},{5,4},{6,7},{7,6},{8,9},{9,8},{10,11... | collective-permute-start | bytes 1179656 | tf_op jit(solution)/shard_map/ppermute | solution.py:334
  33.9 19.0 %collective-permute-start.6 = (f32[128,768]{1,0:T(8,128)S(1)}, f32[128,768]{1,0:T(8,128)S(1)}, u32[]{:S(2)}, u32[]{:S(2)}) collective-permute-start(f32[128,768]{1,0:T(8,128)S(1)} %cache_grad.5.dep.own), channel_id=1, source_target_pairs={{0,1},{1,0},{2,3},{3,2},{4,5},{5,4},{6,7},{7,6},{8,9},{9,8},{10,11... | collective-permute-start | bytes 1179656 | tf_op jit(solution)/shard_map/ppermute | solution.py:334
  39.3 5.8 %copy-start = (s32[3,1024]{1,0:T(4,128)S(1)}, s32[3,1024]{1,0:T(4,128)}, u32[]{:S(2)}) copy-start(s32[3,1024]{1,0:T(4,128)} %pos_ref.3) | copy-start | bytes 36868
  39.3 5.8 %copy-start.2 = (s32[3]{0:T(128)S(1)}, s32[3]{0:T(128)}, u32[]{:S(2)}) copy-start(s32[3]{0:T(128)} %owner.5) | copy-start | bytes 40
  40.9 12.0 %collective-permute-start.5 = (f32[128,768]{1,0:T(8,128)S(1)}, f32[128,768]{1,0:T(8,128)S(1)}, u32[]{:S(2)}, u32[]{:S(2)}) collective-permute-start(f32[128,768]{1,0:T(8,128)S(1)} %line_early.1.dep.inner), channel_id=1, source_target_pairs={{1,2},{2,1},{5,6},{6,5},{9,10},{10,9},{13,14},{14,13},{17,18},{18,... | collective-permute-start | bytes 1179656 | tf_op jit(solution)/shard_map/ppermute | solution.py:337
  41.6 24.1 %collective-permute-start.7 = (f32[128,768]{1,0:T(8,128)S(1)}, f32[128,768]{1,0:T(8,128)S(1)}, u32[]{:S(2)}, u32[]{:S(2)}) collective-permute-start(f32[128,768]{1,0:T(8,128)S(1)} %cache_grad.6.dep.refs_0_), channel_id=1, source_target_pairs={{0,1},{1,0},{2,3},{3,2},{4,5},{5,4},{6,7},{7,6},{8,9},{9,8},{10,11... | collective-permute-start | bytes 1179656 | tf_op jit(solution)/shard_map/ppermute | solution.py:334
  53.1 12.7 %collective-permute-start.8 = (f32[128,768]{1,0:T(8,128)S(1)}, f32[128,768]{1,0:T(8,128)S(1)}, u32[]{:S(2)}, u32[]{:S(2)}) collective-permute-start(f32[128,768]{1,0:T(8,128)S(1)} %get-tuple-element.71.dep.refs_2_), channel_id=1, source_target_pairs={{1,2},{2,1},{5,6},{6,5},{9,10},{10,9},{13,14},{14,13},{17,18},{18,... | collective-permute-start | bytes 1179656 | tf_op jit(solution)/shard_map/ppermute | solution.py:337
  53.7 12.0 %collective-permute-start.9 = (f32[128,768]{1,0:T(8,128)S(1)}, f32[128,768]{1,0:T(8,128)S(1)}, u32[]{:S(2)}, u32[]{:S(2)}) collective-permute-start(f32[128,768]{1,0:T(8,128)S(1)} %get-tuple-element.73), channel_id=1, source_target_pairs={{0,1},{1,0},{2,3},{3,2},{4,5},{5,4},{6,7},{7,6},{8,9},{9,8},{10,11... | collective-permute-start | bytes 1179656 | tf_op jit(solution)/shard_map/ppermute | solution.py:334
  66.2 17.4 %collective-permute-start.10 = (f32[4,3,128,768]{3,2,1,0:T(8,128)S(1)}, f32[4,3,128,768]{3,2,1,0:T(8,128)S(1)}, u32[]{:S(2)}, u32[]{:S(2)}) collective-permute-start(f32[4,3,128,768]{3,2,1,0:T(8,128)S(1)} %home_start.1), channel_id=1, source_target_pairs={{0,4},{4,0},{8,12},{12,8},{16,20},{20,16},{24,28},{28,24},{1,5},{5... | collective-permute-start | bytes 14155784 | tf_op jit(solution)/shard_map/ppermute | solution.py:443
  66.3 6.1 %collective-permute-start.13 = (f32[64,768]{1,0:T(8,128)S(1)}, f32[64,768]{1,0:T(8,128)S(1)}, u32[]{:S(2)}, u32[]{:S(2)}) collective-permute-start(f32[64,768]{1,0:T(8,128)S(1)} %get-tuple-element.74.dep.refs_8_.refs_2_), channel_id=1, source_target_pairs={{1,2},{2,1},{5,6},{6,5},{9,10},{10,9},{13,14},{14,13},{17,18},{18,... | collective-permute-start | bytes 589832 | tf_op jit(solution)/shard_map/ppermute | solution.py:337
  66.9 7.8 %collective-permute-start.14 = (f32[64,768]{1,0:T(8,128)S(1)}, f32[64,768]{1,0:T(8,128)S(1)}, u32[]{:S(2)}, u32[]{:S(2)}) collective-permute-start(f32[64,768]{1,0:T(8,128)S(1)} %get-tuple-element.80), channel_id=1, source_target_pairs={{0,1},{1,0},{2,3},{3,2},{4,5},{5,4},{6,7},{7,6},{8,9},{9,8},{10,11... | collective-permute-start | bytes 589832 | tf_op jit(solution)/shard_map/ppermute | solution.py:334
  69.1 11.0 %collective-permute-start.11 = (f32[64,768]{1,0:T(8,128)S(1)}, f32[64,768]{1,0:T(8,128)S(1)}, u32[]{:S(2)}, u32[]{:S(2)}) collective-permute-start(f32[64,768]{1,0:T(8,128)S(1)} %get-tuple-element.76.refs_8_.refs_2_), channel_id=1, source_target_pairs={{1,2},{2,1},{5,6},{6,5},{9,10},{10,9},{13,14},{14,13},{17,18},{18,... | collective-permute-start | bytes 589832 | tf_op jit(solution)/shard_map/ppermute | solution.py:337
  69.8 10.3 %collective-permute-start.12 = (f32[64,768]{1,0:T(8,128)S(1)}, f32[64,768]{1,0:T(8,128)S(1)}, u32[]{:S(2)}, u32[]{:S(2)}) collective-permute-start(f32[64,768]{1,0:T(8,128)S(1)} %get-tuple-element.78), channel_id=1, source_target_pairs={{0,1},{1,0},{2,3},{3,2},{4,5},{5,4},{6,7},{7,6},{8,9},{9,8},{10,11... | collective-permute-start | bytes 589832 | tf_op jit(solution)/shard_map/ppermute | solution.py:334
  74.8 9.4 %collective-permute-start.19 = (f32[64,768]{1,0:T(8,128)S(1)}, f32[64,768]{1,0:T(8,128)S(1)}, u32[]{:S(2)}, u32[]{:S(2)}) collective-permute-start(f32[64,768]{1,0:T(8,128)S(1)} %get-tuple-element.83.refs_8_.refs_2_), channel_id=1, source_target_pairs={{1,2},{2,1},{5,6},{6,5},{9,10},{10,9},{13,14},{14,13},{17,18},{18,... | collective-permute-start | bytes 589832 | tf_op jit(solution)/shard_map/ppermute | solution.py:337
  75.5 8.7 %collective-permute-start.20 = (f32[64,768]{1,0:T(8,128)S(1)}, f32[64,768]{1,0:T(8,128)S(1)}, u32[]{:S(2)}, u32[]{:S(2)}) collective-permute-start(f32[64,768]{1,0:T(8,128)S(1)} %get-tuple-element.92), channel_id=1, source_target_pairs={{0,1},{1,0},{2,3},{3,2},{4,5},{5,4},{6,7},{7,6},{8,9},{9,8},{10,11... | collective-permute-start | bytes 589832 | tf_op jit(solution)/shard_map/ppermute | solution.py:334
  80.2 8.8 %collective-permute-start.17 = (f32[64,768]{1,0:T(8,128)S(1)}, f32[64,768]{1,0:T(8,128)S(1)}, u32[]{:S(2)}, u32[]{:S(2)}) collective-permute-start(f32[64,768]{1,0:T(8,128)S(1)} %get-tuple-element.84.refs_2_.refs_8_), channel_id=1, source_target_pairs={{1,2},{2,1},{5,6},{6,5},{9,10},{10,9},{13,14},{14,13},{17,18},{18,... | collective-permute-start | bytes 589832 | tf_op jit(solution)/shard_map/ppermute | solution.py:337
  80.9 9.2 %collective-permute-start.18 = (f32[64,768]{1,0:T(8,128)S(1)}, f32[64,768]{1,0:T(8,128)S(1)}, u32[]{:S(2)}, u32[]{:S(2)}) collective-permute-start(f32[64,768]{1,0:T(8,128)S(1)} %get-tuple-element.90), channel_id=1, source_target_pairs={{0,1},{1,0},{2,3},{3,2},{4,5},{5,4},{6,7},{7,6},{8,9},{9,8},{10,11... | collective-permute-start | bytes 589832 | tf_op jit(solution)/shard_map/ppermute | solution.py:334
  84.3 7.3 %collective-permute-start.23 = (f32[64,768]{1,0:T(8,128)S(1)}, f32[64,768]{1,0:T(8,128)S(1)}, u32[]{:S(2)}, u32[]{:S(2)}) collective-permute-start(f32[64,768]{1,0:T(8,128)S(1)} %get-tuple-element.95.refs_8_.refs_2_), channel_id=1, source_target_pairs={{1,2},{2,1},{5,6},{6,5},{9,10},{10,9},{13,14},{14,13},{17,18},{18,... | collective-permute-start | bytes 589832 | tf_op jit(solution)/shard_map/ppermute | solution.py:337
  84.9 9.4 %collective-permute-start.24 = (f32[64,768]{1,0:T(8,128)S(1)}, f32[64,768]{1,0:T(8,128)S(1)}, u32[]{:S(2)}, u32[]{:S(2)}) collective-permute-start(f32[64,768]{1,0:T(8,128)S(1)} %get-tuple-element.100), channel_id=1, source_target_pairs={{0,1},{1,0},{2,3},{3,2},{4,5},{5,4},{6,7},{7,6},{8,9},{9,8},{10,11... | collective-permute-start | bytes 589832 | tf_op jit(solution)/shard_map/ppermute | solution.py:334
  89.0 24.4 %collective-permute-start.15 = (f32[2,3,64,768]{3,2,1,0:T(8,128)S(1)}, f32[2,3,64,768]{3,2,1,0:T(8,128)S(1)}, u32[]{:S(2)}, u32[]{:S(2)}) collective-permute-start(f32[2,3,64,768]{3,2,1,0:T(8,128)S(1)} %get-tuple-element.86), channel_id=1, source_target_pairs={{0,8},{4,12},{8,0},{12,4},{16,24},{20,28},{24,16},{28,20},{1,9},{5... | collective-permute-start | bytes 3538952 | tf_op jit(solution)/shard_map/ppermute | solution.py:443
  89.0 27.4 %collective-permute-start.16 = (f32[2,3,64,768]{3,2,1,0:T(8,128)S(1)}, f32[2,3,64,768]{3,2,1,0:T(8,128)S(1)}, u32[]{:S(2)}, u32[]{:S(2)}) collective-permute-start(f32[2,3,64,768]{3,2,1,0:T(8,128)S(1)} %get-tuple-element.88), channel_id=1, source_target_pairs={{0,16},{4,20},{8,24},{12,28},{16,0},{20,4},{24,8},{28,12},{1,17},{... | collective-permute-start | bytes 3538952 | tf_op jit(solution)/shard_map/ppermute | solution.py:443
  90.2 6.2 %collective-permute-start.21 = (f32[64,768]{1,0:T(8,128)S(1)}, f32[64,768]{1,0:T(8,128)S(1)}, u32[]{:S(2)}, u32[]{:S(2)}) collective-permute-start(f32[64,768]{1,0:T(8,128)S(1)} %get-tuple-element.96), channel_id=1, source_target_pairs={{0,1},{1,0},{2,3},{3,2},{4,5},{5,4},{6,7},{7,6},{8,9},{9,8},{10,11... | collective-permute-start | bytes 589832 | tf_op jit(solution)/shard_map/ppermute | solution.py:334
  91.6 8.3 %collective-permute-start.22 = (f32[64,768]{1,0:T(8,128)S(1)}, f32[64,768]{1,0:T(8,128)S(1)}, u32[]{:S(2)}, u32[]{:S(2)}) collective-permute-start(f32[64,768]{1,0:T(8,128)S(1)} %get-tuple-element.97.refs_8_.refs_2_), channel_id=1, source_target_pairs={{1,2},{2,1},{5,6},{6,5},{9,10},{10,9},{13,14},{14,13},{17,18},{18,... | collective-permute-start | bytes 589832 | tf_op jit(solution)/shard_map/ppermute | solution.py:337
  94.4 6.3 %collective-permute-start.27 = (f32[64,768]{1,0:T(8,128)S(1)}, f32[64,768]{1,0:T(8,128)S(1)}, u32[]{:S(2)}, u32[]{:S(2)}) collective-permute-start(f32[64,768]{1,0:T(8,128)S(1)} %get-tuple-element.103.refs_8_.refs_2_), channel_id=1, source_target_pairs={{1,2},{2,1},{5,6},{6,5},{9,10},{10,9},{13,14},{14,13},{17,18},{18,... | collective-permute-start | bytes 589832 | tf_op jit(solution)/shard_map/ppermute | solution.py:337
  96.4 10.2 %collective-permute-start.28 = (f32[64,768]{1,0:T(8,128)S(1)}, f32[64,768]{1,0:T(8,128)S(1)}, u32[]{:S(2)}, u32[]{:S(2)}) collective-permute-start(f32[64,768]{1,0:T(8,128)S(1)} %get-tuple-element.108), channel_id=1, source_target_pairs={{0,1},{1,0},{2,3},{3,2},{4,5},{5,4},{6,7},{7,6},{8,9},{9,8},{10,11... | collective-permute-start | bytes 589832 | tf_op jit(solution)/shard_map/ppermute | solution.py:334
  100.0 7.4 %collective-permute-start.25 = (f32[64,768]{1,0:T(8,128)S(1)}, f32[64,768]{1,0:T(8,128)S(1)}, u32[]{:S(2)}, u32[]{:S(2)}) collective-permute-start(f32[64,768]{1,0:T(8,128)S(1)} %get-tuple-element.104.refs_7_.refs_2_), channel_id=1, source_target_pairs={{1,2},{2,1},{5,6},{6,5},{9,10},{10,9},{13,14},{14,13},{17,18},{18,... | collective-permute-start | bytes 589832 | tf_op jit(solution)/shard_map/ppermute | solution.py:337
  100.7 10.9 %collective-permute-start.26 = (f32[64,768]{1,0:T(8,128)S(1)}, f32[64,768]{1,0:T(8,128)S(1)}, u32[]{:S(2)}, u32[]{:S(2)}) collective-permute-start(f32[64,768]{1,0:T(8,128)S(1)} %get-tuple-element.106), channel_id=1, source_target_pairs={{0,1},{1,0},{2,3},{3,2},{4,5},{5,4},{6,7},{7,6},{8,9},{9,8},{10,11... | collective-permute-start | bytes 589832 | tf_op jit(solution)/shard_map/ppermute | solution.py:334
  106.6 10.1 %collective-permute-start.33 = (f32[64,768]{1,0:T(8,128)S(1)}, f32[64,768]{1,0:T(8,128)S(1)}, u32[]{:S(2)}, u32[]{:S(2)}) collective-permute-start(f32[64,768]{1,0:T(8,128)S(1)} %get-tuple-element.111.refs_7_.refs_2_), channel_id=1, source_target_pairs={{1,2},{2,1},{5,6},{6,5},{9,10},{10,9},{13,14},{14,13},{17,18},{18,... | collective-permute-start | bytes 589832 | tf_op jit(solution)/shard_map/ppermute | solution.py:337
  107.3 9.4 %collective-permute-start.34 = (f32[64,768]{1,0:T(8,128)S(1)}, f32[64,768]{1,0:T(8,128)S(1)}, u32[]{:S(2)}, u32[]{:S(2)}) collective-permute-start(f32[64,768]{1,0:T(8,128)S(1)} %get-tuple-element.118.refs_4_), channel_id=1, source_target_pairs={{0,1},{1,0},{2,3},{3,2},{4,5},{5,4},{6,7},{7,6},{8,9},{9,8},{10,11... | collective-permute-start | bytes 589832 | tf_op jit(solution)/shard_map/ppermute | solution.py:334
  111.7 8.9 %collective-permute-start.31 = (f32[64,768]{1,0:T(8,128)S(1)}, f32[64,768]{1,0:T(8,128)S(1)}, u32[]{:S(2)}, u32[]{:S(2)}) collective-permute-start(f32[64,768]{1,0:T(8,128)S(1)} %get-tuple-element.112.refs_4_.refs_7_.refs_2_), channel_id=1, source_target_pairs={{1,2},{2,1},{5,6},{6,5},{9,10},{10,9},{13,14},{14,13},{17,18},{18,... | collective-permute-start | bytes 589832 | tf_op jit(solution)/shard_map/ppermute | solution.py:337
  113.4 7.8 %collective-permute-start.32 = (f32[64,768]{1,0:T(8,128)S(1)}, f32[64,768]{1,0:T(8,128)S(1)}, u32[]{:S(2)}, u32[]{:S(2)}) collective-permute-start(f32[64,768]{1,0:T(8,128)S(1)} %get-tuple-element.117.refs_4_), channel_id=1, source_target_pairs={{0,1},{1,0},{2,3},{3,2},{4,5},{5,4},{6,7},{7,6},{8,9},{9,8},{10,11... | collective-permute-start | bytes 589832 | tf_op jit(solution)/shard_map/ppermute | solution.py:334
  116.8 5.2 %collective-permute-start.37 = (f32[64,768]{1,0:T(8,128)S(1)}, f32[64,768]{1,0:T(8,128)S(1)}, u32[]{:S(2)}, u32[]{:S(2)}) collective-permute-start(f32[64,768]{1,0:T(8,128)S(1)} %get-tuple-element.121.refs_7_.refs_0_), channel_id=1, source_target_pairs={{1,2},{2,1},{5,6},{6,5},{9,10},{10,9},{13,14},{14,13},{17,18},{18,... | collective-permute-start | bytes 589832 | tf_op jit(solution)/shard_map/ppermute | solution.py:337
  117.5 8.9 %collective-permute-start.38 = (f32[64,768]{1,0:T(8,128)S(1)}, f32[64,768]{1,0:T(8,128)S(1)}, u32[]{:S(2)}, u32[]{:S(2)}) collective-permute-start(f32[64,768]{1,0:T(8,128)S(1)} %get-tuple-element.124.refs_2_), channel_id=1, source_target_pairs={{0,1},{1,0},{2,3},{3,2},{4,5},{5,4},{6,7},{7,6},{8,9},{9,8},{10,11... | collective-permute-start | bytes 589832 | tf_op jit(solution)/shard_map/ppermute | solution.py:334
  120.6 12.2 %collective-permute-start.29 = (f32[1,3,64,768]{3,2,1,0:T(8,128)S(1)}, f32[1,3,64,768]{3,2,1,0:T(8,128)S(1)}, u32[]{:S(2)}, u32[]{:S(2)}) collective-permute-start(f32[1,3,64,768]{3,2,1,0:T(8,128)S(1)} %get-tuple-element.114), channel_id=1, source_target_pairs={{0,16},{4,20},{8,24},{12,28},{16,0},{20,4},{24,8},{28,12},{1,17},{... | collective-permute-start | bytes 1769480 | tf_op jit(solution)/shard_map/ppermute | solution.py:443
  120.6 12.2 %collective-permute-start.30 = (f32[1,3,64,768]{3,2,1,0:T(8,128)S(1)}, f32[1,3,64,768]{3,2,1,0:T(8,128)S(1)}, u32[]{:S(2)}, u32[]{:S(2)}) collective-permute-start(f32[1,3,64,768]{3,2,1,0:T(8,128)S(1)} %get-tuple-element.116), channel_id=1, source_target_pairs={{0,8},{4,12},{8,0},{12,4},{16,24},{20,28},{24,16},{28,20},{1,9},{5... | collective-permute-start | bytes 1769480 | tf_op jit(solution)/shard_map/ppermute | solution.py:443
  121.4 7.2 %collective-permute-start.35 = (f32[64,768]{1,0:T(8,128)S(1)}, f32[64,768]{1,0:T(8,128)S(1)}, u32[]{:S(2)}, u32[]{:S(2)}) collective-permute-start(f32[64,768]{1,0:T(8,128)S(1)} %get-tuple-element.122.refs_5_.refs_0_), channel_id=1, source_target_pairs={{1,2},{2,1},{5,6},{6,5},{9,10},{10,9},{13,14},{14,13},{17,18},{18,... | collective-permute-start | bytes 589832 | tf_op jit(solution)/shard_map/ppermute | solution.py:337
  122.1 8.8 %collective-permute-start.36 = (f32[64,768]{1,0:T(8,128)S(1)}, f32[64,768]{1,0:T(8,128)S(1)}, u32[]{:S(2)}, u32[]{:S(2)}) collective-permute-start(f32[64,768]{1,0:T(8,128)S(1)} %get-tuple-element.123.refs_2_), channel_id=1, source_target_pairs={{0,1},{1,0},{2,3},{3,2},{4,5},{5,4},{6,7},{7,6},{8,9},{9,8},{10,11... | collective-permute-start | bytes 589832 | tf_op jit(solution)/shard_map/ppermute | solution.py:334
  126.4 7.5 %collective-permute-start.40 = (f32[64,768]{1,0:T(8,128)S(1)}, f32[64,768]{1,0:T(8,128)S(1)}, u32[]{:S(2)}, u32[]{:S(2)}) collective-permute-start(f32[64,768]{1,0:T(8,128)S(1)} %get-tuple-element.127.refs_5_.refs_0_), channel_id=1, source_target_pairs={{0,1},{1,0},{2,3},{3,2},{4,5},{5,4},{6,7},{7,6},{8,9},{9,8},{10,11... | collective-permute-start | bytes 589832 | tf_op jit(solution)/shard_map/ppermute | solution.py:334
  130.9 5.7 %collective-permute-start.39 = (f32[64,768]{1,0:T(8,128)S(1)}, f32[64,768]{1,0:T(8,128)S(1)}, u32[]{:S(2)}, u32[]{:S(2)}) collective-permute-start(f32[64,768]{1,0:T(8,128)S(1)} %get-tuple-element.128.refs_4_.refs_3_.refs_0_), channel_id=1, source_target_pairs={{0,1},{1,0},{2,3},{3,2},{4,5},{5,4},{6,7},{7,6},{8,9},{9,8},{10,11... | collective-permute-start | bytes 589832 | tf_op jit(solution)/shard_map/ppermute | solution.py:334
